TPU v7x, 32 devices: a whole 2x2x4 slice. The times are simulated.
32 devices in a mesh: section: 4 (over y, core), row: 4 (over z), col: 2 (over x).
Axes of the slice: x: 2, y: 2, z: 4, core: 2. Of those that a mesh axis runs over, the one named last changes fastest.
Arguments:
- inputs: bfloat16 [4, 768, 5120], P('section', 'row', 'col'), may hold values from -12 to 12
- down_weight: bfloat16 [4, 512, 5120], P('section', 'row', 'col'), may hold values from -5 to 5
- up_weight: bfloat16 [4, 512, 8192], P('section', 'row', 'col'), may hold values from -0.25 to 0.25
- value_grad: bfloat16 [4, 768, 8192], P('section', 'row', 'col'), may hold values from -1.1953125 to 1.1953125
Outputs:
- passed_grad: bfloat16 [4, 768, 5120], P('section', 'row', 'col')
- down_grad: bfloat16 [4, 512, 5120], P('section', 'row', 'col')
- up_grad: bfloat16 [4, 512, 8192], P('section', 'row', 'col')
All inputs are finite; a program needn't handle non-finite values.
Results may differ from a plain program's by a relative error of at most 0.03.
Values may be sent and summed in bfloat16 or wider, within the bound.
No kernel may reach another device: no remote copies, remote signals or barrier semaphores. Data moves between devices by JAX's collectives and lax.ppermute only.
A program may use at most 64 MiB of HBM per device.

v0:
```python
import jax
import jax.numpy as jnp
from jax import lax
from jax.sharding import PartitionSpec as P

F32 = jnp.float32
BF16 = jnp.bfloat16


def shifted(value, axis, steps):
    count = lax.axis_size(axis)
    leading, last = (max(0, -steps), min(count, count - steps))
    return lax.ppermute(value, axis, [(source, source + steps) for source in range(leading, last)])


def general_body(inputs, down_weight, up_weight, value_grad):
    tokens = inputs[0]
    cotangent = value_grad[0]
    down_full = lax.all_gather(down_weight[0], "row", axis=0, tiled=True)
    up_full = lax.all_gather(up_weight[0], "row", axis=0, tiled=True)
    latent_part = jnp.einsum("td,ld->tl", tokens, down_full, preferred_element_type=F32)
    grad_part = jnp.einsum("tf,lf->tl", cotangent, up_full, preferred_element_type=F32)
    latent = lax.psum(latent_part.astype(BF16), "col").astype(F32)
    normed_grad = lax.psum(grad_part.astype(BF16), "col").astype(F32)
    inv_rms = lax.rsqrt(jnp.mean(latent * latent, axis=-1, keepdims=True) + 1e-06)
    normed = latent * inv_rms
    normed_bf = normed.astype(BF16)
    inner = jnp.mean(normed_grad * normed, axis=-1, keepdims=True)
    latent_bf = (inv_rms * (normed_grad - normed * inner)).astype(BF16)
    up_grad = lax.psum_scatter(
        jnp.einsum("tl,tf->lf", normed_bf, cotangent, preferred_element_type=F32).astype(BF16),
        "row",
        scatter_dimension=0,
        tiled=True,
    )
    down_grad = lax.psum_scatter(
        jnp.einsum("tl,td->ld", latent_bf, tokens, preferred_element_type=F32).astype(BF16),
        "row",
        scatter_dimension=0,
        tiled=True,
    )
    input_grad = jnp.einsum("tl,ld->td", latent_bf, down_full, preferred_element_type=F32)
    passed = shifted(input_grad.astype(BF16), "section", -1)
    return (passed[None], down_grad[None], up_grad[None])


def inward(value):
    return lax.ppermute(value, "row", [(0, 1), (3, 2)])


def across(value):
    return lax.ppermute(value, "row", [(1, 2), (2, 1)])


def outward(value):
    return lax.ppermute(value, "row", [(1, 0), (2, 3)])


def other_col(value):
    return lax.ppermute(value, "col", [(0, 1), (1, 0)])


def after(value, *earlier):
    return lax.optimization_barrier((value, *earlier))[0]


def rows_dot(left, right):
    return lax.dot_general(left, right, (((1,), (1,)), ((), ())), preferred_element_type=F32)


def tokens_dot(left, right):
    return lax.dot_general(left, right, (((0,), (0,)), ((), ())), preferred_element_type=F32)


def col_sum(part):
    sent = part.astype(BF16)
    return sent.astype(F32) + other_col(sent).astype(F32)


def folded_body(inputs, down_weight, up_weight, value_grad):
    tokens, down, up, cotangent = inputs[0], down_weight[0], up_weight[0], value_grad[0]
    rows, width = tokens.shape
    lat = down.shape[0]
    feat = cotangent.shape[1]
    sections = lax.axis_size("section")
    place = lax.axis_index("row")
    middle = (place == 1) | (place == 2)

    half = feat // 2
    cuts = (slice(0, half), slice(half, feat))
    cot_own = [cotangent[:, cut] for cut in cuts]
    down_end = inward(down)
    down_other = across(down)
    cot_end_first = inward(cot_own[0])
    cot_other = across(cotangent)
    tokens_end = inward(tokens)
    down_other_end = across(down_end)
    cot_other_end_first = across(cot_end_first)
    cot_end_second = inward(after(cot_own[1], down_end, down_other))
    up_end = inward(after(up, tokens_end, cot_end_first))

    tokens_mine = jnp.concatenate([tokens, tokens_end], axis=0)
    down_all = jnp.concatenate([down, down_end, down_other, down_other_end], axis=0)
    latent = col_sum(rows_dot(tokens_mine, down_all))
    inv_rms = lax.rsqrt(jnp.mean(latent * latent, axis=-1, keepdims=True) + 1e-06)
    normed = latent * inv_rms
    normed_bf = normed.astype(BF16)
    normed_sent = normed_bf[:, 2 * lat :]
    normed_other = across(normed_sent)
    normed_all = jnp.concatenate([normed_bf[:, : 2 * lat], normed_other], axis=0)

    cot_end = (cot_end_first, cot_end_second)
    cot_other_end = (cot_other_end_first, across(after(cot_end_second, normed_sent)))

    up_local, up_back = [], []
    for k, cut in enumerate(cuts):
        values = jnp.concatenate(
            [cotangent[:, cut], cot_end[k], cot_other[:, cut], cot_other_end[k]], axis=0
        )
        up_piece = tokens_dot(normed_all, values).astype(BF16)
        up_local.append(up_piece)
        up_back.append(outward(up_piece[lat:]))
    up_grad = jnp.concatenate(
        [jnp.where(middle, piece[:lat], back) for piece, back in zip(up_local, up_back)], axis=1
    )

    up_mine = jnp.concatenate([up, after(up_end, up_local[0])], axis=0)
    early = rows_dot(jnp.concatenate([cotangent, cot_other], axis=0), up_mine)
    early_end = sum(rows_dot(cot_end[k], up_mine[:, cut]) for k, cut in enumerate(cuts))
    late = sum(rows_dot(cot_other_end[k], up_mine[:, cut]) for k, cut in enumerate(cuts))
    early = col_sum(jnp.concatenate([early, early_end], axis=0))
    late = col_sum(late)

    def latent_grad(which, mine, other):
        normed_grad = jnp.concatenate([mine, other.astype(F32)], axis=1)
        inner = jnp.mean(normed_grad * normed[which], axis=-1, keepdims=True)
        return (inv_rms[which] * (normed_grad - normed[which] * inner)).astype(BF16)

    own_rows, end_rows = slice(0, rows), slice(rows, 2 * rows)
    grad_own = across(early[rows : 2 * rows].astype(BF16))
    grad_end = across(late.astype(BF16))
    latent_own = latent_grad(own_rows, early[:rows], grad_own)
    latent_end = latent_grad(end_rows, early[2 * rows :], grad_end)
    latent_bf = jnp.concatenate([latent_own, latent_end], axis=0)
    sums = [
        tokens_dot(latent_bf[:, j * lat : (j + 1) * lat], tokens_mine) for j in range(4)
    ]
    sent_end, sent_own = sums[3].astype(BF16), sums[2].astype(BF16)
    from_end, from_own = across(sent_end), across(sent_own)
    down_end_grad = outward((sums[1] + from_end.astype(F32)).astype(BF16))
    down_own_grad = (sums[0] + from_own.astype(F32)).astype(BF16)
    down_grad = jnp.where(middle, down_own_grad, down_end_grad)

    latent_bf = after(latent_bf, sent_end, sent_own)
    input_grad = jnp.dot(latent_bf, down_all, preferred_element_type=F32).astype(BF16)
    passed_end = lax.ppermute(
        input_grad[rows:],
        ("section", "row"),
        [
            (4 * s + source, 4 * (s - 1) + target)
            for s in range(1, sections)
            for source, target in ((1, 0), (2, 3))
        ],
    )
    passed_own = shifted(after(input_grad[:rows], from_end), "section", -1)
    passed = jnp.where(middle, passed_own, passed_end)
    return (passed[None], down_grad[None], up_grad[None])


def solution(mesh):
    spec = P("section", "row", "col")
    folds = mesh.shape["row"] == 4 and mesh.shape["col"] == 2
    return jax.shard_map(
        folded_body if folds else general_body,
        mesh=mesh,
        in_specs=(spec,) * 4,
        out_specs=(spec,) * 3,
        check_vma=False,
    )
```

profile of v0, /device:TPU:4, one launch (start us, length us, event | category | flops | bytes accessed | tf_op | source)
XLA Modules:
  0.0 172.9 jit_solution(15152167685777739388)
XLA Ops:
  0.6 0.0 copy-start.16
  0.7 3.7 %collective-permute-start.1 = (bf16[128,2560]{1,0:T(8,128)(2,1)}, bf16[128,2560]{1,0:T(8,128)(2,1)S(1)}, u32[]{:S(2)}, u32[]{:S(2)}) collective-permute-start(bf16[128,2560]{1,0:T(8,128)(2,1)} %bitcast.43), channel_id=1, source_target_pairs={{0,2},{6,4},{1,3},{7,5},{8,10},{14,12},{9,11},{15,13},{16,18},{22,... | collective-permute-start | bytes 1966088 | tf_op jit(solution)/shard_map/ppermute | solution.py:48
  4.3 1.4 collective-permute-start
  5.7 0.7 collective-permute-start.2
  6.4 13.3 %collective-permute-done.1 = bf16[128,2560]{1,0:T(8,128)(2,1)S(1)} collective-permute-done((bf16[128,2560]{1,0:T(8,128)(2,1)}, bf16[128,2560]{1,0:T(8,128)(2,1)S(1)}, u32[]{:S(2)}, u32[]{:S(2)}) %collective-permute-start.1) | collective-permute-done | bytes 655392 | tf_op jit(solution)/shard_map/ppermute | solution.py:48
  19.7 0.7 collective-permute-start.3
  20.4 0.8 collective-permute-start.5
  21.2 1.5 fusion.63
  22.8 8.8 %collective-permute-start.6 = (bf16[192,2048]{1,0:T(8,128)(2,1)S(1)}, bf16[192,2048]{1,0:T(8,128)(2,1)S(1)}, u32[]{:S(2)}, u32[]{:S(2)}) collective-permute-start(bf16[192,2048]{1,0:T(8,128)(2,1)S(1)} %get-tuple-element.23), channel_id=1, source_target_pairs={{0,2},{6,4},{1,3},{7,5},{8,10},{14,12},{9,11},{15,13},{16,18},{22,... | collective-permute-start | bytes 2359304 | tf_op jit(solution)/shard_map/ppermute | solution.py:48
  31.6 9.2 %collective-permute-done = bf16[192,2560]{1,0:T(8,128)(2,1)S(1)} collective-permute-done((bf16[192,2560]{1,0:T(8,128)(2,1)}, bf16[192,2560]{1,0:T(8,128)(2,1)S(1)}, u32[]{:S(2)}, u32[]{:S(2)}) %collective-permute-start) | collective-permute-done | bytes 983072 | tf_op jit(solution)/shard_map/ppermute | solution.py:48
  40.8 1.2 convolution_convert_fusion.3
  42.1 1.6 collective-permute-start.4
  43.6 5.2 %collective-permute-start.10 = (bf16[192,2048]{1,0:T(8,128)(2,1)S(1)}, bf16[192,2048]{1,0:T(8,128)(2,1)}, u32[]{:S(2)}, u32[]{:S(2)}) collective-permute-start(bf16[192,2048]{1,0:T(8,128)(2,1)S(1)} %get-tuple-element.11), channel_id=1, source_target_pairs={{0,2},{6,4},{1,3},{7,5},{8,10},{14,12},{9,11},{15,13},{16,18},{22,... | collective-permute-start | bytes 2359304 | tf_op jit(solution)/shard_map/ppermute | solution.py:48
  48.8 8.7 %collective-permute-done.6 = bf16[192,2048]{1,0:T(8,128)(2,1)S(1)} collective-permute-done((bf16[192,2048]{1,0:T(8,128)(2,1)S(1)}, bf16[192,2048]{1,0:T(8,128)(2,1)S(1)}, u32[]{:S(2)}, u32[]{:S(2)}) %collective-permute-start.6) | collective-permute-done | bytes 786464 | tf_op jit(solution)/shard_map/ppermute | solution.py:48
  57.5 0.7 collective-permute-start.9
  58.2 7.2 %collective-permute-start.7 = (bf16[128,4096]{1,0:T(8,128)(2,1)S(1)}, bf16[128,4096]{1,0:T(8,128)(2,1)S(1)}, u32[]{:S(2)}, u32[]{:S(2)}) collective-permute-start(bf16[128,4096]{1,0:T(8,128)(2,1)S(1)} %bitcast.32), channel_id=1, source_target_pairs={{0,2},{6,4},{1,3},{7,5},{8,10},{14,12},{9,11},{15,13},{16,18},{22,... | collective-permute-start | bytes 3145736 | tf_op jit(solution)/shard_map/ppermute | solution.py:48
  65.5 0.2 multiply_reduce_fusion
  65.7 0.2 fusion.59
  65.9 0.7 collective-permute-start.8
  66.6 1.1 fusion.62
  67.7 6.7 %collective-permute-done.10 = bf16[192,2048]{1,0:T(8,128)(2,1)} collective-permute-done((bf16[192,2048]{1,0:T(8,128)(2,1)S(1)}, bf16[192,2048]{1,0:T(8,128)(2,1)}, u32[]{:S(2)}, u32[]{:S(2)}) %collective-permute-start.10) | collective-permute-done | bytes 786464 | tf_op jit(solution)/shard_map/ppermute | solution.py:48
  74.4 1.5 collective-permute-start.13
  75.9 0.9 copy-done.14
  76.8 2.0 %fusion.27 = bf16[256,2048]{1,0:T(8,128)(2,1)} fusion(bf16[192,2048]{1,0:T(8,128)(2,1)S(1)} %collective-permute-done.9, bf16[192,2048]{1,0:T(8,128)(2,1)S(1)} %get-tuple-element.22, bf16[192,2048]{1,0:T(8,128)(2,1)S(1)} %collective-permute-done.6, bf16[192,2048]{1,0:T(8,128)(2,1)S(1)} %get-tuple-element.23, ...), kind=kOutput, calls=%fused_computation.36 | convolution fusion | flops 819200000 | bytes 4587520 | tf_op jit(solution)/shard_map/dot_general | solution.py:72
  78.9 16.8 %collective-permute-done.7 = bf16[128,4096]{1,0:T(8,128)(2,1)S(1)} collective-permute-done((bf16[128,4096]{1,0:T(8,128)(2,1)S(1)}, bf16[128,4096]{1,0:T(8,128)(2,1)S(1)}, u32[]{:S(2)}, u32[]{:S(2)}) %collective-permute-start.7) | collective-permute-done | bytes 1048608 | tf_op jit(solution)/shard_map/ppermute | solution.py:48
  95.7 0.1 fusion.38
  95.8 1.1 fusion.30
  96.9 1.6 fusion.67
  98.5 0.5 fusion.35
  99.1 1.6 collective-permute-start.11
  100.6 0.1 fusion.66
  100.7 1.1 slice.134
  101.8 1.4 collective-permute-start.21
  103.3 3.9 %collective-permute-done.11 = bf16[576,256]{1,0:T(8,128)(2,1)} collective-permute-done((bf16[576,256]{1,0:T(8,128)(2,1)S(1)}, bf16[576,256]{1,0:T(8,128)(2,1)}, u32[]{:S(2)}, u32[]{:S(2)}) %collective-permute-start.11) | collective-permute-done | bytes 294944 | tf_op jit(solution)/shard_map/ppermute | solution.py:60
  107.1 1.0 convert_add_fusion.1
  108.2 0.7 collective-permute-start.12
  108.9 1.6 fusion.68
  110.6 0.5 fusion.36
  111.2 1.6 collective-permute-start.14
  112.7 3.9 %collective-permute-done.21 = bf16[128,2048]{1,0:T(8,128)(2,1)S(1)} collective-permute-done((bf16[128,2048]{1,0:T(8,128)(2,1)S(1)}, bf16[128,2048]{1,0:T(8,128)(2,1)S(1)}, u32[]{:S(2)}, u32[]{:S(2)}) %collective-permute-start.21) | collective-permute-done | bytes 524320 | tf_op jit(solution)/shard_map/ppermute | solution.py:56
  116.6 0.1 slice_select_fusion.1
  116.7 0.7 collective-permute-start.15
  117.5 2.4 %fusion.24 = bf16[256,2048]{1,0:T(8,128)(2,1)S(1)} fusion(bf16[192,2048]{1,0:T(8,128)(2,1)} %collective-permute-done.13, bf16[192,2048]{1,0:T(8,128)(2,1)S(1)} %copy-done.7, bf16[192,2048]{1,0:T(8,128)(2,1)} %collective-permute-done.10, bf16[192,2048]{1,0:T(8,128)(2,1)S(1)} %copy-done.6, bf16[384,256]{1,0:T(8,128)(2,1)S(1)} %copy-done.25, ...), kind=kOutput, calls=%fused_computation.35 | convolution fusion | flops 819200000 | bytes 4587520 | tf_op jit(solution)/shard_map/dot_general | solution.py:72
  119.9 1.3 collective-permute-start.22
  121.2 0.2 multiply_reduce_fusion.2
  121.4 0.2 multiply_convert_fusion.1
  121.7 0.7 copy-done.11
  122.4 0.3 copy-done.13
  122.7 0.5 convolution_convert_fusion.2
  123.3 0.8 collective-permute-start.16
  124.1 0.5 convolution_convert_fusion.1
  124.7 0.7 collective-permute-start.19
  125.4 1.4 convolution_convert_fusion
  126.8 0.1 fusion.61
  127.0 1.3 collective-permute-start.18
  128.3 0.5 fusion.1
  128.8 1.3 collective-permute-start.20
  130.1 1.9 %collective-permute-start.17 = (bf16[192,2560]{1,0:T(8,128)(2,1)S(1)}, bf16[192,2560]{1,0:T(8,128)(2,1)S(1)}, u32[]{:S(2)}, u32[]{:S(2)}) collective-permute-start(bf16[192,2560]{1,0:T(8,128)(2,1)S(1)} %get-tuple-element.14), channel_id=1, source_target_pairs={{8,0},{16,8},{24,16},{9,1},{17,9},{25,17},{10,2},{18,10},{26,18},{... | collective-permute-start | bytes 2949128 | tf_op jit(solution)/shard_map/ppermute | solution.py:13
  132.1 3.8 %collective-permute-done.22 = bf16[128,2048]{1,0:T(8,128)(2,1)S(1)} collective-permute-done((bf16[128,2048]{1,0:T(8,128)(2,1)S(1)}, bf16[128,2048]{1,0:T(8,128)(2,1)S(1)}, u32[]{:S(2)}, u32[]{:S(2)}) %collective-permute-start.22) | collective-permute-done | bytes 524320 | tf_op jit(solution)/shard_map/ppermute | solution.py:56
  135.8 0.1 slice_select_fusion
  135.9 1.1 maximum_bitcast_fusion
  136.9 33.4 %collective-permute-done.20 = bf16[128,2560]{1,0:T(8,128)(2,1)S(1)} collective-permute-done((bf16[128,2560]{1,0:T(8,128)(2,1)S(1)}, bf16[128,2560]{1,0:T(8,128)(2,1)S(1)}, u32[]{:S(2)}, u32[]{:S(2)}) %collective-permute-start.20) | collective-permute-done | bytes 655392 | tf_op jit(solution)/shard_map/ppermute | solution.py:56
  170.4 1.4 fusion.3
  171.8 1.0 select_bitcast_fusion
  (73 shorter events, 0.4 us)
Async XLA Ops:
  0.6 40.2 %copy-start.16 = (bf16[1,128,2560]{2,1,0:T(8,128)(2,1)S(1)}, bf16[1,128,2560]{2,1,0:T(8,128)(2,1)}, u32[]{:S(2)}) copy-start(bf16[1,128,2560]{2,1,0:T(8,128)(2,1)} %param.5) | copy-start | bytes 1966084
  0.6 40.1 %copy-start.10 = (bf16[1,192,2560]{2,1,0:T(8,128)(2,1)S(1)}, bf16[1,192,2560]{2,1,0:T(8,128)(2,1)}, u32[]{:S(2)}) copy-start(bf16[1,192,2560]{2,1,0:T(8,128)(2,1)} %param.4) | copy-start | bytes 2949124
  0.7 19.1 %collective-permute-start.1 = (bf16[128,2560]{1,0:T(8,128)(2,1)}, bf16[128,2560]{1,0:T(8,128)(2,1)S(1)}, u32[]{:S(2)}, u32[]{:S(2)}) collective-permute-start(bf16[128,2560]{1,0:T(8,128)(2,1)} %bitcast.43), channel_id=1, source_target_pairs={{0,2},{6,4},{1,3},{7,5},{8,10},{14,12},{9,11},{15,13},{16,18},{22,... | collective-permute-start | bytes 1966088 | tf_op jit(solution)/shard_map/ppermute | solution.py:48
  4.3 36.5 %collective-permute-start = (bf16[192,2560]{1,0:T(8,128)(2,1)}, bf16[192,2560]{1,0:T(8,128)(2,1)S(1)}, u32[]{:S(2)}, u32[]{:S(2)}) collective-permute-start(bf16[192,2560]{1,0:T(8,128)(2,1)} %bitcast.37), channel_id=1, source_target_pairs={{0,2},{6,4},{1,3},{7,5},{8,10},{14,12},{9,11},{15,13},{16,18},{22,... | collective-permute-start | bytes 2949128 | tf_op jit(solution)/shard_map/ppermute | solution.py:48
  5.7 25.9 %collective-permute-start.2 = (bf16[128,2560]{1,0:T(8,128)(2,1)}, bf16[128,2560]{1,0:T(8,128)(2,1)S(1)}, u32[]{:S(2)}, u32[]{:S(2)}) collective-permute-start(bf16[128,2560]{1,0:T(8,128)(2,1)} %bitcast.44), channel_id=1, source_target_pairs={{2,4},{4,2},{3,5},{5,3},{10,12},{12,10},{11,13},{13,11},{18,20},{2... | collective-permute-start | bytes 1966088 | tf_op jit(solution)/shard_map/ppermute | solution.py:52
  19.7 22.3 %copy-start.18 = (bf16[128,2560]{1,0:T(8,128)(2,1)}, bf16[128,2560]{1,0:T(8,128)(2,1)S(1)}, u32[]{:S(2)}) copy-start(bf16[128,2560]{1,0:T(8,128)(2,1)S(1)} %collective-permute-done.1) | copy-start | bytes 1966084
  19.7 21.1 %collective-permute-start.3 = (bf16[128,2560]{1,0:T(8,128)(2,1)S(1)}, bf16[128,2560]{1,0:T(8,128)(2,1)S(1)}, u32[]{:S(2)}, u32[]{:S(2)}) collective-permute-start(bf16[128,2560]{1,0:T(8,128)(2,1)S(1)} %collective-permute-done.1), channel_id=1, source_target_pairs={{2,4},{4,2},{3,5},{5,3},{10,12},{12,10},{11,13},{13,11},{18,20},{2... | collective-permute-start | bytes 1966088 | tf_op jit(solution)/shard_map/ppermute | solution.py:52
  20.4 46.2 %collective-permute-start.5 = (bf16[192,4096]{1,0:T(8,128)(2,1)}, bf16[192,4096]{1,0:T(8,128)(2,1)S(1)}, u32[]{:S(2)}, u32[]{:S(2)}) collective-permute-start(bf16[192,4096]{1,0:T(8,128)(2,1)} %bitcast.29), channel_id=1, source_target_pairs={{2,4},{4,2},{3,5},{5,3},{10,12},{12,10},{11,13},{13,11},{18,20},{2... | collective-permute-start | bytes 4718600 | tf_op jit(solution)/shard_map/ppermute | solution.py:52
  22.7 20.9 %copy-start.5 = (bf16[192,2048]{1,0:T(8,128)(2,1)}, bf16[192,2048]{1,0:T(8,128)(2,1)S(1)}, u32[]{:S(2)}) copy-start(bf16[192,2048]{1,0:T(8,128)(2,1)S(1)} %get-tuple-element.11) | copy-start | bytes 2359300
  22.7 35.5 %copy-start.1 = (bf16[1,128,4096]{2,1,0:T(8,128)(2,1)S(1)}, bf16[1,128,4096]{2,1,0:T(8,128)(2,1)}, u32[]{:S(2)}) copy-start(bf16[1,128,4096]{2,1,0:T(8,128)(2,1)} %param.6) | copy-start | bytes 3145732
  22.8 34.8 %collective-permute-start.6 = (bf16[192,2048]{1,0:T(8,128)(2,1)S(1)}, bf16[192,2048]{1,0:T(8,128)(2,1)S(1)}, u32[]{:S(2)}, u32[]{:S(2)}) collective-permute-start(bf16[192,2048]{1,0:T(8,128)(2,1)S(1)} %get-tuple-element.23), channel_id=1, source_target_pairs={{0,2},{6,4},{1,3},{7,5},{8,10},{14,12},{9,11},{15,13},{16,18},{22,... | collective-permute-start | bytes 2359304 | tf_op jit(solution)/shard_map/ppermute | solution.py:48
  31.6 10.4 %copy-start.20 = (bf16[128,2560]{1,0:T(8,128)(2,1)}, bf16[128,2560]{1,0:T(8,128)(2,1)S(1)}, u32[]{:S(2)}) copy-start(bf16[128,2560]{1,0:T(8,128)(2,1)S(1)} %collective-permute-done.2) | copy-start | bytes 1966084
  40.8 1.3 copy-start.12
  40.8 1.3 copy-start.22
  42.1 23.4 %collective-permute-start.4 = (bf16[384,512]{1,0:T(8,128)(2,1)S(1)}, bf16[384,512]{1,0:T(8,128)(2,1)S(1)}, u32[]{:S(2)}, u32[]{:S(2)}) collective-permute-start(bf16[384,512]{1,0:T(8,128)(2,1)S(1)} %convolution_convert_fusion.3), channel_id=1, source_target_pairs={{0,1},{1,0},{2,3},{3,2},{4,5},{5,4},{6,7},{7,6},{8,9},{9,8},{10,11... | collective-permute-start | bytes 1179656 | tf_op jit(solution)/shard_map/ppermute | solution.py:60
  43.6 30.8 %collective-permute-start.10 = (bf16[192,2048]{1,0:T(8,128)(2,1)S(1)}, bf16[192,2048]{1,0:T(8,128)(2,1)}, u32[]{:S(2)}, u32[]{:S(2)}) collective-permute-start(bf16[192,2048]{1,0:T(8,128)(2,1)S(1)} %get-tuple-element.11), channel_id=1, source_target_pairs={{0,2},{6,4},{1,3},{7,5},{8,10},{14,12},{9,11},{15,13},{16,18},{22,... | collective-permute-start | bytes 2359304 | tf_op jit(solution)/shard_map/ppermute | solution.py:48
  57.5 18.4 %collective-permute-start.9 = (bf16[192,2048]{1,0:T(8,128)(2,1)S(1)}, bf16[192,2048]{1,0:T(8,128)(2,1)S(1)}, u32[]{:S(2)}, u32[]{:S(2)}) collective-permute-start(bf16[192,2048]{1,0:T(8,128)(2,1)S(1)} %collective-permute-done.6), channel_id=1, source_target_pairs={{2,4},{4,2},{3,5},{5,3},{10,12},{12,10},{11,13},{13,11},{18,20},{2... | collective-permute-start | bytes 2359304 | tf_op jit(solution)/shard_map/ppermute | solution.py:52
  58.2 37.5 %collective-permute-start.7 = (bf16[128,4096]{1,0:T(8,128)(2,1)S(1)}, bf16[128,4096]{1,0:T(8,128)(2,1)S(1)}, u32[]{:S(2)}, u32[]{:S(2)}) collective-permute-start(bf16[128,4096]{1,0:T(8,128)(2,1)S(1)} %bitcast.32), channel_id=1, source_target_pairs={{0,2},{6,4},{1,3},{7,5},{8,10},{14,12},{9,11},{15,13},{16,18},{22,... | collective-permute-start | bytes 3145736 | tf_op jit(solution)/shard_map/ppermute | solution.py:48
  65.9 13.0 %copy-start.8 = (bf16[384,256]{1,0:T(8,128)(2,1)}, bf16[384,256]{1,0:T(8,128)(2,1)S(1)}, u32[]{:S(2)}) copy-start(bf16[384,256]{1,0:T(8,128)(2,1)S(1)} %get-tuple-element.29) | copy-start | bytes 589828
  65.9 10.0 %collective-permute-start.8 = (bf16[384,256]{1,0:T(8,128)(2,1)S(1)}, bf16[384,256]{1,0:T(8,128)(2,1)S(1)}, u32[]{:S(2)}, u32[]{:S(2)}) collective-permute-start(bf16[384,256]{1,0:T(8,128)(2,1)S(1)} %get-tuple-element.30), channel_id=1, source_target_pairs={{2,4},{4,2},{3,5},{5,3},{10,12},{12,10},{11,13},{13,11},{18,20},{2... | collective-permute-start | bytes 589832 | tf_op jit(solution)/shard_map/ppermute | solution.py:52
  74.4 34.5 %collective-permute-start.13 = (bf16[192,2048]{1,0:T(8,128)(2,1)}, bf16[192,2048]{1,0:T(8,128)(2,1)}, u32[]{:S(2)}, u32[]{:S(2)}) collective-permute-start(bf16[192,2048]{1,0:T(8,128)(2,1)} %collective-permute-done.10), channel_id=1, source_target_pairs={{2,4},{4,2},{3,5},{5,3},{10,12},{12,10},{11,13},{13,11},{18,20},{2... | collective-permute-start | bytes 2359304 | tf_op jit(solution)/shard_map/ppermute | solution.py:52
  75.9 0.9 copy-start.14
  75.9 3.0 %copy-start.24 = (bf16[384,256]{1,0:T(8,128)(2,1)}, bf16[384,256]{1,0:T(8,128)(2,1)S(1)}, u32[]{:S(2)}) copy-start(bf16[384,256]{1,0:T(8,128)(2,1)S(1)} %collective-permute-done.8) | copy-start | bytes 589828
  78.9 16.9 %copy-start = (bf16[1,192,4096]{2,1,0:T(8,128)(2,1)S(1)}, bf16[1,192,4096]{2,1,0:T(8,128)(2,1)}, u32[]{:S(2)}) copy-start(bf16[1,192,4096]{2,1,0:T(8,128)(2,1)} %param.7) | copy-start | bytes 4718596
  95.7 2.8 %copy-start.2 = (bf16[128,4096]{1,0:T(8,128)(2,1)}, bf16[128,4096]{1,0:T(8,128)(2,1)S(1)}, u32[]{:S(2)}) copy-start(bf16[128,4096]{1,0:T(8,128)(2,1)S(1)} %collective-permute-done.7) | copy-start | bytes 3145732
  99.1 8.1 %collective-permute-start.11 = (bf16[576,256]{1,0:T(8,128)(2,1)S(1)}, bf16[576,256]{1,0:T(8,128)(2,1)}, u32[]{:S(2)}, u32[]{:S(2)}) collective-permute-start(bf16[576,256]{1,0:T(8,128)(2,1)S(1)} %pad_maximum_fusion.12), channel_id=1, source_target_pairs={{0,1},{1,0},{2,3},{3,2},{4,5},{5,4},{6,7},{7,6},{8,9},{9,8},{10,11... | collective-permute-start | bytes 884744 | tf_op jit(solution)/shard_map/ppermute | solution.py:60
  101.8 8.8 %copy-start.3 = (bf16[128,4096]{1,0:T(8,128)(2,1)S(1)}, bf16[128,4096]{1,0:T(8,128)(2,1)}, u32[]{:S(2)}) copy-start(bf16[128,4096]{1,0:T(8,128)(2,1)} %copy-done.2) | copy-start | bytes 3145732
  101.8 8.8 %copy-start.15 = (bf16[192,2048]{1,0:T(8,128)(2,1)S(1)}, bf16[192,2048]{1,0:T(8,128)(2,1)}, u32[]{:S(2)}) copy-start(bf16[192,2048]{1,0:T(8,128)(2,1)} %copy-done.14) | copy-start | bytes 2359300
  101.8 14.8 %collective-permute-start.21 = (bf16[128,2048]{1,0:T(8,128)(2,1)S(1)}, bf16[128,2048]{1,0:T(8,128)(2,1)S(1)}, u32[]{:S(2)}, u32[]{:S(2)}) collective-permute-start(bf16[128,2048]{1,0:T(8,128)(2,1)S(1)} %slice.134), channel_id=1, source_target_pairs={{2,0},{4,6},{3,1},{5,7},{10,8},{12,14},{11,9},{13,15},{18,16},{20,... | collective-permute-start | bytes 1572872 | tf_op jit(solution)/shard_map/ppermute | solution.py:56
  108.2 8.5 %collective-permute-start.12 = (bf16[192,256]{1,0:T(8,128)(2,1)S(1)}, bf16[192,256]{1,0:T(8,128)(2,1)S(1)}, u32[]{:S(2)}, u32[]{:S(2)}) collective-permute-start(bf16[192,256]{1,0:T(8,128)(2,1)S(1)} %slice.193), channel_id=1, source_target_pairs={{2,4},{4,2},{3,5},{5,3},{10,12},{12,10},{11,13},{13,11},{18,20},{2... | collective-permute-start | bytes 294920 | tf_op jit(solution)/shard_map/ppermute | solution.py:52
  110.6 6.0 %copy-start.4 = (bf16[256,2048]{1,0:T(8,128)(2,1)S(1)}, bf16[256,2048]{1,0:T(8,128)(2,1)}, u32[]{:S(2)}) copy-start(bf16[256,2048]{1,0:T(8,128)(2,1)} %fusion.27) | copy-start | bytes 3145732
  111.1 6.3 %copy-start.6 = (bf16[192,2048]{1,0:T(8,128)(2,1)S(1)}, bf16[192,2048]{1,0:T(8,128)(2,1)}, u32[]{:S(2)}) copy-start(bf16[192,2048]{1,0:T(8,128)(2,1)} %copy-done.5) | copy-start | bytes 2359300
  111.1 6.3 %copy-start.7 = (bf16[192,2048]{1,0:T(8,128)(2,1)S(1)}, bf16[192,2048]{1,0:T(8,128)(2,1)}, u32[]{:S(2)}) copy-start(bf16[192,2048]{1,0:T(8,128)(2,1)} %get-tuple-element.21) | copy-start | bytes 2359300
  111.1 6.3 %copy-start.9 = (bf16[384,256]{1,0:T(8,128)(2,1)S(1)}, bf16[384,256]{1,0:T(8,128)(2,1)}, u32[]{:S(2)}) copy-start(bf16[384,256]{1,0:T(8,128)(2,1)} %copy-done.8) | copy-start | bytes 589828
  111.1 6.3 %copy-start.25 = (bf16[384,256]{1,0:T(8,128)(2,1)S(1)}, bf16[384,256]{1,0:T(8,128)(2,1)}, u32[]{:S(2)}) copy-start(bf16[384,256]{1,0:T(8,128)(2,1)} %copy-done.24) | copy-start | bytes 589828
  111.2 5.5 %collective-permute-start.14 = (bf16[192,256]{1,0:T(8,128)(2,1)S(1)}, bf16[192,256]{1,0:T(8,128)(2,1)S(1)}, u32[]{:S(2)}, u32[]{:S(2)}) collective-permute-start(bf16[192,256]{1,0:T(8,128)(2,1)S(1)} %fusion.36), channel_id=1, source_target_pairs={{0,1},{1,0},{2,3},{3,2},{4,5},{5,4},{6,7},{7,6},{8,9},{9,8},{10,11... | collective-permute-start | bytes 294920 | tf_op jit(solution)/shard_map/ppermute | solution.py:60
  116.7 4.4 %collective-permute-start.15 = (bf16[192,256]{1,0:T(8,128)(2,1)S(1)}, bf16[192,256]{1,0:T(8,128)(2,1)S(1)}, u32[]{:S(2)}, u32[]{:S(2)}) collective-permute-start(bf16[192,256]{1,0:T(8,128)(2,1)S(1)} %add_convert_fusion), channel_id=1, source_target_pairs={{2,4},{4,2},{3,5},{5,3},{10,12},{12,10},{11,13},{13,11},{18,20},{2... | collective-permute-start | bytes 294920 | tf_op jit(solution)/shard_map/ppermute | solution.py:52
  119.9 15.9 %collective-permute-start.22 = (bf16[128,2048]{1,0:T(8,128)(2,1)S(1)}, bf16[128,2048]{1,0:T(8,128)(2,1)S(1)}, u32[]{:S(2)}, u32[]{:S(2)}) collective-permute-start(bf16[128,2048]{1,0:T(8,128)(2,1)S(1)} %slice.137), channel_id=1, source_target_pairs={{2,0},{4,6},{3,1},{5,7},{10,8},{12,14},{11,9},{13,15},{18,16},{20,... | collective-permute-start | bytes 1572872 | tf_op jit(solution)/shard_map/ppermute | solution.py:56
  121.2 1.2 copy-start.11
  121.2 1.5 copy-start.13
  123.3 2.1 %copy-start.17 = (bf16[1,128,2560]{2,1,0:T(8,128)(2,1)S(1)}, bf16[1,128,2560]{2,1,0:T(8,128)(2,1)}, u32[]{:S(2)}) copy-start(bf16[1,128,2560]{2,1,0:T(8,128)(2,1)} %param.5) | copy-start | bytes 1966084
  123.3 2.1 %copy-start.19 = (bf16[128,2560]{1,0:T(8,128)(2,1)S(1)}, bf16[128,2560]{1,0:T(8,128)(2,1)}, u32[]{:S(2)}) copy-start(bf16[128,2560]{1,0:T(8,128)(2,1)} %copy-done.18) | copy-start | bytes 1966084
  123.3 2.1 %copy-start.21 = (bf16[128,2560]{1,0:T(8,128)(2,1)S(1)}, bf16[128,2560]{1,0:T(8,128)(2,1)}, u32[]{:S(2)}) copy-start(bf16[128,2560]{1,0:T(8,128)(2,1)} %copy-done.20) | copy-start | bytes 1966084
  123.3 2.1 %copy-start.23 = (bf16[128,2560]{1,0:T(8,128)(2,1)S(1)}, bf16[128,2560]{1,0:T(8,128)(2,1)}, u32[]{:S(2)}) copy-start(bf16[128,2560]{1,0:T(8,128)(2,1)} %copy-done.22) | copy-start | bytes 1966084
  123.3 5.0 %collective-permute-start.16 = (bf16[128,2560]{1,0:T(8,128)(2,1)S(1)}, bf16[128,2560]{1,0:T(8,128)(2,1)S(1)}, u32[]{:S(2)}, u32[]{:S(2)}) collective-permute-start(bf16[128,2560]{1,0:T(8,128)(2,1)S(1)} %convolution_convert_fusion.2), channel_id=1, source_target_pairs={{2,4},{4,2},{3,5},{5,3},{10,12},{12,10},{11,13},{13,11},{18,20},{2... | collective-permute-start | bytes 1966088 | tf_op jit(solution)/shard_map/ppermute | solution.py:52
  124.7 12.3 %collective-permute-start.19 = (bf16[128,2560]{1,0:T(8,128)(2,1)S(1)}, bf16[128,2560]{1,0:T(8,128)(2,1)S(1)}, u32[]{:S(2)}, u32[]{:S(2)}) collective-permute-start(bf16[128,2560]{1,0:T(8,128)(2,1)S(1)} %convolution_convert_fusion.1), channel_id=1, source_target_pairs={{2,4},{4,2},{3,5},{5,3},{10,12},{12,10},{11,13},{13,11},{18,20},{2... | collective-permute-start | bytes 1966088 | tf_op jit(solution)/shard_map/ppermute | solution.py:52
  127.0 44.8 %collective-permute-start.18 = (bf16[192,2560]{1,0:T(8,128)(2,1)S(1)}, bf16[192,2560]{1,0:T(8,128)(2,1)S(1)}, u32[]{:S(2)}, u32[]{:S(2)}) collective-permute-start(bf16[192,2560]{1,0:T(8,128)(2,1)S(1)} %get-tuple-element.19), channel_id=1, source_target_pairs={{10,0},{12,6},{18,8},{20,14},{26,16},{28,22},{11,1},{13,7},{19,9},... | collective-permute-start | bytes 2949128 | tf_op jit(solution)/shard_map/ppermute | solution.py:156
  128.8 41.5 %collective-permute-start.20 = (bf16[128,2560]{1,0:T(8,128)(2,1)S(1)}, bf16[128,2560]{1,0:T(8,128)(2,1)S(1)}, u32[]{:S(2)}, u32[]{:S(2)}) collective-permute-start(bf16[128,2560]{1,0:T(8,128)(2,1)S(1)} %fusion.1), channel_id=1, source_target_pairs={{2,0},{4,6},{3,1},{5,7},{10,8},{12,14},{11,9},{13,15},{18,16},{20,... | collective-permute-start | bytes 1966088 | tf_op jit(solution)/shard_map/ppermute | solution.py:56
  130.1 41.7 %collective-permute-start.17 = (bf16[192,2560]{1,0:T(8,128)(2,1)S(1)}, bf16[192,2560]{1,0:T(8,128)(2,1)S(1)}, u32[]{:S(2)}, u32[]{:S(2)}) collective-permute-start(bf16[192,2560]{1,0:T(8,128)(2,1)S(1)} %get-tuple-element.14), channel_id=1, source_target_pairs={{8,0},{16,8},{24,16},{9,1},{17,9},{25,17},{10,2},{18,10},{26,18},{... | collective-permute-start | bytes 2949128 | tf_op jit(solution)/shard_map/ppermute | solution.py:13
where the time goes:
time: 174 us; the launch traced here: 173 us
  waiting for transfers between devices  99.7 us (57%)
  starting transfers between devices  46.1 us (26%)
  matrix products  15.5 us (9%)
  local copies, waits for them, and re-layouts  6.06 us (3%)
  other arithmetic  4.21 us (2%)
    ppermute x5, waiting for transfers between devices, inward(): return lax.ppermute(value, 'row', [(0, 1), (3, 2)])  54.7 us
    ppermute x3, waiting for transfers between devices, outward(): return lax.ppermute(value, 'row', [(1, 0), (2, 3)])  41.1 us
    ppermute x5, starting transfers between devices, inward(): return lax.ppermute(value, 'row', [(0, 1), (3, 2)])  26.2 us
    ppermute x10, starting transfers between devices, across(): return lax.ppermute(value, 'row', [(1, 2), (2, 1)])  7.93 us
    dot_general x6, matrix products, tokens_dot(): lax.dot_general(left, right, (((0,), (0,)), ((), ())), preferred_element_...  7.44 us
    dot_general x6, matrix products, rows_dot(): lax.dot_general(left, right, (((1,), (1,)), ((), ())), preferred_element_...  6.61 us
    ppermute x3, starting transfers between devices, other_col(): return lax.ppermute(value, 'col', [(0, 1), (1, 0)])  4.66 us
    ppermute x3, starting transfers between devices, outward(): return lax.ppermute(value, 'row', [(1, 0), (2, 3)])  4.01 us
  transfers between devices with their start and end apart: 23, of which 9 were waited for; matrix products, arithmetic and copies ran while one was open for 13% of the time, Pallas kernels for 0%

commit v1 on v0

--- a/solution.py
+++ b/solution.py
@@ -97,7 +97,7 @@
     down_other_end = across(down_end)
     cot_other_end_first = across(cot_end_first)
     cot_end_second = inward(after(cot_own[1], down_end, down_other))
-    up_end = inward(after(up, tokens_end, cot_end_first))
+    up_end = inward(after(up, cot_other, cot_end_first))
 
     tokens_mine = jnp.concatenate([tokens, tokens_end], axis=0)
     down_all = jnp.concatenate([down, down_end, down_other, down_other_end], axis=0)
@@ -110,26 +110,33 @@
     normed_all = jnp.concatenate([normed_bf[:, : 2 * lat], normed_other], axis=0)
 
     cot_end = (cot_end_first, cot_end_second)
-    cot_other_end = (cot_other_end_first, across(after(cot_end_second, normed_sent)))
+    cot_other_end_second = across(after(cot_end_second, normed_sent))
 
-    up_local, up_back = [], []
-    for k, cut in enumerate(cuts):
-        values = jnp.concatenate(
-            [cotangent[:, cut], cot_end[k], cot_other[:, cut], cot_other_end[k]], axis=0
-        )
-        up_piece = tokens_dot(normed_all, values).astype(BF16)
-        up_local.append(up_piece)
-        up_back.append(outward(up_piece[lat:]))
-    up_grad = jnp.concatenate(
-        [jnp.where(middle, piece[:lat], back) for piece, back in zip(up_local, up_back)], axis=1
-    )
+    def up_product(k, other_end):
+        values = [cotangent[:, cuts[k]], cot_end[k], cot_other[:, cuts[k]], other_end]
+        return tokens_dot(normed_all, jnp.concatenate(values, axis=0)).astype(BF16)
 
-    up_mine = jnp.concatenate([up, after(up_end, up_local[0])], axis=0)
+    up_first = up_product(0, cot_other_end_first)
+    up_back_first = outward(up_first[lat:])
+
+    up_mine = jnp.concatenate([up, after(up_end, up_first)], axis=0)
     early = rows_dot(jnp.concatenate([cotangent, cot_other], axis=0), up_mine)
     early_end = sum(rows_dot(cot_end[k], up_mine[:, cut]) for k, cut in enumerate(cuts))
-    late = sum(rows_dot(cot_other_end[k], up_mine[:, cut]) for k, cut in enumerate(cuts))
-    early = col_sum(jnp.concatenate([early, early_end], axis=0))
-    late = col_sum(late)
+    late_first = rows_dot(cot_other_end_first, up_mine[:, cuts[0]])
+    early = after(jnp.concatenate([early, early_end], axis=0).astype(BF16), late_first)
+    early = early.astype(F32) + other_col(early).astype(F32)
+
+    last, _ = lax.optimization_barrier((cot_other_end_second, early))
+    late = col_sum(late_first + rows_dot(last, up_mine[:, cuts[1]]))
+    up_second = up_product(1, last)
+    up_back_second = outward(up_second[lat:])
+    up_grad = jnp.concatenate(
+        [
+            jnp.where(middle, up_first[:lat], up_back_first),
+            jnp.where(middle, up_second[:lat], up_back_second),
+        ],
+        axis=1,
+    )
 
     def latent_grad(which, mine, other):
         normed_grad = jnp.concatenate([mine, other.astype(F32)], axis=1)
@@ -138,23 +145,12 @@
 
     own_rows, end_rows = slice(0, rows), slice(rows, 2 * rows)
     grad_own = across(early[rows : 2 * rows].astype(BF16))
-    grad_end = across(late.astype(BF16))
+    grad_end = across(after(late.astype(BF16), up_second))
     latent_own = latent_grad(own_rows, early[:rows], grad_own)
     latent_end = latent_grad(end_rows, early[2 * rows :], grad_end)
-    latent_bf = jnp.concatenate([latent_own, latent_end], axis=0)
-    sums = [
-        tokens_dot(latent_bf[:, j * lat : (j + 1) * lat], tokens_mine) for j in range(4)
-    ]
-    sent_end, sent_own = sums[3].astype(BF16), sums[2].astype(BF16)
-    from_end, from_own = across(sent_end), across(sent_own)
-    down_end_grad = outward((sums[1] + from_end.astype(F32)).astype(BF16))
-    down_own_grad = (sums[0] + from_own.astype(F32)).astype(BF16)
-    down_grad = jnp.where(middle, down_own_grad, down_end_grad)
-
-    latent_bf = after(latent_bf, sent_end, sent_own)
-    input_grad = jnp.dot(latent_bf, down_all, preferred_element_type=F32).astype(BF16)
+    input_end = jnp.dot(latent_end, down_all, preferred_element_type=F32).astype(BF16)
     passed_end = lax.ppermute(
-        input_grad[rows:],
+        input_end,
         ("section", "row"),
         [
             (4 * s + source, 4 * (s - 1) + target)
@@ -162,7 +158,20 @@
             for source, target in ((1, 0), (2, 3))
         ],
     )
-    passed_own = shifted(after(input_grad[:rows], from_end), "section", -1)
+
+    latent_bf = after(jnp.concatenate([latent_own, latent_end], axis=0), input_end)
+    sums = [
+        tokens_dot(latent_bf[:, j * lat : (j + 1) * lat], tokens_mine) for j in range(4)
+    ]
+    sent_end, sent_own = sums[3].astype(BF16), sums[2].astype(BF16)
+    from_end, from_own = across(sent_end), across(after(sent_own, up_back_second))
+    down_end_grad = outward((sums[1] + from_end.astype(F32)).astype(BF16))
+    down_own_grad = (sums[0] + from_own.astype(F32)).astype(BF16)
+    down_grad = jnp.where(middle, down_own_grad, down_end_grad)
+
+    latent_own = after(latent_own, sent_end, sent_own)
+    input_own = jnp.dot(latent_own, down_all, preferred_element_type=F32).astype(BF16)
+    passed_own = shifted(after(input_own, from_end, passed_end), "section", -1)
     passed = jnp.where(middle, passed_own, passed_end)
     return (passed[None], down_grad[None], up_grad[None])
 

time: 174 us -> 196 us (1.13); the launches traced: 173 us -> 193 us
  starting transfers between devices: 46.1 us -> 66.7 us
    ppermute x5, starting transfers between devices: 26.2 us -> 48.8 us  [inward(): return lax.ppermute(value, 'row', [(0, 1), (3, 2)])]
    ppermute x3, waiting for transfers between devices: 41.1 us -> 43.6 us  [outward(): return lax.ppermute(value, 'row', [(1, 0), (2, 3)])]
    ppermute x5, waiting for transfers between devices: 54.7 us -> 52.2 us  [inward(): return lax.ppermute(value, 'row', [(0, 1), (3, 2)])]
    ppermute x3, starting transfers between devices: 4.66 us -> 2.7 us  [other_col(): return lax.ppermute(value, 'col', [(0, 1), (1, 0)])]
  transfers between devices with their start and end apart: 23 -> 23, of which waited for: 9 -> 8; matrix products, arithmetic and copies ran while one was open for 13% -> 11% of each run, Pallas kernels for 0% -> 0%
where the time goes in v1:
time: 196 us; the launch traced here: 193 us
  waiting for transfers between devices  101 us (52%)
  starting transfers between devices  66.7 us (34%)
  matrix products  16.2 us (8%)
  local copies, waits for them, and re-layouts  4.15 us (2%)
  other arithmetic  3.14 us (2%)
    ppermute x5, waiting for transfers between devices, inward(): return lax.ppermute(value, 'row', [(0, 1), (3, 2)])  52.2 us
    ppermute x5, starting transfers between devices, inward(): return lax.ppermute(value, 'row', [(0, 1), (3, 2)])  48.8 us
    ppermute x3, waiting for transfers between devices, outward(): return lax.ppermute(value, 'row', [(1, 0), (2, 3)])  43.6 us
    ppermute x10, starting transfers between devices, across(): return lax.ppermute(value, 'row', [(1, 2), (2, 1)])  7.92 us
    dot_general x6, matrix products, rows_dot(): lax.dot_general(left, right, (((1,), (1,)), ((), ())), preferred_element_...  7.77 us
    dot_general x6, matrix products, tokens_dot(): lax.dot_general(left, right, (((0,), (0,)), ((), ())), preferred_element_...  6.63 us
    ppermute x3, waiting for transfers between devices, other_col(): return lax.ppermute(value, 'col', [(0, 1), (1, 0)])  5.66 us
    ppermute x3, starting transfers between devices, outward(): return lax.ppermute(value, 'row', [(1, 0), (2, 3)])  4.01 us
  transfers between devices with their start and end apart: 23, of which 8 were waited for; matrix products, arithmetic and copies ran while one was open for 11% of the time, Pallas kernels for 0%

profile of v1, /device:TPU:4, one launch (start us, length us, event | category | flops | bytes accessed | tf_op | source)
XLA Modules:
  0.0 192.9 jit_solution(8489258633104808618)
XLA Ops:
  0.6 3.5 %collective-permute-start.1 = (bf16[128,2560]{1,0:T(8,128)(2,1)}, bf16[128,2560]{1,0:T(8,128)(2,1)S(1)}, u32[]{:S(2)}, u32[]{:S(2)}) collective-permute-start(bf16[128,2560]{1,0:T(8,128)(2,1)} %bitcast.39), channel_id=1, source_target_pairs={{0,2},{6,4},{1,3},{7,5},{8,10},{14,12},{9,11},{15,13},{16,18},{22,... | collective-permute-start | bytes 1966088 | tf_op jit(solution)/shard_map/ppermute | solution.py:48
  4.2 1.4 collective-permute-start
  5.5 0.0 copy-start.10
  5.5 0.9 collective-permute-start.5
  6.4 0.7 collective-permute-start.2
  7.2 12.4 %collective-permute-done.1 = bf16[128,2560]{1,0:T(8,128)(2,1)S(1)} collective-permute-done((bf16[128,2560]{1,0:T(8,128)(2,1)}, bf16[128,2560]{1,0:T(8,128)(2,1)S(1)}, u32[]{:S(2)}, u32[]{:S(2)}) %collective-permute-start.1) | collective-permute-done | bytes 655392 | tf_op jit(solution)/shard_map/ppermute | solution.py:48
  19.6 0.7 collective-permute-start.3
  20.3 1.5 fusion.54
  21.8 0.0 copy-start.2
  21.8 7.2 %collective-permute-start.6 = (bf16[192,2048]{1,0:T(8,128)(2,1)S(1)}, bf16[192,2048]{1,0:T(8,128)(2,1)S(1)}, u32[]{:S(2)}, u32[]{:S(2)}) collective-permute-start(bf16[192,2048]{1,0:T(8,128)(2,1)S(1)} %get-tuple-element.31), channel_id=1, source_target_pairs={{0,2},{6,4},{1,3},{7,5},{8,10},{14,12},{9,11},{15,13},{16,18},{22,... | collective-permute-start | bytes 2359304 | tf_op jit(solution)/shard_map/ppermute | solution.py:48
  29.1 11.6 %collective-permute-done = bf16[192,2560]{1,0:T(8,128)(2,1)S(1)} collective-permute-done((bf16[192,2560]{1,0:T(8,128)(2,1)}, bf16[192,2560]{1,0:T(8,128)(2,1)S(1)}, u32[]{:S(2)}, u32[]{:S(2)}) %collective-permute-start) | collective-permute-done | bytes 983072 | tf_op jit(solution)/shard_map/ppermute | solution.py:48
  40.6 0.0 copy-start.16
  40.7 1.2 convolution_convert_fusion.4
  41.9 1.6 collective-permute-start.4
  43.5 33.5 %collective-permute-start.10 = (bf16[192,2048]{1,0:T(8,128)(2,1)S(1)}, bf16[192,2048]{1,0:T(8,128)(2,1)}, u32[]{:S(2)}, u32[]{:S(2)}) collective-permute-start(bf16[192,2048]{1,0:T(8,128)(2,1)S(1)} %get-tuple-element.16), channel_id=1, source_target_pairs={{0,2},{6,4},{1,3},{7,5},{8,10},{14,12},{9,11},{15,13},{16,18},{22,... | collective-permute-start | bytes 2359304 | tf_op jit(solution)/shard_map/ppermute | solution.py:48
  76.9 0.7 collective-permute-start.9
  77.7 3.2 %collective-permute-start.7 = (bf16[128,4096]{1,0:T(8,128)(2,1)S(1)}, bf16[128,4096]{1,0:T(8,128)(2,1)S(1)}, u32[]{:S(2)}, u32[]{:S(2)}) collective-permute-start(bf16[128,4096]{1,0:T(8,128)(2,1)S(1)} %bitcast.27), channel_id=1, source_target_pairs={{0,2},{6,4},{1,3},{7,5},{8,10},{14,12},{9,11},{15,13},{16,18},{22,... | collective-permute-start | bytes 3145736 | tf_op jit(solution)/shard_map/ppermute | solution.py:48
  80.9 0.2 multiply_reduce_fusion
  81.1 0.2 fusion.51
  81.3 0.7 collective-permute-start.8
  82.0 1.1 fusion.53
  83.1 10.9 %collective-permute-done.10 = bf16[192,2048]{1,0:T(8,128)(2,1)} collective-permute-done((bf16[192,2048]{1,0:T(8,128)(2,1)S(1)}, bf16[192,2048]{1,0:T(8,128)(2,1)}, u32[]{:S(2)}, u32[]{:S(2)}) %collective-permute-start.10) | collective-permute-done | bytes 786464 | tf_op jit(solution)/shard_map/ppermute | solution.py:48
  94.0 1.5 collective-permute-start.13
  95.5 1.2 fusion.27
  96.8 17.3 %collective-permute-done.7 = bf16[128,4096]{1,0:T(8,128)(2,1)S(1)} collective-permute-done((bf16[128,4096]{1,0:T(8,128)(2,1)S(1)}, bf16[128,4096]{1,0:T(8,128)(2,1)S(1)}, u32[]{:S(2)}, u32[]{:S(2)}) %collective-permute-start.7) | collective-permute-done | bytes 1048608 | tf_op jit(solution)/shard_map/ppermute | solution.py:48
  114.1 2.0 %fusion.49 = f32[192,256]{1,0:T(8,128)S(1)} fusion(bf16[192,2048]{1,0:T(8,128)(2,1)} %collective-permute-done.10, bf16[128,4096]{1,0:T(8,128)(2,1)S(1)} %bitcast.28, bf16[128,4096]{1,0:T(8,128)(2,1)S(1)} %collective-permute-done.7), kind=kOutput, calls=%fused_computation.78 | convolution fusion | flops 203423744 | bytes 3080192 | tf_op jit(solution)/shard_map/dot_general | solution.py:68
  116.2 1.1 fusion.30
  117.3 0.5 fusion.34
  117.8 1.2 convolution_bitcast_fusion
  119.0 0.5 collective-permute-start.11
  119.6 0.1 fusion.57
  119.7 1.4 collective-permute-start.22
  121.1 4.6 %collective-permute-done.11 = bf16[576,256]{1,0:T(8,128)(2,1)S(1)} collective-permute-done((bf16[576,256]{1,0:T(8,128)(2,1)S(1)}, bf16[576,256]{1,0:T(8,128)(2,1)S(1)}, u32[]{:S(2)}, u32[]{:S(2)}) %collective-permute-start.11) | collective-permute-done | bytes 294944 | tf_op jit(solution)/shard_map/ppermute | solution.py:60
  125.8 0.1 convert_add_fusion.1
  125.9 1.7 fusion.35
  127.6 0.6 collective-permute-start.14
  128.2 0.7 collective-permute-start.12
  128.9 2.4 %fusion.24 = bf16[256,2048]{1,0:T(8,128)(2,1)S(1)} fusion(bf16[192,2048]{1,0:T(8,128)(2,1)} %collective-permute-done.13, bf16[192,2048]{1,0:T(8,128)(2,1)S(1)} %copy-done.1, bf16[192,2048]{1,0:T(8,128)(2,1)} %collective-permute-done.10, bf16[192,2048]{1,0:T(8,128)(2,1)S(1)} %get-tuple-element.16, bf16[384,256]{1,0:T(8,128)(2,1)S(1)} %copy-done.19, ...), kind=kOutput, calls=%fused_computation.36 | convolution fusion | flops 819200000 | bytes 4587520 | tf_op jit(solution)/shard_map/dot_general | solution.py:72
  131.3 1.0 collective-permute-done.14
  132.3 0.7 collective-permute-start.15
  133.2 0.2 multiply_reduce_fusion.1
  133.3 0.2 multiply_convert_fusion
  133.5 0.7 copy-done.11
  134.2 0.2 copy-done.13
  134.4 0.2 copy-done.15
  134.6 0.2 copy-done.17
  134.8 0.9 convolution_convert_fusion.1
  135.7 1.3 collective-permute-start.17
  137.1 0.5 convolution_convert_fusion.3
  137.6 0.7 collective-permute-start.16
  138.3 0.1 slice_select_fusion.1
  138.4 1.3 collective-permute-start.19
  139.7 0.5 convolution_convert_fusion.2
  140.3 0.9 convolution_convert_fusion
  141.2 34.0 %collective-permute-done.19 = bf16[128,2048]{1,0:T(8,128)(2,1)S(1)} collective-permute-done((bf16[128,2048]{1,0:T(8,128)(2,1)S(1)}, bf16[128,2048]{1,0:T(8,128)(2,1)S(1)}, u32[]{:S(2)}, u32[]{:S(2)}) %collective-permute-start.19) | collective-permute-done | bytes 524320 | tf_op jit(solution)/shard_map/ppermute | solution.py:56
  175.2 0.7 collective-permute-start.20
  175.9 0.5 fusion.1
  176.4 1.3 collective-permute-start.21
  177.7 1.9 collective-permute-start.18
  179.7 0.1 slice_select_fusion
  179.8 1.1 maximum_bitcast_fusion
  180.8 9.6 %collective-permute-done.21 = bf16[128,2560]{1,0:T(8,128)(2,1)S(1)} collective-permute-done((bf16[128,2560]{1,0:T(8,128)(2,1)S(1)}, bf16[128,2560]{1,0:T(8,128)(2,1)S(1)}, u32[]{:S(2)}, u32[]{:S(2)}) %collective-permute-start.21) | collective-permute-done | bytes 655392 | tf_op jit(solution)/shard_map/ppermute | solution.py:56
  190.4 1.4 fusion.3
  191.8 1.0 select_bitcast_fusion
  (62 shorter events, 0.4 us)
Async XLA Ops:
  0.6 18.9 %collective-permute-start.1 = (bf16[128,2560]{1,0:T(8,128)(2,1)}, bf16[128,2560]{1,0:T(8,128)(2,1)S(1)}, u32[]{:S(2)}, u32[]{:S(2)}) collective-permute-start(bf16[128,2560]{1,0:T(8,128)(2,1)} %bitcast.39), channel_id=1, source_target_pairs={{0,2},{6,4},{1,3},{7,5},{8,10},{14,12},{9,11},{15,13},{16,18},{22,... | collective-permute-start | bytes 1966088 | tf_op jit(solution)/shard_map/ppermute | solution.py:48
  4.2 36.5 %collective-permute-start = (bf16[192,2560]{1,0:T(8,128)(2,1)}, bf16[192,2560]{1,0:T(8,128)(2,1)S(1)}, u32[]{:S(2)}, u32[]{:S(2)}) collective-permute-start(bf16[192,2560]{1,0:T(8,128)(2,1)} %bitcast.33), channel_id=1, source_target_pairs={{0,2},{6,4},{1,3},{7,5},{8,10},{14,12},{9,11},{15,13},{16,18},{22,... | collective-permute-start | bytes 2949128 | tf_op jit(solution)/shard_map/ppermute | solution.py:48
  5.5 35.1 %copy-start.6 = (bf16[1,192,2560]{2,1,0:T(8,128)(2,1)S(1)}, bf16[1,192,2560]{2,1,0:T(8,128)(2,1)}, u32[]{:S(2)}) copy-start(bf16[1,192,2560]{2,1,0:T(8,128)(2,1)} %param.4) | copy-start | bytes 2949124
  5.5 35.1 %copy-start.10 = (bf16[1,128,2560]{2,1,0:T(8,128)(2,1)S(1)}, bf16[1,128,2560]{2,1,0:T(8,128)(2,1)}, u32[]{:S(2)}) copy-start(bf16[1,128,2560]{2,1,0:T(8,128)(2,1)} %param.5) | copy-start | bytes 1966084
  5.5 72.1 %collective-permute-start.5 = (bf16[192,4096]{1,0:T(8,128)(2,1)}, bf16[192,4096]{1,0:T(8,128)(2,1)S(1)}, u32[]{:S(2)}, u32[]{:S(2)}) collective-permute-start(bf16[192,4096]{1,0:T(8,128)(2,1)} %bitcast.24), channel_id=1, source_target_pairs={{2,4},{4,2},{3,5},{5,3},{10,12},{12,10},{11,13},{13,11},{18,20},{2... | collective-permute-start | bytes 4718600 | tf_op jit(solution)/shard_map/ppermute | solution.py:52
  6.4 22.6 %collective-permute-start.2 = (bf16[128,2560]{1,0:T(8,128)(2,1)}, bf16[128,2560]{1,0:T(8,128)(2,1)S(1)}, u32[]{:S(2)}, u32[]{:S(2)}) collective-permute-start(bf16[128,2560]{1,0:T(8,128)(2,1)} %bitcast.40), channel_id=1, source_target_pairs={{2,4},{4,2},{3,5},{5,3},{10,12},{12,10},{11,13},{13,11},{18,20},{2... | collective-permute-start | bytes 1966088 | tf_op jit(solution)/shard_map/ppermute | solution.py:52
  19.6 21.1 %copy-start.12 = (bf16[128,2560]{1,0:T(8,128)(2,1)}, bf16[128,2560]{1,0:T(8,128)(2,1)S(1)}, u32[]{:S(2)}) copy-start(bf16[128,2560]{1,0:T(8,128)(2,1)S(1)} %collective-permute-done.1) | copy-start | bytes 1966084
  19.6 21.1 %collective-permute-start.3 = (bf16[128,2560]{1,0:T(8,128)(2,1)S(1)}, bf16[128,2560]{1,0:T(8,128)(2,1)S(1)}, u32[]{:S(2)}, u32[]{:S(2)}) collective-permute-start(bf16[128,2560]{1,0:T(8,128)(2,1)S(1)} %collective-permute-done.1), channel_id=1, source_target_pairs={{2,4},{4,2},{3,5},{5,3},{10,12},{12,10},{11,13},{13,11},{18,20},{2... | collective-permute-start | bytes 1966088 | tf_op jit(solution)/shard_map/ppermute | solution.py:52
  21.8 55.9 %copy-start.2 = (bf16[1,128,4096]{2,1,0:T(8,128)(2,1)S(1)}, bf16[1,128,4096]{2,1,0:T(8,128)(2,1)}, u32[]{:S(2)}) copy-start(bf16[1,128,4096]{2,1,0:T(8,128)(2,1)} %param.6) | copy-start | bytes 3145732
  21.8 55.1 %collective-permute-start.6 = (bf16[192,2048]{1,0:T(8,128)(2,1)S(1)}, bf16[192,2048]{1,0:T(8,128)(2,1)S(1)}, u32[]{:S(2)}, u32[]{:S(2)}) collective-permute-start(bf16[192,2048]{1,0:T(8,128)(2,1)S(1)} %get-tuple-element.31), channel_id=1, source_target_pairs={{0,2},{6,4},{1,3},{7,5},{8,10},{14,12},{9,11},{15,13},{16,18},{22,... | collective-permute-start | bytes 2359304 | tf_op jit(solution)/shard_map/ppermute | solution.py:48
  29.0 12.8 %copy-start.14 = (bf16[128,2560]{1,0:T(8,128)(2,1)}, bf16[128,2560]{1,0:T(8,128)(2,1)S(1)}, u32[]{:S(2)}) copy-start(bf16[128,2560]{1,0:T(8,128)(2,1)S(1)} %collective-permute-done.2) | copy-start | bytes 1966084
  40.6 1.3 copy-start.8
  40.6 1.2 copy-start.16
  41.9 39.0 %collective-permute-start.4 = (bf16[384,512]{1,0:T(8,128)(2,1)S(1)}, bf16[384,512]{1,0:T(8,128)(2,1)S(1)}, u32[]{:S(2)}, u32[]{:S(2)}) collective-permute-start(bf16[384,512]{1,0:T(8,128)(2,1)S(1)} %convolution_convert_fusion.4), channel_id=1, source_target_pairs={{0,1},{1,0},{2,3},{3,2},{4,5},{5,4},{6,7},{7,6},{8,9},{9,8},{10,11... | collective-permute-start | bytes 1179656 | tf_op jit(solution)/shard_map/ppermute | solution.py:60
  43.5 50.5 %collective-permute-start.10 = (bf16[192,2048]{1,0:T(8,128)(2,1)S(1)}, bf16[192,2048]{1,0:T(8,128)(2,1)}, u32[]{:S(2)}, u32[]{:S(2)}) collective-permute-start(bf16[192,2048]{1,0:T(8,128)(2,1)S(1)} %get-tuple-element.16), channel_id=1, source_target_pairs={{0,2},{6,4},{1,3},{7,5},{8,10},{14,12},{9,11},{15,13},{16,18},{22,... | collective-permute-start | bytes 2359304 | tf_op jit(solution)/shard_map/ppermute | solution.py:48
  76.9 18.6 %collective-permute-start.9 = (bf16[192,2048]{1,0:T(8,128)(2,1)S(1)}, bf16[192,2048]{1,0:T(8,128)(2,1)S(1)}, u32[]{:S(2)}, u32[]{:S(2)}) collective-permute-start(bf16[192,2048]{1,0:T(8,128)(2,1)S(1)} %collective-permute-done.6), channel_id=1, source_target_pairs={{2,4},{4,2},{3,5},{5,3},{10,12},{12,10},{11,13},{13,11},{18,20},{2... | collective-permute-start | bytes 2359304 | tf_op jit(solution)/shard_map/ppermute | solution.py:52
  77.7 36.5 %collective-permute-start.7 = (bf16[128,4096]{1,0:T(8,128)(2,1)S(1)}, bf16[128,4096]{1,0:T(8,128)(2,1)S(1)}, u32[]{:S(2)}, u32[]{:S(2)}) collective-permute-start(bf16[128,4096]{1,0:T(8,128)(2,1)S(1)} %bitcast.27), channel_id=1, source_target_pairs={{0,2},{6,4},{1,3},{7,5},{8,10},{14,12},{9,11},{15,13},{16,18},{22,... | collective-permute-start | bytes 3145736 | tf_op jit(solution)/shard_map/ppermute | solution.py:48
  81.3 14.2 %collective-permute-start.8 = (bf16[384,256]{1,0:T(8,128)(2,1)S(1)}, bf16[384,256]{1,0:T(8,128)(2,1)S(1)}, u32[]{:S(2)}, u32[]{:S(2)}) collective-permute-start(bf16[384,256]{1,0:T(8,128)(2,1)S(1)} %get-tuple-element.38), channel_id=1, source_target_pairs={{2,4},{4,2},{3,5},{5,3},{10,12},{12,10},{11,13},{13,11},{18,20},{2... | collective-permute-start | bytes 589832 | tf_op jit(solution)/shard_map/ppermute | solution.py:52
  94.0 31.9 %collective-permute-start.13 = (bf16[192,2048]{1,0:T(8,128)(2,1)}, bf16[192,2048]{1,0:T(8,128)(2,1)}, u32[]{:S(2)}, u32[]{:S(2)}) collective-permute-start(bf16[192,2048]{1,0:T(8,128)(2,1)} %collective-permute-done.10), channel_id=1, source_target_pairs={{2,4},{4,2},{3,5},{5,3},{10,12},{12,10},{11,13},{13,11},{18,20},{2... | collective-permute-start | bytes 2359304 | tf_op jit(solution)/shard_map/ppermute | solution.py:52
  95.5 1.2 copy-start.18
  96.8 19.4 %copy-start = (bf16[1,192,4096]{2,1,0:T(8,128)(2,1)S(1)}, bf16[1,192,4096]{2,1,0:T(8,128)(2,1)}, u32[]{:S(2)}) copy-start(bf16[1,192,4096]{2,1,0:T(8,128)(2,1)} %param.7) | copy-start | bytes 4718596
  114.1 3.7 %copy-start.4 = (bf16[128,4096]{1,0:T(8,128)(2,1)}, bf16[128,4096]{1,0:T(8,128)(2,1)S(1)}, u32[]{:S(2)}) copy-start(bf16[128,4096]{1,0:T(8,128)(2,1)S(1)} %collective-permute-done.7) | copy-start | bytes 3145732
  119.0 6.7 %collective-permute-start.11 = (bf16[576,256]{1,0:T(8,128)(2,1)S(1)}, bf16[576,256]{1,0:T(8,128)(2,1)S(1)}, u32[]{:S(2)}, u32[]{:S(2)}) collective-permute-start(bf16[576,256]{1,0:T(8,128)(2,1)S(1)} %pad_maximum_fusion.10), channel_id=1, source_target_pairs={{0,1},{1,0},{2,3},{3,2},{4,5},{5,4},{6,7},{7,6},{8,9},{9,8},{10,11... | collective-permute-start | bytes 884744 | tf_op jit(solution)/shard_map/ppermute | solution.py:60
  119.6 6.3 %copy-start.3 = (bf16[1,128,4096]{2,1,0:T(8,128)(2,1)S(1)}, bf16[1,128,4096]{2,1,0:T(8,128)(2,1)}, u32[]{:S(2)}) copy-start(bf16[1,128,4096]{2,1,0:T(8,128)(2,1)} %param.6) | copy-start | bytes 3145732
  119.6 6.3 %copy-start.5 = (bf16[128,4096]{1,0:T(8,128)(2,1)S(1)}, bf16[128,4096]{1,0:T(8,128)(2,1)}, u32[]{:S(2)}) copy-start(bf16[128,4096]{1,0:T(8,128)(2,1)} %copy-done.4) | copy-start | bytes 3145732
  119.6 6.3 %copy-start.20 = (f32[192,256]{1,0:T(8,128)S(1)}, f32[192,256]{1,0:T(8,128)}, u32[]{:S(2)}) copy-start(f32[192,256]{1,0:T(8,128)} %convolution_bitcast_fusion) | copy-start | bytes 589828
  119.7 18.6 %collective-permute-start.22 = (bf16[128,2048]{1,0:T(8,128)(2,1)S(1)}, bf16[128,2048]{1,0:T(8,128)(2,1)S(1)}, u32[]{:S(2)}, u32[]{:S(2)}) collective-permute-start(bf16[128,2048]{1,0:T(8,128)(2,1)S(1)} %slice.118), channel_id=1, source_target_pairs={{2,0},{4,6},{3,1},{5,7},{10,8},{12,14},{11,9},{13,15},{18,16},{20,... | collective-permute-start | bytes 1572872 | tf_op jit(solution)/shard_map/ppermute | solution.py:56
  125.8 3.0 %copy-start.1 = (bf16[192,2048]{1,0:T(8,128)(2,1)S(1)}, bf16[192,2048]{1,0:T(8,128)(2,1)}, u32[]{:S(2)}) copy-start(bf16[192,2048]{1,0:T(8,128)(2,1)} %get-tuple-element.29) | copy-start | bytes 2359300
  125.9 3.0 %copy-start.19 = (bf16[384,256]{1,0:T(8,128)(2,1)S(1)}, bf16[384,256]{1,0:T(8,128)(2,1)}, u32[]{:S(2)}) copy-start(bf16[384,256]{1,0:T(8,128)(2,1)} %copy-done.18) | copy-start | bytes 589828
  127.6 4.7 %collective-permute-start.14 = (bf16[192,256]{1,0:T(8,128)(2,1)S(1)}, bf16[192,256]{1,0:T(8,128)(2,1)S(1)}, u32[]{:S(2)}, u32[]{:S(2)}) collective-permute-start(bf16[192,256]{1,0:T(8,128)(2,1)S(1)} %fusion.35), channel_id=1, source_target_pairs={{0,1},{1,0},{2,3},{3,2},{4,5},{5,4},{6,7},{7,6},{8,9},{9,8},{10,11... | collective-permute-start | bytes 294920 | tf_op jit(solution)/shard_map/ppermute | solution.py:60
  128.2 4.8 %collective-permute-start.12 = (bf16[192,256]{1,0:T(8,128)(2,1)S(1)}, bf16[192,256]{1,0:T(8,128)(2,1)S(1)}, u32[]{:S(2)}, u32[]{:S(2)}) collective-permute-start(bf16[192,256]{1,0:T(8,128)(2,1)S(1)} %slice.155), channel_id=1, source_target_pairs={{2,4},{4,2},{3,5},{5,3},{10,12},{12,10},{11,13},{13,11},{18,20},{2... | collective-permute-start | bytes 294920 | tf_op jit(solution)/shard_map/ppermute | solution.py:52
  132.3 0.7 collective-permute-start.15
  133.1 1.1 copy-start.11
  133.1 1.3 copy-start.13
  133.1 1.5 copy-start.15
  133.2 1.7 copy-start.17
  134.8 2.2 %copy-start.7 = (bf16[1,192,2560]{2,1,0:T(8,128)(2,1)S(1)}, bf16[1,192,2560]{2,1,0:T(8,128)(2,1)}, u32[]{:S(2)}) copy-start(bf16[1,192,2560]{2,1,0:T(8,128)(2,1)} %param.4) | copy-start | bytes 2949124
  134.8 2.3 %copy-start.9 = (bf16[192,2560]{1,0:T(8,128)(2,1)S(1)}, bf16[192,2560]{1,0:T(8,128)(2,1)}, u32[]{:S(2)}) copy-start(bf16[192,2560]{1,0:T(8,128)(2,1)} %copy-done.8) | copy-start | bytes 2949124
  135.7 42.0 %collective-permute-start.17 = (bf16[192,2560]{1,0:T(8,128)(2,1)S(1)}, bf16[192,2560]{1,0:T(8,128)(2,1)S(1)}, u32[]{:S(2)}, u32[]{:S(2)}) collective-permute-start(bf16[192,2560]{1,0:T(8,128)(2,1)S(1)} %convolution_convert_fusion.1), channel_id=1, source_target_pairs={{10,0},{12,6},{18,8},{20,14},{26,16},{28,22},{11,1},{13,7},{19,9},... | collective-permute-start | bytes 2949128 | tf_op jit(solution)/shard_map/ppermute | solution.py:152
  137.6 38.3 %collective-permute-start.16 = (bf16[128,2560]{1,0:T(8,128)(2,1)S(1)}, bf16[128,2560]{1,0:T(8,128)(2,1)S(1)}, u32[]{:S(2)}, u32[]{:S(2)}) collective-permute-start(bf16[128,2560]{1,0:T(8,128)(2,1)S(1)} %convolution_convert_fusion.3), channel_id=1, source_target_pairs={{2,4},{4,2},{3,5},{5,3},{10,12},{12,10},{11,13},{13,11},{18,20},{2... | collective-permute-start | bytes 1966088 | tf_op jit(solution)/shard_map/ppermute | solution.py:52
  138.4 36.7 %collective-permute-start.19 = (bf16[128,2048]{1,0:T(8,128)(2,1)S(1)}, bf16[128,2048]{1,0:T(8,128)(2,1)S(1)}, u32[]{:S(2)}, u32[]{:S(2)}) collective-permute-start(bf16[128,2048]{1,0:T(8,128)(2,1)S(1)} %slice.116), channel_id=1, source_target_pairs={{2,0},{4,6},{3,1},{5,7},{10,8},{12,14},{11,9},{13,15},{18,16},{20,... | collective-permute-start | bytes 1572872 | tf_op jit(solution)/shard_map/ppermute | solution.py:56
  175.2 5.6 %collective-permute-start.20 = (bf16[128,2560]{1,0:T(8,128)(2,1)S(1)}, bf16[128,2560]{1,0:T(8,128)(2,1)S(1)}, u32[]{:S(2)}, u32[]{:S(2)}) collective-permute-start(bf16[128,2560]{1,0:T(8,128)(2,1)S(1)} %convolution_convert_fusion.2), channel_id=1, source_target_pairs={{2,4},{4,2},{3,5},{5,3},{10,12},{12,10},{11,13},{13,11},{18,20},{2... | collective-permute-start | bytes 1966088 | tf_op jit(solution)/shard_map/ppermute | solution.py:52
  176.4 14.0 %collective-permute-start.21 = (bf16[128,2560]{1,0:T(8,128)(2,1)S(1)}, bf16[128,2560]{1,0:T(8,128)(2,1)S(1)}, u32[]{:S(2)}, u32[]{:S(2)}) collective-permute-start(bf16[128,2560]{1,0:T(8,128)(2,1)S(1)} %fusion.1), channel_id=1, source_target_pairs={{2,0},{4,6},{3,1},{5,7},{10,8},{12,14},{11,9},{13,15},{18,16},{20,... | collective-permute-start | bytes 1966088 | tf_op jit(solution)/shard_map/ppermute | solution.py:56
  177.7 14.1 %collective-permute-start.18 = (bf16[192,2560]{1,0:T(8,128)(2,1)S(1)}, bf16[192,2560]{1,0:T(8,128)(2,1)S(1)}, u32[]{:S(2)}, u32[]{:S(2)}) collective-permute-start(bf16[192,2560]{1,0:T(8,128)(2,1)S(1)} %convolution_convert_fusion), channel_id=1, source_target_pairs={{8,0},{16,8},{24,16},{9,1},{17,9},{25,17},{10,2},{18,10},{26,18},{... | collective-permute-start | bytes 2949128 | tf_op jit(solution)/shard_map/ppermute | solution.py:13

commit v2 on v1

--- a/solution.py
+++ b/solution.py
@@ -86,18 +86,19 @@
     place = lax.axis_index("row")
     middle = (place == 1) | (place == 2)
 
-    half = feat // 2
-    cuts = (slice(0, half), slice(half, feat))
-    cot_own = [cotangent[:, cut] for cut in cuts]
+    cut = feat * 5 // 8 // 128 * 128
+    cuts = (slice(0, cut), slice(cut, feat))
+    cot_own = [cotangent[:, c] for c in cuts]
     down_end = inward(down)
+    tokens_end = inward(tokens)
+    cot_other = [across(cot_own[0])]
     down_other = across(down)
-    cot_end_first = inward(cot_own[0])
-    cot_other = across(cotangent)
-    tokens_end = inward(tokens)
+    cot_end = [inward(after(cot_own[0], down_end, cot_other[0]))]
     down_other_end = across(down_end)
-    cot_other_end_first = across(cot_end_first)
-    cot_end_second = inward(after(cot_own[1], down_end, down_other))
-    up_end = inward(after(up, cot_other, cot_end_first))
+    cot_other.append(across(cot_own[1]))
+    cot_end.append(inward(after(cot_own[1], tokens_end, down_other)))
+    cot_other_end = [across(cot_end[0])]
+    up_end = inward(after(up, cot_end[0], cot_other[1]))
 
     tokens_mine = jnp.concatenate([tokens, tokens_end], axis=0)
     down_all = jnp.concatenate([down, down_end, down_other, down_other_end], axis=0)
@@ -109,46 +110,33 @@
     normed_other = across(normed_sent)
     normed_all = jnp.concatenate([normed_bf[:, : 2 * lat], normed_other], axis=0)
 
-    cot_end = (cot_end_first, cot_end_second)
-    cot_other_end_second = across(after(cot_end_second, normed_sent))
+    cot_other_end.append(across(after(cot_end[1], normed_sent)))
+    cot_all = [
+        jnp.concatenate([cot_own[k], cot_end[k], cot_other[k], cot_other_end[k]], axis=0)
+        for k in range(2)
+    ]
 
-    def up_product(k, other_end):
-        values = [cotangent[:, cuts[k]], cot_end[k], cot_other[:, cuts[k]], other_end]
-        return tokens_dot(normed_all, jnp.concatenate(values, axis=0)).astype(BF16)
-
-    up_first = up_product(0, cot_other_end_first)
-    up_back_first = outward(up_first[lat:])
-
+    up_first = tokens_dot(normed_all, cot_all[0]).astype(BF16)
+    back_first = outward(up_first[lat:])
     up_mine = jnp.concatenate([up, after(up_end, up_first)], axis=0)
-    early = rows_dot(jnp.concatenate([cotangent, cot_other], axis=0), up_mine)
-    early_end = sum(rows_dot(cot_end[k], up_mine[:, cut]) for k, cut in enumerate(cuts))
-    late_first = rows_dot(cot_other_end_first, up_mine[:, cuts[0]])
-    early = after(jnp.concatenate([early, early_end], axis=0).astype(BF16), late_first)
-    early = early.astype(F32) + other_col(early).astype(F32)
-
-    last, _ = lax.optimization_barrier((cot_other_end_second, early))
-    late = col_sum(late_first + rows_dot(last, up_mine[:, cuts[1]]))
-    up_second = up_product(1, last)
-    up_back_second = outward(up_second[lat:])
+    grad = rows_dot(cot_all[0], up_mine[:, cuts[0]]) + rows_dot(cot_all[1], up_mine[:, cuts[1]])
+    grad_other = col_sum(grad[2 * rows :])
+    grad_mine = col_sum(grad[: 2 * rows])
+    up_second = tokens_dot(normed_all, cot_all[1]).astype(BF16)
+    back_second = outward(up_second[lat:])
     up_grad = jnp.concatenate(
         [
-            jnp.where(middle, up_first[:lat], up_back_first),
-            jnp.where(middle, up_second[:lat], up_back_second),
+            jnp.where(middle, up_first[:lat], back_first),
+            jnp.where(middle, up_second[:lat], back_second),
         ],
         axis=1,
     )
 
-    def latent_grad(which, mine, other):
-        normed_grad = jnp.concatenate([mine, other.astype(F32)], axis=1)
-        inner = jnp.mean(normed_grad * normed[which], axis=-1, keepdims=True)
-        return (inv_rms[which] * (normed_grad - normed[which] * inner)).astype(BF16)
-
-    own_rows, end_rows = slice(0, rows), slice(rows, 2 * rows)
-    grad_own = across(early[rows : 2 * rows].astype(BF16))
-    grad_end = across(after(late.astype(BF16), up_second))
-    latent_own = latent_grad(own_rows, early[:rows], grad_own)
-    latent_end = latent_grad(end_rows, early[2 * rows :], grad_end)
-    input_end = jnp.dot(latent_end, down_all, preferred_element_type=F32).astype(BF16)
+    grad_sent = after(grad_other.astype(BF16), up_second, back_first)
+    normed_grad = jnp.concatenate([grad_mine, across(grad_sent).astype(F32)], axis=1)
+    inner = jnp.mean(normed_grad * normed, axis=-1, keepdims=True)
+    latent_bf = (inv_rms * (normed_grad - normed * inner)).astype(BF16)
+    input_end = jnp.dot(latent_bf[rows:], down_all, preferred_element_type=F32).astype(BF16)
     passed_end = lax.ppermute(
         input_end,
         ("section", "row"),
@@ -159,17 +147,17 @@
         ],
     )
 
-    latent_bf = after(jnp.concatenate([latent_own, latent_end], axis=0), input_end)
+    latent_bf = after(latent_bf, input_end)
     sums = [
         tokens_dot(latent_bf[:, j * lat : (j + 1) * lat], tokens_mine) for j in range(4)
     ]
     sent_end, sent_own = sums[3].astype(BF16), sums[2].astype(BF16)
-    from_end, from_own = across(sent_end), across(after(sent_own, up_back_second))
+    from_end, from_own = across(sent_end), across(sent_own)
     down_end_grad = outward((sums[1] + from_end.astype(F32)).astype(BF16))
     down_own_grad = (sums[0] + from_own.astype(F32)).astype(BF16)
     down_grad = jnp.where(middle, down_own_grad, down_end_grad)
 
-    latent_own = after(latent_own, sent_end, sent_own)
+    latent_own = after(latent_bf[:rows], sent_end, sent_own)
     input_own = jnp.dot(latent_own, down_all, preferred_element_type=F32).astype(BF16)
     passed_own = shifted(after(input_own, from_end, passed_end), "section", -1)
     passed = jnp.where(middle, passed_own, passed_end)

time: 196 us -> 181 us (0.923)
  waiting for transfers between devices: 101 us -> 76.6 us
  starting transfers between devices: 66.7 us -> 80.7 us
  matrix products: 16.2 us -> 10.3 us
    ppermute x5, waiting for transfers between devices: 52.2 us -> 30.3 us  [inward(): return lax.ppermute(value, 'row', [(0, 1), (3, 2)])]
    ppermute x3, waiting for transfers between devices: 43.6 us -> 27.9 us  [outward(): return lax.ppermute(value, 'row', [(1, 0), (2, 3)])]
    ppermute x1, waiting for transfers between devices: 0.01 us -> 12 us  [folded_body(): lax.ppermute(input_end, ('section', 'row'), [(4 * s + source, 4 * (s - 1)...]
    ppermute x5, starting transfers between devices: 48.8 us -> 56.9 us  [inward(): return lax.ppermute(value, 'row', [(0, 1), (3, 2)])]
    ppermute x1, starting transfers between devices: 1.92 us -> 8.06 us  [shifted(): lax.ppermute(value, axis, [(source, source + steps) for source in range(l...]
    dot_general x6 -> x3, matrix products: 7.77 us -> 3.23 us  [rows_dot(): lax.dot_general(left, right, (((1,), (1,)), ((), ())), preferred_element_...]
  transfers between devices with their start and end apart: 23 -> 23, of which waited for: 8 -> 10; matrix products, arithmetic and copies ran while one was open for 11% -> 9% of each run, Pallas kernels for 0% -> 0%
where the time goes in v2:
time: 181 us; the launch traced here: 178 us
  starting transfers between devices  80.7 us (45%)
  waiting for transfers between devices  76.6 us (42%)
  matrix products  10.3 us (6%)
  other arithmetic  4.98 us (3%)
  local copies, waits for them, and re-layouts  3.71 us (2%)
    ppermute x5, starting transfers between devices, inward(): return lax.ppermute(value, 'row', [(0, 1), (3, 2)])  56.9 us
    ppermute x5, waiting for transfers between devices, inward(): return lax.ppermute(value, 'row', [(0, 1), (3, 2)])  30.3 us
    ppermute x3, waiting for transfers between devices, outward(): return lax.ppermute(value, 'row', [(1, 0), (2, 3)])  27.9 us
    ppermute x1, waiting for transfers between devices, folded_body(): lax.ppermute(input_end, ('section', 'row'), [(4 * s + source, 4 * (s - 1)...  12 us
    ppermute x1, starting transfers between devices, shifted(): lax.ppermute(value, axis, [(source, source + steps) for source in range(l...  8.06 us
    ppermute x10, starting transfers between devices, across(): return lax.ppermute(value, 'row', [(1, 2), (2, 1)])  6.98 us
    dot_general x6, matrix products, tokens_dot(): lax.dot_general(left, right, (((0,), (0,)), ((), ())), preferred_element_...  5.28 us
    ppermute x3, waiting for transfers between devices, other_col(): return lax.ppermute(value, 'col', [(0, 1), (1, 0)])  4.95 us
  transfers between devices with their start and end apart: 23, of which 10 were waited for; matrix products, arithmetic and copies ran while one was open for 9% of the time, Pallas kernels for 0%

profile of v2, /device:TPU:4, one launch (start us, length us, event | category | flops | bytes accessed | tf_op | source)
XLA Modules:
  0.0 177.5 jit_solution(11100405971812327762)
XLA Ops:
  0.6 0.0 copy-start.5
  0.6 0.0 copy-start.1
  0.7 3.7 %collective-permute-start.1 = (bf16[128,2560]{1,0:T(8,128)(2,1)}, bf16[128,2560]{1,0:T(8,128)(2,1)S(1)}, u32[]{:S(2)}, u32[]{:S(2)}) collective-permute-start(bf16[128,2560]{1,0:T(8,128)(2,1)} %bitcast.22), channel_id=1, source_target_pairs={{0,2},{6,4},{1,3},{7,5},{8,10},{14,12},{9,11},{15,13},{16,18},{22,... | collective-permute-start | bytes 1966088 | tf_op jit(solution)/shard_map/ppermute | solution.py:48
  4.3 1.3 slice.74
  5.6 0.7 collective-permute-start.5
  6.3 4.1 %collective-permute-start = (bf16[192,2560]{1,0:T(8,128)(2,1)S(1)}, bf16[192,2560]{1,0:T(8,128)(2,1)S(1)}, u32[]{:S(2)}, u32[]{:S(2)}) collective-permute-start(bf16[192,2560]{1,0:T(8,128)(2,1)S(1)} %bitcast.16), channel_id=1, source_target_pairs={{0,2},{6,4},{1,3},{7,5},{8,10},{14,12},{9,11},{15,13},{16,18},{22,... | collective-permute-start | bytes 2949128 | tf_op jit(solution)/shard_map/ppermute | solution.py:48
  10.4 0.7 collective-permute-start.2
  11.1 8.6 %collective-permute-done.1 = bf16[128,2560]{1,0:T(8,128)(2,1)S(1)} collective-permute-done((bf16[128,2560]{1,0:T(8,128)(2,1)}, bf16[128,2560]{1,0:T(8,128)(2,1)S(1)}, u32[]{:S(2)}, u32[]{:S(2)}) %collective-permute-start.1) | collective-permute-done | bytes 655392 | tf_op jit(solution)/shard_map/ppermute | solution.py:48
  19.7 0.7 collective-permute-start.3
  20.4 13.0 %collective-permute-start.6 = (bf16[192,2560]{1,0:T(8,128)(2,1)S(1)}, bf16[192,2560]{1,0:T(8,128)(2,1)S(1)}, u32[]{:S(2)}, u32[]{:S(2)}) collective-permute-start(bf16[192,2560]{1,0:T(8,128)(2,1)S(1)} %slice.74), channel_id=1, source_target_pairs={{0,2},{6,4},{1,3},{7,5},{8,10},{14,12},{9,11},{15,13},{16,18},{22,... | collective-permute-start | bytes 2949128 | tf_op jit(solution)/shard_map/ppermute | solution.py:48
  33.4 0.0 copy-start.9
  33.5 7.2 %collective-permute-done = bf16[192,2560]{1,0:T(8,128)(2,1)S(1)} collective-permute-done((bf16[192,2560]{1,0:T(8,128)(2,1)S(1)}, bf16[192,2560]{1,0:T(8,128)(2,1)S(1)}, u32[]{:S(2)}, u32[]{:S(2)}) %collective-permute-start) | collective-permute-done | bytes 983072 | tf_op jit(solution)/shard_map/ppermute | solution.py:48
  40.7 1.2 convolution_convert_fusion.6
  41.9 1.6 collective-permute-start.4
  43.5 1.1 slice.75
  44.6 0.7 collective-permute-start.8
  45.3 22.5 %collective-permute-start.11 = (bf16[192,1536]{1,0:T(8,128)(2,1)S(1)}, bf16[192,1536]{1,0:T(8,128)(2,1)S(1)}, u32[]{:S(2)}, u32[]{:S(2)}) collective-permute-start(bf16[192,1536]{1,0:T(8,128)(2,1)S(1)} %slice.75), channel_id=1, source_target_pairs={{0,2},{6,4},{1,3},{7,5},{8,10},{14,12},{9,11},{15,13},{16,18},{22,... | collective-permute-start | bytes 1769480 | tf_op jit(solution)/shard_map/ppermute | solution.py:48
  67.8 0.7 collective-permute-start.7
  68.5 0.2 multiply_reduce_fusion.1
  68.8 13.7 %collective-permute-start.9 = (bf16[128,4096]{1,0:T(8,128)(2,1)S(1)}, bf16[128,4096]{1,0:T(8,128)(2,1)S(1)}, u32[]{:S(2)}, u32[]{:S(2)}) collective-permute-start(bf16[128,4096]{1,0:T(8,128)(2,1)S(1)} %bitcast.13), channel_id=1, source_target_pairs={{0,2},{6,4},{1,3},{7,5},{8,10},{14,12},{9,11},{15,13},{16,18},{22,... | collective-permute-start | bytes 3145736 | tf_op jit(solution)/shard_map/ppermute | solution.py:48
  82.5 0.1 fusion.16
  82.7 0.7 collective-permute-start.10
  83.3 0.7 collective-permute-start.12
  84.1 1.4 convolution_convert_fusion
  85.6 1.3 collective-permute-start.15
  86.9 14.5 %collective-permute-done.9 = bf16[128,4096]{1,0:T(8,128)(2,1)S(1)} collective-permute-done((bf16[128,4096]{1,0:T(8,128)(2,1)S(1)}, bf16[128,4096]{1,0:T(8,128)(2,1)S(1)}, u32[]{:S(2)}, u32[]{:S(2)}) %collective-permute-start.9) | collective-permute-done | bytes 1048608 | tf_op jit(solution)/shard_map/ppermute | solution.py:48
  101.4 0.8 fusion.13
  102.2 1.2 fusion.10
  103.4 0.6 collective-permute-start.13
  104.0 1.5 collective-permute-start.14
  105.5 0.8 convolution_convert_fusion.5
  106.3 2.8 %collective-permute-done.13 = bf16[384,256]{1,0:T(8,128)(2,1)S(1)} collective-permute-done((bf16[384,256]{1,0:T(8,128)(2,1)S(1)}, bf16[384,256]{1,0:T(8,128)(2,1)S(1)}, u32[]{:S(2)}, u32[]{:S(2)}) %collective-permute-start.13) | collective-permute-done | bytes 196640 | tf_op jit(solution)/shard_map/ppermute | solution.py:60
  109.2 2.1 %collective-permute-done.14 = bf16[384,256]{1,0:T(8,128)(2,1)S(1)} collective-permute-done((bf16[384,256]{1,0:T(8,128)(2,1)S(1)}, bf16[384,256]{1,0:T(8,128)(2,1)S(1)}, u32[]{:S(2)}, u32[]{:S(2)}) %collective-permute-start.14) | collective-permute-done | bytes 196640 | tf_op jit(solution)/shard_map/ppermute | solution.py:60
  111.3 0.8 convert_add_fusion.1
  112.0 6.9 %collective-permute-done.15 = bf16[128,2560]{1,0:T(8,128)(2,1)} collective-permute-done((bf16[128,2560]{1,0:T(8,128)(2,1)S(1)}, bf16[128,2560]{1,0:T(8,128)(2,1)}, u32[]{:S(2)}, u32[]{:S(2)}) %collective-permute-start.15) | collective-permute-done | bytes 655392 | tf_op jit(solution)/shard_map/ppermute | solution.py:56
  119.0 0.7 collective-permute-start.16
  119.7 1.3 collective-permute-start.22
  121.0 0.0 copy-start.6
  121.1 0.0 copy-start.10
  121.1 0.3 multiply_reduce_fusion
  121.3 0.2 multiply_convert_fusion
  121.6 0.5 copy-done.6
  122.1 0.2 copy-done.8
  122.3 0.2 copy-done.10
  122.5 0.2 copy-done.12
  122.7 0.9 convolution_convert_fusion.2
  123.6 1.3 collective-permute-start.18
  124.9 0.5 convolution_convert_fusion.4
  125.5 0.7 collective-permute-start.17
  126.2 14.6 %collective-permute-done.22 = bf16[128,1536]{1,0:T(8,128)(2,1)S(1)} collective-permute-done((bf16[128,1536]{1,0:T(8,128)(2,1)S(1)}, bf16[128,1536]{1,0:T(8,128)(2,1)S(1)}, u32[]{:S(2)}, u32[]{:S(2)}) %collective-permute-start.22) | collective-permute-done | bytes 393248 | tf_op jit(solution)/shard_map/ppermute | solution.py:56
  140.8 0.1 slice_select_fusion.1
  140.8 0.5 convolution_convert_fusion.3
  141.4 0.7 collective-permute-start.20
  142.1 0.9 convolution_convert_fusion.1
  143.0 0.5 fusion.1
  143.5 1.3 collective-permute-start.21
  144.8 12.0 %collective-permute-done.18 = bf16[192,2560]{1,0:T(8,128)(2,1)S(1)} collective-permute-done((bf16[192,2560]{1,0:T(8,128)(2,1)S(1)}, bf16[192,2560]{1,0:T(8,128)(2,1)S(1)}, u32[]{:S(2)}, u32[]{:S(2)}) %collective-permute-start.18) | collective-permute-done | bytes 983072 | tf_op jit(solution)/shard_map/ppermute | solution.py:140
  156.8 8.1 %collective-permute-start.19 = (bf16[192,2560]{1,0:T(8,128)(2,1)S(1)}, bf16[192,2560]{1,0:T(8,128)(2,1)S(1)}, u32[]{:S(2)}, u32[]{:S(2)}) collective-permute-start(bf16[192,2560]{1,0:T(8,128)(2,1)S(1)} %convolution_convert_fusion.1), channel_id=1, source_target_pairs={{8,0},{16,8},{24,16},{9,1},{17,9},{25,17},{10,2},{18,10},{26,18},{... | collective-permute-start | bytes 2949128 | tf_op jit(solution)/shard_map/ppermute | solution.py:13
  164.9 1.2 slice_select_fusion
  166.1 1.1 maximum_bitcast_fusion
  167.1 6.4 %collective-permute-done.21 = bf16[128,2560]{1,0:T(8,128)(2,1)S(1)} collective-permute-done((bf16[128,2560]{1,0:T(8,128)(2,1)S(1)}, bf16[128,2560]{1,0:T(8,128)(2,1)S(1)}, u32[]{:S(2)}, u32[]{:S(2)}) %collective-permute-start.21) | collective-permute-done | bytes 655392 | tf_op jit(solution)/shard_map/ppermute | solution.py:56
  173.5 1.4 fusion.3
  174.9 1.5 collective-permute-done.19
  176.5 1.0 select_bitcast_fusion
  (38 shorter events, 0.3 us)
Async XLA Ops:
  0.6 9.8 %copy-start.5 = (bf16[1,128,2560]{2,1,0:T(8,128)(2,1)S(1)}, bf16[1,128,2560]{2,1,0:T(8,128)(2,1)}, u32[]{:S(2)}) copy-start(bf16[1,128,2560]{2,1,0:T(8,128)(2,1)} %param.5) | copy-start | bytes 1966084
  0.6 5.7 %copy-start.1 = (bf16[1,192,2560]{2,1,0:T(8,128)(2,1)S(1)}, bf16[1,192,2560]{2,1,0:T(8,128)(2,1)}, u32[]{:S(2)}) copy-start(bf16[1,192,2560]{2,1,0:T(8,128)(2,1)} %param.4) | copy-start | bytes 2949124
  0.7 19.1 %collective-permute-start.1 = (bf16[128,2560]{1,0:T(8,128)(2,1)}, bf16[128,2560]{1,0:T(8,128)(2,1)S(1)}, u32[]{:S(2)}, u32[]{:S(2)}) collective-permute-start(bf16[128,2560]{1,0:T(8,128)(2,1)} %bitcast.22), channel_id=1, source_target_pairs={{0,2},{6,4},{1,3},{7,5},{8,10},{14,12},{9,11},{15,13},{16,18},{22,... | collective-permute-start | bytes 1966088 | tf_op jit(solution)/shard_map/ppermute | solution.py:48
  5.6 14.8 %collective-permute-start.5 = (bf16[192,2560]{1,0:T(8,128)(2,1)S(1)}, bf16[192,2560]{1,0:T(8,128)(2,1)S(1)}, u32[]{:S(2)}, u32[]{:S(2)}) collective-permute-start(bf16[192,2560]{1,0:T(8,128)(2,1)S(1)} %slice.74), channel_id=1, source_target_pairs={{2,4},{4,2},{3,5},{5,3},{10,12},{12,10},{11,13},{13,11},{18,20},{2... | collective-permute-start | bytes 2949128 | tf_op jit(solution)/shard_map/ppermute | solution.py:52
  6.3 34.3 %collective-permute-start = (bf16[192,2560]{1,0:T(8,128)(2,1)S(1)}, bf16[192,2560]{1,0:T(8,128)(2,1)S(1)}, u32[]{:S(2)}, u32[]{:S(2)}) collective-permute-start(bf16[192,2560]{1,0:T(8,128)(2,1)S(1)} %bitcast.16), channel_id=1, source_target_pairs={{0,2},{6,4},{1,3},{7,5},{8,10},{14,12},{9,11},{15,13},{16,18},{22,... | collective-permute-start | bytes 2949128 | tf_op jit(solution)/shard_map/ppermute | solution.py:48
  10.4 23.0 %collective-permute-start.2 = (bf16[128,2560]{1,0:T(8,128)(2,1)S(1)}, bf16[128,2560]{1,0:T(8,128)(2,1)S(1)}, u32[]{:S(2)}, u32[]{:S(2)}) collective-permute-start(bf16[128,2560]{1,0:T(8,128)(2,1)S(1)} %bitcast.23), channel_id=1, source_target_pairs={{2,4},{4,2},{3,5},{5,3},{10,12},{12,10},{11,13},{13,11},{18,20},{2... | collective-permute-start | bytes 1966088 | tf_op jit(solution)/shard_map/ppermute | solution.py:52
  19.7 22.2 %copy-start.7 = (bf16[128,2560]{1,0:T(8,128)(2,1)}, bf16[128,2560]{1,0:T(8,128)(2,1)S(1)}, u32[]{:S(2)}) copy-start(bf16[128,2560]{1,0:T(8,128)(2,1)S(1)} %collective-permute-done.1) | copy-start | bytes 1966084
  19.7 21.0 %collective-permute-start.3 = (bf16[128,2560]{1,0:T(8,128)(2,1)S(1)}, bf16[128,2560]{1,0:T(8,128)(2,1)S(1)}, u32[]{:S(2)}, u32[]{:S(2)}) collective-permute-start(bf16[128,2560]{1,0:T(8,128)(2,1)S(1)} %collective-permute-done.1), channel_id=1, source_target_pairs={{2,4},{4,2},{3,5},{5,3},{10,12},{12,10},{11,13},{13,11},{18,20},{2... | collective-permute-start | bytes 1966088 | tf_op jit(solution)/shard_map/ppermute | solution.py:52
  20.4 47.4 %collective-permute-start.6 = (bf16[192,2560]{1,0:T(8,128)(2,1)S(1)}, bf16[192,2560]{1,0:T(8,128)(2,1)S(1)}, u32[]{:S(2)}, u32[]{:S(2)}) collective-permute-start(bf16[192,2560]{1,0:T(8,128)(2,1)S(1)} %slice.74), channel_id=1, source_target_pairs={{0,2},{6,4},{1,3},{7,5},{8,10},{14,12},{9,11},{15,13},{16,18},{22,... | collective-permute-start | bytes 2949128 | tf_op jit(solution)/shard_map/ppermute | solution.py:48
  33.4 8.5 %copy-start.9 = (bf16[128,2560]{1,0:T(8,128)(2,1)}, bf16[128,2560]{1,0:T(8,128)(2,1)S(1)}, u32[]{:S(2)}) copy-start(bf16[128,2560]{1,0:T(8,128)(2,1)S(1)} %collective-permute-done.2) | copy-start | bytes 1966084
  40.7 1.2 copy-start.3
  40.7 1.2 copy-start.11
  41.9 26.8 %copy-start = (bf16[1,128,4096]{2,1,0:T(8,128)(2,1)S(1)}, bf16[1,128,4096]{2,1,0:T(8,128)(2,1)}, u32[]{:S(2)}) copy-start(bf16[1,128,4096]{2,1,0:T(8,128)(2,1)} %param.6) | copy-start | bytes 3145732
  41.9 26.6 %collective-permute-start.4 = (bf16[384,512]{1,0:T(8,128)(2,1)S(1)}, bf16[384,512]{1,0:T(8,128)(2,1)S(1)}, u32[]{:S(2)}, u32[]{:S(2)}) collective-permute-start(bf16[384,512]{1,0:T(8,128)(2,1)S(1)} %convolution_convert_fusion.6), channel_id=1, source_target_pairs={{0,1},{1,0},{2,3},{3,2},{4,5},{5,4},{6,7},{7,6},{8,9},{9,8},{10,11... | collective-permute-start | bytes 1179656 | tf_op jit(solution)/shard_map/ppermute | solution.py:60
  44.6 24.1 %collective-permute-start.8 = (bf16[192,1536]{1,0:T(8,128)(2,1)S(1)}, bf16[192,1536]{1,0:T(8,128)(2,1)S(1)}, u32[]{:S(2)}, u32[]{:S(2)}) collective-permute-start(bf16[192,1536]{1,0:T(8,128)(2,1)S(1)} %slice.75), channel_id=1, source_target_pairs={{2,4},{4,2},{3,5},{5,3},{10,12},{12,10},{11,13},{13,11},{18,20},{2... | collective-permute-start | bytes 1769480 | tf_op jit(solution)/shard_map/ppermute | solution.py:52
  45.3 38.0 %collective-permute-start.11 = (bf16[192,1536]{1,0:T(8,128)(2,1)S(1)}, bf16[192,1536]{1,0:T(8,128)(2,1)S(1)}, u32[]{:S(2)}, u32[]{:S(2)}) collective-permute-start(bf16[192,1536]{1,0:T(8,128)(2,1)S(1)} %slice.75), channel_id=1, source_target_pairs={{0,2},{6,4},{1,3},{7,5},{8,10},{14,12},{9,11},{15,13},{16,18},{22,... | collective-permute-start | bytes 1769480 | tf_op jit(solution)/shard_map/ppermute | solution.py:48
  67.8 16.3 %collective-permute-start.7 = (bf16[192,2560]{1,0:T(8,128)(2,1)S(1)}, bf16[192,2560]{1,0:T(8,128)(2,1)S(1)}, u32[]{:S(2)}, u32[]{:S(2)}) collective-permute-start(bf16[192,2560]{1,0:T(8,128)(2,1)S(1)} %collective-permute-done.6), channel_id=1, source_target_pairs={{2,4},{4,2},{3,5},{5,3},{10,12},{12,10},{11,13},{13,11},{18,20},{2... | collective-permute-start | bytes 2949128 | tf_op jit(solution)/shard_map/ppermute | solution.py:52
  68.8 32.6 %collective-permute-start.9 = (bf16[128,4096]{1,0:T(8,128)(2,1)S(1)}, bf16[128,4096]{1,0:T(8,128)(2,1)S(1)}, u32[]{:S(2)}, u32[]{:S(2)}) collective-permute-start(bf16[128,4096]{1,0:T(8,128)(2,1)S(1)} %bitcast.13), channel_id=1, source_target_pairs={{0,2},{6,4},{1,3},{7,5},{8,10},{14,12},{9,11},{15,13},{16,18},{22,... | collective-permute-start | bytes 3145736 | tf_op jit(solution)/shard_map/ppermute | solution.py:48
  82.7 1.4 collective-permute-start.10
  83.3 18.0 %collective-permute-start.12 = (bf16[192,1536]{1,0:T(8,128)(2,1)S(1)}, bf16[192,1536]{1,0:T(8,128)(2,1)S(1)}, u32[]{:S(2)}, u32[]{:S(2)}) collective-permute-start(bf16[192,1536]{1,0:T(8,128)(2,1)S(1)} %collective-permute-done.11), channel_id=1, source_target_pairs={{2,4},{4,2},{3,5},{5,3},{10,12},{12,10},{11,13},{13,11},{18,20},{2... | collective-permute-start | bytes 1769480 | tf_op jit(solution)/shard_map/ppermute | solution.py:52
  85.6 33.4 %collective-permute-start.15 = (bf16[128,2560]{1,0:T(8,128)(2,1)S(1)}, bf16[128,2560]{1,0:T(8,128)(2,1)}, u32[]{:S(2)}, u32[]{:S(2)}) collective-permute-start(bf16[128,2560]{1,0:T(8,128)(2,1)S(1)} %slice.82), channel_id=1, source_target_pairs={{2,0},{4,6},{3,1},{5,7},{10,8},{12,14},{11,9},{13,15},{18,16},{20,... | collective-permute-start | bytes 1966088 | tf_op jit(solution)/shard_map/ppermute | solution.py:56
  103.4 5.7 %collective-permute-start.13 = (bf16[384,256]{1,0:T(8,128)(2,1)S(1)}, bf16[384,256]{1,0:T(8,128)(2,1)S(1)}, u32[]{:S(2)}, u32[]{:S(2)}) collective-permute-start(bf16[384,256]{1,0:T(8,128)(2,1)S(1)} %get-tuple-element.23), channel_id=1, source_target_pairs={{0,1},{1,0},{2,3},{3,2},{4,5},{5,4},{6,7},{7,6},{8,9},{9,8},{10,11... | collective-permute-start | bytes 589832 | tf_op jit(solution)/shard_map/ppermute | solution.py:60
  104.0 7.2 %collective-permute-start.14 = (bf16[384,256]{1,0:T(8,128)(2,1)S(1)}, bf16[384,256]{1,0:T(8,128)(2,1)S(1)}, u32[]{:S(2)}, u32[]{:S(2)}) collective-permute-start(bf16[384,256]{1,0:T(8,128)(2,1)S(1)} %get-tuple-element.24), channel_id=1, source_target_pairs={{0,1},{1,0},{2,3},{3,2},{4,5},{5,4},{6,7},{7,6},{8,9},{9,8},{10,11... | collective-permute-start | bytes 589832 | tf_op jit(solution)/shard_map/ppermute | solution.py:60
  119.0 2.0 %collective-permute-start.16 = (bf16[384,256]{1,0:T(8,128)(2,1)}, bf16[384,256]{1,0:T(8,128)(2,1)S(1)}, u32[]{:S(2)}, u32[]{:S(2)}) collective-permute-start(bf16[384,256]{1,0:T(8,128)(2,1)} %get-tuple-element.17), channel_id=1, source_target_pairs={{2,4},{4,2},{3,5},{5,3},{10,12},{12,10},{11,13},{13,11},{18,20},{2... | collective-permute-start | bytes 589832 | tf_op jit(solution)/shard_map/ppermute | solution.py:52
  119.7 21.1 %collective-permute-start.22 = (bf16[128,1536]{1,0:T(8,128)(2,1)S(1)}, bf16[128,1536]{1,0:T(8,128)(2,1)S(1)}, u32[]{:S(2)}, u32[]{:S(2)}) collective-permute-start(bf16[128,1536]{1,0:T(8,128)(2,1)S(1)} %slice.86), channel_id=1, source_target_pairs={{2,0},{4,6},{3,1},{5,7},{10,8},{12,14},{11,9},{13,15},{18,16},{20,... | collective-permute-start | bytes 1179656 | tf_op jit(solution)/shard_map/ppermute | solution.py:56
  121.0 1.1 copy-start.6
  121.0 1.3 copy-start.8
  121.1 1.5 copy-start.10
  121.1 1.7 copy-start.12
  122.7 2.2 %copy-start.2 = (bf16[1,192,2560]{2,1,0:T(8,128)(2,1)S(1)}, bf16[1,192,2560]{2,1,0:T(8,128)(2,1)}, u32[]{:S(2)}) copy-start(bf16[1,192,2560]{2,1,0:T(8,128)(2,1)} %param.4) | copy-start | bytes 2949124
  122.7 2.2 %copy-start.4 = (bf16[192,2560]{1,0:T(8,128)(2,1)S(1)}, bf16[192,2560]{1,0:T(8,128)(2,1)}, u32[]{:S(2)}) copy-start(bf16[192,2560]{1,0:T(8,128)(2,1)} %copy-done.3) | copy-start | bytes 2949124
  123.6 33.2 %collective-permute-start.18 = (bf16[192,2560]{1,0:T(8,128)(2,1)S(1)}, bf16[192,2560]{1,0:T(8,128)(2,1)S(1)}, u32[]{:S(2)}, u32[]{:S(2)}) collective-permute-start(bf16[192,2560]{1,0:T(8,128)(2,1)S(1)} %convolution_convert_fusion.2), channel_id=1, source_target_pairs={{10,0},{12,6},{18,8},{20,14},{26,16},{28,22},{11,1},{13,7},{19,9},... | collective-permute-start | bytes 2949128 | tf_op jit(solution)/shard_map/ppermute | solution.py:140
  125.5 17.5 %collective-permute-start.17 = (bf16[128,2560]{1,0:T(8,128)(2,1)S(1)}, bf16[128,2560]{1,0:T(8,128)(2,1)S(1)}, u32[]{:S(2)}, u32[]{:S(2)}) collective-permute-start(bf16[128,2560]{1,0:T(8,128)(2,1)S(1)} %convolution_convert_fusion.4), channel_id=1, source_target_pairs={{2,4},{4,2},{3,5},{5,3},{10,12},{12,10},{11,13},{13,11},{18,20},{2... | collective-permute-start | bytes 1966088 | tf_op jit(solution)/shard_map/ppermute | solution.py:52
  141.4 25.8 %collective-permute-start.20 = (bf16[128,2560]{1,0:T(8,128)(2,1)S(1)}, bf16[128,2560]{1,0:T(8,128)(2,1)S(1)}, u32[]{:S(2)}, u32[]{:S(2)}) collective-permute-start(bf16[128,2560]{1,0:T(8,128)(2,1)S(1)} %convolution_convert_fusion.3), channel_id=1, source_target_pairs={{2,4},{4,2},{3,5},{5,3},{10,12},{12,10},{11,13},{13,11},{18,20},{2... | collective-permute-start | bytes 1966088 | tf_op jit(solution)/shard_map/ppermute | solution.py:52
  143.5 30.0 %collective-permute-start.21 = (bf16[128,2560]{1,0:T(8,128)(2,1)S(1)}, bf16[128,2560]{1,0:T(8,128)(2,1)S(1)}, u32[]{:S(2)}, u32[]{:S(2)}) collective-permute-start(bf16[128,2560]{1,0:T(8,128)(2,1)S(1)} %fusion.1), channel_id=1, source_target_pairs={{2,0},{4,6},{3,1},{5,7},{10,8},{12,14},{11,9},{13,15},{18,16},{20,... | collective-permute-start | bytes 1966088 | tf_op jit(solution)/shard_map/ppermute | solution.py:56
  156.8 19.7 %collective-permute-start.19 = (bf16[192,2560]{1,0:T(8,128)(2,1)S(1)}, bf16[192,2560]{1,0:T(8,128)(2,1)S(1)}, u32[]{:S(2)}, u32[]{:S(2)}) collective-permute-start(bf16[192,2560]{1,0:T(8,128)(2,1)S(1)} %convolution_convert_fusion.1), channel_id=1, source_target_pairs={{8,0},{16,8},{24,16},{9,1},{17,9},{25,17},{10,2},{18,10},{26,18},{... | collective-permute-start | bytes 2949128 | tf_op jit(solution)/shard_map/ppermute | solution.py:13

commit v3 on v2

--- a/solution.py
+++ b/solution.py
@@ -79,49 +79,57 @@
 
 def folded_body(inputs, down_weight, up_weight, value_grad):
     tokens, down, up, cotangent = inputs[0], down_weight[0], up_weight[0], value_grad[0]
-    rows, width = tokens.shape
+    rows = tokens.shape[0]
     lat = down.shape[0]
     feat = cotangent.shape[1]
-    sections = lax.axis_size("section")
     place = lax.axis_index("row")
     middle = (place == 1) | (place == 2)
 
-    cut = feat * 5 // 8 // 128 * 128
+    cut = feat // 2
     cuts = (slice(0, cut), slice(cut, feat))
-    cot_own = [cotangent[:, c] for c in cuts]
     down_end = inward(down)
     tokens_end = inward(tokens)
-    cot_other = [across(cot_own[0])]
     down_other = across(down)
-    cot_end = [inward(after(cot_own[0], down_end, cot_other[0]))]
+    cot_other = across(cotangent)
+    cot_end = [inward(cotangent[:, cuts[0]])]
     down_other_end = across(down_end)
-    cot_other.append(across(cot_own[1]))
-    cot_end.append(inward(after(cot_own[1], tokens_end, down_other)))
+    cot_end.append(inward(after(cotangent[:, cuts[1]], down_end, down_other)))
     cot_other_end = [across(cot_end[0])]
-    up_end = inward(after(up, cot_end[0], cot_other[1]))
+    up_end = inward(after(up, tokens_end, cot_end[0]))
+    down_there = [outward(down), outward(down_other), outward(down_other_end)]
 
-    tokens_mine = jnp.concatenate([tokens, tokens_end], axis=0)
+    tokens_mine = jnp.concatenate([tokens, after(tokens_end, down_there[0])], axis=0)
     down_all = jnp.concatenate([down, down_end, down_other, down_other_end], axis=0)
+    down_used = jnp.where(
+        middle,
+        down_all,
+        jnp.concatenate([down_there[0], down, down_there[1], down_there[2]], axis=0),
+    )
+
     latent = col_sum(rows_dot(tokens_mine, down_all))
     inv_rms = lax.rsqrt(jnp.mean(latent * latent, axis=-1, keepdims=True) + 1e-06)
     normed = latent * inv_rms
     normed_bf = normed.astype(BF16)
-    normed_sent = normed_bf[:, 2 * lat :]
+    normed_sent = after(normed_bf[:, 2 * lat :], down_there[1])
     normed_other = across(normed_sent)
     normed_all = jnp.concatenate([normed_bf[:, : 2 * lat], normed_other], axis=0)
 
     cot_other_end.append(across(after(cot_end[1], normed_sent)))
     cot_all = [
-        jnp.concatenate([cot_own[k], cot_end[k], cot_other[k], cot_other_end[k]], axis=0)
+        jnp.concatenate(
+            [cotangent[:, cuts[k]], cot_end[k], cot_other[:, cuts[k]], cot_other_end[k]], axis=0
+        )
         for k in range(2)
     ]
 
-    up_first = tokens_dot(normed_all, cot_all[0]).astype(BF16)
+    up_first = tokens_dot(after(normed_all, down_there[2]), cot_all[0]).astype(BF16)
     back_first = outward(up_first[lat:])
-    up_mine = jnp.concatenate([up, after(up_end, up_first)], axis=0)
+    up_mine = jnp.concatenate([up, after(up_end, up_first, down_used)], axis=0)
     grad = rows_dot(cot_all[0], up_mine[:, cuts[0]]) + rows_dot(cot_all[1], up_mine[:, cuts[1]])
-    grad_other = col_sum(grad[2 * rows :])
-    grad_mine = col_sum(grad[: 2 * rows])
+    grad = grad.astype(BF16)
+    from_col = other_col(grad[2 * rows :])
+    mine_from_col = other_col(grad[: 2 * rows])
+    grad_other = grad[2 * rows :].astype(F32) + from_col.astype(F32)
     up_second = tokens_dot(normed_all, cot_all[1]).astype(BF16)
     back_second = outward(up_second[lat:])
     up_grad = jnp.concatenate(
@@ -133,34 +141,24 @@
     )
 
     grad_sent = after(grad_other.astype(BF16), up_second, back_first)
+    grad_mine = grad[: 2 * rows].astype(F32) + after(mine_from_col, grad_sent).astype(F32)
     normed_grad = jnp.concatenate([grad_mine, across(grad_sent).astype(F32)], axis=1)
     inner = jnp.mean(normed_grad * normed, axis=-1, keepdims=True)
     latent_bf = (inv_rms * (normed_grad - normed * inner)).astype(BF16)
-    input_end = jnp.dot(latent_bf[rows:], down_all, preferred_element_type=F32).astype(BF16)
-    passed_end = lax.ppermute(
-        input_end,
-        ("section", "row"),
-        [
-            (4 * s + source, 4 * (s - 1) + target)
-            for s in range(1, sections)
-            for source, target in ((1, 0), (2, 3))
-        ],
-    )
+    latent_there = outward(latent_bf[rows:])
+    latent_used = jnp.where(middle, latent_bf[:rows], latent_there)
 
-    latent_bf = after(latent_bf, input_end)
     sums = [
         tokens_dot(latent_bf[:, j * lat : (j + 1) * lat], tokens_mine) for j in range(4)
     ]
     sent_end, sent_own = sums[3].astype(BF16), sums[2].astype(BF16)
-    from_end, from_own = across(sent_end), across(sent_own)
+    from_end, from_own = across(sent_end), across(after(sent_own, latent_there))
     down_end_grad = outward((sums[1] + from_end.astype(F32)).astype(BF16))
     down_own_grad = (sums[0] + from_own.astype(F32)).astype(BF16)
     down_grad = jnp.where(middle, down_own_grad, down_end_grad)
 
-    latent_own = after(latent_bf[:rows], sent_end, sent_own)
-    input_own = jnp.dot(latent_own, down_all, preferred_element_type=F32).astype(BF16)
-    passed_own = shifted(after(input_own, from_end, passed_end), "section", -1)
-    passed = jnp.where(middle, passed_own, passed_end)
+    input_grad = jnp.dot(latent_used, down_used, preferred_element_type=F32).astype(BF16)
+    passed = shifted(input_grad, "section", -1)
     return (passed[None], down_grad[None], up_grad[None])
 
 

time: 181 us -> 169 us (0.934)
  starting transfers between devices: 80.7 us -> 43 us
  waiting for transfers between devices: 76.6 us -> 103 us
    ppermute x5, starting transfers between devices: 56.9 us -> 21.9 us  [inward(): return lax.ppermute(value, 'row', [(0, 1), (3, 2)])]
    ppermute x3 -> x7, waiting for transfers between devices: 27.9 us -> 49.2 us  [outward(): return lax.ppermute(value, 'row', [(1, 0), (2, 3)])]
    ppermute x5, waiting for transfers between devices: 30.3 us -> 46.4 us  [inward(): return lax.ppermute(value, 'row', [(0, 1), (3, 2)])]
    ppermute x1 -> x0, waiting for transfers between devices: 12 us -> none  [folded_body(): lax.ppermute(input_end, ('section', 'row'), [(4 * s + source, 4 * (s - 1)...]
    ppermute x1, waiting for transfers between devices: 1.54 us -> 7.89 us  [shifted(): lax.ppermute(value, axis, [(source, source + steps) for source in range(l...]
    ppermute x1, starting transfers between devices: 8.06 us -> 1.92 us  [shifted(): lax.ppermute(value, axis, [(source, source + steps) for source in range(l...]
    ppermute x3 -> x7, starting transfers between devices: 3.88 us -> 9.18 us  [outward(): return lax.ppermute(value, 'row', [(1, 0), (2, 3)])]
    ppermute x3, waiting for transfers between devices: 4.95 us -> 0.01 us  [other_col(): return lax.ppermute(value, 'col', [(0, 1), (1, 0)])]
  transfers between devices with their start and end apart: 23 -> 25, of which waited for: 10 -> 12; matrix products, arithmetic and copies ran while one was open for 9% -> 10% of each run, Pallas kernels for 0% -> 0%
where the time goes in v3:
time: 169 us; the launch traced here: 167 us
  waiting for transfers between devices  103 us (61%)
  starting transfers between devices  43 us (25%)
  matrix products  11.2 us (7%)
  local copies, waits for them, and re-layouts  4.03 us (2%)
  other arithmetic  3.94 us (2%)
    ppermute x7, waiting for transfers between devices, outward(): return lax.ppermute(value, 'row', [(1, 0), (2, 3)])  49.2 us
    ppermute x5, waiting for transfers between devices, inward(): return lax.ppermute(value, 'row', [(0, 1), (3, 2)])  46.4 us
    ppermute x5, starting transfers between devices, inward(): return lax.ppermute(value, 'row', [(0, 1), (3, 2)])  21.9 us
    ppermute x7, starting transfers between devices, outward(): return lax.ppermute(value, 'row', [(1, 0), (2, 3)])  9.18 us
    ppermute x1, waiting for transfers between devices, shifted(): lax.ppermute(value, axis, [(source, source + steps) for source in range(l...  7.89 us
    ppermute x9, starting transfers between devices, across(): return lax.ppermute(value, 'row', [(1, 2), (2, 1)])  6.44 us
    dot_general x6, matrix products, tokens_dot(): lax.dot_general(left, right, (((0,), (0,)), ((), ())), preferred_element_...  5.87 us
    dot_general x3, matrix products, rows_dot(): lax.dot_general(left, right, (((1,), (1,)), ((), ())), preferred_element_...  4.62 us
  transfers between devices with their start and end apart: 25, of which 12 were waited for; matrix products, arithmetic and copies ran while one was open for 10% of the time, Pallas kernels for 0%

profile of v3, /device:TPU:4, one launch (start us, length us, event | category | flops | bytes accessed | tf_op | source)
XLA Modules:
  0.0 166.8 jit_solution(12648829520414097919)
XLA Ops:
  0.6 0.0 copy-start.4
  0.7 3.7 %collective-permute-start.2 = (bf16[128,2560]{1,0:T(8,128)(2,1)}, bf16[128,2560]{1,0:T(8,128)(2,1)S(1)}, u32[]{:S(2)}, u32[]{:S(2)}) collective-permute-start(bf16[128,2560]{1,0:T(8,128)(2,1)} %bitcast.20), channel_id=1, source_target_pairs={{0,2},{6,4},{1,3},{7,5},{8,10},{14,12},{9,11},{15,13},{16,18},{22,... | collective-permute-start | bytes 1966088 | tf_op jit(solution)/shard_map/ppermute | solution.py:48
  4.3 1.4 collective-permute-start
  5.7 1.3 collective-permute-start.1
  7.0 0.7 collective-permute-start.3
  7.7 12.0 %collective-permute-done.2 = bf16[128,2560]{1,0:T(8,128)(2,1)S(1)} collective-permute-done((bf16[128,2560]{1,0:T(8,128)(2,1)}, bf16[128,2560]{1,0:T(8,128)(2,1)S(1)}, u32[]{:S(2)}, u32[]{:S(2)}) %collective-permute-start.2) | collective-permute-done | bytes 655392 | tf_op jit(solution)/shard_map/ppermute | solution.py:48
  19.7 0.7 collective-permute-start.4
  20.4 0.8 collective-permute-start.7
  21.2 2.7 %fusion.24 = (bf16[192,2048]{1,0:T(8,128)(2,1)}, bf16[192,2048]{1,0:T(8,128)(2,1)}) fusion(bf16[192,4096]{1,0:T(8,128)(2,1)} %bitcast.12), kind=kLoop, calls=%fused_computation.52 | loop fusion | bytes 3145728 | tf_op jit(solution)/shard_map/slice | solution.py:120
  23.9 0.1 collective-permute-done.1
  24.0 9.5 %collective-permute-start.6 = (bf16[192,2048]{1,0:T(8,128)(2,1)}, bf16[192,2048]{1,0:T(8,128)(2,1)}, u32[]{:S(2)}, u32[]{:S(2)}) collective-permute-start(bf16[192,2048]{1,0:T(8,128)(2,1)} %get-tuple-element.26), channel_id=1, source_target_pairs={{0,2},{6,4},{1,3},{7,5},{8,10},{14,12},{9,11},{15,13},{16,18},{22,... | collective-permute-start | bytes 2359304 | tf_op jit(solution)/shard_map/ppermute | solution.py:48
  33.4 7.3 %collective-permute-done = bf16[192,2560]{1,0:T(8,128)(2,1)S(1)} collective-permute-done((bf16[192,2560]{1,0:T(8,128)(2,1)}, bf16[192,2560]{1,0:T(8,128)(2,1)S(1)}, u32[]{:S(2)}, u32[]{:S(2)}) %collective-permute-start) | collective-permute-done | bytes 983072 | tf_op jit(solution)/shard_map/ppermute | solution.py:48
  40.8 0.0 copy-start.12
  40.8 1.2 convolution_convert_fusion.5
  42.1 0.1 copy-done.12
  42.2 1.5 collective-permute-start.5
  43.6 4.7 %collective-permute-start.13 = (bf16[192,2048]{1,0:T(8,128)(2,1)}, bf16[192,2048]{1,0:T(8,128)(2,1)S(1)}, u32[]{:S(2)}, u32[]{:S(2)}) collective-permute-start(bf16[192,2048]{1,0:T(8,128)(2,1)} %get-tuple-element.18), channel_id=1, source_target_pairs={{0,2},{6,4},{1,3},{7,5},{8,10},{14,12},{9,11},{15,13},{16,18},{22,... | collective-permute-start | bytes 2359304 | tf_op jit(solution)/shard_map/ppermute | solution.py:48
  48.4 1.3 collective-permute-start.10
  49.7 7.9 %collective-permute-done.6 = bf16[192,2048]{1,0:T(8,128)(2,1)} collective-permute-done((bf16[192,2048]{1,0:T(8,128)(2,1)}, bf16[192,2048]{1,0:T(8,128)(2,1)}, u32[]{:S(2)}, u32[]{:S(2)}) %collective-permute-start.6) | collective-permute-done | bytes 786464 | tf_op jit(solution)/shard_map/ppermute | solution.py:48
  57.6 0.7 collective-permute-start.8
  58.3 1.3 collective-permute-start.12
  59.6 0.2 multiply_reduce_fusion.1
  59.9 0.1 fusion.8
  60.0 4.6 %collective-permute-done.10 = bf16[128,2560]{1,0:T(8,128)(2,1)S(1)} collective-permute-done((bf16[128,2560]{1,0:T(8,128)(2,1)}, bf16[128,2560]{1,0:T(8,128)(2,1)S(1)}, u32[]{:S(2)}, u32[]{:S(2)}) %collective-permute-start.10) | collective-permute-done | bytes 655392 | tf_op jit(solution)/shard_map/ppermute | solution.py:56
  64.7 2.7 %collective-permute-start.9 = (bf16[128,4096]{1,0:T(8,128)(2,1)S(1)}, bf16[128,4096]{1,0:T(8,128)(2,1)S(1)}, u32[]{:S(2)}, u32[]{:S(2)}) collective-permute-start(bf16[128,4096]{1,0:T(8,128)(2,1)S(1)} %bitcast.25), channel_id=1, source_target_pairs={{0,2},{6,4},{1,3},{7,5},{8,10},{14,12},{9,11},{15,13},{16,18},{22,... | collective-permute-start | bytes 3145736 | tf_op jit(solution)/shard_map/ppermute | solution.py:48
  67.3 0.7 collective-permute-start.11
  68.0 0.1 fusion.23
  68.1 6.3 %collective-permute-done.13 = bf16[192,2048]{1,0:T(8,128)(2,1)S(1)} collective-permute-done((bf16[192,2048]{1,0:T(8,128)(2,1)}, bf16[192,2048]{1,0:T(8,128)(2,1)S(1)}, u32[]{:S(2)}, u32[]{:S(2)}) %collective-permute-start.13) | collective-permute-done | bytes 786464 | tf_op jit(solution)/shard_map/ppermute | solution.py:48
  74.5 0.7 collective-permute-start.14
  75.2 2.9 %collective-permute-done.12 = bf16[128,2560]{1,0:T(8,128)(2,1)S(1)} collective-permute-done((bf16[128,2560]{1,0:T(8,128)(2,1)}, bf16[128,2560]{1,0:T(8,128)(2,1)S(1)}, u32[]{:S(2)}, u32[]{:S(2)}) %collective-permute-start.12) | collective-permute-done | bytes 655392 | tf_op jit(solution)/shard_map/ppermute | solution.py:56
  78.2 0.0 copy-start.13
  78.2 2.5 %convolution_convert_fusion.4 = bf16[256,2048]{1,0:T(8,128)(2,1)S(1)} fusion(bf16[768,256]{1,0:T(8,128)(2,1)S(1)} %pad_maximum_fusion.12, bf16[192,2048]{1,0:T(8,128)(2,1)S(1)} %collective-permute-done.8, bf16[192,2048]{1,0:T(8,128)(2,1)S(1)} %get-tuple-element.24, bf16[192,2048]{1,0:T(8,128)(2,1)} %collective-permute-done.6, ...), kind=kOutput, calls=%fused_computation.8 | convolution fusion | flops 818413568 | bytes 4587520 | tf_op jit(solution)/shard_map/dot_general | solution.py:72
  80.8 1.4 collective-permute-start.17
  82.3 0.7 maximum_select_fusion
  83.0 12.7 %collective-permute-done.9 = bf16[128,4096]{1,0:T(8,128)(2,1)S(1)} collective-permute-done((bf16[128,4096]{1,0:T(8,128)(2,1)S(1)}, bf16[128,4096]{1,0:T(8,128)(2,1)S(1)}, u32[]{:S(2)}, u32[]{:S(2)}) %collective-permute-start.9) | collective-permute-done | bytes 1048608 | tf_op jit(solution)/shard_map/ppermute | solution.py:48
  95.7 1.0 fusion.3
  96.7 2.4 %fusion = bf16[768,256]{1,0:T(8,128)(2,1)S(1)} fusion(f32[768,256]{1,0:T(8,128)S(1)} %fusion.3, bf16[128,4096]{1,0:T(8,128)(2,1)S(1)} %bitcast.27, bf16[128,4096]{1,0:T(8,128)(2,1)S(1)} %collective-permute-done.9, bf16[192,2048]{1,0:T(8,128)(2,1)S(1)} %collective-permute-done.8, bf16[192,2048]{1,0:T(8,128)(2,1)S(1)} %get-tuple-element.24, ...), kind=kOutput, calls=%fused_computation.15 | convolution fusion | flops 820379648 | bytes 6422528 | tf_op jit(solution)/shard_map/dot_general | solution.py:68
  99.2 1.6 collective-permute-start.16
  100.7 0.5 collective-permute-start.15
  101.3 1.2 convolution_convert_fusion.3
  102.5 1.3 collective-permute-start.24
  103.8 7.2 %collective-permute-done.17 = bf16[128,2048]{1,0:T(8,128)(2,1)S(1)} collective-permute-done((bf16[128,2048]{1,0:T(8,128)(2,1)S(1)}, bf16[128,2048]{1,0:T(8,128)(2,1)S(1)}, u32[]{:S(2)}, u32[]{:S(2)}) %collective-permute-start.17) | collective-permute-done | bytes 524320 | tf_op jit(solution)/shard_map/ppermute | solution.py:56
  111.0 0.1 slice_select_fusion.1
  111.1 0.1 add_convert_fusion.2
  111.2 0.8 collective-permute-start.18
  112.1 0.3 multiply_reduce_fusion
  112.4 0.2 multiply_convert_fusion
  112.6 0.5 convolution_convert_fusion.1
  113.1 0.7 collective-permute-start.22
  113.9 0.5 fusion.16
  114.4 1.3 collective-permute-start.19
  115.7 0.5 convolution_convert_fusion.2
  116.3 25.6 %collective-permute-done.19 = bf16[192,512]{1,0:T(8,128)(2,1)S(1)} collective-permute-done((bf16[192,512]{1,0:T(8,128)(2,1)S(1)}, bf16[192,512]{1,0:T(8,128)(2,1)S(1)}, u32[]{:S(2)}, u32[]{:S(2)}) %collective-permute-start.19) | collective-permute-done | bytes 196640 | tf_op jit(solution)/shard_map/ppermute | solution.py:56
  141.8 0.7 convolution_convert_fusion
  142.5 1.9 %collective-permute-start.20 = (bf16[192,2560]{1,0:T(8,128)(2,1)S(1)}, bf16[192,2560]{1,0:T(8,128)(2,1)S(1)}, u32[]{:S(2)}, u32[]{:S(2)}) collective-permute-start(bf16[192,2560]{1,0:T(8,128)(2,1)S(1)} %convolution_convert_fusion), channel_id=1, source_target_pairs={{8,0},{16,8},{24,16},{9,1},{17,9},{25,17},{10,2},{18,10},{26,18},{... | collective-permute-start | bytes 2949128 | tf_op jit(solution)/shard_map/ppermute | solution.py:13
  144.4 0.7 collective-permute-start.21
  145.2 0.5 add_convert_fusion
  145.7 1.3 collective-permute-start.23
  147.0 0.1 slice_select_fusion
  147.1 1.1 maximum_bitcast_fusion
  148.2 7.9 %collective-permute-done.20 = bf16[192,2560]{1,0:T(8,128)(2,1)S(1)} collective-permute-done((bf16[192,2560]{1,0:T(8,128)(2,1)S(1)}, bf16[192,2560]{1,0:T(8,128)(2,1)S(1)}, u32[]{:S(2)}, u32[]{:S(2)}) %collective-permute-start.20) | collective-permute-done | bytes 983072 | tf_op jit(solution)/shard_map/ppermute | solution.py:13
  156.0 8.8 %collective-permute-done.23 = bf16[128,2560]{1,0:T(8,128)(2,1)S(1)} collective-permute-done((bf16[128,2560]{1,0:T(8,128)(2,1)S(1)}, bf16[128,2560]{1,0:T(8,128)(2,1)S(1)}, u32[]{:S(2)}, u32[]{:S(2)}) %collective-permute-start.23) | collective-permute-done | bytes 655392 | tf_op jit(solution)/shard_map/ppermute | solution.py:56
  164.8 1.1 fusion.7
  165.9 0.9 copy.12
  (49 shorter events, 0.4 us)
Async XLA Ops:
  0.6 40.2 %copy-start.4 = (bf16[1,128,2560]{2,1,0:T(8,128)(2,1)S(1)}, bf16[1,128,2560]{2,1,0:T(8,128)(2,1)}, u32[]{:S(2)}) copy-start(bf16[1,128,2560]{2,1,0:T(8,128)(2,1)} %param.5) | copy-start | bytes 1966084
  0.6 40.2 %copy-start = (bf16[1,192,2560]{2,1,0:T(8,128)(2,1)S(1)}, bf16[1,192,2560]{2,1,0:T(8,128)(2,1)}, u32[]{:S(2)}) copy-start(bf16[1,192,2560]{2,1,0:T(8,128)(2,1)} %param.4) | copy-start | bytes 2949124
  0.7 19.1 %collective-permute-start.2 = (bf16[128,2560]{1,0:T(8,128)(2,1)}, bf16[128,2560]{1,0:T(8,128)(2,1)S(1)}, u32[]{:S(2)}, u32[]{:S(2)}) collective-permute-start(bf16[128,2560]{1,0:T(8,128)(2,1)} %bitcast.20), channel_id=1, source_target_pairs={{0,2},{6,4},{1,3},{7,5},{8,10},{14,12},{9,11},{15,13},{16,18},{22,... | collective-permute-start | bytes 1966088 | tf_op jit(solution)/shard_map/ppermute | solution.py:48
  4.3 36.5 %collective-permute-start = (bf16[192,2560]{1,0:T(8,128)(2,1)}, bf16[192,2560]{1,0:T(8,128)(2,1)S(1)}, u32[]{:S(2)}, u32[]{:S(2)}) collective-permute-start(bf16[192,2560]{1,0:T(8,128)(2,1)} %bitcast.13), channel_id=1, source_target_pairs={{0,2},{6,4},{1,3},{7,5},{8,10},{14,12},{9,11},{15,13},{16,18},{22,... | collective-permute-start | bytes 2949128 | tf_op jit(solution)/shard_map/ppermute | solution.py:48
  5.7 18.3 %collective-permute-start.1 = (bf16[128,2560]{1,0:T(8,128)(2,1)}, bf16[128,2560]{1,0:T(8,128)(2,1)S(1)}, u32[]{:S(2)}, u32[]{:S(2)}) collective-permute-start(bf16[128,2560]{1,0:T(8,128)(2,1)} %bitcast.21), channel_id=1, source_target_pairs={{2,0},{4,6},{3,1},{5,7},{10,8},{12,14},{11,9},{13,15},{18,16},{20,... | collective-permute-start | bytes 1966088 | tf_op jit(solution)/shard_map/ppermute | solution.py:56
  7.0 33.8 %collective-permute-start.3 = (bf16[128,2560]{1,0:T(8,128)(2,1)}, bf16[128,2560]{1,0:T(8,128)(2,1)S(1)}, u32[]{:S(2)}, u32[]{:S(2)}) collective-permute-start(bf16[128,2560]{1,0:T(8,128)(2,1)} %bitcast.22), channel_id=1, source_target_pairs={{2,4},{4,2},{3,5},{5,3},{10,12},{12,10},{11,13},{13,11},{18,20},{2... | collective-permute-start | bytes 1966088 | tf_op jit(solution)/shard_map/ppermute | solution.py:52
  19.7 22.3 %copy-start.6 = (bf16[128,2560]{1,0:T(8,128)(2,1)}, bf16[128,2560]{1,0:T(8,128)(2,1)S(1)}, u32[]{:S(2)}) copy-start(bf16[128,2560]{1,0:T(8,128)(2,1)S(1)} %collective-permute-done.2) | copy-start | bytes 1966084
  19.7 21.1 %collective-permute-start.4 = (bf16[128,2560]{1,0:T(8,128)(2,1)S(1)}, bf16[128,2560]{1,0:T(8,128)(2,1)S(1)}, u32[]{:S(2)}, u32[]{:S(2)}) collective-permute-start(bf16[128,2560]{1,0:T(8,128)(2,1)S(1)} %collective-permute-done.2), channel_id=1, source_target_pairs={{2,4},{4,2},{3,5},{5,3},{10,12},{12,10},{11,13},{13,11},{18,20},{2... | collective-permute-start | bytes 1966088 | tf_op jit(solution)/shard_map/ppermute | solution.py:52
  20.4 46.9 %collective-permute-start.7 = (bf16[192,4096]{1,0:T(8,128)(2,1)}, bf16[192,4096]{1,0:T(8,128)(2,1)S(1)}, u32[]{:S(2)}, u32[]{:S(2)}) collective-permute-start(bf16[192,4096]{1,0:T(8,128)(2,1)} %bitcast.11), channel_id=1, source_target_pairs={{2,4},{4,2},{3,5},{5,3},{10,12},{12,10},{11,13},{13,11},{18,20},{2... | collective-permute-start | bytes 4718600 | tf_op jit(solution)/shard_map/ppermute | solution.py:52
  24.0 16.8 %copy-start.8 = (bf16[128,2560]{1,0:T(8,128)(2,1)}, bf16[128,2560]{1,0:T(8,128)(2,1)S(1)}, u32[]{:S(2)}) copy-start(bf16[128,2560]{1,0:T(8,128)(2,1)S(1)} %collective-permute-done.1) | copy-start | bytes 1966084
  24.0 33.7 %collective-permute-start.6 = (bf16[192,2048]{1,0:T(8,128)(2,1)}, bf16[192,2048]{1,0:T(8,128)(2,1)}, u32[]{:S(2)}, u32[]{:S(2)}) collective-permute-start(bf16[192,2048]{1,0:T(8,128)(2,1)} %get-tuple-element.26), channel_id=1, source_target_pairs={{0,2},{6,4},{1,3},{7,5},{8,10},{14,12},{9,11},{15,13},{16,18},{22,... | collective-permute-start | bytes 2359304 | tf_op jit(solution)/shard_map/ppermute | solution.py:48
  40.8 1.3 copy-start.1
  40.8 1.3 copy-start.10
  40.8 1.3 copy-start.12
  42.2 16.2 %collective-permute-start.5 = (bf16[384,512]{1,0:T(8,128)(2,1)S(1)}, bf16[384,512]{1,0:T(8,128)(2,1)S(1)}, u32[]{:S(2)}, u32[]{:S(2)}) collective-permute-start(bf16[384,512]{1,0:T(8,128)(2,1)S(1)} %convolution_convert_fusion.5), channel_id=1, source_target_pairs={{0,1},{1,0},{2,3},{3,2},{4,5},{5,4},{6,7},{7,6},{8,9},{9,8},{10,11... | collective-permute-start | bytes 1179656 | tf_op jit(solution)/shard_map/ppermute | solution.py:60
  43.6 21.0 %copy-start.14 = (bf16[1,128,4096]{2,1,0:T(8,128)(2,1)S(1)}, bf16[1,128,4096]{2,1,0:T(8,128)(2,1)}, u32[]{:S(2)}) copy-start(bf16[1,128,4096]{2,1,0:T(8,128)(2,1)} %param.6) | copy-start | bytes 3145732
  43.6 30.8 %collective-permute-start.13 = (bf16[192,2048]{1,0:T(8,128)(2,1)}, bf16[192,2048]{1,0:T(8,128)(2,1)S(1)}, u32[]{:S(2)}, u32[]{:S(2)}) collective-permute-start(bf16[192,2048]{1,0:T(8,128)(2,1)} %get-tuple-element.18), channel_id=1, source_target_pairs={{0,2},{6,4},{1,3},{7,5},{8,10},{14,12},{9,11},{15,13},{16,18},{22,... | collective-permute-start | bytes 2359304 | tf_op jit(solution)/shard_map/ppermute | solution.py:48
  48.4 16.3 %collective-permute-start.10 = (bf16[128,2560]{1,0:T(8,128)(2,1)}, bf16[128,2560]{1,0:T(8,128)(2,1)S(1)}, u32[]{:S(2)}, u32[]{:S(2)}) collective-permute-start(bf16[128,2560]{1,0:T(8,128)(2,1)} %copy-done.10), channel_id=1, source_target_pairs={{2,0},{4,6},{3,1},{5,7},{10,8},{12,14},{11,9},{13,15},{18,16},{20,... | collective-permute-start | bytes 1966088 | tf_op jit(solution)/shard_map/ppermute | solution.py:56
  57.6 20.5 %collective-permute-start.8 = (bf16[192,2048]{1,0:T(8,128)(2,1)}, bf16[192,2048]{1,0:T(8,128)(2,1)S(1)}, u32[]{:S(2)}, u32[]{:S(2)}) collective-permute-start(bf16[192,2048]{1,0:T(8,128)(2,1)} %collective-permute-done.6), channel_id=1, source_target_pairs={{2,4},{4,2},{3,5},{5,3},{10,12},{12,10},{11,13},{13,11},{18,20},{2... | collective-permute-start | bytes 2359304 | tf_op jit(solution)/shard_map/ppermute | solution.py:52
  58.3 19.8 %collective-permute-start.12 = (bf16[128,2560]{1,0:T(8,128)(2,1)}, bf16[128,2560]{1,0:T(8,128)(2,1)S(1)}, u32[]{:S(2)}, u32[]{:S(2)}) collective-permute-start(bf16[128,2560]{1,0:T(8,128)(2,1)} %copy-done.12), channel_id=1, source_target_pairs={{2,0},{4,6},{3,1},{5,7},{10,8},{12,14},{11,9},{13,15},{18,16},{20,... | collective-permute-start | bytes 1966088 | tf_op jit(solution)/shard_map/ppermute | solution.py:56
  64.7 31.0 %collective-permute-start.9 = (bf16[128,4096]{1,0:T(8,128)(2,1)S(1)}, bf16[128,4096]{1,0:T(8,128)(2,1)S(1)}, u32[]{:S(2)}, u32[]{:S(2)}) collective-permute-start(bf16[128,4096]{1,0:T(8,128)(2,1)S(1)} %bitcast.25), channel_id=1, source_target_pairs={{0,2},{6,4},{1,3},{7,5},{8,10},{14,12},{9,11},{15,13},{16,18},{22,... | collective-permute-start | bytes 3145736 | tf_op jit(solution)/shard_map/ppermute | solution.py:48
  67.3 7.8 %collective-permute-start.11 = (bf16[384,256]{1,0:T(8,128)(2,1)S(1)}, bf16[384,256]{1,0:T(8,128)(2,1)S(1)}, u32[]{:S(2)}, u32[]{:S(2)}) collective-permute-start(bf16[384,256]{1,0:T(8,128)(2,1)S(1)} %get-tuple-element.15), channel_id=1, source_target_pairs={{2,4},{4,2},{3,5},{5,3},{10,12},{12,10},{11,13},{13,11},{18,20},{2... | collective-permute-start | bytes 589832 | tf_op jit(solution)/shard_map/ppermute | solution.py:52
  74.5 21.2 %collective-permute-start.14 = (bf16[192,2048]{1,0:T(8,128)(2,1)S(1)}, bf16[192,2048]{1,0:T(8,128)(2,1)S(1)}, u32[]{:S(2)}, u32[]{:S(2)}) collective-permute-start(bf16[192,2048]{1,0:T(8,128)(2,1)S(1)} %collective-permute-done.13), channel_id=1, source_target_pairs={{2,4},{4,2},{3,5},{5,3},{10,12},{12,10},{11,13},{13,11},{18,20},{2... | collective-permute-start | bytes 2359304 | tf_op jit(solution)/shard_map/ppermute | solution.py:52
  78.2 4.1 %copy-start.5 = (bf16[1,128,2560]{2,1,0:T(8,128)(2,1)S(1)}, bf16[1,128,2560]{2,1,0:T(8,128)(2,1)}, u32[]{:S(2)}) copy-start(bf16[1,128,2560]{2,1,0:T(8,128)(2,1)} %param.5) | copy-start | bytes 1966084
  78.2 4.1 %copy-start.7 = (bf16[128,2560]{1,0:T(8,128)(2,1)S(1)}, bf16[128,2560]{1,0:T(8,128)(2,1)}, u32[]{:S(2)}) copy-start(bf16[128,2560]{1,0:T(8,128)(2,1)} %copy-done.6) | copy-start | bytes 1966084
  78.2 4.1 %copy-start.9 = (bf16[128,2560]{1,0:T(8,128)(2,1)S(1)}, bf16[128,2560]{1,0:T(8,128)(2,1)}, u32[]{:S(2)}) copy-start(bf16[128,2560]{1,0:T(8,128)(2,1)} %copy-done.8) | copy-start | bytes 1966084
  78.2 4.1 %copy-start.11 = (bf16[128,2560]{1,0:T(8,128)(2,1)S(1)}, bf16[128,2560]{1,0:T(8,128)(2,1)}, u32[]{:S(2)}) copy-start(bf16[128,2560]{1,0:T(8,128)(2,1)} %copy-done.10) | copy-start | bytes 1966084
  78.2 4.1 %copy-start.13 = (bf16[128,2560]{1,0:T(8,128)(2,1)S(1)}, bf16[128,2560]{1,0:T(8,128)(2,1)}, u32[]{:S(2)}) copy-start(bf16[128,2560]{1,0:T(8,128)(2,1)} %copy-done.12) | copy-start | bytes 1966084
  80.8 14.9 %copy-start.3 = (bf16[192,2048]{1,0:T(8,128)(2,1)S(1)}, bf16[192,2048]{1,0:T(8,128)(2,1)}, u32[]{:S(2)}) copy-start(bf16[192,2048]{1,0:T(8,128)(2,1)} %get-tuple-element.18) | copy-start | bytes 2359300
  80.8 30.3 %collective-permute-start.17 = (bf16[128,2048]{1,0:T(8,128)(2,1)S(1)}, bf16[128,2048]{1,0:T(8,128)(2,1)S(1)}, u32[]{:S(2)}, u32[]{:S(2)}) collective-permute-start(bf16[128,2048]{1,0:T(8,128)(2,1)S(1)} %slice.94), channel_id=1, source_target_pairs={{2,0},{4,6},{3,1},{5,7},{10,8},{12,14},{11,9},{13,15},{18,16},{20,... | collective-permute-start | bytes 1572872 | tf_op jit(solution)/shard_map/ppermute | solution.py:56
  99.2 11.9 %collective-permute-start.16 = (bf16[384,256]{1,0:T(8,128)(2,1)S(1)}, bf16[384,256]{1,0:T(8,128)(2,1)S(1)}, u32[]{:S(2)}, u32[]{:S(2)}) collective-permute-start(bf16[384,256]{1,0:T(8,128)(2,1)S(1)} %get-tuple-element.28), channel_id=1, source_target_pairs={{0,1},{1,0},{2,3},{3,2},{4,5},{5,4},{6,7},{7,6},{8,9},{9,8},{10,11... | collective-permute-start | bytes 589832 | tf_op jit(solution)/shard_map/ppermute | solution.py:60
  100.7 11.3 %collective-permute-start.15 = (bf16[384,256]{1,0:T(8,128)(2,1)S(1)}, bf16[384,256]{1,0:T(8,128)(2,1)S(1)}, u32[]{:S(2)}, u32[]{:S(2)}) collective-permute-start(bf16[384,256]{1,0:T(8,128)(2,1)S(1)} %get-tuple-element.27), channel_id=1, source_target_pairs={{0,1},{1,0},{2,3},{3,2},{4,5},{5,4},{6,7},{7,6},{8,9},{9,8},{10,11... | collective-permute-start | bytes 589832 | tf_op jit(solution)/shard_map/ppermute | solution.py:60
  102.5 44.5 %collective-permute-start.24 = (bf16[128,2048]{1,0:T(8,128)(2,1)S(1)}, bf16[128,2048]{1,0:T(8,128)(2,1)S(1)}, u32[]{:S(2)}, u32[]{:S(2)}) collective-permute-start(bf16[128,2048]{1,0:T(8,128)(2,1)S(1)} %slice.103), channel_id=1, source_target_pairs={{2,0},{4,6},{3,1},{5,7},{10,8},{12,14},{11,9},{13,15},{18,16},{20,... | collective-permute-start | bytes 1572872 | tf_op jit(solution)/shard_map/ppermute | solution.py:56
  111.1 1.5 copy-start.2
  111.2 0.9 collective-permute-start.18
  113.1 32.0 %collective-permute-start.22 = (bf16[128,2560]{1,0:T(8,128)(2,1)S(1)}, bf16[128,2560]{1,0:T(8,128)(2,1)S(1)}, u32[]{:S(2)}, u32[]{:S(2)}) collective-permute-start(bf16[128,2560]{1,0:T(8,128)(2,1)S(1)} %convolution_convert_fusion.1), channel_id=1, source_target_pairs={{2,4},{4,2},{3,5},{5,3},{10,12},{12,10},{11,13},{13,11},{18,20},{2... | collective-permute-start | bytes 1966088 | tf_op jit(solution)/shard_map/ppermute | solution.py:52
  114.4 27.4 %collective-permute-start.19 = (bf16[192,512]{1,0:T(8,128)(2,1)S(1)}, bf16[192,512]{1,0:T(8,128)(2,1)S(1)}, u32[]{:S(2)}, u32[]{:S(2)}) collective-permute-start(bf16[192,512]{1,0:T(8,128)(2,1)S(1)} %slice.96), channel_id=1, source_target_pairs={{2,0},{4,6},{3,1},{5,7},{10,8},{12,14},{11,9},{13,15},{18,16},{20,... | collective-permute-start | bytes 589832 | tf_op jit(solution)/shard_map/ppermute | solution.py:56
  142.5 13.5 %collective-permute-start.20 = (bf16[192,2560]{1,0:T(8,128)(2,1)S(1)}, bf16[192,2560]{1,0:T(8,128)(2,1)S(1)}, u32[]{:S(2)}, u32[]{:S(2)}) collective-permute-start(bf16[192,2560]{1,0:T(8,128)(2,1)S(1)} %convolution_convert_fusion), channel_id=1, source_target_pairs={{8,0},{16,8},{24,16},{9,1},{17,9},{25,17},{10,2},{18,10},{26,18},{... | collective-permute-start | bytes 2949128 | tf_op jit(solution)/shard_map/ppermute | solution.py:13
  144.4 11.6 %collective-permute-start.21 = (bf16[128,2560]{1,0:T(8,128)(2,1)S(1)}, bf16[128,2560]{1,0:T(8,128)(2,1)S(1)}, u32[]{:S(2)}, u32[]{:S(2)}) collective-permute-start(bf16[128,2560]{1,0:T(8,128)(2,1)S(1)} %convolution_convert_fusion.2), channel_id=1, source_target_pairs={{2,4},{4,2},{3,5},{5,3},{10,12},{12,10},{11,13},{13,11},{18,20},{2... | collective-permute-start | bytes 1966088 | tf_op jit(solution)/shard_map/ppermute | solution.py:52
  145.7 19.1 %collective-permute-start.23 = (bf16[128,2560]{1,0:T(8,128)(2,1)S(1)}, bf16[128,2560]{1,0:T(8,128)(2,1)S(1)}, u32[]{:S(2)}, u32[]{:S(2)}) collective-permute-start(bf16[128,2560]{1,0:T(8,128)(2,1)S(1)} %add_convert_fusion), channel_id=1, source_target_pairs={{2,0},{4,6},{3,1},{5,7},{10,8},{12,14},{11,9},{13,15},{18,16},{20,... | collective-permute-start | bytes 1966088 | tf_op jit(solution)/shard_map/ppermute | solution.py:56

commit v4 on v3

--- a/solution.py
+++ b/solution.py
@@ -115,22 +115,22 @@
     normed_all = jnp.concatenate([normed_bf[:, : 2 * lat], normed_other], axis=0)
 
     cot_other_end.append(across(after(cot_end[1], normed_sent)))
-    cot_all = [
-        jnp.concatenate(
-            [cotangent[:, cuts[k]], cot_end[k], cot_other[:, cuts[k]], cot_other_end[k]], axis=0
-        )
-        for k in range(2)
-    ]
+    def early_rows(k):
+        return jnp.concatenate([cotangent[:, cuts[k]], cot_end[k], cot_other[:, cuts[k]]], axis=0)
 
-    up_first = tokens_dot(after(normed_all, down_there[2]), cot_all[0]).astype(BF16)
+    values = jnp.concatenate([early_rows(0), cot_other_end[0]], axis=0)
+    up_first = tokens_dot(after(normed_all, down_there[2]), values).astype(BF16)
     back_first = outward(up_first[lat:])
     up_mine = jnp.concatenate([up, after(up_end, up_first, down_used)], axis=0)
-    grad = rows_dot(cot_all[0], up_mine[:, cuts[0]]) + rows_dot(cot_all[1], up_mine[:, cuts[1]])
-    grad = grad.astype(BF16)
-    from_col = other_col(grad[2 * rows :])
-    mine_from_col = other_col(grad[: 2 * rows])
-    grad_other = grad[2 * rows :].astype(F32) + from_col.astype(F32)
-    up_second = tokens_dot(normed_all, cot_all[1]).astype(BF16)
+    grad = rows_dot(values, up_mine[:, cuts[0]])
+    early = grad[: 3 * rows] + rows_dot(early_rows(1), up_mine[:, cuts[1]])
+    early = early.astype(BF16)
+    early_sum = early.astype(F32) + other_col(early).astype(F32)
+
+    last = after(cot_other_end[1], early)
+    late = col_sum(grad[3 * rows :] + rows_dot(last, up_mine[:, cuts[1]]))
+    values = jnp.concatenate([early_rows(1), last], axis=0)
+    up_second = tokens_dot(normed_all, values).astype(BF16)
     back_second = outward(up_second[lat:])
     up_grad = jnp.concatenate(
         [
@@ -140,9 +140,9 @@
         axis=1,
     )
 
-    grad_sent = after(grad_other.astype(BF16), up_second, back_first)
-    grad_mine = grad[: 2 * rows].astype(F32) + after(mine_from_col, grad_sent).astype(F32)
-    normed_grad = jnp.concatenate([grad_mine, across(grad_sent).astype(F32)], axis=1)
+    grad_sent = jnp.concatenate([early_sum[2 * rows :], late], axis=0).astype(BF16)
+    from_across = across(after(grad_sent, up_second, back_first))
+    normed_grad = jnp.concatenate([early_sum[: 2 * rows], from_across.astype(F32)], axis=1)
     inner = jnp.mean(normed_grad * normed, axis=-1, keepdims=True)
     latent_bf = (inv_rms * (normed_grad - normed * inner)).astype(BF16)
     latent_there = outward(latent_bf[rows:])
@@ -151,9 +151,14 @@
     sums = [
         tokens_dot(latent_bf[:, j * lat : (j + 1) * lat], tokens_mine) for j in range(4)
     ]
+    width = tokens.shape[1] // 2
+    halves = (slice(0, width), slice(width, 2 * width))
     sent_end, sent_own = sums[3].astype(BF16), sums[2].astype(BF16)
-    from_end, from_own = across(sent_end), across(after(sent_own, latent_there))
-    down_end_grad = outward((sums[1] + from_end.astype(F32)).astype(BF16))
+    from_end = [across(sent_end[:, half]) for half in halves]
+    from_own = across(after(sent_own, from_end[0]))
+    end_first = (sums[1][:, halves[0]] + from_end[0].astype(F32)).astype(BF16)
+    end_second = sums[1][:, halves[1]] + after(from_end[1], end_first).astype(F32)
+    down_end_grad = jnp.concatenate([outward(end_first), outward(end_second.astype(BF16))], axis=1)
     down_own_grad = (sums[0] + from_own.astype(F32)).astype(BF16)
     down_grad = jnp.where(middle, down_own_grad, down_end_grad)
 

time: 169 us -> 163 us (0.964)
  waiting for transfers between devices: 103 us -> 93.2 us
  starting transfers between devices: 43 us -> 45.8 us
    ppermute x7 -> x8, waiting for transfers between devices: 49.2 us -> 39.5 us  [outward(): return lax.ppermute(value, 'row', [(1, 0), (2, 3)])]
    ppermute x1, waiting for transfers between devices: 7.89 us -> 0.01 us  [shifted(): lax.ppermute(value, axis, [(source, source + steps) for source in range(l...]
    ppermute x3, waiting for transfers between devices: 0.01 us -> 5.62 us  [other_col(): return lax.ppermute(value, 'col', [(0, 1), (1, 0)])]
    ppermute x5, waiting for transfers between devices: 46.4 us -> 48.1 us  [inward(): return lax.ppermute(value, 'row', [(0, 1), (3, 2)])]
    ppermute x7 -> x8, starting transfers between devices: 9.18 us -> 10.3 us  [outward(): return lax.ppermute(value, 'row', [(1, 0), (2, 3)])]
    ppermute x9 -> x10, starting transfers between devices: 6.44 us -> 6.95 us  [across(): return lax.ppermute(value, 'row', [(1, 2), (2, 1)])]
    dot_general x3 -> x4, matrix products: 4.62 us -> 4.98 us  [rows_dot(): lax.dot_general(left, right, (((1,), (1,)), ((), ())), preferred_element_...]
  transfers between devices with their start and end apart: 25 -> 27, of which waited for: 12 -> 13; matrix products, arithmetic and copies ran while one was open for 10% -> 12% of each run, Pallas kernels for 0% -> 0%
where the time goes in v4:
time: 163 us; the launch traced here: 161 us
  waiting for transfers between devices  93.2 us (57%)
  starting transfers between devices  45.8 us (28%)
  matrix products  12.4 us (8%)
  local copies, waits for them, and re-layouts  4.96 us (3%)
  other arithmetic  3.1 us (2%)
    ppermute x5, waiting for transfers between devices, inward(): return lax.ppermute(value, 'row', [(0, 1), (3, 2)])  48.1 us
    ppermute x8, waiting for transfers between devices, outward(): return lax.ppermute(value, 'row', [(1, 0), (2, 3)])  39.5 us
    ppermute x5, starting transfers between devices, inward(): return lax.ppermute(value, 'row', [(0, 1), (3, 2)])  22 us
    ppermute x8, starting transfers between devices, outward(): return lax.ppermute(value, 'row', [(1, 0), (2, 3)])  10.3 us
    ppermute x10, starting transfers between devices, across(): return lax.ppermute(value, 'row', [(1, 2), (2, 1)])  6.95 us
    dot_general x6, matrix products, tokens_dot(): lax.dot_general(left, right, (((0,), (0,)), ((), ())), preferred_element_...  6.73 us
    ppermute x3, waiting for transfers between devices, other_col(): return lax.ppermute(value, 'col', [(0, 1), (1, 0)])  5.62 us
    dot_general x4, matrix products, rows_dot(): lax.dot_general(left, right, (((1,), (1,)), ((), ())), preferred_element_...  4.98 us
  transfers between devices with their start and end apart: 27, of which 13 were waited for; matrix products, arithmetic and copies ran while one was open for 12% of the time, Pallas kernels for 0%

profile of v4, /device:TPU:4, one launch (start us, length us, event | category | flops | bytes accessed | tf_op | source)
XLA Modules:
  0.0 160.8 jit_solution(3720716825244293547)
XLA Ops:
  0.7 3.7 %collective-permute-start.2 = (bf16[128,2560]{1,0:T(8,128)(2,1)}, bf16[128,2560]{1,0:T(8,128)(2,1)S(1)}, u32[]{:S(2)}, u32[]{:S(2)}) collective-permute-start(bf16[128,2560]{1,0:T(8,128)(2,1)} %bitcast.25), channel_id=1, source_target_pairs={{0,2},{6,4},{1,3},{7,5},{8,10},{14,12},{9,11},{15,13},{16,18},{22,... | collective-permute-start | bytes 1966088 | tf_op jit(solution)/shard_map/ppermute | solution.py:48
  4.3 1.4 collective-permute-start
  5.7 1.3 collective-permute-start.1
  7.0 0.7 collective-permute-start.3
  7.7 12.0 %collective-permute-done.2 = bf16[128,2560]{1,0:T(8,128)(2,1)S(1)} collective-permute-done((bf16[128,2560]{1,0:T(8,128)(2,1)}, bf16[128,2560]{1,0:T(8,128)(2,1)S(1)}, u32[]{:S(2)}, u32[]{:S(2)}) %collective-permute-start.2) | collective-permute-done | bytes 655392 | tf_op jit(solution)/shard_map/ppermute | solution.py:48
  19.7 0.7 collective-permute-start.4
  20.4 0.8 collective-permute-start.7
  21.2 2.7 %fusion.47 = (bf16[192,2048]{1,0:T(8,128)(2,1)}, bf16[192,2048]{1,0:T(8,128)(2,1)}) fusion(bf16[192,4096]{1,0:T(8,128)(2,1)} %bitcast.13), kind=kLoop, calls=%fused_computation.73 | loop fusion | bytes 3145728 | tf_op jit(solution)/shard_map/slice | solution.py:119
  23.9 0.1 collective-permute-done.1
  24.0 9.5 %collective-permute-start.6 = (bf16[192,2048]{1,0:T(8,128)(2,1)}, bf16[192,2048]{1,0:T(8,128)(2,1)}, u32[]{:S(2)}, u32[]{:S(2)}) collective-permute-start(bf16[192,2048]{1,0:T(8,128)(2,1)} %get-tuple-element.28), channel_id=1, source_target_pairs={{0,2},{6,4},{1,3},{7,5},{8,10},{14,12},{9,11},{15,13},{16,18},{22,... | collective-permute-start | bytes 2359304 | tf_op jit(solution)/shard_map/ppermute | solution.py:48
  33.4 7.3 %collective-permute-done = bf16[192,2560]{1,0:T(8,128)(2,1)S(1)} collective-permute-done((bf16[192,2560]{1,0:T(8,128)(2,1)}, bf16[192,2560]{1,0:T(8,128)(2,1)S(1)}, u32[]{:S(2)}, u32[]{:S(2)}) %collective-permute-start) | collective-permute-done | bytes 983072 | tf_op jit(solution)/shard_map/ppermute | solution.py:48
  40.8 1.2 convolution_convert_fusion.4
  42.2 1.5 collective-permute-start.5
  43.7 4.6 %collective-permute-start.13 = (bf16[192,2048]{1,0:T(8,128)(2,1)}, bf16[192,2048]{1,0:T(8,128)(2,1)S(1)}, u32[]{:S(2)}, u32[]{:S(2)}) collective-permute-start(bf16[192,2048]{1,0:T(8,128)(2,1)} %get-tuple-element.19), channel_id=1, source_target_pairs={{0,2},{6,4},{1,3},{7,5},{8,10},{14,12},{9,11},{15,13},{16,18},{22,... | collective-permute-start | bytes 2359304 | tf_op jit(solution)/shard_map/ppermute | solution.py:48
  48.3 1.3 collective-permute-start.10
  49.6 8.1 %collective-permute-done.6 = bf16[192,2048]{1,0:T(8,128)(2,1)} collective-permute-done((bf16[192,2048]{1,0:T(8,128)(2,1)}, bf16[192,2048]{1,0:T(8,128)(2,1)}, u32[]{:S(2)}, u32[]{:S(2)}) %collective-permute-start.6) | collective-permute-done | bytes 786464 | tf_op jit(solution)/shard_map/ppermute | solution.py:48
  57.6 0.7 collective-permute-start.8
  58.3 1.3 collective-permute-start.12
  59.6 0.2 multiply_reduce_fusion.1
  59.9 0.1 fusion.25
  60.0 4.4 %collective-permute-done.10 = bf16[128,2560]{1,0:T(8,128)(2,1)S(1)} collective-permute-done((bf16[128,2560]{1,0:T(8,128)(2,1)}, bf16[128,2560]{1,0:T(8,128)(2,1)S(1)}, u32[]{:S(2)}, u32[]{:S(2)}) %collective-permute-start.10) | collective-permute-done | bytes 655392 | tf_op jit(solution)/shard_map/ppermute | solution.py:56
  64.4 2.9 %collective-permute-start.9 = (bf16[128,4096]{1,0:T(8,128)(2,1)S(1)}, bf16[128,4096]{1,0:T(8,128)(2,1)S(1)}, u32[]{:S(2)}, u32[]{:S(2)}) collective-permute-start(bf16[128,4096]{1,0:T(8,128)(2,1)S(1)} %bitcast.14), channel_id=1, source_target_pairs={{0,2},{6,4},{1,3},{7,5},{8,10},{14,12},{9,11},{15,13},{16,18},{22,... | collective-permute-start | bytes 3145736 | tf_op jit(solution)/shard_map/ppermute | solution.py:48
  67.3 0.7 collective-permute-start.11
  68.0 0.1 fusion.46
  68.1 6.3 %collective-permute-done.13 = bf16[192,2048]{1,0:T(8,128)(2,1)S(1)} collective-permute-done((bf16[192,2048]{1,0:T(8,128)(2,1)}, bf16[192,2048]{1,0:T(8,128)(2,1)S(1)}, u32[]{:S(2)}, u32[]{:S(2)}) %collective-permute-start.13) | collective-permute-done | bytes 786464 | tf_op jit(solution)/shard_map/ppermute | solution.py:48
  74.5 0.7 collective-permute-start.15
  75.2 2.8 %collective-permute-done.12 = bf16[128,2560]{1,0:T(8,128)(2,1)S(1)} collective-permute-done((bf16[128,2560]{1,0:T(8,128)(2,1)}, bf16[128,2560]{1,0:T(8,128)(2,1)S(1)}, u32[]{:S(2)}, u32[]{:S(2)}) %collective-permute-start.12) | collective-permute-done | bytes 655392 | tf_op jit(solution)/shard_map/ppermute | solution.py:56
  78.1 2.5 %convolution_convert_fusion.3 = bf16[256,2048]{1,0:T(8,128)(2,1)S(1)} fusion(bf16[768,256]{1,0:T(8,128)(2,1)S(1)} %pad_maximum_fusion.8, bf16[192,2048]{1,0:T(8,128)(2,1)S(1)} %collective-permute-done.8, bf16[192,2048]{1,0:T(8,128)(2,1)S(1)} %get-tuple-element.26, bf16[192,2048]{1,0:T(8,128)(2,1)} %collective-permute-done.6, ...), kind=kOutput, calls=%fused_computation.15 | convolution fusion | flops 818413568 | bytes 4587520 | tf_op jit(solution)/shard_map/dot_general | solution.py:72
  80.7 0.7 maximum_select_fusion
  81.4 14.3 %collective-permute-done.9 = bf16[128,4096]{1,0:T(8,128)(2,1)S(1)} collective-permute-done((bf16[128,4096]{1,0:T(8,128)(2,1)S(1)}, bf16[128,4096]{1,0:T(8,128)(2,1)S(1)}, u32[]{:S(2)}, u32[]{:S(2)}) %collective-permute-start.9) | collective-permute-done | bytes 1048608 | tf_op jit(solution)/shard_map/ppermute | solution.py:48
  95.7 2.4 %fusion.18 = f32[768,256]{1,0:T(8,128)S(1)} fusion(bf16[128,4096]{1,0:T(8,128)(2,1)S(1)} %bitcast.15, bf16[128,4096]{1,0:T(8,128)(2,1)S(1)} %collective-permute-done.9, bf16[192,2048]{1,0:T(8,128)(2,1)S(1)} %collective-permute-done.8, bf16[192,2048]{1,0:T(8,128)(2,1)S(1)} %get-tuple-element.26, bf16[192,2048]{1,0:T(8,128)(2,1)} %collective-permute-done.6, ...), kind=kOutput, calls=%fused_computation.28 | convolution fusion | flops 819986432 | bytes 6029312 | tf_op jit(solution)/shard_map/dot_general | solution.py:68
  98.1 0.9 fusion.26
  99.0 1.6 collective-permute-start.14
  100.6 1.3 collective-permute-start.17
  101.9 5.0 %collective-permute-done.14 = bf16[576,256]{1,0:T(8,128)(2,1)S(1)} collective-permute-done((bf16[576,256]{1,0:T(8,128)(2,1)S(1)}, bf16[576,256]{1,0:T(8,128)(2,1)S(1)}, u32[]{:S(2)}, u32[]{:S(2)}) %collective-permute-start.14) | collective-permute-done | bytes 294944 | tf_op jit(solution)/shard_map/ppermute | solution.py:60
  107.1 0.5 fusion.27
  107.6 1.6 collective-permute-start.16
  109.1 1.2 fusion.8
  110.4 1.3 collective-permute-start.26
  111.7 0.6 collective-permute-done.16
  112.3 4.0 %collective-permute-done.17 = bf16[128,2048]{1,0:T(8,128)(2,1)S(1)} collective-permute-done((bf16[128,2048]{1,0:T(8,128)(2,1)S(1)}, bf16[128,2048]{1,0:T(8,128)(2,1)S(1)}, u32[]{:S(2)}, u32[]{:S(2)}) %collective-permute-start.17) | collective-permute-done | bytes 524320 | tf_op jit(solution)/shard_map/ppermute | solution.py:56
  116.3 0.7 collective-permute-start.18
  117.0 0.1 slice_select_fusion.1
  117.1 0.3 multiply_reduce_fusion
  117.4 0.2 multiply_convert_fusion
  117.7 0.6 copy-done.2
  118.3 0.3 copy-done.4
  118.6 0.5 convolution_convert_fusion.1
  119.1 0.5 fusion.32
  119.6 1.3 collective-permute-start.19
  121.0 0.7 collective-permute-start.21
  121.7 0.7 collective-permute-start.24
  122.4 0.5 convolution_convert_fusion.2
  122.9 9.9 %collective-permute-done.19 = bf16[192,512]{1,0:T(8,128)(2,1)S(1)} collective-permute-done((bf16[192,512]{1,0:T(8,128)(2,1)S(1)}, bf16[192,512]{1,0:T(8,128)(2,1)S(1)}, u32[]{:S(2)}, u32[]{:S(2)}) %collective-permute-start.19) | collective-permute-done | bytes 196640 | tf_op jit(solution)/shard_map/ppermute | solution.py:56
  132.8 0.7 convolution_convert_fusion
  133.5 1.9 %collective-permute-start.20 = (bf16[192,2560]{1,0:T(8,128)(2,1)S(1)}, bf16[192,2560]{1,0:T(8,128)(2,1)S(1)}, u32[]{:S(2)}, u32[]{:S(2)}) collective-permute-start(bf16[192,2560]{1,0:T(8,128)(2,1)S(1)} %convolution_convert_fusion), channel_id=1, source_target_pairs={{8,0},{16,8},{24,16},{9,1},{17,9},{25,17},{10,2},{18,10},{26,18},{... | collective-permute-start | bytes 2949128 | tf_op jit(solution)/shard_map/ppermute | solution.py:13
  135.5 0.7 collective-permute-start.22
  136.2 0.1 fusion.24
  136.3 1.3 collective-permute-start.23
  137.7 1.3 collective-permute-start.25
  139.0 1.1 maximum_bitcast_fusion
  140.0 18.3 %collective-permute-done.25 = bf16[128,1280]{1,0:T(8,128)(2,1)S(1)} collective-permute-done((bf16[128,1280]{1,0:T(8,128)(2,1)S(1)}, bf16[128,1280]{1,0:T(8,128)(2,1)S(1)}, u32[]{:S(2)}, u32[]{:S(2)}) %collective-permute-start.25) | collective-permute-done | bytes 327712 | tf_op jit(solution)/shard_map/ppermute | solution.py:56
  158.4 1.4 fusion.22
  159.8 0.9 copy.8
  (60 shorter events, 0.7 us)
Async XLA Ops:
  0.6 40.2 %copy-start.6 = (bf16[1,128,2560]{2,1,0:T(8,128)(2,1)S(1)}, bf16[1,128,2560]{2,1,0:T(8,128)(2,1)}, u32[]{:S(2)}) copy-start(bf16[1,128,2560]{2,1,0:T(8,128)(2,1)} %param.5) | copy-start | bytes 1966084
  0.6 40.2 %copy-start.1 = (bf16[1,192,2560]{2,1,0:T(8,128)(2,1)S(1)}, bf16[1,192,2560]{2,1,0:T(8,128)(2,1)}, u32[]{:S(2)}) copy-start(bf16[1,192,2560]{2,1,0:T(8,128)(2,1)} %param.4) | copy-start | bytes 2949124
  0.7 19.1 %collective-permute-start.2 = (bf16[128,2560]{1,0:T(8,128)(2,1)}, bf16[128,2560]{1,0:T(8,128)(2,1)S(1)}, u32[]{:S(2)}, u32[]{:S(2)}) collective-permute-start(bf16[128,2560]{1,0:T(8,128)(2,1)} %bitcast.25), channel_id=1, source_target_pairs={{0,2},{6,4},{1,3},{7,5},{8,10},{14,12},{9,11},{15,13},{16,18},{22,... | collective-permute-start | bytes 1966088 | tf_op jit(solution)/shard_map/ppermute | solution.py:48
  4.3 36.5 %collective-permute-start = (bf16[192,2560]{1,0:T(8,128)(2,1)}, bf16[192,2560]{1,0:T(8,128)(2,1)S(1)}, u32[]{:S(2)}, u32[]{:S(2)}) collective-permute-start(bf16[192,2560]{1,0:T(8,128)(2,1)} %bitcast.18), channel_id=1, source_target_pairs={{0,2},{6,4},{1,3},{7,5},{8,10},{14,12},{9,11},{15,13},{16,18},{22,... | collective-permute-start | bytes 2949128 | tf_op jit(solution)/shard_map/ppermute | solution.py:48
  5.7 18.3 %collective-permute-start.1 = (bf16[128,2560]{1,0:T(8,128)(2,1)}, bf16[128,2560]{1,0:T(8,128)(2,1)S(1)}, u32[]{:S(2)}, u32[]{:S(2)}) collective-permute-start(bf16[128,2560]{1,0:T(8,128)(2,1)} %bitcast.26), channel_id=1, source_target_pairs={{2,0},{4,6},{3,1},{5,7},{10,8},{12,14},{11,9},{13,15},{18,16},{20,... | collective-permute-start | bytes 1966088 | tf_op jit(solution)/shard_map/ppermute | solution.py:56
  7.0 33.8 %collective-permute-start.3 = (bf16[128,2560]{1,0:T(8,128)(2,1)}, bf16[128,2560]{1,0:T(8,128)(2,1)S(1)}, u32[]{:S(2)}, u32[]{:S(2)}) collective-permute-start(bf16[128,2560]{1,0:T(8,128)(2,1)} %bitcast.27), channel_id=1, source_target_pairs={{2,4},{4,2},{3,5},{5,3},{10,12},{12,10},{11,13},{13,11},{18,20},{2... | collective-permute-start | bytes 1966088 | tf_op jit(solution)/shard_map/ppermute | solution.py:52
  19.7 22.3 %copy-start.8 = (bf16[128,2560]{1,0:T(8,128)(2,1)}, bf16[128,2560]{1,0:T(8,128)(2,1)S(1)}, u32[]{:S(2)}) copy-start(bf16[128,2560]{1,0:T(8,128)(2,1)S(1)} %collective-permute-done.2) | copy-start | bytes 1966084
  19.7 21.1 %collective-permute-start.4 = (bf16[128,2560]{1,0:T(8,128)(2,1)S(1)}, bf16[128,2560]{1,0:T(8,128)(2,1)S(1)}, u32[]{:S(2)}, u32[]{:S(2)}) collective-permute-start(bf16[128,2560]{1,0:T(8,128)(2,1)S(1)} %collective-permute-done.2), channel_id=1, source_target_pairs={{2,4},{4,2},{3,5},{5,3},{10,12},{12,10},{11,13},{13,11},{18,20},{2... | collective-permute-start | bytes 1966088 | tf_op jit(solution)/shard_map/ppermute | solution.py:52
  20.4 46.9 %collective-permute-start.7 = (bf16[192,4096]{1,0:T(8,128)(2,1)}, bf16[192,4096]{1,0:T(8,128)(2,1)S(1)}, u32[]{:S(2)}, u32[]{:S(2)}) collective-permute-start(bf16[192,4096]{1,0:T(8,128)(2,1)} %bitcast.12), channel_id=1, source_target_pairs={{2,4},{4,2},{3,5},{5,3},{10,12},{12,10},{11,13},{13,11},{18,20},{2... | collective-permute-start | bytes 4718600 | tf_op jit(solution)/shard_map/ppermute | solution.py:52
  24.0 16.8 %copy-start.10 = (bf16[128,2560]{1,0:T(8,128)(2,1)}, bf16[128,2560]{1,0:T(8,128)(2,1)S(1)}, u32[]{:S(2)}) copy-start(bf16[128,2560]{1,0:T(8,128)(2,1)S(1)} %collective-permute-done.1) | copy-start | bytes 1966084
  24.0 33.6 %collective-permute-start.6 = (bf16[192,2048]{1,0:T(8,128)(2,1)}, bf16[192,2048]{1,0:T(8,128)(2,1)}, u32[]{:S(2)}, u32[]{:S(2)}) collective-permute-start(bf16[192,2048]{1,0:T(8,128)(2,1)} %get-tuple-element.28), channel_id=1, source_target_pairs={{0,2},{6,4},{1,3},{7,5},{8,10},{14,12},{9,11},{15,13},{16,18},{22,... | collective-permute-start | bytes 2359304 | tf_op jit(solution)/shard_map/ppermute | solution.py:48
  40.8 1.3 copy-start.3
  40.8 1.3 copy-start.12
  40.8 1.3 copy-start.14
  42.2 22.3 %copy-start = (bf16[1,128,4096]{2,1,0:T(8,128)(2,1)S(1)}, bf16[1,128,4096]{2,1,0:T(8,128)(2,1)}, u32[]{:S(2)}) copy-start(bf16[1,128,4096]{2,1,0:T(8,128)(2,1)} %param.6) | copy-start | bytes 3145732
  42.2 16.2 %collective-permute-start.5 = (bf16[384,512]{1,0:T(8,128)(2,1)S(1)}, bf16[384,512]{1,0:T(8,128)(2,1)S(1)}, u32[]{:S(2)}, u32[]{:S(2)}) collective-permute-start(bf16[384,512]{1,0:T(8,128)(2,1)S(1)} %convolution_convert_fusion.4), channel_id=1, source_target_pairs={{0,1},{1,0},{2,3},{3,2},{4,5},{5,4},{6,7},{7,6},{8,9},{9,8},{10,11... | collective-permute-start | bytes 1179656 | tf_op jit(solution)/shard_map/ppermute | solution.py:60
  43.7 30.8 %collective-permute-start.13 = (bf16[192,2048]{1,0:T(8,128)(2,1)}, bf16[192,2048]{1,0:T(8,128)(2,1)S(1)}, u32[]{:S(2)}, u32[]{:S(2)}) collective-permute-start(bf16[192,2048]{1,0:T(8,128)(2,1)} %get-tuple-element.19), channel_id=1, source_target_pairs={{0,2},{6,4},{1,3},{7,5},{8,10},{14,12},{9,11},{15,13},{16,18},{22,... | collective-permute-start | bytes 2359304 | tf_op jit(solution)/shard_map/ppermute | solution.py:48
  48.3 16.2 %collective-permute-start.10 = (bf16[128,2560]{1,0:T(8,128)(2,1)}, bf16[128,2560]{1,0:T(8,128)(2,1)S(1)}, u32[]{:S(2)}, u32[]{:S(2)}) collective-permute-start(bf16[128,2560]{1,0:T(8,128)(2,1)} %copy-done.12), channel_id=1, source_target_pairs={{2,0},{4,6},{3,1},{5,7},{10,8},{12,14},{11,9},{13,15},{18,16},{20,... | collective-permute-start | bytes 1966088 | tf_op jit(solution)/shard_map/ppermute | solution.py:56
  57.6 20.4 %collective-permute-start.8 = (bf16[192,2048]{1,0:T(8,128)(2,1)}, bf16[192,2048]{1,0:T(8,128)(2,1)S(1)}, u32[]{:S(2)}, u32[]{:S(2)}) collective-permute-start(bf16[192,2048]{1,0:T(8,128)(2,1)} %collective-permute-done.6), channel_id=1, source_target_pairs={{2,4},{4,2},{3,5},{5,3},{10,12},{12,10},{11,13},{13,11},{18,20},{2... | collective-permute-start | bytes 2359304 | tf_op jit(solution)/shard_map/ppermute | solution.py:52
  58.3 19.7 %collective-permute-start.12 = (bf16[128,2560]{1,0:T(8,128)(2,1)}, bf16[128,2560]{1,0:T(8,128)(2,1)S(1)}, u32[]{:S(2)}, u32[]{:S(2)}) collective-permute-start(bf16[128,2560]{1,0:T(8,128)(2,1)} %copy-done.14), channel_id=1, source_target_pairs={{2,0},{4,6},{3,1},{5,7},{10,8},{12,14},{11,9},{13,15},{18,16},{20,... | collective-permute-start | bytes 1966088 | tf_op jit(solution)/shard_map/ppermute | solution.py:56
  64.4 31.3 %collective-permute-start.9 = (bf16[128,4096]{1,0:T(8,128)(2,1)S(1)}, bf16[128,4096]{1,0:T(8,128)(2,1)S(1)}, u32[]{:S(2)}, u32[]{:S(2)}) collective-permute-start(bf16[128,4096]{1,0:T(8,128)(2,1)S(1)} %bitcast.14), channel_id=1, source_target_pairs={{0,2},{6,4},{1,3},{7,5},{8,10},{14,12},{9,11},{15,13},{16,18},{22,... | collective-permute-start | bytes 3145736 | tf_op jit(solution)/shard_map/ppermute | solution.py:48
  67.3 7.8 %collective-permute-start.11 = (bf16[384,256]{1,0:T(8,128)(2,1)S(1)}, bf16[384,256]{1,0:T(8,128)(2,1)S(1)}, u32[]{:S(2)}, u32[]{:S(2)}) collective-permute-start(bf16[384,256]{1,0:T(8,128)(2,1)S(1)} %get-tuple-element.16), channel_id=1, source_target_pairs={{2,4},{4,2},{3,5},{5,3},{10,12},{12,10},{11,13},{13,11},{18,20},{2... | collective-permute-start | bytes 589832 | tf_op jit(solution)/shard_map/ppermute | solution.py:52
  74.5 32.6 %collective-permute-start.15 = (bf16[192,2048]{1,0:T(8,128)(2,1)S(1)}, bf16[192,2048]{1,0:T(8,128)(2,1)S(1)}, u32[]{:S(2)}, u32[]{:S(2)}) collective-permute-start(bf16[192,2048]{1,0:T(8,128)(2,1)S(1)} %collective-permute-done.13), channel_id=1, source_target_pairs={{2,4},{4,2},{3,5},{5,3},{10,12},{12,10},{11,13},{13,11},{18,20},{2... | collective-permute-start | bytes 2359304 | tf_op jit(solution)/shard_map/ppermute | solution.py:52
  78.0 2.6 %copy-start.7 = (bf16[1,128,2560]{2,1,0:T(8,128)(2,1)S(1)}, bf16[1,128,2560]{2,1,0:T(8,128)(2,1)}, u32[]{:S(2)}) copy-start(bf16[1,128,2560]{2,1,0:T(8,128)(2,1)} %param.5) | copy-start | bytes 1966084
  78.0 2.6 %copy-start.9 = (bf16[128,2560]{1,0:T(8,128)(2,1)S(1)}, bf16[128,2560]{1,0:T(8,128)(2,1)}, u32[]{:S(2)}) copy-start(bf16[128,2560]{1,0:T(8,128)(2,1)} %copy-done.8) | copy-start | bytes 1966084
  78.0 2.6 %copy-start.11 = (bf16[128,2560]{1,0:T(8,128)(2,1)S(1)}, bf16[128,2560]{1,0:T(8,128)(2,1)}, u32[]{:S(2)}) copy-start(bf16[128,2560]{1,0:T(8,128)(2,1)} %copy-done.10) | copy-start | bytes 1966084
  78.0 2.6 %copy-start.13 = (bf16[128,2560]{1,0:T(8,128)(2,1)S(1)}, bf16[128,2560]{1,0:T(8,128)(2,1)}, u32[]{:S(2)}) copy-start(bf16[128,2560]{1,0:T(8,128)(2,1)} %copy-done.12) | copy-start | bytes 1966084
  78.1 2.6 %copy-start.15 = (bf16[128,2560]{1,0:T(8,128)(2,1)S(1)}, bf16[128,2560]{1,0:T(8,128)(2,1)}, u32[]{:S(2)}) copy-start(bf16[128,2560]{1,0:T(8,128)(2,1)} %copy-done.14) | copy-start | bytes 1966084
  81.4 16.7 %copy-start.5 = (bf16[192,2048]{1,0:T(8,128)(2,1)S(1)}, bf16[192,2048]{1,0:T(8,128)(2,1)}, u32[]{:S(2)}) copy-start(bf16[192,2048]{1,0:T(8,128)(2,1)} %get-tuple-element.19) | copy-start | bytes 2359300
  99.0 7.9 %collective-permute-start.14 = (bf16[576,256]{1,0:T(8,128)(2,1)S(1)}, bf16[576,256]{1,0:T(8,128)(2,1)S(1)}, u32[]{:S(2)}, u32[]{:S(2)}) collective-permute-start(bf16[576,256]{1,0:T(8,128)(2,1)S(1)} %fusion.26), channel_id=1, source_target_pairs={{0,1},{1,0},{2,3},{3,2},{4,5},{5,4},{6,7},{7,6},{8,9},{9,8},{10,11... | collective-permute-start | bytes 884744 | tf_op jit(solution)/shard_map/ppermute | solution.py:60
  100.6 15.7 %collective-permute-start.17 = (bf16[128,2048]{1,0:T(8,128)(2,1)S(1)}, bf16[128,2048]{1,0:T(8,128)(2,1)S(1)}, u32[]{:S(2)}, u32[]{:S(2)}) collective-permute-start(bf16[128,2048]{1,0:T(8,128)(2,1)S(1)} %slice.122), channel_id=1, source_target_pairs={{2,0},{4,6},{3,1},{5,7},{10,8},{12,14},{11,9},{13,15},{18,16},{20,... | collective-permute-start | bytes 1572872 | tf_op jit(solution)/shard_map/ppermute | solution.py:56
  107.6 4.7 %collective-permute-start.16 = (bf16[192,256]{1,0:T(8,128)(2,1)S(1)}, bf16[192,256]{1,0:T(8,128)(2,1)S(1)}, u32[]{:S(2)}, u32[]{:S(2)}) collective-permute-start(bf16[192,256]{1,0:T(8,128)(2,1)S(1)} %fusion.27), channel_id=1, source_target_pairs={{0,1},{1,0},{2,3},{3,2},{4,5},{5,4},{6,7},{7,6},{8,9},{9,8},{10,11... | collective-permute-start | bytes 294920 | tf_op jit(solution)/shard_map/ppermute | solution.py:60
  110.4 25.0 %collective-permute-start.26 = (bf16[128,2048]{1,0:T(8,128)(2,1)S(1)}, bf16[128,2048]{1,0:T(8,128)(2,1)S(1)}, u32[]{:S(2)}, u32[]{:S(2)}) collective-permute-start(bf16[128,2048]{1,0:T(8,128)(2,1)S(1)} %slice.135), channel_id=1, source_target_pairs={{2,0},{4,6},{3,1},{5,7},{10,8},{12,14},{11,9},{13,15},{18,16},{20,... | collective-permute-start | bytes 1572872 | tf_op jit(solution)/shard_map/ppermute | solution.py:56
  116.3 0.8 collective-permute-start.18
  117.1 1.2 copy-start.2
  117.1 1.5 copy-start.4
  119.6 13.1 %collective-permute-start.19 = (bf16[192,512]{1,0:T(8,128)(2,1)S(1)}, bf16[192,512]{1,0:T(8,128)(2,1)S(1)}, u32[]{:S(2)}, u32[]{:S(2)}) collective-permute-start(bf16[192,512]{1,0:T(8,128)(2,1)S(1)} %slice.124), channel_id=1, source_target_pairs={{2,0},{4,6},{3,1},{5,7},{10,8},{12,14},{11,9},{13,15},{18,16},{20,... | collective-permute-start | bytes 589832 | tf_op jit(solution)/shard_map/ppermute | solution.py:56
  121.0 14.5 %collective-permute-start.21 = (bf16[128,1280]{1,0:T(8,128)(2,1)S(1)}, bf16[128,1280]{1,0:T(8,128)(2,1)S(1)}, u32[]{:S(2)}, u32[]{:S(2)}) collective-permute-start(bf16[128,1280]{1,0:T(8,128)(2,1)S(1)} %get-tuple-element.30), channel_id=1, source_target_pairs={{2,4},{4,2},{3,5},{5,3},{10,12},{12,10},{11,13},{13,11},{18,20},{2... | collective-permute-start | bytes 983048 | tf_op jit(solution)/shard_map/ppermute | solution.py:52
  121.7 15.9 %collective-permute-start.24 = (bf16[128,1280]{1,0:T(8,128)(2,1)S(1)}, bf16[128,1280]{1,0:T(8,128)(2,1)S(1)}, u32[]{:S(2)}, u32[]{:S(2)}) collective-permute-start(bf16[128,1280]{1,0:T(8,128)(2,1)S(1)} %get-tuple-element.29), channel_id=1, source_target_pairs={{2,4},{4,2},{3,5},{5,3},{10,12},{12,10},{11,13},{13,11},{18,20},{2... | collective-permute-start | bytes 983048 | tf_op jit(solution)/shard_map/ppermute | solution.py:52
  133.5 26.3 %collective-permute-start.20 = (bf16[192,2560]{1,0:T(8,128)(2,1)S(1)}, bf16[192,2560]{1,0:T(8,128)(2,1)S(1)}, u32[]{:S(2)}, u32[]{:S(2)}) collective-permute-start(bf16[192,2560]{1,0:T(8,128)(2,1)S(1)} %convolution_convert_fusion), channel_id=1, source_target_pairs={{8,0},{16,8},{24,16},{9,1},{17,9},{25,17},{10,2},{18,10},{26,18},{... | collective-permute-start | bytes 2949128 | tf_op jit(solution)/shard_map/ppermute | solution.py:13
  135.5 22.9 %collective-permute-start.22 = (bf16[128,2560]{1,0:T(8,128)(2,1)S(1)}, bf16[128,2560]{1,0:T(8,128)(2,1)S(1)}, u32[]{:S(2)}, u32[]{:S(2)}) collective-permute-start(bf16[128,2560]{1,0:T(8,128)(2,1)S(1)} %convolution_convert_fusion.2), channel_id=1, source_target_pairs={{2,4},{4,2},{3,5},{5,3},{10,12},{12,10},{11,13},{13,11},{18,20},{2... | collective-permute-start | bytes 1966088 | tf_op jit(solution)/shard_map/ppermute | solution.py:52
  136.3 22.1 %collective-permute-start.23 = (bf16[128,1280]{1,0:T(8,128)(2,1)S(1)}, bf16[128,1280]{1,0:T(8,128)(2,1)S(1)}, u32[]{:S(2)}, u32[]{:S(2)}) collective-permute-start(bf16[128,1280]{1,0:T(8,128)(2,1)S(1)} %fusion.24), channel_id=1, source_target_pairs={{2,0},{4,6},{3,1},{5,7},{10,8},{12,14},{11,9},{13,15},{18,16},{20,... | collective-permute-start | bytes 983048 | tf_op jit(solution)/shard_map/ppermute | solution.py:56
  137.7 20.7 %collective-permute-start.25 = (bf16[128,1280]{1,0:T(8,128)(2,1)S(1)}, bf16[128,1280]{1,0:T(8,128)(2,1)S(1)}, u32[]{:S(2)}, u32[]{:S(2)}) collective-permute-start(bf16[128,1280]{1,0:T(8,128)(2,1)S(1)} %fusion.23), channel_id=1, source_target_pairs={{2,0},{4,6},{3,1},{5,7},{10,8},{12,14},{11,9},{13,15},{18,16},{20,... | collective-permute-start | bytes 983048 | tf_op jit(solution)/shard_map/ppermute | solution.py:56

commit v5 on v4

--- a/solution.py
+++ b/solution.py
@@ -145,8 +145,6 @@
     normed_grad = jnp.concatenate([early_sum[: 2 * rows], from_across.astype(F32)], axis=1)
     inner = jnp.mean(normed_grad * normed, axis=-1, keepdims=True)
     latent_bf = (inv_rms * (normed_grad - normed * inner)).astype(BF16)
-    latent_there = outward(latent_bf[rows:])
-    latent_used = jnp.where(middle, latent_bf[:rows], latent_there)
 
     sums = [
         tokens_dot(latent_bf[:, j * lat : (j + 1) * lat], tokens_mine) for j in range(4)
@@ -155,15 +153,18 @@
     halves = (slice(0, width), slice(width, 2 * width))
     sent_end, sent_own = sums[3].astype(BF16), sums[2].astype(BF16)
     from_end = [across(sent_end[:, half]) for half in halves]
-    from_own = across(after(sent_own, from_end[0]))
+    latent_there = outward(after(latent_bf[rows:], sent_end, sent_own))
+    latent_used = jnp.where(middle, latent_bf[:rows], latent_there)
     end_first = (sums[1][:, halves[0]] + from_end[0].astype(F32)).astype(BF16)
+    from_own = across(after(sent_own, end_first))
     end_second = sums[1][:, halves[1]] + after(from_end[1], end_first).astype(F32)
     down_end_grad = jnp.concatenate([outward(end_first), outward(end_second.astype(BF16))], axis=1)
-    down_own_grad = (sums[0] + from_own.astype(F32)).astype(BF16)
-    down_grad = jnp.where(middle, down_own_grad, down_end_grad)
-
     input_grad = jnp.dot(latent_used, down_used, preferred_element_type=F32).astype(BF16)
     passed = shifted(input_grad, "section", -1)
+    final = lax.axis_index("section") == lax.axis_size("section") - 1
+    passed = jnp.where(final, jnp.zeros_like(passed), passed)
+    down_own_grad = (sums[0] + after(from_own, passed).astype(F32)).astype(BF16)
+    down_grad = jnp.where(middle, down_own_grad, down_end_grad)
     return (passed[None], down_grad[None], up_grad[None])
 
 

time: 163 us -> 167 us (1.025)
  matrix products: 12.4 us -> 18.7 us
  waiting for transfers between devices: 93.2 us -> 87.9 us
  other arithmetic: 3.1 us -> 5.17 us
    ppermute x8, waiting for transfers between devices: 39.5 us -> 31.4 us  [outward(): return lax.ppermute(value, 'row', [(1, 0), (2, 3)])]
    ppermute x1, waiting for transfers between devices: 0.01 us -> 6.96 us  [shifted(): lax.ppermute(value, axis, [(source, source + steps) for source in range(l...]
    dot_general x4, matrix products: 4.98 us -> 9.07 us  [rows_dot(): lax.dot_general(left, right, (((1,), (1,)), ((), ())), preferred_element_...]
    ppermute x5, waiting for transfers between devices: 48.1 us -> 45.4 us  [inward(): return lax.ppermute(value, 'row', [(0, 1), (3, 2)])]
    dot_general x6, matrix products: 6.73 us -> 8.93 us  [tokens_dot(): lax.dot_general(left, right, (((0,), (0,)), ((), ())), preferred_element_...]
  transfers between devices with their start and end apart: 27 -> 27, of which waited for: 13 -> 13; matrix products, arithmetic and copies ran while one was open for 12% -> 16% of each run, Pallas kernels for 0% -> 0%
where the time goes in v5:
time: 167 us; the launch traced here: 164 us
  waiting for transfers between devices  87.9 us (53%)
  starting transfers between devices  46 us (28%)
  matrix products  18.7 us (11%)
  other arithmetic  5.17 us (3%)
  local copies, waits for them, and re-layouts  4.89 us (3%)
    ppermute x5, waiting for transfers between devices, inward(): return lax.ppermute(value, 'row', [(0, 1), (3, 2)])  45.4 us
    ppermute x8, waiting for transfers between devices, outward(): return lax.ppermute(value, 'row', [(1, 0), (2, 3)])  31.4 us
    ppermute x5, starting transfers between devices, inward(): return lax.ppermute(value, 'row', [(0, 1), (3, 2)])  21.2 us
    ppermute x8, starting transfers between devices, outward(): return lax.ppermute(value, 'row', [(1, 0), (2, 3)])  10.5 us
    dot_general x4, matrix products, rows_dot(): lax.dot_general(left, right, (((1,), (1,)), ((), ())), preferred_element_...  9.07 us
    dot_general x6, matrix products, tokens_dot(): lax.dot_general(left, right, (((0,), (0,)), ((), ())), preferred_element_...  8.93 us
    ppermute x10, starting transfers between devices, across(): return lax.ppermute(value, 'row', [(1, 2), (2, 1)])  7.81 us
    ppermute x1, waiting for transfers between devices, shifted(): lax.ppermute(value, axis, [(source, source + steps) for source in range(l...  6.96 us
  transfers between devices with their start and end apart: 27, of which 13 were waited for; matrix products, arithmetic and copies ran while one was open for 16% of the time, Pallas kernels for 0%

profile of v5, /device:TPU:4, one launch (start us, length us, event | category | flops | bytes accessed | tf_op | source)
XLA Modules:
  0.0 163.9 jit_solution(1572213089110542086)
XLA Ops:
  0.7 3.7 %collective-permute-start.2 = (bf16[128,2560]{1,0:T(8,128)(2,1)}, bf16[128,2560]{1,0:T(8,128)(2,1)S(1)}, u32[]{:S(2)}, u32[]{:S(2)}) collective-permute-start(bf16[128,2560]{1,0:T(8,128)(2,1)} %bitcast.21), channel_id=1, source_target_pairs={{0,2},{6,4},{1,3},{7,5},{8,10},{14,12},{9,11},{15,13},{16,18},{22,... | collective-permute-start | bytes 1966088 | tf_op jit(solution)/shard_map/ppermute | solution.py:48
  4.3 1.4 collective-permute-start
  5.7 1.3 collective-permute-start.1
  7.0 0.7 collective-permute-start.3
  7.7 12.0 %collective-permute-done.2 = bf16[128,2560]{1,0:T(8,128)(2,1)S(1)} collective-permute-done((bf16[128,2560]{1,0:T(8,128)(2,1)}, bf16[128,2560]{1,0:T(8,128)(2,1)S(1)}, u32[]{:S(2)}, u32[]{:S(2)}) %collective-permute-start.2) | collective-permute-done | bytes 655392 | tf_op jit(solution)/shard_map/ppermute | solution.py:48
  19.7 0.7 collective-permute-start.4
  20.4 0.8 collective-permute-start.7
  21.2 2.4 %fusion.47 = (bf16[192,2048]{1,0:T(8,128)(2,1)S(1)}, bf16[192,2048]{1,0:T(8,128)(2,1)}) fusion(bf16[192,4096]{1,0:T(8,128)(2,1)} %bitcast.14), kind=kLoop, calls=%fused_computation.74 | loop fusion | bytes 3145728 | tf_op jit(solution)/shard_map/slice | solution.py:119
  23.6 0.4 collective-permute-done.1
  24.0 9.2 %collective-permute-start.6 = (bf16[192,2048]{1,0:T(8,128)(2,1)}, bf16[192,2048]{1,0:T(8,128)(2,1)}, u32[]{:S(2)}, u32[]{:S(2)}) collective-permute-start(bf16[192,2048]{1,0:T(8,128)(2,1)} %get-tuple-element.32), channel_id=1, source_target_pairs={{0,2},{6,4},{1,3},{7,5},{8,10},{14,12},{9,11},{15,13},{16,18},{22,... | collective-permute-start | bytes 2359304 | tf_op jit(solution)/shard_map/ppermute | solution.py:48
  33.2 7.6 %collective-permute-done = bf16[192,2560]{1,0:T(8,128)(2,1)S(1)} collective-permute-done((bf16[192,2560]{1,0:T(8,128)(2,1)}, bf16[192,2560]{1,0:T(8,128)(2,1)S(1)}, u32[]{:S(2)}, u32[]{:S(2)}) %collective-permute-start) | collective-permute-done | bytes 983072 | tf_op jit(solution)/shard_map/ppermute | solution.py:48
  40.8 1.2 convolution_convert_fusion.4
  42.2 1.5 collective-permute-start.5
  43.7 5.4 %collective-permute-start.13 = (bf16[192,2048]{1,0:T(8,128)(2,1)S(1)}, bf16[192,2048]{1,0:T(8,128)(2,1)}, u32[]{:S(2)}, u32[]{:S(2)}) collective-permute-start(bf16[192,2048]{1,0:T(8,128)(2,1)S(1)} %get-tuple-element.21), channel_id=1, source_target_pairs={{0,2},{6,4},{1,3},{7,5},{8,10},{14,12},{9,11},{15,13},{16,18},{22,... | collective-permute-start | bytes 2359304 | tf_op jit(solution)/shard_map/ppermute | solution.py:48
  49.1 1.3 collective-permute-start.10
  50.4 7.3 %collective-permute-done.6 = bf16[192,2048]{1,0:T(8,128)(2,1)} collective-permute-done((bf16[192,2048]{1,0:T(8,128)(2,1)}, bf16[192,2048]{1,0:T(8,128)(2,1)}, u32[]{:S(2)}, u32[]{:S(2)}) %collective-permute-start.6) | collective-permute-done | bytes 786464 | tf_op jit(solution)/shard_map/ppermute | solution.py:48
  57.6 0.7 collective-permute-start.8
  58.3 1.3 collective-permute-start.12
  59.6 0.2 multiply_reduce_fusion.1
  59.9 0.1 fusion.25
  60.1 6.0 %collective-permute-done.10 = bf16[128,2560]{1,0:T(8,128)(2,1)S(1)} collective-permute-done((bf16[128,2560]{1,0:T(8,128)(2,1)}, bf16[128,2560]{1,0:T(8,128)(2,1)S(1)}, u32[]{:S(2)}, u32[]{:S(2)}) %collective-permute-start.10) | collective-permute-done | bytes 655392 | tf_op jit(solution)/shard_map/ppermute | solution.py:56
  66.0 1.6 collective-permute-start.9
  67.7 0.7 collective-permute-start.11
  68.4 0.1 fusion.46
  68.5 5.9 %collective-permute-done.13 = bf16[192,2048]{1,0:T(8,128)(2,1)} collective-permute-done((bf16[192,2048]{1,0:T(8,128)(2,1)S(1)}, bf16[192,2048]{1,0:T(8,128)(2,1)}, u32[]{:S(2)}, u32[]{:S(2)}) %collective-permute-start.13) | collective-permute-done | bytes 786464 | tf_op jit(solution)/shard_map/ppermute | solution.py:48
  74.4 1.6 collective-permute-start.15
  76.0 2.9 %collective-permute-done.12 = bf16[128,2560]{1,0:T(8,128)(2,1)S(1)} collective-permute-done((bf16[128,2560]{1,0:T(8,128)(2,1)}, bf16[128,2560]{1,0:T(8,128)(2,1)S(1)}, u32[]{:S(2)}, u32[]{:S(2)}) %collective-permute-start.12) | collective-permute-done | bytes 655392 | tf_op jit(solution)/shard_map/ppermute | solution.py:56
  78.9 3.5 %convolution_convert_fusion.3 = bf16[256,2048]{1,0:T(8,128)(2,1)} fusion(bf16[768,256]{1,0:T(8,128)(2,1)S(1)} %pad_maximum_fusion.8, bf16[192,2048]{1,0:T(8,128)(2,1)S(1)} %collective-permute-done.8, bf16[192,2048]{1,0:T(8,128)(2,1)S(1)} %get-tuple-element.30, bf16[192,2048]{1,0:T(8,128)(2,1)} %collective-permute-done.6, ...), kind=kOutput, calls=%fused_computation.15 | convolution fusion | flops 818413568 | bytes 4587520 | tf_op jit(solution)/shard_map/dot_general | solution.py:72
  82.5 0.7 maximum_select_fusion
  83.2 12.6 %collective-permute-done.9 = bf16[128,4096]{1,0:T(8,128)(2,1)S(1)} collective-permute-done((bf16[128,4096]{1,0:T(8,128)(2,1)}, bf16[128,4096]{1,0:T(8,128)(2,1)S(1)}, u32[]{:S(2)}, u32[]{:S(2)}) %collective-permute-start.9) | collective-permute-done | bytes 1048608 | tf_op jit(solution)/shard_map/ppermute | solution.py:48
  95.8 2.9 %fusion.18 = f32[768,256]{1,0:T(8,128)S(1)} fusion(bf16[128,4096]{1,0:T(8,128)(2,1)} %bitcast.3, bf16[128,4096]{1,0:T(8,128)(2,1)S(1)} %collective-permute-done.9, bf16[192,2048]{1,0:T(8,128)(2,1)S(1)} %collective-permute-done.8, bf16[192,2048]{1,0:T(8,128)(2,1)S(1)} %get-tuple-element.30, bf16[192,2048]{1,0:T(8,128)(2,1)} %collective-permute-done.6, ...), kind=kOutput, calls=%fused_computation.28 | convolution fusion | flops 819986432 | bytes 6029312 | tf_op jit(solution)/shard_map/dot_general | solution.py:68
  98.8 3.1 %fusion.26 = bf16[576,256]{1,0:T(8,128)(2,1)} fusion(f32[768,256]{1,0:T(8,128)S(1)} %fusion.18, bf16[128,4096]{1,0:T(8,128)(2,1)S(1)} %collective-permute-done.9, bf16[128,4096]{1,0:T(8,128)(2,1)} %bitcast.3, bf16[192,2048]{1,0:T(8,128)(2,1)S(1)} %get-tuple-element.29, bf16[192,2048]{1,0:T(8,128)(2,1)} %collective-permute-done.13, ...), kind=kOutput, calls=%fused_computation.46 | convolution fusion | flops 613449728 | bytes 5341184 | tf_op jit(solution)/shard_map/dot_general | solution.py:68
  101.9 1.5 collective-permute-start.14
  103.4 1.2 slice.122
  104.6 1.4 collective-permute-start.17
  106.0 4.1 %collective-permute-done.14 = bf16[576,256]{1,0:T(8,128)(2,1)} collective-permute-done((bf16[576,256]{1,0:T(8,128)(2,1)}, bf16[576,256]{1,0:T(8,128)(2,1)}, u32[]{:S(2)}, u32[]{:S(2)}) %collective-permute-start.14) | collective-permute-done | bytes 294944 | tf_op jit(solution)/shard_map/ppermute | solution.py:60
  110.1 1.1 convert_add_fusion.1
  111.3 1.8 %fusion.27 = bf16[192,256]{1,0:T(8,128)(2,1)S(1)} fusion(f32[768,256]{1,0:T(8,128)} %copy-done.26, bf16[192,2048]{1,0:T(8,128)(2,1)} %collective-permute-done.15, bf16[128,4096]{1,0:T(8,128)(2,1)S(1)} %copy-done.1, bf16[128,4096]{1,0:T(8,128)(2,1)} %bitcast.3), kind=kOutput, calls=%fused_computation.53 | convolution fusion | flops 203522048 | bytes 3178496 | tf_op jit(solution)/shard_map/dot_general | solution.py:68
  113.1 1.6 collective-permute-start.16
  114.7 2.4 %fusion.8 = bf16[256,2048]{1,0:T(8,128)(2,1)S(1)} fusion(bf16[192,2048]{1,0:T(8,128)(2,1)} %collective-permute-done.15, bf16[192,2048]{1,0:T(8,128)(2,1)S(1)} %copy-done.11, bf16[192,2048]{1,0:T(8,128)(2,1)} %collective-permute-done.13, bf16[192,2048]{1,0:T(8,128)(2,1)S(1)} %copy-done.9, bf16[384,256]{1,0:T(8,128)(2,1)S(1)} %copy-done.25, ...), kind=kOutput, calls=%fused_computation.14 | convolution fusion | flops 819200000 | bytes 4587520 | tf_op jit(solution)/shard_map/dot_general | solution.py:72
  117.1 1.3 collective-permute-start.26
  118.5 4.2 %collective-permute-done.17 = bf16[128,2048]{1,0:T(8,128)(2,1)S(1)} collective-permute-done((bf16[128,2048]{1,0:T(8,128)(2,1)S(1)}, bf16[128,2048]{1,0:T(8,128)(2,1)S(1)}, u32[]{:S(2)}, u32[]{:S(2)}) %collective-permute-start.17) | collective-permute-done | bytes 524320 | tf_op jit(solution)/shard_map/ppermute | solution.py:56
  122.7 0.7 collective-permute-start.18
  123.5 0.3 multiply_reduce_fusion
  123.8 0.2 multiply_convert_fusion
  124.0 0.6 copy-done.4
  124.6 0.3 copy-done.6
  124.9 0.5 convolution_convert_fusion.2
  125.4 0.5 convolution_convert_fusion.1
  126.0 1.3 collective-permute-start.19
  127.3 0.7 collective-permute-start.21
  128.0 0.7 collective-permute-start.24
  128.7 0.5 fusion.32
  129.2 9.9 %collective-permute-done.19 = bf16[192,512]{1,0:T(8,128)(2,1)S(1)} collective-permute-done((bf16[192,512]{1,0:T(8,128)(2,1)S(1)}, bf16[192,512]{1,0:T(8,128)(2,1)S(1)}, u32[]{:S(2)}, u32[]{:S(2)}) %collective-permute-start.19) | collective-permute-done | bytes 196640 | tf_op jit(solution)/shard_map/ppermute | solution.py:56
  139.1 0.7 convolution_convert_fusion
  139.8 1.9 %collective-permute-start.20 = (bf16[192,2560]{1,0:T(8,128)(2,1)S(1)}, bf16[192,2560]{1,0:T(8,128)(2,1)S(1)}, u32[]{:S(2)}, u32[]{:S(2)}) collective-permute-start(bf16[192,2560]{1,0:T(8,128)(2,1)S(1)} %convolution_convert_fusion), channel_id=1, source_target_pairs={{8,0},{16,8},{24,16},{9,1},{17,9},{25,17},{10,2},{18,10},{26,18},{... | collective-permute-start | bytes 2949128 | tf_op jit(solution)/shard_map/ppermute | solution.py:13
  141.8 1.1 maximum_bitcast_fusion
  143.0 1.3 collective-permute-start.23
  144.3 0.7 collective-permute-start.22
  145.1 1.3 collective-permute-start.25
  146.4 7.0 %collective-permute-done.20 = bf16[192,2560]{1,0:T(8,128)(2,1)S(1)} collective-permute-done((bf16[192,2560]{1,0:T(8,128)(2,1)S(1)}, bf16[192,2560]{1,0:T(8,128)(2,1)S(1)}, u32[]{:S(2)}, u32[]{:S(2)}) %collective-permute-start.20) | collective-permute-done | bytes 983072 | tf_op jit(solution)/shard_map/ppermute | solution.py:13
  153.3 1.0 fusion.53
  154.3 8.1 %collective-permute-done.25 = bf16[128,1280]{1,0:T(8,128)(2,1)S(1)} collective-permute-done((bf16[128,1280]{1,0:T(8,128)(2,1)S(1)}, bf16[128,1280]{1,0:T(8,128)(2,1)S(1)}, u32[]{:S(2)}, u32[]{:S(2)}) %collective-permute-start.25) | collective-permute-done | bytes 327712 | tf_op jit(solution)/shard_map/ppermute | solution.py:56
  162.5 1.4 fusion.22
  (82 shorter events, 0.8 us)
Async XLA Ops:
  0.6 40.2 %copy-start.14 = (bf16[1,128,2560]{2,1,0:T(8,128)(2,1)S(1)}, bf16[1,128,2560]{2,1,0:T(8,128)(2,1)}, u32[]{:S(2)}) copy-start(bf16[1,128,2560]{2,1,0:T(8,128)(2,1)} %param.5) | copy-start | bytes 1966084
  0.6 40.2 %copy-start.3 = (bf16[1,192,2560]{2,1,0:T(8,128)(2,1)S(1)}, bf16[1,192,2560]{2,1,0:T(8,128)(2,1)}, u32[]{:S(2)}) copy-start(bf16[1,192,2560]{2,1,0:T(8,128)(2,1)} %param.4) | copy-start | bytes 2949124
  0.7 19.1 %collective-permute-start.2 = (bf16[128,2560]{1,0:T(8,128)(2,1)}, bf16[128,2560]{1,0:T(8,128)(2,1)S(1)}, u32[]{:S(2)}, u32[]{:S(2)}) collective-permute-start(bf16[128,2560]{1,0:T(8,128)(2,1)} %bitcast.21), channel_id=1, source_target_pairs={{0,2},{6,4},{1,3},{7,5},{8,10},{14,12},{9,11},{15,13},{16,18},{22,... | collective-permute-start | bytes 1966088 | tf_op jit(solution)/shard_map/ppermute | solution.py:48
  4.3 36.5 %collective-permute-start = (bf16[192,2560]{1,0:T(8,128)(2,1)}, bf16[192,2560]{1,0:T(8,128)(2,1)S(1)}, u32[]{:S(2)}, u32[]{:S(2)}) collective-permute-start(bf16[192,2560]{1,0:T(8,128)(2,1)} %bitcast.15), channel_id=1, source_target_pairs={{0,2},{6,4},{1,3},{7,5},{8,10},{14,12},{9,11},{15,13},{16,18},{22,... | collective-permute-start | bytes 2949128 | tf_op jit(solution)/shard_map/ppermute | solution.py:48
  5.7 18.3 %collective-permute-start.1 = (bf16[128,2560]{1,0:T(8,128)(2,1)}, bf16[128,2560]{1,0:T(8,128)(2,1)S(1)}, u32[]{:S(2)}, u32[]{:S(2)}) collective-permute-start(bf16[128,2560]{1,0:T(8,128)(2,1)} %bitcast.22), channel_id=1, source_target_pairs={{2,0},{4,6},{3,1},{5,7},{10,8},{12,14},{11,9},{13,15},{18,16},{20,... | collective-permute-start | bytes 1966088 | tf_op jit(solution)/shard_map/ppermute | solution.py:56
  7.0 33.8 %collective-permute-start.3 = (bf16[128,2560]{1,0:T(8,128)(2,1)}, bf16[128,2560]{1,0:T(8,128)(2,1)S(1)}, u32[]{:S(2)}, u32[]{:S(2)}) collective-permute-start(bf16[128,2560]{1,0:T(8,128)(2,1)} %bitcast.23), channel_id=1, source_target_pairs={{2,4},{4,2},{3,5},{5,3},{10,12},{12,10},{11,13},{13,11},{18,20},{2... | collective-permute-start | bytes 1966088 | tf_op jit(solution)/shard_map/ppermute | solution.py:52
  19.7 22.3 %copy-start.16 = (bf16[128,2560]{1,0:T(8,128)(2,1)}, bf16[128,2560]{1,0:T(8,128)(2,1)S(1)}, u32[]{:S(2)}) copy-start(bf16[128,2560]{1,0:T(8,128)(2,1)S(1)} %collective-permute-done.2) | copy-start | bytes 1966084
  19.7 21.1 %collective-permute-start.4 = (bf16[128,2560]{1,0:T(8,128)(2,1)S(1)}, bf16[128,2560]{1,0:T(8,128)(2,1)S(1)}, u32[]{:S(2)}, u32[]{:S(2)}) collective-permute-start(bf16[128,2560]{1,0:T(8,128)(2,1)S(1)} %collective-permute-done.2), channel_id=1, source_target_pairs={{2,4},{4,2},{3,5},{5,3},{10,12},{12,10},{11,13},{13,11},{18,20},{2... | collective-permute-start | bytes 1966088 | tf_op jit(solution)/shard_map/ppermute | solution.py:52
  20.4 47.3 %collective-permute-start.7 = (bf16[192,4096]{1,0:T(8,128)(2,1)}, bf16[192,4096]{1,0:T(8,128)(2,1)S(1)}, u32[]{:S(2)}, u32[]{:S(2)}) collective-permute-start(bf16[192,4096]{1,0:T(8,128)(2,1)} %bitcast.13), channel_id=1, source_target_pairs={{2,4},{4,2},{3,5},{5,3},{10,12},{12,10},{11,13},{13,11},{18,20},{2... | collective-permute-start | bytes 4718600 | tf_op jit(solution)/shard_map/ppermute | solution.py:52
  23.6 20.1 %copy-start.7 = (bf16[192,2048]{1,0:T(8,128)(2,1)}, bf16[192,2048]{1,0:T(8,128)(2,1)S(1)}, u32[]{:S(2)}) copy-start(bf16[192,2048]{1,0:T(8,128)(2,1)S(1)} %get-tuple-element.21) | copy-start | bytes 2359300
  24.0 16.8 %copy-start.18 = (bf16[128,2560]{1,0:T(8,128)(2,1)}, bf16[128,2560]{1,0:T(8,128)(2,1)S(1)}, u32[]{:S(2)}) copy-start(bf16[128,2560]{1,0:T(8,128)(2,1)S(1)} %collective-permute-done.1) | copy-start | bytes 1966084
  24.0 33.6 %collective-permute-start.6 = (bf16[192,2048]{1,0:T(8,128)(2,1)}, bf16[192,2048]{1,0:T(8,128)(2,1)}, u32[]{:S(2)}, u32[]{:S(2)}) collective-permute-start(bf16[192,2048]{1,0:T(8,128)(2,1)} %get-tuple-element.32), channel_id=1, source_target_pairs={{0,2},{6,4},{1,3},{7,5},{8,10},{14,12},{9,11},{15,13},{16,18},{22,... | collective-permute-start | bytes 2359304 | tf_op jit(solution)/shard_map/ppermute | solution.py:48
  40.8 1.3 copy-start.5
  40.8 1.3 copy-start.20
  40.8 1.3 copy-start.22
  42.2 16.2 %collective-permute-start.5 = (bf16[384,512]{1,0:T(8,128)(2,1)S(1)}, bf16[384,512]{1,0:T(8,128)(2,1)S(1)}, u32[]{:S(2)}, u32[]{:S(2)}) collective-permute-start(bf16[384,512]{1,0:T(8,128)(2,1)S(1)} %convolution_convert_fusion.4), channel_id=1, source_target_pairs={{0,1},{1,0},{2,3},{3,2},{4,5},{5,4},{6,7},{7,6},{8,9},{9,8},{10,11... | collective-permute-start | bytes 1179656 | tf_op jit(solution)/shard_map/ppermute | solution.py:60
  43.7 30.7 %collective-permute-start.13 = (bf16[192,2048]{1,0:T(8,128)(2,1)S(1)}, bf16[192,2048]{1,0:T(8,128)(2,1)}, u32[]{:S(2)}, u32[]{:S(2)}) collective-permute-start(bf16[192,2048]{1,0:T(8,128)(2,1)S(1)} %get-tuple-element.21), channel_id=1, source_target_pairs={{0,2},{6,4},{1,3},{7,5},{8,10},{14,12},{9,11},{15,13},{16,18},{22,... | collective-permute-start | bytes 2359304 | tf_op jit(solution)/shard_map/ppermute | solution.py:48
  49.1 17.0 %collective-permute-start.10 = (bf16[128,2560]{1,0:T(8,128)(2,1)}, bf16[128,2560]{1,0:T(8,128)(2,1)S(1)}, u32[]{:S(2)}, u32[]{:S(2)}) collective-permute-start(bf16[128,2560]{1,0:T(8,128)(2,1)} %copy-done.20), channel_id=1, source_target_pairs={{2,0},{4,6},{3,1},{5,7},{10,8},{12,14},{11,9},{13,15},{18,16},{20,... | collective-permute-start | bytes 1966088 | tf_op jit(solution)/shard_map/ppermute | solution.py:56
  57.6 21.2 %collective-permute-start.8 = (bf16[192,2048]{1,0:T(8,128)(2,1)}, bf16[192,2048]{1,0:T(8,128)(2,1)S(1)}, u32[]{:S(2)}, u32[]{:S(2)}) collective-permute-start(bf16[192,2048]{1,0:T(8,128)(2,1)} %collective-permute-done.6), channel_id=1, source_target_pairs={{2,4},{4,2},{3,5},{5,3},{10,12},{12,10},{11,13},{13,11},{18,20},{2... | collective-permute-start | bytes 2359304 | tf_op jit(solution)/shard_map/ppermute | solution.py:52
  58.3 20.5 %collective-permute-start.12 = (bf16[128,2560]{1,0:T(8,128)(2,1)}, bf16[128,2560]{1,0:T(8,128)(2,1)S(1)}, u32[]{:S(2)}, u32[]{:S(2)}) collective-permute-start(bf16[128,2560]{1,0:T(8,128)(2,1)} %copy-done.22), channel_id=1, source_target_pairs={{2,0},{4,6},{3,1},{5,7},{10,8},{12,14},{11,9},{13,15},{18,16},{20,... | collective-permute-start | bytes 1966088 | tf_op jit(solution)/shard_map/ppermute | solution.py:56
  60.0 15.9 %copy-start.12 = (bf16[384,256]{1,0:T(8,128)(2,1)}, bf16[384,256]{1,0:T(8,128)(2,1)S(1)}, u32[]{:S(2)}) copy-start(bf16[384,256]{1,0:T(8,128)(2,1)S(1)} %get-tuple-element.35) | copy-start | bytes 589828
  66.0 29.8 %collective-permute-start.9 = (bf16[128,4096]{1,0:T(8,128)(2,1)}, bf16[128,4096]{1,0:T(8,128)(2,1)S(1)}, u32[]{:S(2)}, u32[]{:S(2)}) collective-permute-start(bf16[128,4096]{1,0:T(8,128)(2,1)} %bitcast.3), channel_id=1, source_target_pairs={{0,2},{6,4},{1,3},{7,5},{8,10},{14,12},{9,11},{15,13},{16,18},{22,... | collective-permute-start | bytes 3145736 | tf_op jit(solution)/shard_map/ppermute | solution.py:48
  67.7 8.3 %collective-permute-start.11 = (bf16[384,256]{1,0:T(8,128)(2,1)S(1)}, bf16[384,256]{1,0:T(8,128)(2,1)S(1)}, u32[]{:S(2)}, u32[]{:S(2)}) collective-permute-start(bf16[384,256]{1,0:T(8,128)(2,1)S(1)} %get-tuple-element.18), channel_id=1, source_target_pairs={{2,4},{4,2},{3,5},{5,3},{10,12},{12,10},{11,13},{13,11},{18,20},{2... | collective-permute-start | bytes 589832 | tf_op jit(solution)/shard_map/ppermute | solution.py:52
  68.5 30.3 %copy-start.10 = (bf16[192,2048]{1,0:T(8,128)(2,1)}, bf16[192,2048]{1,0:T(8,128)(2,1)S(1)}, u32[]{:S(2)}) copy-start(bf16[192,2048]{1,0:T(8,128)(2,1)S(1)} %get-tuple-element.29) | copy-start | bytes 2359300
  74.4 36.9 %collective-permute-start.15 = (bf16[192,2048]{1,0:T(8,128)(2,1)}, bf16[192,2048]{1,0:T(8,128)(2,1)}, u32[]{:S(2)}, u32[]{:S(2)}) collective-permute-start(bf16[192,2048]{1,0:T(8,128)(2,1)} %collective-permute-done.13), channel_id=1, source_target_pairs={{2,4},{4,2},{3,5},{5,3},{10,12},{12,10},{11,13},{13,11},{18,20},{2... | collective-permute-start | bytes 2359304 | tf_op jit(solution)/shard_map/ppermute | solution.py:52
  75.9 2.9 %copy-start.24 = (bf16[384,256]{1,0:T(8,128)(2,1)}, bf16[384,256]{1,0:T(8,128)(2,1)S(1)}, u32[]{:S(2)}) copy-start(bf16[384,256]{1,0:T(8,128)(2,1)S(1)} %collective-permute-done.11) | copy-start | bytes 589828
  78.8 3.6 %copy-start.15 = (bf16[1,128,2560]{2,1,0:T(8,128)(2,1)S(1)}, bf16[1,128,2560]{2,1,0:T(8,128)(2,1)}, u32[]{:S(2)}) copy-start(bf16[1,128,2560]{2,1,0:T(8,128)(2,1)} %param.5) | copy-start | bytes 1966084
  78.8 3.6 %copy-start.17 = (bf16[128,2560]{1,0:T(8,128)(2,1)S(1)}, bf16[128,2560]{1,0:T(8,128)(2,1)}, u32[]{:S(2)}) copy-start(bf16[128,2560]{1,0:T(8,128)(2,1)} %copy-done.16) | copy-start | bytes 1966084
  78.9 3.6 %copy-start.19 = (bf16[128,2560]{1,0:T(8,128)(2,1)S(1)}, bf16[128,2560]{1,0:T(8,128)(2,1)}, u32[]{:S(2)}) copy-start(bf16[128,2560]{1,0:T(8,128)(2,1)} %copy-done.18) | copy-start | bytes 1966084
  78.9 3.6 %copy-start.21 = (bf16[128,2560]{1,0:T(8,128)(2,1)S(1)}, bf16[128,2560]{1,0:T(8,128)(2,1)}, u32[]{:S(2)}) copy-start(bf16[128,2560]{1,0:T(8,128)(2,1)} %copy-done.20) | copy-start | bytes 1966084
  78.9 3.6 %copy-start.23 = (bf16[128,2560]{1,0:T(8,128)(2,1)S(1)}, bf16[128,2560]{1,0:T(8,128)(2,1)}, u32[]{:S(2)}) copy-start(bf16[128,2560]{1,0:T(8,128)(2,1)} %copy-done.22) | copy-start | bytes 1966084
  83.2 15.6 %copy-start.8 = (bf16[192,2048]{1,0:T(8,128)(2,1)S(1)}, bf16[192,2048]{1,0:T(8,128)(2,1)}, u32[]{:S(2)}) copy-start(bf16[192,2048]{1,0:T(8,128)(2,1)} %copy-done.7) | copy-start | bytes 2359300
  95.8 2.9 %copy-start = (bf16[128,4096]{1,0:T(8,128)(2,1)}, bf16[128,4096]{1,0:T(8,128)(2,1)S(1)}, u32[]{:S(2)}) copy-start(bf16[128,4096]{1,0:T(8,128)(2,1)S(1)} %collective-permute-done.9) | copy-start | bytes 3145732
  98.7 3.1 %copy-start.26 = (f32[768,256]{1,0:T(8,128)}, f32[768,256]{1,0:T(8,128)S(1)}, u32[]{:S(2)}) copy-start(f32[768,256]{1,0:T(8,128)S(1)} %fusion.18) | copy-start | bytes 2359300
  101.9 8.2 %collective-permute-start.14 = (bf16[576,256]{1,0:T(8,128)(2,1)}, bf16[576,256]{1,0:T(8,128)(2,1)}, u32[]{:S(2)}, u32[]{:S(2)}) collective-permute-start(bf16[576,256]{1,0:T(8,128)(2,1)} %fusion.26), channel_id=1, source_target_pairs={{0,1},{1,0},{2,3},{3,2},{4,5},{5,4},{6,7},{7,6},{8,9},{9,8},{10,11... | collective-permute-start | bytes 884744 | tf_op jit(solution)/shard_map/ppermute | solution.py:60
  103.4 7.9 %copy-start.1 = (bf16[128,4096]{1,0:T(8,128)(2,1)S(1)}, bf16[128,4096]{1,0:T(8,128)(2,1)}, u32[]{:S(2)}) copy-start(bf16[128,4096]{1,0:T(8,128)(2,1)} %copy-done) | copy-start | bytes 3145732
  104.5 10.1 %copy-start.9 = (bf16[192,2048]{1,0:T(8,128)(2,1)S(1)}, bf16[192,2048]{1,0:T(8,128)(2,1)}, u32[]{:S(2)}) copy-start(bf16[192,2048]{1,0:T(8,128)(2,1)} %copy-done.7) | copy-start | bytes 2359300
  104.6 10.1 %copy-start.11 = (bf16[192,2048]{1,0:T(8,128)(2,1)S(1)}, bf16[192,2048]{1,0:T(8,128)(2,1)}, u32[]{:S(2)}) copy-start(bf16[192,2048]{1,0:T(8,128)(2,1)} %copy-done.10) | copy-start | bytes 2359300
  104.6 10.1 %copy-start.13 = (bf16[384,256]{1,0:T(8,128)(2,1)S(1)}, bf16[384,256]{1,0:T(8,128)(2,1)}, u32[]{:S(2)}) copy-start(bf16[384,256]{1,0:T(8,128)(2,1)} %copy-done.12) | copy-start | bytes 589828
  104.6 10.1 %copy-start.25 = (bf16[384,256]{1,0:T(8,128)(2,1)S(1)}, bf16[384,256]{1,0:T(8,128)(2,1)}, u32[]{:S(2)}) copy-start(bf16[384,256]{1,0:T(8,128)(2,1)} %copy-done.24) | copy-start | bytes 589828
  104.6 18.1 %collective-permute-start.17 = (bf16[128,2048]{1,0:T(8,128)(2,1)S(1)}, bf16[128,2048]{1,0:T(8,128)(2,1)S(1)}, u32[]{:S(2)}, u32[]{:S(2)}) collective-permute-start(bf16[128,2048]{1,0:T(8,128)(2,1)S(1)} %slice.122), channel_id=1, source_target_pairs={{2,0},{4,6},{3,1},{5,7},{10,8},{12,14},{11,9},{13,15},{18,16},{20,... | collective-permute-start | bytes 1572872 | tf_op jit(solution)/shard_map/ppermute | solution.py:56
  113.1 10.2 %copy-start.2 = (bf16[256,2048]{1,0:T(8,128)(2,1)S(1)}, bf16[256,2048]{1,0:T(8,128)(2,1)}, u32[]{:S(2)}) copy-start(bf16[256,2048]{1,0:T(8,128)(2,1)} %convolution_convert_fusion.3) | copy-start | bytes 3145732
  113.1 5.3 %collective-permute-start.16 = (bf16[192,256]{1,0:T(8,128)(2,1)S(1)}, bf16[192,256]{1,0:T(8,128)(2,1)S(1)}, u32[]{:S(2)}, u32[]{:S(2)}) collective-permute-start(bf16[192,256]{1,0:T(8,128)(2,1)S(1)} %fusion.27), channel_id=1, source_target_pairs={{0,1},{1,0},{2,3},{3,2},{4,5},{5,4},{6,7},{7,6},{8,9},{9,8},{10,11... | collective-permute-start | bytes 294920 | tf_op jit(solution)/shard_map/ppermute | solution.py:60
  117.1 24.6 %collective-permute-start.26 = (bf16[128,2048]{1,0:T(8,128)(2,1)S(1)}, bf16[128,2048]{1,0:T(8,128)(2,1)S(1)}, u32[]{:S(2)}, u32[]{:S(2)}) collective-permute-start(bf16[128,2048]{1,0:T(8,128)(2,1)S(1)} %slice.135), channel_id=1, source_target_pairs={{2,0},{4,6},{3,1},{5,7},{10,8},{12,14},{11,9},{13,15},{18,16},{20,... | collective-permute-start | bytes 1572872 | tf_op jit(solution)/shard_map/ppermute | solution.py:56
  122.7 0.8 collective-permute-start.18
  123.4 1.2 copy-start.4
  123.4 1.5 copy-start.6
  126.0 13.1 %collective-permute-start.19 = (bf16[192,512]{1,0:T(8,128)(2,1)S(1)}, bf16[192,512]{1,0:T(8,128)(2,1)S(1)}, u32[]{:S(2)}, u32[]{:S(2)}) collective-permute-start(bf16[192,512]{1,0:T(8,128)(2,1)S(1)} %slice.124), channel_id=1, source_target_pairs={{2,0},{4,6},{3,1},{5,7},{10,8},{12,14},{11,9},{13,15},{18,16},{20,... | collective-permute-start | bytes 589832 | tf_op jit(solution)/shard_map/ppermute | solution.py:56
  127.3 15.6 %collective-permute-start.21 = (bf16[128,1280]{1,0:T(8,128)(2,1)S(1)}, bf16[128,1280]{1,0:T(8,128)(2,1)S(1)}, u32[]{:S(2)}, u32[]{:S(2)}) collective-permute-start(bf16[128,1280]{1,0:T(8,128)(2,1)S(1)} %get-tuple-element.34), channel_id=1, source_target_pairs={{2,4},{4,2},{3,5},{5,3},{10,12},{12,10},{11,13},{13,11},{18,20},{2... | collective-permute-start | bytes 983048 | tf_op jit(solution)/shard_map/ppermute | solution.py:52
  128.0 17.0 %collective-permute-start.24 = (bf16[128,1280]{1,0:T(8,128)(2,1)S(1)}, bf16[128,1280]{1,0:T(8,128)(2,1)S(1)}, u32[]{:S(2)}, u32[]{:S(2)}) collective-permute-start(bf16[128,1280]{1,0:T(8,128)(2,1)S(1)} %get-tuple-element.33), channel_id=1, source_target_pairs={{2,4},{4,2},{3,5},{5,3},{10,12},{12,10},{11,13},{13,11},{18,20},{2... | collective-permute-start | bytes 983048 | tf_op jit(solution)/shard_map/ppermute | solution.py:52
  139.8 13.5 %collective-permute-start.20 = (bf16[192,2560]{1,0:T(8,128)(2,1)S(1)}, bf16[192,2560]{1,0:T(8,128)(2,1)S(1)}, u32[]{:S(2)}, u32[]{:S(2)}) collective-permute-start(bf16[192,2560]{1,0:T(8,128)(2,1)S(1)} %convolution_convert_fusion), channel_id=1, source_target_pairs={{8,0},{16,8},{24,16},{9,1},{17,9},{25,17},{10,2},{18,10},{26,18},{... | collective-permute-start | bytes 2949128 | tf_op jit(solution)/shard_map/ppermute | solution.py:13
  143.0 19.5 %collective-permute-start.23 = (bf16[128,1280]{1,0:T(8,128)(2,1)S(1)}, bf16[128,1280]{1,0:T(8,128)(2,1)S(1)}, u32[]{:S(2)}, u32[]{:S(2)}) collective-permute-start(bf16[128,1280]{1,0:T(8,128)(2,1)S(1)} %fusion.24), channel_id=1, source_target_pairs={{2,0},{4,6},{3,1},{5,7},{10,8},{12,14},{11,9},{13,15},{18,16},{20,... | collective-permute-start | bytes 983048 | tf_op jit(solution)/shard_map/ppermute | solution.py:56
  144.3 10.1 %collective-permute-start.22 = (bf16[128,2560]{1,0:T(8,128)(2,1)S(1)}, bf16[128,2560]{1,0:T(8,128)(2,1)S(1)}, u32[]{:S(2)}, u32[]{:S(2)}) collective-permute-start(bf16[128,2560]{1,0:T(8,128)(2,1)S(1)} %convolution_convert_fusion.1), channel_id=1, source_target_pairs={{2,4},{4,2},{3,5},{5,3},{10,12},{12,10},{11,13},{13,11},{18,20},{2... | collective-permute-start | bytes 1966088 | tf_op jit(solution)/shard_map/ppermute | solution.py:52
  145.1 17.4 %collective-permute-start.25 = (bf16[128,1280]{1,0:T(8,128)(2,1)S(1)}, bf16[128,1280]{1,0:T(8,128)(2,1)S(1)}, u32[]{:S(2)}, u32[]{:S(2)}) collective-permute-start(bf16[128,1280]{1,0:T(8,128)(2,1)S(1)} %fusion.23), channel_id=1, source_target_pairs={{2,0},{4,6},{3,1},{5,7},{10,8},{12,14},{11,9},{13,15},{18,16},{20,... | collective-permute-start | bytes 983048 | tf_op jit(solution)/shard_map/ppermute | solution.py:56

commit v6 on v4

--- a/solution.py
+++ b/solution.py
@@ -108,9 +108,14 @@
 
     latent = col_sum(rows_dot(tokens_mine, down_all))
     inv_rms = lax.rsqrt(jnp.mean(latent * latent, axis=-1, keepdims=True) + 1e-06)
+    def parts(value):
+        high = value.astype(BF16)
+        return [high, (value - high.astype(F32)).astype(BF16)]
+
     normed = latent * inv_rms
     normed_bf = normed.astype(BF16)
-    normed_sent = after(normed_bf[:, 2 * lat :], down_there[1])
+    inv_parts = parts(inv_rms)
+    normed_sent = after(normed_bf[:, 2 * lat :], down_there[1], *inv_parts)
     normed_other = across(normed_sent)
     normed_all = jnp.concatenate([normed_bf[:, : 2 * lat], normed_other], axis=0)
 
@@ -128,7 +133,9 @@
     early_sum = early.astype(F32) + other_col(early).astype(F32)
 
     last = after(cot_other_end[1], early)
-    late = col_sum(grad[3 * rows :] + rows_dot(last, up_mine[:, cuts[1]]))
+    late = (grad[3 * rows :] + rows_dot(last, up_mine[:, cuts[1]])).astype(BF16)
+    early_mine = after(early_sum[: 2 * rows], late)
+    late = late.astype(F32) + other_col(late).astype(F32)
     values = jnp.concatenate([early_rows(1), last], axis=0)
     up_second = tokens_dot(normed_all, values).astype(BF16)
     back_second = outward(up_second[lat:])
@@ -140,30 +147,56 @@
         axis=1,
     )
 
-    grad_sent = jnp.concatenate([early_sum[2 * rows :], late], axis=0).astype(BF16)
-    from_across = across(after(grad_sent, up_second, back_first))
-    normed_grad = jnp.concatenate([early_sum[: 2 * rows], from_across.astype(F32)], axis=1)
+    width = tokens.shape[1]
+    first, share = width // 10 // 128 * 128, 3 * width // 10 // 128 * 128
+    half = (share + width) // 2 // 128 * 128
+    moved_first = across(tokens_mine[:, :first])
+
+    row_sum = jnp.sum(early_mine * normed[:, : 2 * lat], axis=-1, keepdims=True)
+    riders = parts(row_sum) + inv_parts
+    riders.append(jnp.zeros((2 * rows, 124), BF16))
+    grad_other = jnp.concatenate([early_sum[2 * rows :], late], axis=0)
+    grad_sent = jnp.concatenate([grad_other.astype(BF16)] + riders, axis=1)
+    grad_sent = after(grad_sent, up_second, back_first, moved_first)
+    moved_second = across(after(tokens_mine[:, first:share], grad_sent))
+    from_across = across(grad_sent).astype(F32)
+    normed_grad = jnp.concatenate([early_mine, from_across[:, : 2 * lat]], axis=1)
     inner = jnp.mean(normed_grad * normed, axis=-1, keepdims=True)
     latent_bf = (inv_rms * (normed_grad - normed * inner)).astype(BF16)
     latent_there = outward(latent_bf[rows:])
     latent_used = jnp.where(middle, latent_bf[:rows], latent_there)
 
     sums = [
-        tokens_dot(latent_bf[:, j * lat : (j + 1) * lat], tokens_mine) for j in range(4)
+        tokens_dot(latent_bf[:, j * lat : (j + 1) * lat], tokens_mine[:, share:]) for j in range(4)
     ]
-    width = tokens.shape[1] // 2
-    halves = (slice(0, width), slice(width, 2 * width))
     sent_end, sent_own = sums[3].astype(BF16), sums[2].astype(BF16)
-    from_end = [across(sent_end[:, half]) for half in halves]
-    from_own = across(after(sent_own, from_end[0]))
-    end_first = (sums[1][:, halves[0]] + from_end[0].astype(F32)).astype(BF16)
-    end_second = sums[1][:, halves[1]] + after(from_end[1], end_first).astype(F32)
-    down_end_grad = jnp.concatenate([outward(end_first), outward(end_second.astype(BF16))], axis=1)
-    down_own_grad = (sums[0] + from_own.astype(F32)).astype(BF16)
-    down_grad = jnp.where(middle, down_own_grad, down_end_grad)
+    from_end = [across(sent_end[:, : half - share]), across(sent_end[:, half - share :])]
+
+    riders = from_across[:, 2 * lat : 2 * lat + 4]
+    row_sum_other, inv_rms_other = riders[:, :1] + riders[:, 1:2], riders[:, 2:3] + riders[:, 3:]
+    values = normed_other.astype(F32)
+    inner = row_sum_other + jnp.sum(grad_other * values, axis=-1, keepdims=True)
+    inner = inner / (4 * lat)
+    latent_other = (inv_rms_other * (grad_other - values * inner)).astype(BF16)
+    moved = jnp.concatenate([moved_first, moved_second], axis=1)
+    direct = tokens_dot(
+        jnp.concatenate([latent_bf[:, : 2 * lat], latent_other], axis=0),
+        jnp.concatenate([tokens_mine[:, :share], moved], axis=0),
+    ).astype(BF16)
+
+    from_own = across(after(sent_own, from_end[0], direct))
+    end_first = (sums[1][:, : half - share] + from_end[0].astype(F32)).astype(BF16)
+    end_second = sums[1][:, half - share :] + after(from_end[1], end_first).astype(F32)
+    down_end_grad = jnp.concatenate(
+        [outward(direct[lat:]), outward(end_first), outward(end_second.astype(BF16))], axis=1
+    )
 
     input_grad = jnp.dot(latent_used, down_used, preferred_element_type=F32).astype(BF16)
     passed = shifted(input_grad, "section", -1)
+    final = lax.axis_index("section") == lax.axis_size("section") - 1
+    passed = jnp.where(final, jnp.zeros_like(passed), passed)
+    own_rest = (sums[0] + after(from_own, passed).astype(F32)).astype(BF16)
+    down_grad = jnp.where(middle, jnp.concatenate([direct[:lat], own_rest], axis=1), down_end_grad)
     return (passed[None], down_grad[None], up_grad[None])
 
 

time: 163 us -> 184 us (1.13)
  other arithmetic: 3.1 us -> 15 us
  waiting for transfers between devices: 93.2 us -> 82.4 us
  local copies, waits for them, and re-layouts: 4.96 us -> 12.1 us
  matrix products: 12.4 us -> 19.4 us
  starting transfers between devices: 45.8 us -> 51 us
    ppermute x5, waiting for transfers between devices: 48.1 us -> 41.5 us  [inward(): return lax.ppermute(value, 'row', [(0, 1), (3, 2)])]
    ppermute x1, waiting for transfers between devices: 0.01 us -> 5.98 us  [shifted(): lax.ppermute(value, axis, [(source, source + steps) for source in range(l...]
    ppermute x8 -> x9, waiting for transfers between devices: 39.5 us -> 33.7 us  [outward(): return lax.ppermute(value, 'row', [(1, 0), (2, 3)])]
    ppermute x3, waiting for transfers between devices: 5.62 us -> 1.24 us  [other_col(): return lax.ppermute(value, 'col', [(0, 1), (1, 0)])]
    ppermute x10 -> x12, starting transfers between devices: 6.95 us -> 11.1 us  [across(): return lax.ppermute(value, 'row', [(1, 2), (2, 1)])]
    dot_general x4, matrix products: 4.98 us -> 8.5 us  [rows_dot(): lax.dot_general(left, right, (((1,), (1,)), ((), ())), preferred_element_...]
    dot_general x6 -> x7, matrix products: 6.73 us -> 10.2 us  [tokens_dot(): lax.dot_general(left, right, (((0,), (0,)), ((), ())), preferred_element_...]
    concatenate x0 -> x1, local copies, waits for them, and re-layouts: none -> 2.1 us  [folded_body(): grad_sent = jnp.concatenate([grad_other.astype(BF16)] + riders, axis=1)]
  transfers between devices with their start and end apart: 27 -> 30, of which waited for: 13 -> 11; matrix products, arithmetic and copies ran while one was open for 12% -> 24% of each run, Pallas kernels for 0% -> 0%
where the time goes in v6:
time: 184 us; the launch traced here: 181 us
  waiting for transfers between devices  82.4 us (45%)
  starting transfers between devices  51 us (28%)
  matrix products  19.4 us (11%)
  other arithmetic  15 us (8%)
  local copies, waits for them, and re-layouts  12.1 us (7%)
    ppermute x5, waiting for transfers between devices, inward(): return lax.ppermute(value, 'row', [(0, 1), (3, 2)])  41.5 us
    ppermute x9, waiting for transfers between devices, outward(): return lax.ppermute(value, 'row', [(1, 0), (2, 3)])  33.7 us
    ppermute x5, starting transfers between devices, inward(): return lax.ppermute(value, 'row', [(0, 1), (3, 2)])  21.6 us
    ppermute x9, starting transfers between devices, outward(): return lax.ppermute(value, 'row', [(1, 0), (2, 3)])  11.9 us
    ppermute x12, starting transfers between devices, across(): return lax.ppermute(value, 'row', [(1, 2), (2, 1)])  11.1 us
    dot_general x7, matrix products, tokens_dot(): lax.dot_general(left, right, (((0,), (0,)), ((), ())), preferred_element_...  10.2 us
    dot_general x4, matrix products, rows_dot(): lax.dot_general(left, right, (((1,), (1,)), ((), ())), preferred_element_...  8.5 us
    ppermute x1, waiting for transfers between devices, shifted(): lax.ppermute(value, axis, [(source, source + steps) for source in range(l...  5.98 us
  transfers between devices with their start and end apart: 30, of which 11 were waited for; matrix products, arithmetic and copies ran while one was open for 24% of the time, Pallas kernels for 0%

profile of v6, /device:TPU:4, one launch (start us, length us, event | category | flops | bytes accessed | tf_op | source)
XLA Modules:
  0.0 181.3 jit_solution(305428192293438357)
XLA Ops:
  0.7 3.7 %collective-permute-start.2 = (bf16[128,2560]{1,0:T(8,128)(2,1)}, bf16[128,2560]{1,0:T(8,128)(2,1)S(1)}, u32[]{:S(2)}, u32[]{:S(2)}) collective-permute-start(bf16[128,2560]{1,0:T(8,128)(2,1)} %bitcast.33), channel_id=1, source_target_pairs={{0,2},{6,4},{1,3},{7,5},{8,10},{14,12},{9,11},{15,13},{16,18},{22,... | collective-permute-start | bytes 1966088 | tf_op jit(solution)/shard_map/ppermute | solution.py:48
  4.3 1.4 collective-permute-start
  5.7 1.3 collective-permute-start.1
  7.0 0.7 collective-permute-start.3
  7.7 12.0 %collective-permute-done.2 = bf16[128,2560]{1,0:T(8,128)(2,1)S(1)} collective-permute-done((bf16[128,2560]{1,0:T(8,128)(2,1)}, bf16[128,2560]{1,0:T(8,128)(2,1)S(1)}, u32[]{:S(2)}, u32[]{:S(2)}) %collective-permute-start.2) | collective-permute-done | bytes 655392 | tf_op jit(solution)/shard_map/ppermute | solution.py:48
  19.7 0.7 collective-permute-start.4
  20.4 1.9 %collective-permute-start.7 = (bf16[192,4096]{1,0:T(8,128)(2,1)}, bf16[192,4096]{1,0:T(8,128)(2,1)}, u32[]{:S(2)}, u32[]{:S(2)}) collective-permute-start(bf16[192,4096]{1,0:T(8,128)(2,1)} %bitcast.27), channel_id=1, source_target_pairs={{2,4},{4,2},{3,5},{5,3},{10,12},{12,10},{11,13},{13,11},{18,20},{2... | collective-permute-start | bytes 4718600 | tf_op jit(solution)/shard_map/ppermute | solution.py:52
  22.3 2.4 %fusion.75 = (bf16[192,2048]{1,0:T(8,128)(2,1)}, bf16[192,2048]{1,0:T(8,128)(2,1)S(1)}) fusion(bf16[192,4096]{1,0:T(8,128)(2,1)} %bitcast.28), kind=kLoop, calls=%fused_computation.111 | loop fusion | bytes 3145728 | tf_op jit(solution)/shard_map/slice | solution.py:124
  24.7 8.5 %collective-permute-start.6 = (bf16[192,2048]{1,0:T(8,128)(2,1)S(1)}, bf16[192,2048]{1,0:T(8,128)(2,1)}, u32[]{:S(2)}, u32[]{:S(2)}) collective-permute-start(bf16[192,2048]{1,0:T(8,128)(2,1)S(1)} %get-tuple-element.38), channel_id=1, source_target_pairs={{0,2},{6,4},{1,3},{7,5},{8,10},{14,12},{9,11},{15,13},{16,18},{22,... | collective-permute-start | bytes 2359304 | tf_op jit(solution)/shard_map/ppermute | solution.py:48
  33.1 7.6 %collective-permute-done = bf16[192,2560]{1,0:T(8,128)(2,1)S(1)} collective-permute-done((bf16[192,2560]{1,0:T(8,128)(2,1)}, bf16[192,2560]{1,0:T(8,128)(2,1)S(1)}, u32[]{:S(2)}, u32[]{:S(2)}) %collective-permute-start) | collective-permute-done | bytes 983072 | tf_op jit(solution)/shard_map/ppermute | solution.py:48
  40.8 1.2 fusion.21
  42.1 1.6 collective-permute-start.5
  43.6 5.6 %collective-permute-start.13 = (bf16[192,2048]{1,0:T(8,128)(2,1)}, bf16[192,2048]{1,0:T(8,128)(2,1)}, u32[]{:S(2)}, u32[]{:S(2)}) collective-permute-start(bf16[192,2048]{1,0:T(8,128)(2,1)} %get-tuple-element.22), channel_id=1, source_target_pairs={{0,2},{6,4},{1,3},{7,5},{8,10},{14,12},{9,11},{15,13},{16,18},{22,... | collective-permute-start | bytes 2359304 | tf_op jit(solution)/shard_map/ppermute | solution.py:48
  49.2 1.3 collective-permute-start.10
  50.5 7.0 %collective-permute-done.6 = bf16[192,2048]{1,0:T(8,128)(2,1)} collective-permute-done((bf16[192,2048]{1,0:T(8,128)(2,1)S(1)}, bf16[192,2048]{1,0:T(8,128)(2,1)}, u32[]{:S(2)}, u32[]{:S(2)}) %collective-permute-start.6) | collective-permute-done | bytes 786464 | tf_op jit(solution)/shard_map/ppermute | solution.py:48
  57.5 0.7 collective-permute-start.8
  58.2 1.3 collective-permute-start.12
  60.0 0.8 fusion.47
  60.7 0.8 rsqrt.31
  61.5 4.8 %collective-permute-done.10 = bf16[128,2560]{1,0:T(8,128)(2,1)S(1)} collective-permute-done((bf16[128,2560]{1,0:T(8,128)(2,1)}, bf16[128,2560]{1,0:T(8,128)(2,1)S(1)}, u32[]{:S(2)}, u32[]{:S(2)}) %collective-permute-start.10) | collective-permute-done | bytes 655392 | tf_op jit(solution)/shard_map/ppermute | solution.py:56
  66.3 2.5 %collective-permute-start.9 = (bf16[128,4096]{1,0:T(8,128)(2,1)S(1)}, bf16[128,4096]{1,0:T(8,128)(2,1)S(1)}, u32[]{:S(2)}, u32[]{:S(2)}) collective-permute-start(bf16[128,4096]{1,0:T(8,128)(2,1)S(1)} %bitcast.29), channel_id=1, source_target_pairs={{0,2},{6,4},{1,3},{7,5},{8,10},{14,12},{9,11},{15,13},{16,18},{22,... | collective-permute-start | bytes 3145736 | tf_op jit(solution)/shard_map/ppermute | solution.py:48
  69.6 1.5 fusion.74
  71.1 3.4 %collective-permute-done.13 = bf16[192,2048]{1,0:T(8,128)(2,1)} collective-permute-done((bf16[192,2048]{1,0:T(8,128)(2,1)}, bf16[192,2048]{1,0:T(8,128)(2,1)}, u32[]{:S(2)}, u32[]{:S(2)}) %collective-permute-start.13) | collective-permute-done | bytes 786464 | tf_op jit(solution)/shard_map/ppermute | solution.py:48
  74.5 1.6 collective-permute-start.15
  76.1 2.9 %collective-permute-done.12 = bf16[128,2560]{1,0:T(8,128)(2,1)S(1)} collective-permute-done((bf16[128,2560]{1,0:T(8,128)(2,1)}, bf16[128,2560]{1,0:T(8,128)(2,1)S(1)}, u32[]{:S(2)}, u32[]{:S(2)}) %collective-permute-start.12) | collective-permute-done | bytes 655392 | tf_op jit(solution)/shard_map/ppermute | solution.py:56
  79.0 3.3 %convolution_convert_fusion.1 = bf16[256,2048]{1,0:T(8,128)(2,1)} fusion(bf16[768,256]{1,0:T(8,128)(2,1)S(1)} %pad_maximum_fusion.10, bf16[192,2048]{1,0:T(8,128)(2,1)S(1)} %collective-permute-done.8, bf16[192,2048]{1,0:T(8,128)(2,1)S(1)} %get-tuple-element.36, bf16[192,2048]{1,0:T(8,128)(2,1)} %collective-permute-done.6, bf16[192,2048]{1,0:T(8,128)(2,1)S(1)} %copy-done.11), kind=kOutput, calls=%fused_computation.13 | convolution fusion | flops 818413568 | bytes 4587520 | tf_op jit(solution)/shard_map/dot_general | solution.py:72
  82.4 1.9 %maximum_select_fusion = bf16[512,2560]{1,0:T(8,128)(2,1)} fusion(bf16[128,2560]{1,0:T(8,128)(2,1)S(1)} %collective-permute-done.12, bf16[128,2560]{1,0:T(8,128)(2,1)S(1)} %collective-permute-done.10, bf16[128,2560]{1,0:T(8,128)(2,1)S(1)} %bitcast.37, bf16[128,2560]{1,0:T(8,128)(2,1)S(1)} %copy-done.21, pred[]{:T(512)S(6)} %or.3, ...), kind=kLoop, calls=%fused_computation.11 | loop fusion | flops 22282240 | bytes 7208961 | tf_op jit(solution)/shard_map/jit(_where)/select_n | solution.py:103
  84.2 11.5 %collective-permute-done.9 = bf16[128,4096]{1,0:T(8,128)(2,1)S(1)} collective-permute-done((bf16[128,4096]{1,0:T(8,128)(2,1)S(1)}, bf16[128,4096]{1,0:T(8,128)(2,1)S(1)}, u32[]{:S(2)}, u32[]{:S(2)}) %collective-permute-start.9) | collective-permute-done | bytes 1048608 | tf_op jit(solution)/shard_map/ppermute | solution.py:48
  95.7 2.5 %fusion.31 = f32[768,256]{1,0:T(8,128)S(1)} fusion(bf16[128,4096]{1,0:T(8,128)(2,1)S(1)} %bitcast.30, bf16[128,4096]{1,0:T(8,128)(2,1)S(1)} %collective-permute-done.9, bf16[192,2048]{1,0:T(8,128)(2,1)S(1)} %collective-permute-done.8, bf16[192,2048]{1,0:T(8,128)(2,1)S(1)} %get-tuple-element.36, bf16[192,2048]{1,0:T(8,128)(2,1)} %collective-permute-done.6, ...), kind=kOutput, calls=%fused_computation.38 | convolution fusion | flops 819986432 | bytes 6029312 | tf_op jit(solution)/shard_map/dot_general | solution.py:68
  98.3 2.5 %fusion.34 = bf16[576,256]{1,0:T(8,128)(2,1)S(1)} fusion(f32[768,256]{1,0:T(8,128)S(1)} %fusion.31, bf16[128,4096]{1,0:T(8,128)(2,1)S(1)} %collective-permute-done.9, bf16[128,4096]{1,0:T(8,128)(2,1)S(1)} %bitcast.31, bf16[192,2048]{1,0:T(8,128)(2,1)S(1)} %get-tuple-element.35, bf16[192,2048]{1,0:T(8,128)(2,1)} %collective-permute-done.13, ...), kind=kOutput, calls=%fused_computation.51 | convolution fusion | flops 613449728 | bytes 5341184 | tf_op jit(solution)/shard_map/dot_general | solution.py:68
  100.7 1.6 collective-permute-start.14
  102.3 0.7 pad_maximum_fusion.12
  103.0 1.5 collective-permute-start.18
  104.5 0.8 pad_maximum_fusion.9
  105.3 0.9 slice.182
  106.1 1.4 collective-permute-start.17
  107.5 1.2 collective-permute-done.14
  108.8 1.0 convert_add_fusion.1
  109.9 2.3 %fusion.52 = bf16[192,256]{1,0:T(8,128)(2,1)} fusion(f32[768,256]{1,0:T(8,128)} %copy-done.26, bf16[192,2048]{1,0:T(8,128)(2,1)} %collective-permute-done.15, bf16[128,4096]{1,0:T(8,128)(2,1)S(1)} %copy-done.7, bf16[128,4096]{1,0:T(8,128)(2,1)S(1)} %bitcast.32), kind=kOutput, calls=%fused_computation.88 | convolution fusion | flops 203522048 | bytes 3178496 | tf_op jit(solution)/shard_map/dot_general | solution.py:68
  112.2 1.5 collective-permute-start.16
  113.7 3.6 %fusion.8 = bf16[256,2048]{1,0:T(8,128)(2,1)} fusion(bf16[192,2048]{1,0:T(8,128)(2,1)} %collective-permute-done.15, bf16[192,2048]{1,0:T(8,128)(2,1)S(1)} %copy-done.13, bf16[192,2048]{1,0:T(8,128)(2,1)} %collective-permute-done.13, bf16[192,2048]{1,0:T(8,128)(2,1)} %get-tuple-element.22, bf16[384,256]{1,0:T(8,128)(2,1)S(1)} %collective-permute-done.11, ...), kind=kOutput, calls=%fused_computation.12 | convolution fusion | flops 819200000 | bytes 4587520 | tf_op jit(solution)/shard_map/dot_general | solution.py:72
  117.5 0.8 copy.14
  118.3 0.8 copy.15
  119.1 1.9 %slice.203 = bf16[128,2048]{1,0:T(8,128)(2,1)} slice(bf16[256,2048]{1,0:T(8,128)(2,1)} %fusion.8), slice={[128:256], [0:2048]} | slice | bytes 1048576 | tf_op jit(solution)/shard_map/slice | solution.py:141
  121.0 1.3 collective-permute-start.29
  122.3 1.0 convert_add_fusion.2
  123.2 0.7 fusion.46
  124.6 2.1 %concatenate.83 = bf16[384,384]{1,0:T(8,128)(2,1)} concatenate(bf16[384,256]{1,0:T(8,128)(2,1)} %fusion.46, bf16[384,1]{1,0:T(8,128)(2,1)} %copy.14, bf16[384,1]{1,0:T(8,128)(2,1)} %copy.15, bf16[384,1]{1,0:T(8,128)(2,1)} %rsqrt.31, bf16[384,1]{1,0:T(8,128)(2,1)} %fusion.47, bf16[384,124]{1,0:T(8,128)(2,1)} %broadcast_in_dim.20), dimensions={1} | concatenate | bytes 589824 | tf_op jit(solution)/shard_map/concatenate | solution.py:159
  127.4 1.3 slice_select_fusion.1
  129.4 1.1 fusion.38
  131.8 1.3 collective-permute-start.20
  135.6 1.6 convolution_convert_fusion.4
  137.2 1.4 collective-permute-start.25
  138.6 16.3 %collective-permute-done.20 = bf16[192,512]{1,0:T(8,128)(2,1)S(1)} collective-permute-done((bf16[192,512]{1,0:T(8,128)(2,1)S(1)}, bf16[192,512]{1,0:T(8,128)(2,1)S(1)}, u32[]{:S(2)}, u32[]{:S(2)}) %collective-permute-start.20) | collective-permute-done | bytes 196640 | tf_op jit(solution)/shard_map/ppermute | solution.py:56
  155.0 0.7 convolution_convert_fusion
  155.7 1.9 %collective-permute-start.21 = (bf16[192,2560]{1,0:T(8,128)(2,1)S(1)}, bf16[192,2560]{1,0:T(8,128)(2,1)S(1)}, u32[]{:S(2)}, u32[]{:S(2)}) collective-permute-start(bf16[192,2560]{1,0:T(8,128)(2,1)S(1)} %convolution_convert_fusion), channel_id=1, source_target_pairs={{8,0},{16,8},{24,16},{9,1},{17,9},{25,17},{10,2},{18,10},{26,18},{... | collective-permute-start | bytes 2949128 | tf_op jit(solution)/shard_map/ppermute | solution.py:13
  157.6 1.1 slice_select_fusion
  158.7 1.1 maximum_bitcast_fusion
  160.6 1.3 collective-permute-start.26
  161.9 1.3 collective-permute-start.28
  163.2 6.0 %collective-permute-done.21 = bf16[192,2560]{1,0:T(8,128)(2,1)S(1)} collective-permute-done((bf16[192,2560]{1,0:T(8,128)(2,1)S(1)}, bf16[192,2560]{1,0:T(8,128)(2,1)S(1)}, u32[]{:S(2)}, u32[]{:S(2)}) %collective-permute-start.21) | collective-permute-done | bytes 983072 | tf_op jit(solution)/shard_map/ppermute | solution.py:13
  169.7 9.6 %collective-permute-done.28 = bf16[128,896]{1,0:T(8,128)(2,1)S(1)} collective-permute-done((bf16[128,896]{1,0:T(8,128)(2,1)S(1)}, bf16[128,896]{1,0:T(8,128)(2,1)S(1)}, u32[]{:S(2)}, u32[]{:S(2)}) %collective-permute-start.28) | collective-permute-done | bytes 229408 | tf_op jit(solution)/shard_map/ppermute | solution.py:56
  179.3 1.0 maximum_select_fusion.1
  180.3 1.0 fusion.82
  (107 shorter events, 8.4 us)
Async XLA Ops:
  0.6 40.2 %copy-start.16 = (bf16[1,128,2560]{2,1,0:T(8,128)(2,1)S(1)}, bf16[1,128,2560]{2,1,0:T(8,128)(2,1)}, u32[]{:S(2)}) copy-start(bf16[1,128,2560]{2,1,0:T(8,128)(2,1)} %param.5) | copy-start | bytes 1966084
  0.6 40.2 %copy-start = (bf16[1,192,2560]{2,1,0:T(8,128)(2,1)S(1)}, bf16[1,192,2560]{2,1,0:T(8,128)(2,1)}, u32[]{:S(2)}) copy-start(bf16[1,192,2560]{2,1,0:T(8,128)(2,1)} %param.4) | copy-start | bytes 2949124
  0.7 19.1 %collective-permute-start.2 = (bf16[128,2560]{1,0:T(8,128)(2,1)}, bf16[128,2560]{1,0:T(8,128)(2,1)S(1)}, u32[]{:S(2)}, u32[]{:S(2)}) collective-permute-start(bf16[128,2560]{1,0:T(8,128)(2,1)} %bitcast.33), channel_id=1, source_target_pairs={{0,2},{6,4},{1,3},{7,5},{8,10},{14,12},{9,11},{15,13},{16,18},{22,... | collective-permute-start | bytes 1966088 | tf_op jit(solution)/shard_map/ppermute | solution.py:48
  4.3 36.5 %collective-permute-start = (bf16[192,2560]{1,0:T(8,128)(2,1)}, bf16[192,2560]{1,0:T(8,128)(2,1)S(1)}, u32[]{:S(2)}, u32[]{:S(2)}) collective-permute-start(bf16[192,2560]{1,0:T(8,128)(2,1)} %bitcast.18), channel_id=1, source_target_pairs={{0,2},{6,4},{1,3},{7,5},{8,10},{14,12},{9,11},{15,13},{16,18},{22,... | collective-permute-start | bytes 2949128 | tf_op jit(solution)/shard_map/ppermute | solution.py:48
  5.7 19.0 %collective-permute-start.1 = (bf16[128,2560]{1,0:T(8,128)(2,1)}, bf16[128,2560]{1,0:T(8,128)(2,1)S(1)}, u32[]{:S(2)}, u32[]{:S(2)}) collective-permute-start(bf16[128,2560]{1,0:T(8,128)(2,1)} %bitcast.34), channel_id=1, source_target_pairs={{2,0},{4,6},{3,1},{5,7},{10,8},{12,14},{11,9},{13,15},{18,16},{20,... | collective-permute-start | bytes 1966088 | tf_op jit(solution)/shard_map/ppermute | solution.py:56
  7.0 33.8 %collective-permute-start.3 = (bf16[128,2560]{1,0:T(8,128)(2,1)}, bf16[128,2560]{1,0:T(8,128)(2,1)S(1)}, u32[]{:S(2)}, u32[]{:S(2)}) collective-permute-start(bf16[128,2560]{1,0:T(8,128)(2,1)} %bitcast.35), channel_id=1, source_target_pairs={{2,4},{4,2},{3,5},{5,3},{10,12},{12,10},{11,13},{13,11},{18,20},{2... | collective-permute-start | bytes 1966088 | tf_op jit(solution)/shard_map/ppermute | solution.py:52
  19.7 22.3 %copy-start.18 = (bf16[128,2560]{1,0:T(8,128)(2,1)}, bf16[128,2560]{1,0:T(8,128)(2,1)S(1)}, u32[]{:S(2)}) copy-start(bf16[128,2560]{1,0:T(8,128)(2,1)S(1)} %collective-permute-done.2) | copy-start | bytes 1966084
  19.7 21.1 %collective-permute-start.4 = (bf16[128,2560]{1,0:T(8,128)(2,1)S(1)}, bf16[128,2560]{1,0:T(8,128)(2,1)S(1)}, u32[]{:S(2)}, u32[]{:S(2)}) collective-permute-start(bf16[128,2560]{1,0:T(8,128)(2,1)S(1)} %collective-permute-done.2), channel_id=1, source_target_pairs={{2,4},{4,2},{3,5},{5,3},{10,12},{12,10},{11,13},{13,11},{18,20},{2... | collective-permute-start | bytes 1966088 | tf_op jit(solution)/shard_map/ppermute | solution.py:52
  20.4 48.5 %collective-permute-start.7 = (bf16[192,4096]{1,0:T(8,128)(2,1)}, bf16[192,4096]{1,0:T(8,128)(2,1)}, u32[]{:S(2)}, u32[]{:S(2)}) collective-permute-start(bf16[192,4096]{1,0:T(8,128)(2,1)} %bitcast.27), channel_id=1, source_target_pairs={{2,4},{4,2},{3,5},{5,3},{10,12},{12,10},{11,13},{13,11},{18,20},{2... | collective-permute-start | bytes 4718600 | tf_op jit(solution)/shard_map/ppermute | solution.py:52
  24.7 17.4 %copy-start.10 = (bf16[192,2048]{1,0:T(8,128)(2,1)}, bf16[192,2048]{1,0:T(8,128)(2,1)S(1)}, u32[]{:S(2)}) copy-start(bf16[192,2048]{1,0:T(8,128)(2,1)S(1)} %get-tuple-element.38) | copy-start | bytes 2359300
  24.7 16.1 %copy-start.20 = (bf16[128,2560]{1,0:T(8,128)(2,1)}, bf16[128,2560]{1,0:T(8,128)(2,1)S(1)}, u32[]{:S(2)}) copy-start(bf16[128,2560]{1,0:T(8,128)(2,1)S(1)} %collective-permute-done.1) | copy-start | bytes 1966084
  24.7 32.9 %collective-permute-start.6 = (bf16[192,2048]{1,0:T(8,128)(2,1)S(1)}, bf16[192,2048]{1,0:T(8,128)(2,1)}, u32[]{:S(2)}, u32[]{:S(2)}) collective-permute-start(bf16[192,2048]{1,0:T(8,128)(2,1)S(1)} %get-tuple-element.38), channel_id=1, source_target_pairs={{0,2},{6,4},{1,3},{7,5},{8,10},{14,12},{9,11},{15,13},{16,18},{22,... | collective-permute-start | bytes 2359304 | tf_op jit(solution)/shard_map/ppermute | solution.py:48
  40.8 1.3 copy-start.22
  40.8 1.3 copy-start.24
  42.1 16.2 %collective-permute-start.5 = (bf16[384,512]{1,0:T(8,128)(2,1)S(1)}, bf16[384,512]{1,0:T(8,128)(2,1)S(1)}, u32[]{:S(2)}, u32[]{:S(2)}) collective-permute-start(bf16[384,512]{1,0:T(8,128)(2,1)S(1)} %fusion.21), channel_id=1, source_target_pairs={{0,1},{1,0},{2,3},{3,2},{4,5},{5,4},{6,7},{7,6},{8,9},{9,8},{10,11... | collective-permute-start | bytes 1179656 | tf_op jit(solution)/shard_map/ppermute | solution.py:60
  43.6 22.7 %copy-start.4 = (bf16[1,128,4096]{2,1,0:T(8,128)(2,1)S(1)}, bf16[1,128,4096]{2,1,0:T(8,128)(2,1)}, u32[]{:S(2)}) copy-start(bf16[1,128,4096]{2,1,0:T(8,128)(2,1)} %param.6) | copy-start | bytes 3145732
  43.6 30.8 %collective-permute-start.13 = (bf16[192,2048]{1,0:T(8,128)(2,1)}, bf16[192,2048]{1,0:T(8,128)(2,1)}, u32[]{:S(2)}, u32[]{:S(2)}) collective-permute-start(bf16[192,2048]{1,0:T(8,128)(2,1)} %get-tuple-element.22), channel_id=1, source_target_pairs={{0,2},{6,4},{1,3},{7,5},{8,10},{14,12},{9,11},{15,13},{16,18},{22,... | collective-permute-start | bytes 2359304 | tf_op jit(solution)/shard_map/ppermute | solution.py:48
  49.2 17.1 %collective-permute-start.10 = (bf16[128,2560]{1,0:T(8,128)(2,1)}, bf16[128,2560]{1,0:T(8,128)(2,1)S(1)}, u32[]{:S(2)}, u32[]{:S(2)}) collective-permute-start(bf16[128,2560]{1,0:T(8,128)(2,1)} %copy-done.22), channel_id=1, source_target_pairs={{2,0},{4,6},{3,1},{5,7},{10,8},{12,14},{11,9},{13,15},{18,16},{20,... | collective-permute-start | bytes 1966088 | tf_op jit(solution)/shard_map/ppermute | solution.py:56
  57.5 21.5 %collective-permute-start.8 = (bf16[192,2048]{1,0:T(8,128)(2,1)}, bf16[192,2048]{1,0:T(8,128)(2,1)S(1)}, u32[]{:S(2)}, u32[]{:S(2)}) collective-permute-start(bf16[192,2048]{1,0:T(8,128)(2,1)} %collective-permute-done.6), channel_id=1, source_target_pairs={{2,4},{4,2},{3,5},{5,3},{10,12},{12,10},{11,13},{13,11},{18,20},{2... | collective-permute-start | bytes 2359304 | tf_op jit(solution)/shard_map/ppermute | solution.py:52
  58.2 20.7 %collective-permute-start.12 = (bf16[128,2560]{1,0:T(8,128)(2,1)}, bf16[128,2560]{1,0:T(8,128)(2,1)S(1)}, u32[]{:S(2)}, u32[]{:S(2)}) collective-permute-start(bf16[128,2560]{1,0:T(8,128)(2,1)} %copy-done.24), channel_id=1, source_target_pairs={{2,0},{4,6},{3,1},{5,7},{10,8},{12,14},{11,9},{13,15},{18,16},{20,... | collective-permute-start | bytes 1966088 | tf_op jit(solution)/shard_map/ppermute | solution.py:56
  59.9 19.1 %copy-start.11 = (bf16[192,2048]{1,0:T(8,128)(2,1)S(1)}, bf16[192,2048]{1,0:T(8,128)(2,1)}, u32[]{:S(2)}) copy-start(bf16[192,2048]{1,0:T(8,128)(2,1)} %copy-done.10) | copy-start | bytes 2359300
  60.0 22.3 %copy-start.14 = (bf16[384,256]{1,0:T(8,128)(2,1)}, bf16[384,256]{1,0:T(8,128)(2,1)S(1)}, u32[]{:S(2)}) copy-start(bf16[384,256]{1,0:T(8,128)(2,1)S(1)} %get-tuple-element.43) | copy-start | bytes 589828
  66.3 29.4 %collective-permute-start.9 = (bf16[128,4096]{1,0:T(8,128)(2,1)S(1)}, bf16[128,4096]{1,0:T(8,128)(2,1)S(1)}, u32[]{:S(2)}, u32[]{:S(2)}) collective-permute-start(bf16[128,4096]{1,0:T(8,128)(2,1)S(1)} %bitcast.29), channel_id=1, source_target_pairs={{0,2},{6,4},{1,3},{7,5},{8,10},{14,12},{9,11},{15,13},{16,18},{22,... | collective-permute-start | bytes 3145736 | tf_op jit(solution)/shard_map/ppermute | solution.py:48
  68.9 7.2 %collective-permute-start.11 = (bf16[384,256]{1,0:T(8,128)(2,1)S(1)}, bf16[384,256]{1,0:T(8,128)(2,1)S(1)}, u32[]{:S(2)}, u32[]{:S(2)}) collective-permute-start(bf16[384,256]{1,0:T(8,128)(2,1)S(1)} %get-tuple-element.19), channel_id=1, source_target_pairs={{2,4},{4,2},{3,5},{5,3},{10,12},{12,10},{11,13},{13,11},{18,20},{2... | collective-permute-start | bytes 589832 | tf_op jit(solution)/shard_map/ppermute | solution.py:52
  71.1 27.1 %copy-start.12 = (bf16[192,2048]{1,0:T(8,128)(2,1)}, bf16[192,2048]{1,0:T(8,128)(2,1)S(1)}, u32[]{:S(2)}) copy-start(bf16[192,2048]{1,0:T(8,128)(2,1)S(1)} %get-tuple-element.35) | copy-start | bytes 2359300
  74.5 35.4 %collective-permute-start.15 = (bf16[192,2048]{1,0:T(8,128)(2,1)}, bf16[192,2048]{1,0:T(8,128)(2,1)}, u32[]{:S(2)}, u32[]{:S(2)}) collective-permute-start(bf16[192,2048]{1,0:T(8,128)(2,1)} %collective-permute-done.13), channel_id=1, source_target_pairs={{2,4},{4,2},{3,5},{5,3},{10,12},{12,10},{11,13},{13,11},{18,20},{2... | collective-permute-start | bytes 2359304 | tf_op jit(solution)/shard_map/ppermute | solution.py:52
  76.1 37.7 %copy-start.2 = (bf16[384,256]{1,0:T(8,128)(2,1)}, bf16[384,256]{1,0:T(8,128)(2,1)S(1)}, u32[]{:S(2)}) copy-start(bf16[384,256]{1,0:T(8,128)(2,1)S(1)} %collective-permute-done.11) | copy-start | bytes 589828
  79.0 3.3 %copy-start.17 = (bf16[1,128,2560]{2,1,0:T(8,128)(2,1)S(1)}, bf16[1,128,2560]{2,1,0:T(8,128)(2,1)}, u32[]{:S(2)}) copy-start(bf16[1,128,2560]{2,1,0:T(8,128)(2,1)} %param.5) | copy-start | bytes 1966084
  79.0 3.3 %copy-start.19 = (bf16[128,2560]{1,0:T(8,128)(2,1)S(1)}, bf16[128,2560]{1,0:T(8,128)(2,1)}, u32[]{:S(2)}) copy-start(bf16[128,2560]{1,0:T(8,128)(2,1)} %copy-done.18) | copy-start | bytes 1966084
  79.0 3.3 %copy-start.21 = (bf16[128,2560]{1,0:T(8,128)(2,1)S(1)}, bf16[128,2560]{1,0:T(8,128)(2,1)}, u32[]{:S(2)}) copy-start(bf16[128,2560]{1,0:T(8,128)(2,1)} %copy-done.20) | copy-start | bytes 1966084
  79.0 3.3 %copy-start.23 = (bf16[128,2560]{1,0:T(8,128)(2,1)S(1)}, bf16[128,2560]{1,0:T(8,128)(2,1)}, u32[]{:S(2)}) copy-start(bf16[128,2560]{1,0:T(8,128)(2,1)} %copy-done.22) | copy-start | bytes 1966084
  79.0 3.3 %copy-start.25 = (bf16[128,2560]{1,0:T(8,128)(2,1)S(1)}, bf16[128,2560]{1,0:T(8,128)(2,1)}, u32[]{:S(2)}) copy-start(bf16[128,2560]{1,0:T(8,128)(2,1)} %copy-done.24) | copy-start | bytes 1966084
  95.7 2.6 %copy-start.6 = (bf16[128,4096]{1,0:T(8,128)(2,1)}, bf16[128,4096]{1,0:T(8,128)(2,1)S(1)}, u32[]{:S(2)}) copy-start(bf16[128,4096]{1,0:T(8,128)(2,1)S(1)} %collective-permute-done.9) | copy-start | bytes 3145732
  98.2 2.5 %copy-start.26 = (f32[768,256]{1,0:T(8,128)}, f32[768,256]{1,0:T(8,128)S(1)}, u32[]{:S(2)}) copy-start(f32[768,256]{1,0:T(8,128)S(1)} %fusion.31) | copy-start | bytes 2359300
  100.7 8.0 %collective-permute-start.14 = (bf16[576,256]{1,0:T(8,128)(2,1)S(1)}, bf16[576,256]{1,0:T(8,128)(2,1)}, u32[]{:S(2)}, u32[]{:S(2)}) collective-permute-start(bf16[576,256]{1,0:T(8,128)(2,1)S(1)} %fusion.34), channel_id=1, source_target_pairs={{0,1},{1,0},{2,3},{3,2},{4,5},{5,4},{6,7},{7,6},{8,9},{9,8},{10,11... | collective-permute-start | bytes 884744 | tf_op jit(solution)/shard_map/ppermute | solution.py:60
  102.3 3.0 %copy-start.9 = (bf16[256,2048]{1,0:T(8,128)(2,1)S(1)}, bf16[256,2048]{1,0:T(8,128)(2,1)}, u32[]{:S(2)}) copy-start(bf16[256,2048]{1,0:T(8,128)(2,1)} %convolution_convert_fusion.1) | copy-start | bytes 3145732
  103.0 6.9 %copy-start.5 = (bf16[1,128,4096]{2,1,0:T(8,128)(2,1)S(1)}, bf16[1,128,4096]{2,1,0:T(8,128)(2,1)}, u32[]{:S(2)}) copy-start(bf16[1,128,4096]{2,1,0:T(8,128)(2,1)} %param.6) | copy-start | bytes 3145732
  103.0 6.9 %copy-start.7 = (bf16[128,4096]{1,0:T(8,128)(2,1)S(1)}, bf16[128,4096]{1,0:T(8,128)(2,1)}, u32[]{:S(2)}) copy-start(bf16[128,4096]{1,0:T(8,128)(2,1)} %copy-done.6) | copy-start | bytes 3145732
  103.0 23.7 %collective-permute-start.18 = (bf16[384,256]{1,0:T(8,128)(2,1)}, bf16[384,256]{1,0:T(8,128)(2,1)}, u32[]{:S(2)}, u32[]{:S(2)}) collective-permute-start(bf16[384,256]{1,0:T(8,128)(2,1)} %pad_maximum_fusion.12), channel_id=1, source_target_pairs={{2,4},{4,2},{3,5},{5,3},{10,12},{12,10},{11,13},{13,11},{18,20},{2... | collective-permute-start | bytes 589832 | tf_op jit(solution)/shard_map/ppermute | solution.py:52
  106.1 7.6 %copy-start.13 = (bf16[192,2048]{1,0:T(8,128)(2,1)S(1)}, bf16[192,2048]{1,0:T(8,128)(2,1)}, u32[]{:S(2)}) copy-start(bf16[192,2048]{1,0:T(8,128)(2,1)} %copy-done.12) | copy-start | bytes 2359300
  106.1 7.6 %copy-start.15 = (bf16[384,256]{1,0:T(8,128)(2,1)S(1)}, bf16[384,256]{1,0:T(8,128)(2,1)}, u32[]{:S(2)}) copy-start(bf16[384,256]{1,0:T(8,128)(2,1)} %copy-done.14) | copy-start | bytes 589828
  106.1 20.6 %collective-permute-start.17 = (bf16[128,2048]{1,0:T(8,128)(2,1)}, bf16[128,2048]{1,0:T(8,128)(2,1)}, u32[]{:S(2)}, u32[]{:S(2)}) collective-permute-start(bf16[128,2048]{1,0:T(8,128)(2,1)} %slice.182), channel_id=1, source_target_pairs={{2,0},{4,6},{3,1},{5,7},{10,8},{12,14},{11,9},{13,15},{18,16},{20,... | collective-permute-start | bytes 1572872 | tf_op jit(solution)/shard_map/ppermute | solution.py:56
  112.2 10.0 %collective-permute-start.16 = (bf16[192,256]{1,0:T(8,128)(2,1)}, bf16[192,256]{1,0:T(8,128)(2,1)}, u32[]{:S(2)}, u32[]{:S(2)}) collective-permute-start(bf16[192,256]{1,0:T(8,128)(2,1)} %fusion.52), channel_id=1, source_target_pairs={{0,1},{1,0},{2,3},{3,2},{4,5},{5,4},{6,7},{7,6},{8,9},{9,8},{10,11... | collective-permute-start | bytes 294920 | tf_op jit(solution)/shard_map/ppermute | solution.py:60
  121.0 36.6 %collective-permute-start.29 = (bf16[128,2048]{1,0:T(8,128)(2,1)}, bf16[128,2048]{1,0:T(8,128)(2,1)}, u32[]{:S(2)}, u32[]{:S(2)}) collective-permute-start(bf16[128,2048]{1,0:T(8,128)(2,1)} %slice.203), channel_id=1, source_target_pairs={{2,0},{4,6},{3,1},{5,7},{10,8},{12,14},{11,9},{13,15},{18,16},{20,... | collective-permute-start | bytes 1572872 | tf_op jit(solution)/shard_map/ppermute | solution.py:56
  126.7 3.7 %collective-permute-start.19 = (bf16[384,384]{1,0:T(8,128)(2,1)}, bf16[384,384]{1,0:T(8,128)(2,1)S(1)}, u32[]{:S(2)}, u32[]{:S(2)}) collective-permute-start(bf16[384,384]{1,0:T(8,128)(2,1)} %concatenate.83), channel_id=1, source_target_pairs={{2,4},{4,2},{3,5},{5,3},{10,12},{12,10},{11,13},{13,11},{18,20},{2... | collective-permute-start | bytes 884744 | tf_op jit(solution)/shard_map/ppermute | solution.py:52
  128.7 6.9 %collective-permute-start.22 = (bf16[384,512]{1,0:T(8,128)(2,1)}, bf16[384,512]{1,0:T(8,128)(2,1)S(1)}, u32[]{:S(2)}, u32[]{:S(2)}) collective-permute-start(bf16[384,512]{1,0:T(8,128)(2,1)} %pad_maximum_fusion.9), channel_id=1, source_target_pairs={{2,4},{4,2},{3,5},{5,3},{10,12},{12,10},{11,13},{13,11},{18,20},{2... | collective-permute-start | bytes 1179656 | tf_op jit(solution)/shard_map/ppermute | solution.py:52
  131.3 3.6 %copy-start.3 = (bf16[384,256]{1,0:T(8,128)(2,1)S(1)}, bf16[384,256]{1,0:T(8,128)(2,1)}, u32[]{:S(2)}) copy-start(bf16[384,256]{1,0:T(8,128)(2,1)} %copy-done.2) | copy-start | bytes 589828
  131.8 23.2 %collective-permute-start.20 = (bf16[192,512]{1,0:T(8,128)(2,1)S(1)}, bf16[192,512]{1,0:T(8,128)(2,1)S(1)}, u32[]{:S(2)}, u32[]{:S(2)}) collective-permute-start(bf16[192,512]{1,0:T(8,128)(2,1)S(1)} %slice.185), channel_id=1, source_target_pairs={{2,0},{4,6},{3,1},{5,7},{10,8},{12,14},{11,9},{13,15},{18,16},{20,... | collective-permute-start | bytes 589832 | tf_op jit(solution)/shard_map/ppermute | solution.py:56
  133.1 26.7 %collective-permute-start.23 = (bf16[128,896]{1,0:T(8,128)(2,1)S(1)}, bf16[128,896]{1,0:T(8,128)(2,1)S(1)}, u32[]{:S(2)}, u32[]{:S(2)}) collective-permute-start(bf16[128,896]{1,0:T(8,128)(2,1)S(1)} %get-tuple-element.40), channel_id=1, source_target_pairs={{2,4},{4,2},{3,5},{5,3},{10,12},{12,10},{11,13},{13,11},{18,20},{2... | collective-permute-start | bytes 688136 | tf_op jit(solution)/shard_map/ppermute | solution.py:52
  133.8 28.1 %collective-permute-start.27 = (bf16[128,896]{1,0:T(8,128)(2,1)S(1)}, bf16[128,896]{1,0:T(8,128)(2,1)S(1)}, u32[]{:S(2)}, u32[]{:S(2)}) collective-permute-start(bf16[128,896]{1,0:T(8,128)(2,1)S(1)} %get-tuple-element.39), channel_id=1, source_target_pairs={{2,4},{4,2},{3,5},{5,3},{10,12},{12,10},{11,13},{13,11},{18,20},{2... | collective-permute-start | bytes 688136 | tf_op jit(solution)/shard_map/ppermute | solution.py:52
  135.6 19.4 %copy-start.1 = (bf16[512,2560]{1,0:T(8,128)(2,1)S(1)}, bf16[512,2560]{1,0:T(8,128)(2,1)}, u32[]{:S(2)}) copy-start(bf16[512,2560]{1,0:T(8,128)(2,1)} %maximum_select_fusion) | copy-start | bytes 7864324
  137.2 20.4 %copy-start.8 = (bf16[256,2048]{1,0:T(8,128)(2,1)S(1)}, bf16[256,2048]{1,0:T(8,128)(2,1)}, u32[]{:S(2)}) copy-start(bf16[256,2048]{1,0:T(8,128)(2,1)} %fusion.8) | copy-start | bytes 3145732
  137.2 32.4 %collective-permute-start.25 = (bf16[128,768]{1,0:T(8,128)(2,1)S(1)}, bf16[128,768]{1,0:T(8,128)(2,1)S(1)}, u32[]{:S(2)}, u32[]{:S(2)}) collective-permute-start(bf16[128,768]{1,0:T(8,128)(2,1)S(1)} %get-tuple-element.41), channel_id=1, source_target_pairs={{2,0},{4,6},{3,1},{5,7},{10,8},{12,14},{11,9},{13,15},{18,16},{20,... | collective-permute-start | bytes 589832 | tf_op jit(solution)/shard_map/ppermute | solution.py:56
  155.7 13.5 %collective-permute-start.21 = (bf16[192,2560]{1,0:T(8,128)(2,1)S(1)}, bf16[192,2560]{1,0:T(8,128)(2,1)S(1)}, u32[]{:S(2)}, u32[]{:S(2)}) collective-permute-start(bf16[192,2560]{1,0:T(8,128)(2,1)S(1)} %convolution_convert_fusion), channel_id=1, source_target_pairs={{8,0},{16,8},{24,16},{9,1},{17,9},{25,17},{10,2},{18,10},{26,18},{... | collective-permute-start | bytes 2949128 | tf_op jit(solution)/shard_map/ppermute | solution.py:13
  159.8 9.4 %collective-permute-start.24 = (bf16[128,1792]{1,0:T(8,128)(2,1)S(1)}, bf16[128,1792]{1,0:T(8,128)(2,1)S(1)}, u32[]{:S(2)}, u32[]{:S(2)}) collective-permute-start(bf16[128,1792]{1,0:T(8,128)(2,1)S(1)} %convolution_convert_fusion.3), channel_id=1, source_target_pairs={{2,4},{4,2},{3,5},{5,3},{10,12},{12,10},{11,13},{13,11},{18,20},{2... | collective-permute-start | bytes 1376264 | tf_op jit(solution)/shard_map/ppermute | solution.py:52
  160.6 18.7 %collective-permute-start.26 = (bf16[128,896]{1,0:T(8,128)(2,1)S(1)}, bf16[128,896]{1,0:T(8,128)(2,1)S(1)}, u32[]{:S(2)}, u32[]{:S(2)}) collective-permute-start(bf16[128,896]{1,0:T(8,128)(2,1)S(1)} %fusion.37), channel_id=1, source_target_pairs={{2,0},{4,6},{3,1},{5,7},{10,8},{12,14},{11,9},{13,15},{18,16},{20,... | collective-permute-start | bytes 688136 | tf_op jit(solution)/shard_map/ppermute | solution.py:56
  161.9 17.4 %collective-permute-start.28 = (bf16[128,896]{1,0:T(8,128)(2,1)S(1)}, bf16[128,896]{1,0:T(8,128)(2,1)S(1)}, u32[]{:S(2)}, u32[]{:S(2)}) collective-permute-start(bf16[128,896]{1,0:T(8,128)(2,1)S(1)} %fusion.36), channel_id=1, source_target_pairs={{2,0},{4,6},{3,1},{5,7},{10,8},{12,14},{11,9},{13,15},{18,16},{20,... | collective-permute-start | bytes 688136 | tf_op jit(solution)/shard_map/ppermute | solution.py:56

commit v7 on v4

--- a/solution.py
+++ b/solution.py
@@ -64,6 +64,11 @@
     return lax.optimization_barrier((value, *earlier))[0]
 
 
+def across_other_col(value):
+    pairs = [(2 * a + c, 2 * b + 1 - c) for a, b in ((1, 2), (2, 1)) for c in range(2)]
+    return lax.ppermute(value, ("row", "col"), pairs)
+
+
 def rows_dot(left, right):
     return lax.dot_general(left, right, (((1,), (1,)), ((), ())), preferred_element_type=F32)
 
@@ -128,8 +133,10 @@
     early_sum = early.astype(F32) + other_col(early).astype(F32)
 
     last = after(cot_other_end[1], early)
-    late = col_sum(grad[3 * rows :] + rows_dot(last, up_mine[:, cuts[1]]))
-    values = jnp.concatenate([early_rows(1), last], axis=0)
+    late = (grad[3 * rows :] + rows_dot(last, up_mine[:, cuts[1]])).astype(BF16)
+    straight = across(jnp.concatenate([early_sum[2 * rows :].astype(BF16), late], axis=0))
+    crossed = across_other_col(late)
+    values = jnp.concatenate([early_rows(1), after(last, late)], axis=0)
     up_second = tokens_dot(normed_all, values).astype(BF16)
     back_second = outward(up_second[lat:])
     up_grad = jnp.concatenate(
@@ -140,30 +147,33 @@
         axis=1,
     )
 
-    grad_sent = jnp.concatenate([early_sum[2 * rows :], late], axis=0).astype(BF16)
-    from_across = across(after(grad_sent, up_second, back_first))
-    normed_grad = jnp.concatenate([early_sum[: 2 * rows], from_across.astype(F32)], axis=1)
+    straight = after(straight, up_second, back_first).astype(F32)
+    from_across = jnp.concatenate(
+        [straight[:rows], straight[rows:] + crossed.astype(F32)], axis=0
+    )
+    normed_grad = jnp.concatenate([early_sum[: 2 * rows], from_across], axis=1)
     inner = jnp.mean(normed_grad * normed, axis=-1, keepdims=True)
     latent_bf = (inv_rms * (normed_grad - normed * inner)).astype(BF16)
     latent_there = outward(latent_bf[rows:])
     latent_used = jnp.where(middle, latent_bf[:rows], latent_there)
 
     sums = [
-        tokens_dot(latent_bf[:, j * lat : (j + 1) * lat], tokens_mine) for j in range(4)
+        tokens_dot(latent_bf[:, j * lat : (j + 1) * lat], tokens_mine).astype(BF16)
+        for j in range(4)
     ]
     width = tokens.shape[1] // 2
     halves = (slice(0, width), slice(width, 2 * width))
-    sent_end, sent_own = sums[3].astype(BF16), sums[2].astype(BF16)
+    sent_end, sent_own = sums[3], sums[2]
     from_end = [across(sent_end[:, half]) for half in halves]
     from_own = across(after(sent_own, from_end[0]))
     end_first = (sums[1][:, halves[0]] + from_end[0].astype(F32)).astype(BF16)
     end_second = sums[1][:, halves[1]] + after(from_end[1], end_first).astype(F32)
     down_end_grad = jnp.concatenate([outward(end_first), outward(end_second.astype(BF16))], axis=1)
-    down_own_grad = (sums[0] + from_own.astype(F32)).astype(BF16)
-    down_grad = jnp.where(middle, down_own_grad, down_end_grad)
 
     input_grad = jnp.dot(latent_used, down_used, preferred_element_type=F32).astype(BF16)
     passed = shifted(input_grad, "section", -1)
+    down_own_grad = (sums[0] + after(from_own, passed).astype(F32)).astype(BF16)
+    down_grad = jnp.where(middle, down_own_grad, down_end_grad)
     return (passed[None], down_grad[None], up_grad[None])
 
 

time: 163 us -> 164 us (level)
  waiting for transfers between devices: 93.2 us -> 95.6 us
    ppermute x1, waiting for transfers between devices: 0.01 us -> 6.93 us  [shifted(): lax.ppermute(value, axis, [(source, source + steps) for source in range(l...]
    ppermute x8, waiting for transfers between devices: 39.5 us -> 35.5 us  [outward(): return lax.ppermute(value, 'row', [(1, 0), (2, 3)])]
    ppermute x3 -> x2, starting transfers between devices: 4.62 us -> 3.06 us  [other_col(): return lax.ppermute(value, 'col', [(0, 1), (1, 0)])]
    ppermute x3 -> x2, waiting for transfers between devices: 5.62 us -> 5.05 us  [other_col(): return lax.ppermute(value, 'col', [(0, 1), (1, 0)])]
  transfers between devices with their start and end apart: 27 -> 27, of which waited for: 13 -> 13; matrix products, arithmetic and copies ran while one was open for 12% -> 11% of each run, Pallas kernels for 0% -> 0%
where the time goes in v7:
time: 164 us; the launch traced here: 162 us
  waiting for transfers between devices  95.6 us (58%)
  starting transfers between devices  44.9 us (27%)
  matrix products  12.4 us (8%)
  local copies, waits for them, and re-layouts  4.91 us (3%)
  other arithmetic  3.12 us (2%)
    ppermute x5, waiting for transfers between devices, inward(): return lax.ppermute(value, 'row', [(0, 1), (3, 2)])  48.1 us
    ppermute x8, waiting for transfers between devices, outward(): return lax.ppermute(value, 'row', [(1, 0), (2, 3)])  35.5 us
    ppermute x5, starting transfers between devices, inward(): return lax.ppermute(value, 'row', [(0, 1), (3, 2)])  22 us
    ppermute x8, starting transfers between devices, outward(): return lax.ppermute(value, 'row', [(1, 0), (2, 3)])  10.3 us
    ppermute x10, starting transfers between devices, across(): return lax.ppermute(value, 'row', [(1, 2), (2, 1)])  6.96 us
    ppermute x1, waiting for transfers between devices, shifted(): lax.ppermute(value, axis, [(source, source + steps) for source in range(l...  6.93 us
    dot_general x6, matrix products, tokens_dot(): lax.dot_general(left, right, (((0,), (0,)), ((), ())), preferred_element_...  6.76 us
    ppermute x2, waiting for transfers between devices, other_col(): return lax.ppermute(value, 'col', [(0, 1), (1, 0)])  5.05 us
  transfers between devices with their start and end apart: 27, of which 13 were waited for; matrix products, arithmetic and copies ran while one was open for 11% of the time, Pallas kernels for 0%

profile of v7, /device:TPU:4, one launch (start us, length us, event | category | flops | bytes accessed | tf_op | source)
XLA Modules:
  0.0 162.2 jit_solution(4441818679945079425)
XLA Ops:
  0.7 3.7 %collective-permute-start.2 = (bf16[128,2560]{1,0:T(8,128)(2,1)}, bf16[128,2560]{1,0:T(8,128)(2,1)S(1)}, u32[]{:S(2)}, u32[]{:S(2)}) collective-permute-start(bf16[128,2560]{1,0:T(8,128)(2,1)} %bitcast.19), channel_id=1, source_target_pairs={{0,2},{6,4},{1,3},{7,5},{8,10},{14,12},{9,11},{15,13},{16,18},{22,... | collective-permute-start | bytes 1966088 | tf_op jit(solution)/shard_map/ppermute | solution.py:48
  4.3 1.4 collective-permute-start
  5.7 1.3 collective-permute-start.1
  7.0 0.7 collective-permute-start.3
  7.7 12.0 %collective-permute-done.2 = bf16[128,2560]{1,0:T(8,128)(2,1)S(1)} collective-permute-done((bf16[128,2560]{1,0:T(8,128)(2,1)}, bf16[128,2560]{1,0:T(8,128)(2,1)S(1)}, u32[]{:S(2)}, u32[]{:S(2)}) %collective-permute-start.2) | collective-permute-done | bytes 655392 | tf_op jit(solution)/shard_map/ppermute | solution.py:48
  19.7 0.7 collective-permute-start.4
  20.4 0.8 collective-permute-start.7
  21.2 2.7 %fusion.44 = (bf16[192,2048]{1,0:T(8,128)(2,1)}, bf16[192,2048]{1,0:T(8,128)(2,1)}) fusion(bf16[192,4096]{1,0:T(8,128)(2,1)} %bitcast.13), kind=kLoop, calls=%fused_computation.72 | loop fusion | bytes 3145728 | tf_op jit(solution)/shard_map/slice | solution.py:124
  23.9 0.1 collective-permute-done.1
  24.0 9.5 %collective-permute-start.6 = (bf16[192,2048]{1,0:T(8,128)(2,1)}, bf16[192,2048]{1,0:T(8,128)(2,1)}, u32[]{:S(2)}, u32[]{:S(2)}) collective-permute-start(bf16[192,2048]{1,0:T(8,128)(2,1)} %get-tuple-element.32), channel_id=1, source_target_pairs={{0,2},{6,4},{1,3},{7,5},{8,10},{14,12},{9,11},{15,13},{16,18},{22,... | collective-permute-start | bytes 2359304 | tf_op jit(solution)/shard_map/ppermute | solution.py:48
  33.4 7.3 %collective-permute-done = bf16[192,2560]{1,0:T(8,128)(2,1)S(1)} collective-permute-done((bf16[192,2560]{1,0:T(8,128)(2,1)}, bf16[192,2560]{1,0:T(8,128)(2,1)S(1)}, u32[]{:S(2)}, u32[]{:S(2)}) %collective-permute-start) | collective-permute-done | bytes 983072 | tf_op jit(solution)/shard_map/ppermute | solution.py:48
  40.8 1.2 convolution_convert_fusion.6
  42.2 1.5 collective-permute-start.5
  43.7 4.6 %collective-permute-start.13 = (bf16[192,2048]{1,0:T(8,128)(2,1)}, bf16[192,2048]{1,0:T(8,128)(2,1)S(1)}, u32[]{:S(2)}, u32[]{:S(2)}) collective-permute-start(bf16[192,2048]{1,0:T(8,128)(2,1)} %get-tuple-element.21), channel_id=1, source_target_pairs={{0,2},{6,4},{1,3},{7,5},{8,10},{14,12},{9,11},{15,13},{16,18},{22,... | collective-permute-start | bytes 2359304 | tf_op jit(solution)/shard_map/ppermute | solution.py:48
  48.3 1.3 collective-permute-start.10
  49.6 8.1 %collective-permute-done.6 = bf16[192,2048]{1,0:T(8,128)(2,1)} collective-permute-done((bf16[192,2048]{1,0:T(8,128)(2,1)}, bf16[192,2048]{1,0:T(8,128)(2,1)}, u32[]{:S(2)}, u32[]{:S(2)}) %collective-permute-start.6) | collective-permute-done | bytes 786464 | tf_op jit(solution)/shard_map/ppermute | solution.py:48
  57.6 0.7 collective-permute-start.8
  58.3 1.3 collective-permute-start.12
  59.6 0.2 multiply_reduce_fusion.1
  59.9 0.1 fusion.24
  60.0 4.4 %collective-permute-done.10 = bf16[128,2560]{1,0:T(8,128)(2,1)S(1)} collective-permute-done((bf16[128,2560]{1,0:T(8,128)(2,1)}, bf16[128,2560]{1,0:T(8,128)(2,1)S(1)}, u32[]{:S(2)}, u32[]{:S(2)}) %collective-permute-start.10) | collective-permute-done | bytes 655392 | tf_op jit(solution)/shard_map/ppermute | solution.py:56
  64.4 2.9 %collective-permute-start.9 = (bf16[128,4096]{1,0:T(8,128)(2,1)S(1)}, bf16[128,4096]{1,0:T(8,128)(2,1)S(1)}, u32[]{:S(2)}, u32[]{:S(2)}) collective-permute-start(bf16[128,4096]{1,0:T(8,128)(2,1)S(1)} %bitcast.14), channel_id=1, source_target_pairs={{0,2},{6,4},{1,3},{7,5},{8,10},{14,12},{9,11},{15,13},{16,18},{22,... | collective-permute-start | bytes 3145736 | tf_op jit(solution)/shard_map/ppermute | solution.py:48
  67.3 0.7 collective-permute-start.11
  68.0 0.1 fusion.43
  68.1 6.3 %collective-permute-done.13 = bf16[192,2048]{1,0:T(8,128)(2,1)S(1)} collective-permute-done((bf16[192,2048]{1,0:T(8,128)(2,1)}, bf16[192,2048]{1,0:T(8,128)(2,1)S(1)}, u32[]{:S(2)}, u32[]{:S(2)}) %collective-permute-start.13) | collective-permute-done | bytes 786464 | tf_op jit(solution)/shard_map/ppermute | solution.py:48
  74.5 0.7 collective-permute-start.15
  75.2 2.8 %collective-permute-done.12 = bf16[128,2560]{1,0:T(8,128)(2,1)S(1)} collective-permute-done((bf16[128,2560]{1,0:T(8,128)(2,1)}, bf16[128,2560]{1,0:T(8,128)(2,1)S(1)}, u32[]{:S(2)}, u32[]{:S(2)}) %collective-permute-start.12) | collective-permute-done | bytes 655392 | tf_op jit(solution)/shard_map/ppermute | solution.py:56
  78.1 2.5 %convolution_convert_fusion.5 = bf16[256,2048]{1,0:T(8,128)(2,1)S(1)} fusion(bf16[768,256]{1,0:T(8,128)(2,1)S(1)} %pad_maximum_fusion.7, bf16[192,2048]{1,0:T(8,128)(2,1)S(1)} %collective-permute-done.8, bf16[192,2048]{1,0:T(8,128)(2,1)S(1)} %get-tuple-element.30, bf16[192,2048]{1,0:T(8,128)(2,1)} %collective-permute-done.6, ...), kind=kOutput, calls=%fused_computation.18 | convolution fusion | flops 818413568 | bytes 4587520 | tf_op jit(solution)/shard_map/dot_general | solution.py:77
  80.7 0.7 maximum_select_fusion
  81.4 14.3 %collective-permute-done.9 = bf16[128,4096]{1,0:T(8,128)(2,1)S(1)} collective-permute-done((bf16[128,4096]{1,0:T(8,128)(2,1)S(1)}, bf16[128,4096]{1,0:T(8,128)(2,1)S(1)}, u32[]{:S(2)}, u32[]{:S(2)}) %collective-permute-start.9) | collective-permute-done | bytes 1048608 | tf_op jit(solution)/shard_map/ppermute | solution.py:48
  95.7 2.4 %fusion.19 = f32[768,256]{1,0:T(8,128)S(1)} fusion(bf16[128,4096]{1,0:T(8,128)(2,1)S(1)} %bitcast.15, bf16[128,4096]{1,0:T(8,128)(2,1)S(1)} %collective-permute-done.9, bf16[192,2048]{1,0:T(8,128)(2,1)S(1)} %collective-permute-done.8, bf16[192,2048]{1,0:T(8,128)(2,1)S(1)} %get-tuple-element.30, bf16[192,2048]{1,0:T(8,128)(2,1)} %collective-permute-done.6, ...), kind=kOutput, calls=%fused_computation.31 | convolution fusion | flops 819986432 | bytes 6029312 | tf_op jit(solution)/shard_map/dot_general | solution.py:73
  98.1 0.9 fusion.25
  99.0 1.6 collective-permute-start.14
  100.6 1.3 collective-permute-start.17
  101.9 5.0 %collective-permute-done.14 = bf16[576,256]{1,0:T(8,128)(2,1)S(1)} collective-permute-done((bf16[576,256]{1,0:T(8,128)(2,1)S(1)}, bf16[576,256]{1,0:T(8,128)(2,1)S(1)}, u32[]{:S(2)}, u32[]{:S(2)}) %collective-permute-start.14) | collective-permute-done | bytes 294944 | tf_op jit(solution)/shard_map/ppermute | solution.py:60
  107.1 0.5 fusion.26
  107.6 0.7 collective-permute-start.18
  108.3 0.7 collective-permute-start.16
  109.0 1.2 fusion.9
  110.2 1.3 collective-permute-start.26
  111.5 4.8 %collective-permute-done.17 = bf16[128,2048]{1,0:T(8,128)(2,1)S(1)} collective-permute-done((bf16[128,2048]{1,0:T(8,128)(2,1)S(1)}, bf16[128,2048]{1,0:T(8,128)(2,1)S(1)}, u32[]{:S(2)}, u32[]{:S(2)}) %collective-permute-start.17) | collective-permute-done | bytes 524320 | tf_op jit(solution)/shard_map/ppermute | solution.py:56
  116.5 0.3 multiply_reduce_fusion
  116.8 0.2 multiply_convert_fusion
  117.1 0.5 copy-done.13
  117.6 0.3 copy-done.15
  117.9 0.5 convolution_convert_fusion.3
  118.4 0.5 convolution_convert_fusion.2
  119.0 1.3 collective-permute-start.19
  120.3 0.7 collective-permute-start.21
  121.0 0.5 convolution_convert_fusion.1
  121.5 0.7 collective-permute-start.24
  122.2 15.1 %collective-permute-done.19 = bf16[192,512]{1,0:T(8,128)(2,1)S(1)} collective-permute-done((bf16[192,512]{1,0:T(8,128)(2,1)S(1)}, bf16[192,512]{1,0:T(8,128)(2,1)S(1)}, u32[]{:S(2)}, u32[]{:S(2)}) %collective-permute-start.19) | collective-permute-done | bytes 196640 | tf_op jit(solution)/shard_map/ppermute | solution.py:56
  137.3 0.7 convolution_convert_fusion
  138.0 1.9 %collective-permute-start.20 = (bf16[192,2560]{1,0:T(8,128)(2,1)S(1)}, bf16[192,2560]{1,0:T(8,128)(2,1)S(1)}, u32[]{:S(2)}, u32[]{:S(2)}) collective-permute-start(bf16[192,2560]{1,0:T(8,128)(2,1)S(1)} %convolution_convert_fusion), channel_id=1, source_target_pairs={{8,0},{16,8},{24,16},{9,1},{17,9},{25,17},{10,2},{18,10},{26,18},{... | collective-permute-start | bytes 2949128 | tf_op jit(solution)/shard_map/ppermute | solution.py:13
  139.9 0.7 collective-permute-start.22
  140.7 0.1 add_convert_fusion.2
  140.7 1.3 collective-permute-start.23
  142.1 0.1 add_convert_fusion.1
  142.2 1.3 collective-permute-start.25
  143.5 1.1 maximum_bitcast_fusion
  144.6 6.9 %collective-permute-done.20 = bf16[192,2560]{1,0:T(8,128)(2,1)S(1)} collective-permute-done((bf16[192,2560]{1,0:T(8,128)(2,1)S(1)}, bf16[192,2560]{1,0:T(8,128)(2,1)S(1)}, u32[]{:S(2)}, u32[]{:S(2)}) %collective-permute-start.20) | collective-permute-done | bytes 983072 | tf_op jit(solution)/shard_map/ppermute | solution.py:13
  151.5 8.3 %collective-permute-done.25 = bf16[128,1280]{1,0:T(8,128)(2,1)S(1)} collective-permute-done((bf16[128,1280]{1,0:T(8,128)(2,1)S(1)}, bf16[128,1280]{1,0:T(8,128)(2,1)S(1)}, u32[]{:S(2)}, u32[]{:S(2)}) %collective-permute-start.25) | collective-permute-done | bytes 327712 | tf_op jit(solution)/shard_map/ppermute | solution.py:56
  159.8 1.4 fusion.23
  161.3 0.9 copy.8
  (61 shorter events, 0.7 us)
Async XLA Ops:
  0.6 40.2 %copy-start.2 = (bf16[1,128,2560]{2,1,0:T(8,128)(2,1)S(1)}, bf16[1,128,2560]{2,1,0:T(8,128)(2,1)}, u32[]{:S(2)}) copy-start(bf16[1,128,2560]{2,1,0:T(8,128)(2,1)} %param.5) | copy-start | bytes 1966084
  0.6 40.2 %copy-start.12 = (bf16[1,192,2560]{2,1,0:T(8,128)(2,1)S(1)}, bf16[1,192,2560]{2,1,0:T(8,128)(2,1)}, u32[]{:S(2)}) copy-start(bf16[1,192,2560]{2,1,0:T(8,128)(2,1)} %param.4) | copy-start | bytes 2949124
  0.7 19.1 %collective-permute-start.2 = (bf16[128,2560]{1,0:T(8,128)(2,1)}, bf16[128,2560]{1,0:T(8,128)(2,1)S(1)}, u32[]{:S(2)}, u32[]{:S(2)}) collective-permute-start(bf16[128,2560]{1,0:T(8,128)(2,1)} %bitcast.19), channel_id=1, source_target_pairs={{0,2},{6,4},{1,3},{7,5},{8,10},{14,12},{9,11},{15,13},{16,18},{22,... | collective-permute-start | bytes 1966088 | tf_op jit(solution)/shard_map/ppermute | solution.py:48
  4.3 36.5 %collective-permute-start = (bf16[192,2560]{1,0:T(8,128)(2,1)}, bf16[192,2560]{1,0:T(8,128)(2,1)S(1)}, u32[]{:S(2)}, u32[]{:S(2)}) collective-permute-start(bf16[192,2560]{1,0:T(8,128)(2,1)} %bitcast.24), channel_id=1, source_target_pairs={{0,2},{6,4},{1,3},{7,5},{8,10},{14,12},{9,11},{15,13},{16,18},{22,... | collective-permute-start | bytes 2949128 | tf_op jit(solution)/shard_map/ppermute | solution.py:48
  5.7 18.3 %collective-permute-start.1 = (bf16[128,2560]{1,0:T(8,128)(2,1)}, bf16[128,2560]{1,0:T(8,128)(2,1)S(1)}, u32[]{:S(2)}, u32[]{:S(2)}) collective-permute-start(bf16[128,2560]{1,0:T(8,128)(2,1)} %bitcast.20), channel_id=1, source_target_pairs={{2,0},{4,6},{3,1},{5,7},{10,8},{12,14},{11,9},{13,15},{18,16},{20,... | collective-permute-start | bytes 1966088 | tf_op jit(solution)/shard_map/ppermute | solution.py:56
  7.0 33.8 %collective-permute-start.3 = (bf16[128,2560]{1,0:T(8,128)(2,1)}, bf16[128,2560]{1,0:T(8,128)(2,1)S(1)}, u32[]{:S(2)}, u32[]{:S(2)}) collective-permute-start(bf16[128,2560]{1,0:T(8,128)(2,1)} %bitcast.21), channel_id=1, source_target_pairs={{2,4},{4,2},{3,5},{5,3},{10,12},{12,10},{11,13},{13,11},{18,20},{2... | collective-permute-start | bytes 1966088 | tf_op jit(solution)/shard_map/ppermute | solution.py:52
  19.7 22.3 %copy-start.4 = (bf16[128,2560]{1,0:T(8,128)(2,1)}, bf16[128,2560]{1,0:T(8,128)(2,1)S(1)}, u32[]{:S(2)}) copy-start(bf16[128,2560]{1,0:T(8,128)(2,1)S(1)} %collective-permute-done.2) | copy-start | bytes 1966084
  19.7 21.1 %collective-permute-start.4 = (bf16[128,2560]{1,0:T(8,128)(2,1)S(1)}, bf16[128,2560]{1,0:T(8,128)(2,1)S(1)}, u32[]{:S(2)}, u32[]{:S(2)}) collective-permute-start(bf16[128,2560]{1,0:T(8,128)(2,1)S(1)} %collective-permute-done.2), channel_id=1, source_target_pairs={{2,4},{4,2},{3,5},{5,3},{10,12},{12,10},{11,13},{13,11},{18,20},{2... | collective-permute-start | bytes 1966088 | tf_op jit(solution)/shard_map/ppermute | solution.py:52
  20.4 46.9 %collective-permute-start.7 = (bf16[192,4096]{1,0:T(8,128)(2,1)}, bf16[192,4096]{1,0:T(8,128)(2,1)S(1)}, u32[]{:S(2)}, u32[]{:S(2)}) collective-permute-start(bf16[192,4096]{1,0:T(8,128)(2,1)} %bitcast.12), channel_id=1, source_target_pairs={{2,4},{4,2},{3,5},{5,3},{10,12},{12,10},{11,13},{13,11},{18,20},{2... | collective-permute-start | bytes 4718600 | tf_op jit(solution)/shard_map/ppermute | solution.py:52
  24.0 16.8 %copy-start.6 = (bf16[128,2560]{1,0:T(8,128)(2,1)}, bf16[128,2560]{1,0:T(8,128)(2,1)S(1)}, u32[]{:S(2)}) copy-start(bf16[128,2560]{1,0:T(8,128)(2,1)S(1)} %collective-permute-done.1) | copy-start | bytes 1966084
  24.0 33.6 %collective-permute-start.6 = (bf16[192,2048]{1,0:T(8,128)(2,1)}, bf16[192,2048]{1,0:T(8,128)(2,1)}, u32[]{:S(2)}, u32[]{:S(2)}) collective-permute-start(bf16[192,2048]{1,0:T(8,128)(2,1)} %get-tuple-element.32), channel_id=1, source_target_pairs={{0,2},{6,4},{1,3},{7,5},{8,10},{14,12},{9,11},{15,13},{16,18},{22,... | collective-permute-start | bytes 2359304 | tf_op jit(solution)/shard_map/ppermute | solution.py:48
  40.8 1.3 copy-start.14
  40.8 1.3 copy-start.8
  40.8 1.3 copy-start.10
  42.2 22.3 %copy-start = (bf16[1,128,4096]{2,1,0:T(8,128)(2,1)S(1)}, bf16[1,128,4096]{2,1,0:T(8,128)(2,1)}, u32[]{:S(2)}) copy-start(bf16[1,128,4096]{2,1,0:T(8,128)(2,1)} %param.6) | copy-start | bytes 3145732
  42.2 16.2 %collective-permute-start.5 = (bf16[384,512]{1,0:T(8,128)(2,1)S(1)}, bf16[384,512]{1,0:T(8,128)(2,1)S(1)}, u32[]{:S(2)}, u32[]{:S(2)}) collective-permute-start(bf16[384,512]{1,0:T(8,128)(2,1)S(1)} %convolution_convert_fusion.6), channel_id=1, source_target_pairs={{0,1},{1,0},{2,3},{3,2},{4,5},{5,4},{6,7},{7,6},{8,9},{9,8},{10,11... | collective-permute-start | bytes 1179656 | tf_op jit(solution)/shard_map/ppermute | solution.py:60
  43.7 30.8 %collective-permute-start.13 = (bf16[192,2048]{1,0:T(8,128)(2,1)}, bf16[192,2048]{1,0:T(8,128)(2,1)S(1)}, u32[]{:S(2)}, u32[]{:S(2)}) collective-permute-start(bf16[192,2048]{1,0:T(8,128)(2,1)} %get-tuple-element.21), channel_id=1, source_target_pairs={{0,2},{6,4},{1,3},{7,5},{8,10},{14,12},{9,11},{15,13},{16,18},{22,... | collective-permute-start | bytes 2359304 | tf_op jit(solution)/shard_map/ppermute | solution.py:48
  48.3 16.2 %collective-permute-start.10 = (bf16[128,2560]{1,0:T(8,128)(2,1)}, bf16[128,2560]{1,0:T(8,128)(2,1)S(1)}, u32[]{:S(2)}, u32[]{:S(2)}) collective-permute-start(bf16[128,2560]{1,0:T(8,128)(2,1)} %copy-done.8), channel_id=1, source_target_pairs={{2,0},{4,6},{3,1},{5,7},{10,8},{12,14},{11,9},{13,15},{18,16},{20,... | collective-permute-start | bytes 1966088 | tf_op jit(solution)/shard_map/ppermute | solution.py:56
  57.6 20.4 %collective-permute-start.8 = (bf16[192,2048]{1,0:T(8,128)(2,1)}, bf16[192,2048]{1,0:T(8,128)(2,1)S(1)}, u32[]{:S(2)}, u32[]{:S(2)}) collective-permute-start(bf16[192,2048]{1,0:T(8,128)(2,1)} %collective-permute-done.6), channel_id=1, source_target_pairs={{2,4},{4,2},{3,5},{5,3},{10,12},{12,10},{11,13},{13,11},{18,20},{2... | collective-permute-start | bytes 2359304 | tf_op jit(solution)/shard_map/ppermute | solution.py:52
  58.3 19.7 %collective-permute-start.12 = (bf16[128,2560]{1,0:T(8,128)(2,1)}, bf16[128,2560]{1,0:T(8,128)(2,1)S(1)}, u32[]{:S(2)}, u32[]{:S(2)}) collective-permute-start(bf16[128,2560]{1,0:T(8,128)(2,1)} %copy-done.10), channel_id=1, source_target_pairs={{2,0},{4,6},{3,1},{5,7},{10,8},{12,14},{11,9},{13,15},{18,16},{20,... | collective-permute-start | bytes 1966088 | tf_op jit(solution)/shard_map/ppermute | solution.py:56
  64.4 31.3 %collective-permute-start.9 = (bf16[128,4096]{1,0:T(8,128)(2,1)S(1)}, bf16[128,4096]{1,0:T(8,128)(2,1)S(1)}, u32[]{:S(2)}, u32[]{:S(2)}) collective-permute-start(bf16[128,4096]{1,0:T(8,128)(2,1)S(1)} %bitcast.14), channel_id=1, source_target_pairs={{0,2},{6,4},{1,3},{7,5},{8,10},{14,12},{9,11},{15,13},{16,18},{22,... | collective-permute-start | bytes 3145736 | tf_op jit(solution)/shard_map/ppermute | solution.py:48
  67.3 7.8 %collective-permute-start.11 = (bf16[384,256]{1,0:T(8,128)(2,1)S(1)}, bf16[384,256]{1,0:T(8,128)(2,1)S(1)}, u32[]{:S(2)}, u32[]{:S(2)}) collective-permute-start(bf16[384,256]{1,0:T(8,128)(2,1)S(1)} %get-tuple-element.18), channel_id=1, source_target_pairs={{2,4},{4,2},{3,5},{5,3},{10,12},{12,10},{11,13},{13,11},{18,20},{2... | collective-permute-start | bytes 589832 | tf_op jit(solution)/shard_map/ppermute | solution.py:52
  74.5 32.6 %collective-permute-start.15 = (bf16[192,2048]{1,0:T(8,128)(2,1)S(1)}, bf16[192,2048]{1,0:T(8,128)(2,1)S(1)}, u32[]{:S(2)}, u32[]{:S(2)}) collective-permute-start(bf16[192,2048]{1,0:T(8,128)(2,1)S(1)} %collective-permute-done.13), channel_id=1, source_target_pairs={{2,4},{4,2},{3,5},{5,3},{10,12},{12,10},{11,13},{13,11},{18,20},{2... | collective-permute-start | bytes 2359304 | tf_op jit(solution)/shard_map/ppermute | solution.py:52
  78.0 2.6 %copy-start.3 = (bf16[1,128,2560]{2,1,0:T(8,128)(2,1)S(1)}, bf16[1,128,2560]{2,1,0:T(8,128)(2,1)}, u32[]{:S(2)}) copy-start(bf16[1,128,2560]{2,1,0:T(8,128)(2,1)} %param.5) | copy-start | bytes 1966084
  78.0 2.6 %copy-start.5 = (bf16[128,2560]{1,0:T(8,128)(2,1)S(1)}, bf16[128,2560]{1,0:T(8,128)(2,1)}, u32[]{:S(2)}) copy-start(bf16[128,2560]{1,0:T(8,128)(2,1)} %copy-done.4) | copy-start | bytes 1966084
  78.0 2.6 %copy-start.7 = (bf16[128,2560]{1,0:T(8,128)(2,1)S(1)}, bf16[128,2560]{1,0:T(8,128)(2,1)}, u32[]{:S(2)}) copy-start(bf16[128,2560]{1,0:T(8,128)(2,1)} %copy-done.6) | copy-start | bytes 1966084
  78.0 2.6 %copy-start.9 = (bf16[128,2560]{1,0:T(8,128)(2,1)S(1)}, bf16[128,2560]{1,0:T(8,128)(2,1)}, u32[]{:S(2)}) copy-start(bf16[128,2560]{1,0:T(8,128)(2,1)} %copy-done.8) | copy-start | bytes 1966084
  78.1 2.6 %copy-start.11 = (bf16[128,2560]{1,0:T(8,128)(2,1)S(1)}, bf16[128,2560]{1,0:T(8,128)(2,1)}, u32[]{:S(2)}) copy-start(bf16[128,2560]{1,0:T(8,128)(2,1)} %copy-done.10) | copy-start | bytes 1966084
  81.4 16.7 %copy-start.1 = (bf16[192,2048]{1,0:T(8,128)(2,1)S(1)}, bf16[192,2048]{1,0:T(8,128)(2,1)}, u32[]{:S(2)}) copy-start(bf16[192,2048]{1,0:T(8,128)(2,1)} %get-tuple-element.21) | copy-start | bytes 2359300
  99.0 7.9 %collective-permute-start.14 = (bf16[576,256]{1,0:T(8,128)(2,1)S(1)}, bf16[576,256]{1,0:T(8,128)(2,1)S(1)}, u32[]{:S(2)}, u32[]{:S(2)}) collective-permute-start(bf16[576,256]{1,0:T(8,128)(2,1)S(1)} %fusion.25), channel_id=1, source_target_pairs={{0,1},{1,0},{2,3},{3,2},{4,5},{5,4},{6,7},{7,6},{8,9},{9,8},{10,11... | collective-permute-start | bytes 884744 | tf_op jit(solution)/shard_map/ppermute | solution.py:60
  100.6 15.7 %collective-permute-start.17 = (bf16[128,2048]{1,0:T(8,128)(2,1)S(1)}, bf16[128,2048]{1,0:T(8,128)(2,1)S(1)}, u32[]{:S(2)}, u32[]{:S(2)}) collective-permute-start(bf16[128,2048]{1,0:T(8,128)(2,1)S(1)} %slice.130), channel_id=1, source_target_pairs={{2,0},{4,6},{3,1},{5,7},{10,8},{12,14},{11,9},{13,15},{18,16},{20,... | collective-permute-start | bytes 1572872 | tf_op jit(solution)/shard_map/ppermute | solution.py:56
  107.6 8.9 %collective-permute-start.18 = (bf16[192,256]{1,0:T(8,128)(2,1)S(1)}, bf16[192,256]{1,0:T(8,128)(2,1)S(1)}, u32[]{:S(2)}, u32[]{:S(2)}) collective-permute-start(bf16[192,256]{1,0:T(8,128)(2,1)S(1)} %fusion.26), channel_id=1, source_target_pairs={{2,5},{3,4},{4,3},{5,2},{10,13},{11,12},{12,11},{13,10},{18,21},{1... | collective-permute-start | bytes 294920 | tf_op jit(solution)/shard_map/ppermute | solution.py:69
  108.3 8.1 %collective-permute-start.16 = (bf16[384,256]{1,0:T(8,128)(2,1)S(1)}, bf16[384,256]{1,0:T(8,128)(2,1)S(1)}, u32[]{:S(2)}, u32[]{:S(2)}) collective-permute-start(bf16[384,256]{1,0:T(8,128)(2,1)S(1)} %pad_maximum_fusion.8), channel_id=1, source_target_pairs={{2,4},{4,2},{3,5},{5,3},{10,12},{12,10},{11,13},{13,11},{18,20},{2... | collective-permute-start | bytes 589832 | tf_op jit(solution)/shard_map/ppermute | solution.py:52
  110.2 33.2 %collective-permute-start.26 = (bf16[128,2048]{1,0:T(8,128)(2,1)S(1)}, bf16[128,2048]{1,0:T(8,128)(2,1)S(1)}, u32[]{:S(2)}, u32[]{:S(2)}) collective-permute-start(bf16[128,2048]{1,0:T(8,128)(2,1)S(1)} %slice.145), channel_id=1, source_target_pairs={{2,0},{4,6},{3,1},{5,7},{10,8},{12,14},{11,9},{13,15},{18,16},{20,... | collective-permute-start | bytes 1572872 | tf_op jit(solution)/shard_map/ppermute | solution.py:56
  116.4 1.2 copy-start.13
  116.4 1.5 copy-start.15
  119.0 18.3 %collective-permute-start.19 = (bf16[192,512]{1,0:T(8,128)(2,1)S(1)}, bf16[192,512]{1,0:T(8,128)(2,1)S(1)}, u32[]{:S(2)}, u32[]{:S(2)}) collective-permute-start(bf16[192,512]{1,0:T(8,128)(2,1)S(1)} %slice.134), channel_id=1, source_target_pairs={{2,0},{4,6},{3,1},{5,7},{10,8},{12,14},{11,9},{13,15},{18,16},{20,... | collective-permute-start | bytes 589832 | tf_op jit(solution)/shard_map/ppermute | solution.py:56
  120.3 19.6 %collective-permute-start.21 = (bf16[128,1280]{1,0:T(8,128)(2,1)S(1)}, bf16[128,1280]{1,0:T(8,128)(2,1)S(1)}, u32[]{:S(2)}, u32[]{:S(2)}) collective-permute-start(bf16[128,1280]{1,0:T(8,128)(2,1)S(1)} %get-tuple-element.34), channel_id=1, source_target_pairs={{2,4},{4,2},{3,5},{5,3},{10,12},{12,10},{11,13},{13,11},{18,20},{2... | collective-permute-start | bytes 983048 | tf_op jit(solution)/shard_map/ppermute | solution.py:52
  121.5 20.5 %collective-permute-start.24 = (bf16[128,1280]{1,0:T(8,128)(2,1)S(1)}, bf16[128,1280]{1,0:T(8,128)(2,1)S(1)}, u32[]{:S(2)}, u32[]{:S(2)}) collective-permute-start(bf16[128,1280]{1,0:T(8,128)(2,1)S(1)} %get-tuple-element.33), channel_id=1, source_target_pairs={{2,4},{4,2},{3,5},{5,3},{10,12},{12,10},{11,13},{13,11},{18,20},{2... | collective-permute-start | bytes 983048 | tf_op jit(solution)/shard_map/ppermute | solution.py:52
  138.0 13.5 %collective-permute-start.20 = (bf16[192,2560]{1,0:T(8,128)(2,1)S(1)}, bf16[192,2560]{1,0:T(8,128)(2,1)S(1)}, u32[]{:S(2)}, u32[]{:S(2)}) collective-permute-start(bf16[192,2560]{1,0:T(8,128)(2,1)S(1)} %convolution_convert_fusion), channel_id=1, source_target_pairs={{8,0},{16,8},{24,16},{9,1},{17,9},{25,17},{10,2},{18,10},{26,18},{... | collective-permute-start | bytes 2949128 | tf_op jit(solution)/shard_map/ppermute | solution.py:13
  139.9 11.6 %collective-permute-start.22 = (bf16[128,2560]{1,0:T(8,128)(2,1)S(1)}, bf16[128,2560]{1,0:T(8,128)(2,1)S(1)}, u32[]{:S(2)}, u32[]{:S(2)}) collective-permute-start(bf16[128,2560]{1,0:T(8,128)(2,1)S(1)} %convolution_convert_fusion.3), channel_id=1, source_target_pairs={{2,4},{4,2},{3,5},{5,3},{10,12},{12,10},{11,13},{13,11},{18,20},{2... | collective-permute-start | bytes 1966088 | tf_op jit(solution)/shard_map/ppermute | solution.py:52
  140.7 19.1 %collective-permute-start.23 = (bf16[128,1280]{1,0:T(8,128)(2,1)S(1)}, bf16[128,1280]{1,0:T(8,128)(2,1)S(1)}, u32[]{:S(2)}, u32[]{:S(2)}) collective-permute-start(bf16[128,1280]{1,0:T(8,128)(2,1)S(1)} %add_convert_fusion.2), channel_id=1, source_target_pairs={{2,0},{4,6},{3,1},{5,7},{10,8},{12,14},{11,9},{13,15},{18,16},{20,... | collective-permute-start | bytes 983048 | tf_op jit(solution)/shard_map/ppermute | solution.py:56
  142.2 17.7 %collective-permute-start.25 = (bf16[128,1280]{1,0:T(8,128)(2,1)S(1)}, bf16[128,1280]{1,0:T(8,128)(2,1)S(1)}, u32[]{:S(2)}, u32[]{:S(2)}) collective-permute-start(bf16[128,1280]{1,0:T(8,128)(2,1)S(1)} %add_convert_fusion.1), channel_id=1, source_target_pairs={{2,0},{4,6},{3,1},{5,7},{10,8},{12,14},{11,9},{13,15},{18,16},{20,... | collective-permute-start | bytes 983048 | tf_op jit(solution)/shard_map/ppermute | solution.py:56

commit v8 on v5

--- a/solution.py
+++ b/solution.py
@@ -145,16 +145,17 @@
     normed_grad = jnp.concatenate([early_sum[: 2 * rows], from_across.astype(F32)], axis=1)
     inner = jnp.mean(normed_grad * normed, axis=-1, keepdims=True)
     latent_bf = (inv_rms * (normed_grad - normed * inner)).astype(BF16)
+    latent_there = outward(latent_bf[rows:])
+    latent_used = jnp.where(middle, latent_bf[:rows], latent_there)
 
     sums = [
-        tokens_dot(latent_bf[:, j * lat : (j + 1) * lat], tokens_mine) for j in range(4)
+        tokens_dot(latent_bf[:, j * lat : (j + 1) * lat], tokens_mine).astype(BF16)
+        for j in range(4)
     ]
     width = tokens.shape[1] // 2
     halves = (slice(0, width), slice(width, 2 * width))
-    sent_end, sent_own = sums[3].astype(BF16), sums[2].astype(BF16)
+    sent_end, sent_own = sums[3], sums[2]
     from_end = [across(sent_end[:, half]) for half in halves]
-    latent_there = outward(after(latent_bf[rows:], sent_end, sent_own))
-    latent_used = jnp.where(middle, latent_bf[:rows], latent_there)
     end_first = (sums[1][:, halves[0]] + from_end[0].astype(F32)).astype(BF16)
     from_own = across(after(sent_own, end_first))
     end_second = sums[1][:, halves[1]] + after(from_end[1], end_first).astype(F32)

time: 167 us -> 167 us (level)
  no operation moved by 1% of the time
where the time goes in v8:
time: 167 us; the launch traced here: 164 us
  waiting for transfers between devices  87.9 us (53%)
  starting transfers between devices  46 us (28%)
  matrix products  18.7 us (11%)
  other arithmetic  5.17 us (3%)
  local copies, waits for them, and re-layouts  4.89 us (3%)
    ppermute x5, waiting for transfers between devices, inward(): return lax.ppermute(value, 'row', [(0, 1), (3, 2)])  45.4 us
    ppermute x8, waiting for transfers between devices, outward(): return lax.ppermute(value, 'row', [(1, 0), (2, 3)])  31.4 us
    ppermute x5, starting transfers between devices, inward(): return lax.ppermute(value, 'row', [(0, 1), (3, 2)])  21.2 us
    ppermute x8, starting transfers between devices, outward(): return lax.ppermute(value, 'row', [(1, 0), (2, 3)])  10.5 us
    dot_general x4, matrix products, rows_dot(): lax.dot_general(left, right, (((1,), (1,)), ((), ())), preferred_element_...  9.07 us
    dot_general x6, matrix products, tokens_dot(): lax.dot_general(left, right, (((0,), (0,)), ((), ())), preferred_element_...  8.92 us
    ppermute x10, starting transfers between devices, across(): return lax.ppermute(value, 'row', [(1, 2), (2, 1)])  7.81 us
    ppermute x1, waiting for transfers between devices, shifted(): lax.ppermute(value, axis, [(source, source + steps) for source in range(l...  6.95 us
  transfers between devices with their start and end apart: 27, of which 13 were waited for; matrix products, arithmetic and copies ran while one was open for 16% of the time, Pallas kernels for 0%

profile of v8, /device:TPU:4, one launch (start us, length us, event | category | flops | bytes accessed | tf_op | source)
XLA Modules:
  0.0 163.9 jit_solution(17251911580725885593)
XLA Ops:
  0.7 3.7 %collective-permute-start.2 = (bf16[128,2560]{1,0:T(8,128)(2,1)}, bf16[128,2560]{1,0:T(8,128)(2,1)S(1)}, u32[]{:S(2)}, u32[]{:S(2)}) collective-permute-start(bf16[128,2560]{1,0:T(8,128)(2,1)} %bitcast.15), channel_id=1, source_target_pairs={{0,2},{6,4},{1,3},{7,5},{8,10},{14,12},{9,11},{15,13},{16,18},{22,... | collective-permute-start | bytes 1966088 | tf_op jit(solution)/shard_map/ppermute | solution.py:48
  4.3 1.4 collective-permute-start
  5.7 1.3 collective-permute-start.1
  7.0 0.7 collective-permute-start.3
  7.7 12.0 %collective-permute-done.2 = bf16[128,2560]{1,0:T(8,128)(2,1)S(1)} collective-permute-done((bf16[128,2560]{1,0:T(8,128)(2,1)}, bf16[128,2560]{1,0:T(8,128)(2,1)S(1)}, u32[]{:S(2)}, u32[]{:S(2)}) %collective-permute-start.2) | collective-permute-done | bytes 655392 | tf_op jit(solution)/shard_map/ppermute | solution.py:48
  19.7 0.7 collective-permute-start.4
  20.4 0.8 collective-permute-start.7
  21.2 2.4 %fusion.44 = (bf16[192,2048]{1,0:T(8,128)(2,1)S(1)}, bf16[192,2048]{1,0:T(8,128)(2,1)}) fusion(bf16[192,4096]{1,0:T(8,128)(2,1)} %bitcast.14), kind=kLoop, calls=%fused_computation.73 | loop fusion | bytes 3145728 | tf_op jit(solution)/shard_map/slice | solution.py:119
  23.6 0.4 collective-permute-done.1
  24.0 9.2 %collective-permute-start.6 = (bf16[192,2048]{1,0:T(8,128)(2,1)}, bf16[192,2048]{1,0:T(8,128)(2,1)}, u32[]{:S(2)}, u32[]{:S(2)}) collective-permute-start(bf16[192,2048]{1,0:T(8,128)(2,1)} %get-tuple-element.30), channel_id=1, source_target_pairs={{0,2},{6,4},{1,3},{7,5},{8,10},{14,12},{9,11},{15,13},{16,18},{22,... | collective-permute-start | bytes 2359304 | tf_op jit(solution)/shard_map/ppermute | solution.py:48
  33.2 7.6 %collective-permute-done = bf16[192,2560]{1,0:T(8,128)(2,1)S(1)} collective-permute-done((bf16[192,2560]{1,0:T(8,128)(2,1)}, bf16[192,2560]{1,0:T(8,128)(2,1)S(1)}, u32[]{:S(2)}, u32[]{:S(2)}) %collective-permute-start) | collective-permute-done | bytes 983072 | tf_op jit(solution)/shard_map/ppermute | solution.py:48
  40.8 1.2 convolution_convert_fusion.6
  42.2 1.5 collective-permute-start.5
  43.7 5.4 %collective-permute-start.13 = (bf16[192,2048]{1,0:T(8,128)(2,1)S(1)}, bf16[192,2048]{1,0:T(8,128)(2,1)}, u32[]{:S(2)}, u32[]{:S(2)}) collective-permute-start(bf16[192,2048]{1,0:T(8,128)(2,1)S(1)} %get-tuple-element.20), channel_id=1, source_target_pairs={{0,2},{6,4},{1,3},{7,5},{8,10},{14,12},{9,11},{15,13},{16,18},{22,... | collective-permute-start | bytes 2359304 | tf_op jit(solution)/shard_map/ppermute | solution.py:48
  49.1 1.3 collective-permute-start.10
  50.4 7.3 %collective-permute-done.6 = bf16[192,2048]{1,0:T(8,128)(2,1)} collective-permute-done((bf16[192,2048]{1,0:T(8,128)(2,1)}, bf16[192,2048]{1,0:T(8,128)(2,1)}, u32[]{:S(2)}, u32[]{:S(2)}) %collective-permute-start.6) | collective-permute-done | bytes 786464 | tf_op jit(solution)/shard_map/ppermute | solution.py:48
  57.6 0.7 collective-permute-start.8
  58.3 1.3 collective-permute-start.12
  59.6 0.2 multiply_reduce_fusion.1
  59.9 0.1 fusion.24
  60.1 6.0 %collective-permute-done.10 = bf16[128,2560]{1,0:T(8,128)(2,1)S(1)} collective-permute-done((bf16[128,2560]{1,0:T(8,128)(2,1)}, bf16[128,2560]{1,0:T(8,128)(2,1)S(1)}, u32[]{:S(2)}, u32[]{:S(2)}) %collective-permute-start.10) | collective-permute-done | bytes 655392 | tf_op jit(solution)/shard_map/ppermute | solution.py:56
  66.0 1.6 collective-permute-start.9
  67.7 0.7 collective-permute-start.11
  68.4 0.1 fusion.43
  68.5 5.9 %collective-permute-done.13 = bf16[192,2048]{1,0:T(8,128)(2,1)} collective-permute-done((bf16[192,2048]{1,0:T(8,128)(2,1)S(1)}, bf16[192,2048]{1,0:T(8,128)(2,1)}, u32[]{:S(2)}, u32[]{:S(2)}) %collective-permute-start.13) | collective-permute-done | bytes 786464 | tf_op jit(solution)/shard_map/ppermute | solution.py:48
  74.4 1.6 collective-permute-start.15
  76.0 2.9 %collective-permute-done.12 = bf16[128,2560]{1,0:T(8,128)(2,1)S(1)} collective-permute-done((bf16[128,2560]{1,0:T(8,128)(2,1)}, bf16[128,2560]{1,0:T(8,128)(2,1)S(1)}, u32[]{:S(2)}, u32[]{:S(2)}) %collective-permute-start.12) | collective-permute-done | bytes 655392 | tf_op jit(solution)/shard_map/ppermute | solution.py:56
  78.9 3.5 %convolution_convert_fusion.5 = bf16[256,2048]{1,0:T(8,128)(2,1)} fusion(bf16[768,256]{1,0:T(8,128)(2,1)S(1)} %pad_maximum_fusion.8, bf16[192,2048]{1,0:T(8,128)(2,1)S(1)} %collective-permute-done.8, bf16[192,2048]{1,0:T(8,128)(2,1)S(1)} %get-tuple-element.28, bf16[192,2048]{1,0:T(8,128)(2,1)} %collective-permute-done.6, ...), kind=kOutput, calls=%fused_computation.18 | convolution fusion | flops 818413568 | bytes 4587520 | tf_op jit(solution)/shard_map/dot_general | solution.py:72
  82.5 0.7 maximum_select_fusion
  83.2 12.6 %collective-permute-done.9 = bf16[128,4096]{1,0:T(8,128)(2,1)S(1)} collective-permute-done((bf16[128,4096]{1,0:T(8,128)(2,1)}, bf16[128,4096]{1,0:T(8,128)(2,1)S(1)}, u32[]{:S(2)}, u32[]{:S(2)}) %collective-permute-start.9) | collective-permute-done | bytes 1048608 | tf_op jit(solution)/shard_map/ppermute | solution.py:48
  95.8 2.9 %fusion.19 = f32[768,256]{1,0:T(8,128)S(1)} fusion(bf16[128,4096]{1,0:T(8,128)(2,1)} %bitcast.3, bf16[128,4096]{1,0:T(8,128)(2,1)S(1)} %collective-permute-done.9, bf16[192,2048]{1,0:T(8,128)(2,1)S(1)} %collective-permute-done.8, bf16[192,2048]{1,0:T(8,128)(2,1)S(1)} %get-tuple-element.28, bf16[192,2048]{1,0:T(8,128)(2,1)} %collective-permute-done.6, ...), kind=kOutput, calls=%fused_computation.31 | convolution fusion | flops 819986432 | bytes 6029312 | tf_op jit(solution)/shard_map/dot_general | solution.py:68
  98.8 3.1 %fusion.25 = bf16[576,256]{1,0:T(8,128)(2,1)} fusion(f32[768,256]{1,0:T(8,128)S(1)} %fusion.19, bf16[128,4096]{1,0:T(8,128)(2,1)S(1)} %collective-permute-done.9, bf16[128,4096]{1,0:T(8,128)(2,1)} %bitcast.3, bf16[192,2048]{1,0:T(8,128)(2,1)S(1)} %get-tuple-element.27, bf16[192,2048]{1,0:T(8,128)(2,1)} %collective-permute-done.13, ...), kind=kOutput, calls=%fused_computation.47 | convolution fusion | flops 613449728 | bytes 5341184 | tf_op jit(solution)/shard_map/dot_general | solution.py:68
  101.9 1.5 collective-permute-start.14
  103.4 1.2 slice.122
  104.6 1.4 collective-permute-start.17
  106.0 4.1 %collective-permute-done.14 = bf16[576,256]{1,0:T(8,128)(2,1)} collective-permute-done((bf16[576,256]{1,0:T(8,128)(2,1)}, bf16[576,256]{1,0:T(8,128)(2,1)}, u32[]{:S(2)}, u32[]{:S(2)}) %collective-permute-start.14) | collective-permute-done | bytes 294944 | tf_op jit(solution)/shard_map/ppermute | solution.py:60
  110.1 1.1 convert_add_fusion.1
  111.3 1.8 %fusion.26 = bf16[192,256]{1,0:T(8,128)(2,1)S(1)} fusion(f32[768,256]{1,0:T(8,128)} %copy-done.22, bf16[192,2048]{1,0:T(8,128)(2,1)} %collective-permute-done.15, bf16[128,4096]{1,0:T(8,128)(2,1)S(1)} %copy-done.1, bf16[128,4096]{1,0:T(8,128)(2,1)} %bitcast.3), kind=kOutput, calls=%fused_computation.54 | convolution fusion | flops 203522048 | bytes 3178496 | tf_op jit(solution)/shard_map/dot_general | solution.py:68
  113.1 1.6 collective-permute-start.16
  114.7 2.4 %fusion.9 = bf16[256,2048]{1,0:T(8,128)(2,1)S(1)} fusion(bf16[192,2048]{1,0:T(8,128)(2,1)} %collective-permute-done.15, bf16[192,2048]{1,0:T(8,128)(2,1)S(1)} %copy-done.7, bf16[192,2048]{1,0:T(8,128)(2,1)} %collective-permute-done.13, bf16[192,2048]{1,0:T(8,128)(2,1)S(1)} %copy-done.5, bf16[384,256]{1,0:T(8,128)(2,1)S(1)} %copy-done.21, ...), kind=kOutput, calls=%fused_computation.17 | convolution fusion | flops 819200000 | bytes 4587520 | tf_op jit(solution)/shard_map/dot_general | solution.py:72
  117.1 1.3 collective-permute-start.26
  118.5 4.2 %collective-permute-done.17 = bf16[128,2048]{1,0:T(8,128)(2,1)S(1)} collective-permute-done((bf16[128,2048]{1,0:T(8,128)(2,1)S(1)}, bf16[128,2048]{1,0:T(8,128)(2,1)S(1)}, u32[]{:S(2)}, u32[]{:S(2)}) %collective-permute-start.17) | collective-permute-done | bytes 524320 | tf_op jit(solution)/shard_map/ppermute | solution.py:56
  122.7 0.7 collective-permute-start.18
  123.5 0.3 multiply_reduce_fusion
  123.8 0.2 multiply_convert_fusion
  124.0 0.6 copy-done.24
  124.6 0.3 copy-done.26
  124.9 0.5 convolution_convert_fusion.3
  125.4 0.5 convolution_convert_fusion.1
  126.0 1.3 collective-permute-start.19
  127.3 0.7 collective-permute-start.21
  128.0 0.7 collective-permute-start.24
  128.7 0.5 convolution_convert_fusion.2
  129.2 9.8 %collective-permute-done.19 = bf16[192,512]{1,0:T(8,128)(2,1)S(1)} collective-permute-done((bf16[192,512]{1,0:T(8,128)(2,1)S(1)}, bf16[192,512]{1,0:T(8,128)(2,1)S(1)}, u32[]{:S(2)}, u32[]{:S(2)}) %collective-permute-start.19) | collective-permute-done | bytes 196640 | tf_op jit(solution)/shard_map/ppermute | solution.py:56
  139.0 0.7 convolution_convert_fusion
  139.7 1.9 %collective-permute-start.20 = (bf16[192,2560]{1,0:T(8,128)(2,1)S(1)}, bf16[192,2560]{1,0:T(8,128)(2,1)S(1)}, u32[]{:S(2)}, u32[]{:S(2)}) collective-permute-start(bf16[192,2560]{1,0:T(8,128)(2,1)S(1)} %convolution_convert_fusion), channel_id=1, source_target_pairs={{8,0},{16,8},{24,16},{9,1},{17,9},{25,17},{10,2},{18,10},{26,18},{... | collective-permute-start | bytes 2949128 | tf_op jit(solution)/shard_map/ppermute | solution.py:13
  141.8 1.1 maximum_bitcast_fusion
  142.9 1.3 collective-permute-start.23
  144.2 0.7 collective-permute-start.22
  145.0 1.3 collective-permute-start.25
  146.3 7.0 %collective-permute-done.20 = bf16[192,2560]{1,0:T(8,128)(2,1)S(1)} collective-permute-done((bf16[192,2560]{1,0:T(8,128)(2,1)S(1)}, bf16[192,2560]{1,0:T(8,128)(2,1)S(1)}, u32[]{:S(2)}, u32[]{:S(2)}) %collective-permute-start.20) | collective-permute-done | bytes 983072 | tf_op jit(solution)/shard_map/ppermute | solution.py:13
  153.3 1.0 fusion.50
  154.3 8.2 %collective-permute-done.25 = bf16[128,1280]{1,0:T(8,128)(2,1)S(1)} collective-permute-done((bf16[128,1280]{1,0:T(8,128)(2,1)S(1)}, bf16[128,1280]{1,0:T(8,128)(2,1)S(1)}, u32[]{:S(2)}, u32[]{:S(2)}) %collective-permute-start.25) | collective-permute-done | bytes 327712 | tf_op jit(solution)/shard_map/ppermute | solution.py:56
  162.5 1.4 fusion.23
  (82 shorter events, 0.8 us)
Async XLA Ops:
  0.6 40.2 %copy-start.10 = (bf16[1,128,2560]{2,1,0:T(8,128)(2,1)S(1)}, bf16[1,128,2560]{2,1,0:T(8,128)(2,1)}, u32[]{:S(2)}) copy-start(bf16[1,128,2560]{2,1,0:T(8,128)(2,1)} %param.5) | copy-start | bytes 1966084
  0.6 40.2 %copy-start.23 = (bf16[1,192,2560]{2,1,0:T(8,128)(2,1)S(1)}, bf16[1,192,2560]{2,1,0:T(8,128)(2,1)}, u32[]{:S(2)}) copy-start(bf16[1,192,2560]{2,1,0:T(8,128)(2,1)} %param.4) | copy-start | bytes 2949124
  0.7 19.1 %collective-permute-start.2 = (bf16[128,2560]{1,0:T(8,128)(2,1)}, bf16[128,2560]{1,0:T(8,128)(2,1)S(1)}, u32[]{:S(2)}, u32[]{:S(2)}) collective-permute-start(bf16[128,2560]{1,0:T(8,128)(2,1)} %bitcast.15), channel_id=1, source_target_pairs={{0,2},{6,4},{1,3},{7,5},{8,10},{14,12},{9,11},{15,13},{16,18},{22,... | collective-permute-start | bytes 1966088 | tf_op jit(solution)/shard_map/ppermute | solution.py:48
  4.3 36.5 %collective-permute-start = (bf16[192,2560]{1,0:T(8,128)(2,1)}, bf16[192,2560]{1,0:T(8,128)(2,1)S(1)}, u32[]{:S(2)}, u32[]{:S(2)}) collective-permute-start(bf16[192,2560]{1,0:T(8,128)(2,1)} %bitcast.20), channel_id=1, source_target_pairs={{0,2},{6,4},{1,3},{7,5},{8,10},{14,12},{9,11},{15,13},{16,18},{22,... | collective-permute-start | bytes 2949128 | tf_op jit(solution)/shard_map/ppermute | solution.py:48
  5.7 18.3 %collective-permute-start.1 = (bf16[128,2560]{1,0:T(8,128)(2,1)}, bf16[128,2560]{1,0:T(8,128)(2,1)S(1)}, u32[]{:S(2)}, u32[]{:S(2)}) collective-permute-start(bf16[128,2560]{1,0:T(8,128)(2,1)} %bitcast.16), channel_id=1, source_target_pairs={{2,0},{4,6},{3,1},{5,7},{10,8},{12,14},{11,9},{13,15},{18,16},{20,... | collective-permute-start | bytes 1966088 | tf_op jit(solution)/shard_map/ppermute | solution.py:56
  7.0 33.8 %collective-permute-start.3 = (bf16[128,2560]{1,0:T(8,128)(2,1)}, bf16[128,2560]{1,0:T(8,128)(2,1)S(1)}, u32[]{:S(2)}, u32[]{:S(2)}) collective-permute-start(bf16[128,2560]{1,0:T(8,128)(2,1)} %bitcast.17), channel_id=1, source_target_pairs={{2,4},{4,2},{3,5},{5,3},{10,12},{12,10},{11,13},{13,11},{18,20},{2... | collective-permute-start | bytes 1966088 | tf_op jit(solution)/shard_map/ppermute | solution.py:52
  19.7 22.3 %copy-start.12 = (bf16[128,2560]{1,0:T(8,128)(2,1)}, bf16[128,2560]{1,0:T(8,128)(2,1)S(1)}, u32[]{:S(2)}) copy-start(bf16[128,2560]{1,0:T(8,128)(2,1)S(1)} %collective-permute-done.2) | copy-start | bytes 1966084
  19.7 21.1 %collective-permute-start.4 = (bf16[128,2560]{1,0:T(8,128)(2,1)S(1)}, bf16[128,2560]{1,0:T(8,128)(2,1)S(1)}, u32[]{:S(2)}, u32[]{:S(2)}) collective-permute-start(bf16[128,2560]{1,0:T(8,128)(2,1)S(1)} %collective-permute-done.2), channel_id=1, source_target_pairs={{2,4},{4,2},{3,5},{5,3},{10,12},{12,10},{11,13},{13,11},{18,20},{2... | collective-permute-start | bytes 1966088 | tf_op jit(solution)/shard_map/ppermute | solution.py:52
  20.4 47.3 %collective-permute-start.7 = (bf16[192,4096]{1,0:T(8,128)(2,1)}, bf16[192,4096]{1,0:T(8,128)(2,1)S(1)}, u32[]{:S(2)}, u32[]{:S(2)}) collective-permute-start(bf16[192,4096]{1,0:T(8,128)(2,1)} %bitcast.13), channel_id=1, source_target_pairs={{2,4},{4,2},{3,5},{5,3},{10,12},{12,10},{11,13},{13,11},{18,20},{2... | collective-permute-start | bytes 4718600 | tf_op jit(solution)/shard_map/ppermute | solution.py:52
  23.6 20.1 %copy-start.3 = (bf16[192,2048]{1,0:T(8,128)(2,1)}, bf16[192,2048]{1,0:T(8,128)(2,1)S(1)}, u32[]{:S(2)}) copy-start(bf16[192,2048]{1,0:T(8,128)(2,1)S(1)} %get-tuple-element.20) | copy-start | bytes 2359300
  24.0 16.8 %copy-start.14 = (bf16[128,2560]{1,0:T(8,128)(2,1)}, bf16[128,2560]{1,0:T(8,128)(2,1)S(1)}, u32[]{:S(2)}) copy-start(bf16[128,2560]{1,0:T(8,128)(2,1)S(1)} %collective-permute-done.1) | copy-start | bytes 1966084
  24.0 33.6 %collective-permute-start.6 = (bf16[192,2048]{1,0:T(8,128)(2,1)}, bf16[192,2048]{1,0:T(8,128)(2,1)}, u32[]{:S(2)}, u32[]{:S(2)}) collective-permute-start(bf16[192,2048]{1,0:T(8,128)(2,1)} %get-tuple-element.30), channel_id=1, source_target_pairs={{0,2},{6,4},{1,3},{7,5},{8,10},{14,12},{9,11},{15,13},{16,18},{22,... | collective-permute-start | bytes 2359304 | tf_op jit(solution)/shard_map/ppermute | solution.py:48
  40.8 1.3 copy-start.25
  40.8 1.3 copy-start.16
  40.8 1.3 copy-start.18
  42.2 16.2 %collective-permute-start.5 = (bf16[384,512]{1,0:T(8,128)(2,1)S(1)}, bf16[384,512]{1,0:T(8,128)(2,1)S(1)}, u32[]{:S(2)}, u32[]{:S(2)}) collective-permute-start(bf16[384,512]{1,0:T(8,128)(2,1)S(1)} %convolution_convert_fusion.6), channel_id=1, source_target_pairs={{0,1},{1,0},{2,3},{3,2},{4,5},{5,4},{6,7},{7,6},{8,9},{9,8},{10,11... | collective-permute-start | bytes 1179656 | tf_op jit(solution)/shard_map/ppermute | solution.py:60
  43.7 30.7 %collective-permute-start.13 = (bf16[192,2048]{1,0:T(8,128)(2,1)S(1)}, bf16[192,2048]{1,0:T(8,128)(2,1)}, u32[]{:S(2)}, u32[]{:S(2)}) collective-permute-start(bf16[192,2048]{1,0:T(8,128)(2,1)S(1)} %get-tuple-element.20), channel_id=1, source_target_pairs={{0,2},{6,4},{1,3},{7,5},{8,10},{14,12},{9,11},{15,13},{16,18},{22,... | collective-permute-start | bytes 2359304 | tf_op jit(solution)/shard_map/ppermute | solution.py:48
  49.1 17.0 %collective-permute-start.10 = (bf16[128,2560]{1,0:T(8,128)(2,1)}, bf16[128,2560]{1,0:T(8,128)(2,1)S(1)}, u32[]{:S(2)}, u32[]{:S(2)}) collective-permute-start(bf16[128,2560]{1,0:T(8,128)(2,1)} %copy-done.16), channel_id=1, source_target_pairs={{2,0},{4,6},{3,1},{5,7},{10,8},{12,14},{11,9},{13,15},{18,16},{20,... | collective-permute-start | bytes 1966088 | tf_op jit(solution)/shard_map/ppermute | solution.py:56
  57.6 21.2 %collective-permute-start.8 = (bf16[192,2048]{1,0:T(8,128)(2,1)}, bf16[192,2048]{1,0:T(8,128)(2,1)S(1)}, u32[]{:S(2)}, u32[]{:S(2)}) collective-permute-start(bf16[192,2048]{1,0:T(8,128)(2,1)} %collective-permute-done.6), channel_id=1, source_target_pairs={{2,4},{4,2},{3,5},{5,3},{10,12},{12,10},{11,13},{13,11},{18,20},{2... | collective-permute-start | bytes 2359304 | tf_op jit(solution)/shard_map/ppermute | solution.py:52
  58.3 20.5 %collective-permute-start.12 = (bf16[128,2560]{1,0:T(8,128)(2,1)}, bf16[128,2560]{1,0:T(8,128)(2,1)S(1)}, u32[]{:S(2)}, u32[]{:S(2)}) collective-permute-start(bf16[128,2560]{1,0:T(8,128)(2,1)} %copy-done.18), channel_id=1, source_target_pairs={{2,0},{4,6},{3,1},{5,7},{10,8},{12,14},{11,9},{13,15},{18,16},{20,... | collective-permute-start | bytes 1966088 | tf_op jit(solution)/shard_map/ppermute | solution.py:56
  60.0 15.9 %copy-start.8 = (bf16[384,256]{1,0:T(8,128)(2,1)}, bf16[384,256]{1,0:T(8,128)(2,1)S(1)}, u32[]{:S(2)}) copy-start(bf16[384,256]{1,0:T(8,128)(2,1)S(1)} %get-tuple-element.33) | copy-start | bytes 589828
  66.0 29.8 %collective-permute-start.9 = (bf16[128,4096]{1,0:T(8,128)(2,1)}, bf16[128,4096]{1,0:T(8,128)(2,1)S(1)}, u32[]{:S(2)}, u32[]{:S(2)}) collective-permute-start(bf16[128,4096]{1,0:T(8,128)(2,1)} %bitcast.3), channel_id=1, source_target_pairs={{0,2},{6,4},{1,3},{7,5},{8,10},{14,12},{9,11},{15,13},{16,18},{22,... | collective-permute-start | bytes 3145736 | tf_op jit(solution)/shard_map/ppermute | solution.py:48
  67.7 8.3 %collective-permute-start.11 = (bf16[384,256]{1,0:T(8,128)(2,1)S(1)}, bf16[384,256]{1,0:T(8,128)(2,1)S(1)}, u32[]{:S(2)}, u32[]{:S(2)}) collective-permute-start(bf16[384,256]{1,0:T(8,128)(2,1)S(1)} %get-tuple-element.17), channel_id=1, source_target_pairs={{2,4},{4,2},{3,5},{5,3},{10,12},{12,10},{11,13},{13,11},{18,20},{2... | collective-permute-start | bytes 589832 | tf_op jit(solution)/shard_map/ppermute | solution.py:52
  68.5 30.3 %copy-start.6 = (bf16[192,2048]{1,0:T(8,128)(2,1)}, bf16[192,2048]{1,0:T(8,128)(2,1)S(1)}, u32[]{:S(2)}) copy-start(bf16[192,2048]{1,0:T(8,128)(2,1)S(1)} %get-tuple-element.27) | copy-start | bytes 2359300
  74.4 36.9 %collective-permute-start.15 = (bf16[192,2048]{1,0:T(8,128)(2,1)}, bf16[192,2048]{1,0:T(8,128)(2,1)}, u32[]{:S(2)}, u32[]{:S(2)}) collective-permute-start(bf16[192,2048]{1,0:T(8,128)(2,1)} %collective-permute-done.13), channel_id=1, source_target_pairs={{2,4},{4,2},{3,5},{5,3},{10,12},{12,10},{11,13},{13,11},{18,20},{2... | collective-permute-start | bytes 2359304 | tf_op jit(solution)/shard_map/ppermute | solution.py:52
  75.9 2.9 %copy-start.20 = (bf16[384,256]{1,0:T(8,128)(2,1)}, bf16[384,256]{1,0:T(8,128)(2,1)S(1)}, u32[]{:S(2)}) copy-start(bf16[384,256]{1,0:T(8,128)(2,1)S(1)} %collective-permute-done.11) | copy-start | bytes 589828
  78.8 3.6 %copy-start.11 = (bf16[1,128,2560]{2,1,0:T(8,128)(2,1)S(1)}, bf16[1,128,2560]{2,1,0:T(8,128)(2,1)}, u32[]{:S(2)}) copy-start(bf16[1,128,2560]{2,1,0:T(8,128)(2,1)} %param.5) | copy-start | bytes 1966084
  78.8 3.6 %copy-start.13 = (bf16[128,2560]{1,0:T(8,128)(2,1)S(1)}, bf16[128,2560]{1,0:T(8,128)(2,1)}, u32[]{:S(2)}) copy-start(bf16[128,2560]{1,0:T(8,128)(2,1)} %copy-done.12) | copy-start | bytes 1966084
  78.9 3.6 %copy-start.15 = (bf16[128,2560]{1,0:T(8,128)(2,1)S(1)}, bf16[128,2560]{1,0:T(8,128)(2,1)}, u32[]{:S(2)}) copy-start(bf16[128,2560]{1,0:T(8,128)(2,1)} %copy-done.14) | copy-start | bytes 1966084
  78.9 3.6 %copy-start.17 = (bf16[128,2560]{1,0:T(8,128)(2,1)S(1)}, bf16[128,2560]{1,0:T(8,128)(2,1)}, u32[]{:S(2)}) copy-start(bf16[128,2560]{1,0:T(8,128)(2,1)} %copy-done.16) | copy-start | bytes 1966084
  78.9 3.6 %copy-start.19 = (bf16[128,2560]{1,0:T(8,128)(2,1)S(1)}, bf16[128,2560]{1,0:T(8,128)(2,1)}, u32[]{:S(2)}) copy-start(bf16[128,2560]{1,0:T(8,128)(2,1)} %copy-done.18) | copy-start | bytes 1966084
  83.2 15.6 %copy-start.4 = (bf16[192,2048]{1,0:T(8,128)(2,1)S(1)}, bf16[192,2048]{1,0:T(8,128)(2,1)}, u32[]{:S(2)}) copy-start(bf16[192,2048]{1,0:T(8,128)(2,1)} %copy-done.3) | copy-start | bytes 2359300
  95.8 2.9 %copy-start = (bf16[128,4096]{1,0:T(8,128)(2,1)}, bf16[128,4096]{1,0:T(8,128)(2,1)S(1)}, u32[]{:S(2)}) copy-start(bf16[128,4096]{1,0:T(8,128)(2,1)S(1)} %collective-permute-done.9) | copy-start | bytes 3145732
  98.7 3.1 %copy-start.22 = (f32[768,256]{1,0:T(8,128)}, f32[768,256]{1,0:T(8,128)S(1)}, u32[]{:S(2)}) copy-start(f32[768,256]{1,0:T(8,128)S(1)} %fusion.19) | copy-start | bytes 2359300
  101.9 8.2 %collective-permute-start.14 = (bf16[576,256]{1,0:T(8,128)(2,1)}, bf16[576,256]{1,0:T(8,128)(2,1)}, u32[]{:S(2)}, u32[]{:S(2)}) collective-permute-start(bf16[576,256]{1,0:T(8,128)(2,1)} %fusion.25), channel_id=1, source_target_pairs={{0,1},{1,0},{2,3},{3,2},{4,5},{5,4},{6,7},{7,6},{8,9},{9,8},{10,11... | collective-permute-start | bytes 884744 | tf_op jit(solution)/shard_map/ppermute | solution.py:60
  103.4 7.9 %copy-start.1 = (bf16[128,4096]{1,0:T(8,128)(2,1)S(1)}, bf16[128,4096]{1,0:T(8,128)(2,1)}, u32[]{:S(2)}) copy-start(bf16[128,4096]{1,0:T(8,128)(2,1)} %copy-done) | copy-start | bytes 3145732
  104.5 10.1 %copy-start.5 = (bf16[192,2048]{1,0:T(8,128)(2,1)S(1)}, bf16[192,2048]{1,0:T(8,128)(2,1)}, u32[]{:S(2)}) copy-start(bf16[192,2048]{1,0:T(8,128)(2,1)} %copy-done.3) | copy-start | bytes 2359300
  104.6 10.1 %copy-start.7 = (bf16[192,2048]{1,0:T(8,128)(2,1)S(1)}, bf16[192,2048]{1,0:T(8,128)(2,1)}, u32[]{:S(2)}) copy-start(bf16[192,2048]{1,0:T(8,128)(2,1)} %copy-done.6) | copy-start | bytes 2359300
  104.6 10.1 %copy-start.9 = (bf16[384,256]{1,0:T(8,128)(2,1)S(1)}, bf16[384,256]{1,0:T(8,128)(2,1)}, u32[]{:S(2)}) copy-start(bf16[384,256]{1,0:T(8,128)(2,1)} %copy-done.8) | copy-start | bytes 589828
  104.6 10.1 %copy-start.21 = (bf16[384,256]{1,0:T(8,128)(2,1)S(1)}, bf16[384,256]{1,0:T(8,128)(2,1)}, u32[]{:S(2)}) copy-start(bf16[384,256]{1,0:T(8,128)(2,1)} %copy-done.20) | copy-start | bytes 589828
  104.6 18.1 %collective-permute-start.17 = (bf16[128,2048]{1,0:T(8,128)(2,1)S(1)}, bf16[128,2048]{1,0:T(8,128)(2,1)S(1)}, u32[]{:S(2)}, u32[]{:S(2)}) collective-permute-start(bf16[128,2048]{1,0:T(8,128)(2,1)S(1)} %slice.122), channel_id=1, source_target_pairs={{2,0},{4,6},{3,1},{5,7},{10,8},{12,14},{11,9},{13,15},{18,16},{20,... | collective-permute-start | bytes 1572872 | tf_op jit(solution)/shard_map/ppermute | solution.py:56
  113.1 10.2 %copy-start.2 = (bf16[256,2048]{1,0:T(8,128)(2,1)S(1)}, bf16[256,2048]{1,0:T(8,128)(2,1)}, u32[]{:S(2)}) copy-start(bf16[256,2048]{1,0:T(8,128)(2,1)} %convolution_convert_fusion.5) | copy-start | bytes 3145732
  113.1 5.3 %collective-permute-start.16 = (bf16[192,256]{1,0:T(8,128)(2,1)S(1)}, bf16[192,256]{1,0:T(8,128)(2,1)S(1)}, u32[]{:S(2)}, u32[]{:S(2)}) collective-permute-start(bf16[192,256]{1,0:T(8,128)(2,1)S(1)} %fusion.26), channel_id=1, source_target_pairs={{0,1},{1,0},{2,3},{3,2},{4,5},{5,4},{6,7},{7,6},{8,9},{9,8},{10,11... | collective-permute-start | bytes 294920 | tf_op jit(solution)/shard_map/ppermute | solution.py:60
  117.1 24.5 %collective-permute-start.26 = (bf16[128,2048]{1,0:T(8,128)(2,1)S(1)}, bf16[128,2048]{1,0:T(8,128)(2,1)S(1)}, u32[]{:S(2)}, u32[]{:S(2)}) collective-permute-start(bf16[128,2048]{1,0:T(8,128)(2,1)S(1)} %slice.135), channel_id=1, source_target_pairs={{2,0},{4,6},{3,1},{5,7},{10,8},{12,14},{11,9},{13,15},{18,16},{20,... | collective-permute-start | bytes 1572872 | tf_op jit(solution)/shard_map/ppermute | solution.py:56
  122.7 0.8 collective-permute-start.18
  123.4 1.2 copy-start.24
  123.4 1.5 copy-start.26
  126.0 13.1 %collective-permute-start.19 = (bf16[192,512]{1,0:T(8,128)(2,1)S(1)}, bf16[192,512]{1,0:T(8,128)(2,1)S(1)}, u32[]{:S(2)}, u32[]{:S(2)}) collective-permute-start(bf16[192,512]{1,0:T(8,128)(2,1)S(1)} %slice.124), channel_id=1, source_target_pairs={{2,0},{4,6},{3,1},{5,7},{10,8},{12,14},{11,9},{13,15},{18,16},{20,... | collective-permute-start | bytes 589832 | tf_op jit(solution)/shard_map/ppermute | solution.py:56
  127.3 15.5 %collective-permute-start.21 = (bf16[128,1280]{1,0:T(8,128)(2,1)S(1)}, bf16[128,1280]{1,0:T(8,128)(2,1)S(1)}, u32[]{:S(2)}, u32[]{:S(2)}) collective-permute-start(bf16[128,1280]{1,0:T(8,128)(2,1)S(1)} %get-tuple-element.32), channel_id=1, source_target_pairs={{2,4},{4,2},{3,5},{5,3},{10,12},{12,10},{11,13},{13,11},{18,20},{2... | collective-permute-start | bytes 983048 | tf_op jit(solution)/shard_map/ppermute | solution.py:52
  128.0 16.9 %collective-permute-start.24 = (bf16[128,1280]{1,0:T(8,128)(2,1)S(1)}, bf16[128,1280]{1,0:T(8,128)(2,1)S(1)}, u32[]{:S(2)}, u32[]{:S(2)}) collective-permute-start(bf16[128,1280]{1,0:T(8,128)(2,1)S(1)} %get-tuple-element.31), channel_id=1, source_target_pairs={{2,4},{4,2},{3,5},{5,3},{10,12},{12,10},{11,13},{13,11},{18,20},{2... | collective-permute-start | bytes 983048 | tf_op jit(solution)/shard_map/ppermute | solution.py:52
  139.7 13.5 %collective-permute-start.20 = (bf16[192,2560]{1,0:T(8,128)(2,1)S(1)}, bf16[192,2560]{1,0:T(8,128)(2,1)S(1)}, u32[]{:S(2)}, u32[]{:S(2)}) collective-permute-start(bf16[192,2560]{1,0:T(8,128)(2,1)S(1)} %convolution_convert_fusion), channel_id=1, source_target_pairs={{8,0},{16,8},{24,16},{9,1},{17,9},{25,17},{10,2},{18,10},{26,18},{... | collective-permute-start | bytes 2949128 | tf_op jit(solution)/shard_map/ppermute | solution.py:13
  142.9 19.6 %collective-permute-start.23 = (bf16[128,1280]{1,0:T(8,128)(2,1)S(1)}, bf16[128,1280]{1,0:T(8,128)(2,1)S(1)}, u32[]{:S(2)}, u32[]{:S(2)}) collective-permute-start(bf16[128,1280]{1,0:T(8,128)(2,1)S(1)} %add_convert_fusion.2), channel_id=1, source_target_pairs={{2,0},{4,6},{3,1},{5,7},{10,8},{12,14},{11,9},{13,15},{18,16},{20,... | collective-permute-start | bytes 983048 | tf_op jit(solution)/shard_map/ppermute | solution.py:56
  144.2 10.1 %collective-permute-start.22 = (bf16[128,2560]{1,0:T(8,128)(2,1)S(1)}, bf16[128,2560]{1,0:T(8,128)(2,1)S(1)}, u32[]{:S(2)}, u32[]{:S(2)}) collective-permute-start(bf16[128,2560]{1,0:T(8,128)(2,1)S(1)} %convolution_convert_fusion.3), channel_id=1, source_target_pairs={{2,4},{4,2},{3,5},{5,3},{10,12},{12,10},{11,13},{13,11},{18,20},{2... | collective-permute-start | bytes 1966088 | tf_op jit(solution)/shard_map/ppermute | solution.py:52
  145.0 17.5 %collective-permute-start.25 = (bf16[128,1280]{1,0:T(8,128)(2,1)S(1)}, bf16[128,1280]{1,0:T(8,128)(2,1)S(1)}, u32[]{:S(2)}, u32[]{:S(2)}) collective-permute-start(bf16[128,1280]{1,0:T(8,128)(2,1)S(1)} %add_convert_fusion.1), channel_id=1, source_target_pairs={{2,0},{4,6},{3,1},{5,7},{10,8},{12,14},{11,9},{13,15},{18,16},{20,... | collective-permute-start | bytes 983048 | tf_op jit(solution)/shard_map/ppermute | solution.py:56

commit v9 on v8

--- a/solution.py
+++ b/solution.py
@@ -132,14 +132,6 @@
     values = jnp.concatenate([early_rows(1), last], axis=0)
     up_second = tokens_dot(normed_all, values).astype(BF16)
     back_second = outward(up_second[lat:])
-    up_grad = jnp.concatenate(
-        [
-            jnp.where(middle, up_first[:lat], back_first),
-            jnp.where(middle, up_second[:lat], back_second),
-        ],
-        axis=1,
-    )
-
     grad_sent = jnp.concatenate([early_sum[2 * rows :], late], axis=0).astype(BF16)
     from_across = across(after(grad_sent, up_second, back_first))
     normed_grad = jnp.concatenate([early_sum[: 2 * rows], from_across.astype(F32)], axis=1)
@@ -159,11 +151,18 @@
     end_first = (sums[1][:, halves[0]] + from_end[0].astype(F32)).astype(BF16)
     from_own = across(after(sent_own, end_first))
     end_second = sums[1][:, halves[1]] + after(from_end[1], end_first).astype(F32)
-    down_end_grad = jnp.concatenate([outward(end_first), outward(end_second.astype(BF16))], axis=1)
+    end_second = end_second.astype(BF16)
+    down_end_grad = jnp.concatenate([outward(end_first), outward(end_second)], axis=1)
+    up_grad = jnp.concatenate(
+        [
+            jnp.where(middle, up_first[:lat], back_first),
+            jnp.where(middle, up_second[:lat], after(back_second, end_second)),
+        ],
+        axis=1,
+    )
+
     input_grad = jnp.dot(latent_used, down_used, preferred_element_type=F32).astype(BF16)
     passed = shifted(input_grad, "section", -1)
-    final = lax.axis_index("section") == lax.axis_size("section") - 1
-    passed = jnp.where(final, jnp.zeros_like(passed), passed)
     down_own_grad = (sums[0] + after(from_own, passed).astype(F32)).astype(BF16)
     down_grad = jnp.where(middle, down_own_grad, down_end_grad)
     return (passed[None], down_grad[None], up_grad[None])

time: 167 us -> 160 us (0.958)
  matrix products: 18.7 us -> 12.5 us
  other arithmetic: 5.17 us -> 3.12 us
  waiting for transfers between devices: 87.9 us -> 89.9 us
    dot_general x4, matrix products: 9.07 us -> 4.98 us  [rows_dot(): lax.dot_general(left, right, (((1,), (1,)), ((), ())), preferred_element_...]
    ppermute x5, waiting for transfers between devices: 45.4 us -> 48.1 us  [inward(): return lax.ppermute(value, 'row', [(0, 1), (3, 2)])]
    ppermute x8, waiting for transfers between devices: 31.4 us -> 29.2 us  [outward(): return lax.ppermute(value, 'row', [(1, 0), (2, 3)])]
    dot_general x6, matrix products: 8.92 us -> 6.81 us  [tokens_dot(): lax.dot_general(left, right, (((0,), (0,)), ((), ())), preferred_element_...]
  transfers between devices with their start and end apart: 27 -> 27, of which waited for: 13 -> 14; matrix products, arithmetic and copies ran while one was open for 16% -> 11% of each run, Pallas kernels for 0% -> 0%
where the time goes in v9:
time: 160 us; the launch traced here: 158 us
  waiting for transfers between devices  89.9 us (56%)
  starting transfers between devices  45.8 us (29%)
  matrix products  12.5 us (8%)
  local copies, waits for them, and re-layouts  4.96 us (3%)
  other arithmetic  3.12 us (2%)
    ppermute x5, waiting for transfers between devices, inward(): return lax.ppermute(value, 'row', [(0, 1), (3, 2)])  48.1 us
    ppermute x8, waiting for transfers between devices, outward(): return lax.ppermute(value, 'row', [(1, 0), (2, 3)])  29.2 us
    ppermute x5, starting transfers between devices, inward(): return lax.ppermute(value, 'row', [(0, 1), (3, 2)])  22 us
    ppermute x8, starting transfers between devices, outward(): return lax.ppermute(value, 'row', [(1, 0), (2, 3)])  10.3 us
    ppermute x10, starting transfers between devices, across(): return lax.ppermute(value, 'row', [(1, 2), (2, 1)])  6.95 us
    ppermute x1, waiting for transfers between devices, shifted(): lax.ppermute(value, axis, [(source, source + steps) for source in range(l...  6.93 us
    dot_general x6, matrix products, tokens_dot(): lax.dot_general(left, right, (((0,), (0,)), ((), ())), preferred_element_...  6.81 us
    ppermute x3, waiting for transfers between devices, other_col(): return lax.ppermute(value, 'col', [(0, 1), (1, 0)])  5.62 us
  transfers between devices with their start and end apart: 27, of which 14 were waited for; matrix products, arithmetic and copies ran while one was open for 11% of the time, Pallas kernels for 0%

profile of v9, /device:TPU:4, one launch (start us, length us, event | category | flops | bytes accessed | tf_op | source)
XLA Modules:
  0.0 157.5 jit_solution(14568423223315078372)
XLA Ops:
  0.7 3.7 %collective-permute-start.2 = (bf16[128,2560]{1,0:T(8,128)(2,1)}, bf16[128,2560]{1,0:T(8,128)(2,1)S(1)}, u32[]{:S(2)}, u32[]{:S(2)}) collective-permute-start(bf16[128,2560]{1,0:T(8,128)(2,1)} %bitcast.19), channel_id=1, source_target_pairs={{0,2},{6,4},{1,3},{7,5},{8,10},{14,12},{9,11},{15,13},{16,18},{22,... | collective-permute-start | bytes 1966088 | tf_op jit(solution)/shard_map/ppermute | solution.py:48
  4.3 1.4 collective-permute-start
  5.7 1.3 collective-permute-start.1
  7.0 0.7 collective-permute-start.3
  7.7 12.0 %collective-permute-done.2 = bf16[128,2560]{1,0:T(8,128)(2,1)S(1)} collective-permute-done((bf16[128,2560]{1,0:T(8,128)(2,1)}, bf16[128,2560]{1,0:T(8,128)(2,1)S(1)}, u32[]{:S(2)}, u32[]{:S(2)}) %collective-permute-start.2) | collective-permute-done | bytes 655392 | tf_op jit(solution)/shard_map/ppermute | solution.py:48
  19.7 0.7 collective-permute-start.4
  20.4 0.8 collective-permute-start.7
  21.2 2.7 %fusion.44 = (bf16[192,2048]{1,0:T(8,128)(2,1)}, bf16[192,2048]{1,0:T(8,128)(2,1)}) fusion(bf16[192,4096]{1,0:T(8,128)(2,1)} %bitcast.13), kind=kLoop, calls=%fused_computation.72 | loop fusion | bytes 3145728 | tf_op jit(solution)/shard_map/slice | solution.py:119
  23.9 0.1 collective-permute-done.1
  24.0 9.5 %collective-permute-start.6 = (bf16[192,2048]{1,0:T(8,128)(2,1)}, bf16[192,2048]{1,0:T(8,128)(2,1)}, u32[]{:S(2)}, u32[]{:S(2)}) collective-permute-start(bf16[192,2048]{1,0:T(8,128)(2,1)} %get-tuple-element.32), channel_id=1, source_target_pairs={{0,2},{6,4},{1,3},{7,5},{8,10},{14,12},{9,11},{15,13},{16,18},{22,... | collective-permute-start | bytes 2359304 | tf_op jit(solution)/shard_map/ppermute | solution.py:48
  33.4 7.3 %collective-permute-done = bf16[192,2560]{1,0:T(8,128)(2,1)S(1)} collective-permute-done((bf16[192,2560]{1,0:T(8,128)(2,1)}, bf16[192,2560]{1,0:T(8,128)(2,1)S(1)}, u32[]{:S(2)}, u32[]{:S(2)}) %collective-permute-start) | collective-permute-done | bytes 983072 | tf_op jit(solution)/shard_map/ppermute | solution.py:48
  40.8 1.2 convolution_convert_fusion.6
  42.2 1.5 collective-permute-start.5
  43.7 4.6 %collective-permute-start.13 = (bf16[192,2048]{1,0:T(8,128)(2,1)}, bf16[192,2048]{1,0:T(8,128)(2,1)S(1)}, u32[]{:S(2)}, u32[]{:S(2)}) collective-permute-start(bf16[192,2048]{1,0:T(8,128)(2,1)} %get-tuple-element.21), channel_id=1, source_target_pairs={{0,2},{6,4},{1,3},{7,5},{8,10},{14,12},{9,11},{15,13},{16,18},{22,... | collective-permute-start | bytes 2359304 | tf_op jit(solution)/shard_map/ppermute | solution.py:48
  48.3 1.3 collective-permute-start.10
  49.6 8.1 %collective-permute-done.6 = bf16[192,2048]{1,0:T(8,128)(2,1)} collective-permute-done((bf16[192,2048]{1,0:T(8,128)(2,1)}, bf16[192,2048]{1,0:T(8,128)(2,1)}, u32[]{:S(2)}, u32[]{:S(2)}) %collective-permute-start.6) | collective-permute-done | bytes 786464 | tf_op jit(solution)/shard_map/ppermute | solution.py:48
  57.6 0.7 collective-permute-start.8
  58.3 1.3 collective-permute-start.12
  59.6 0.2 multiply_reduce_fusion.1
  59.9 0.1 fusion.24
  60.0 4.4 %collective-permute-done.10 = bf16[128,2560]{1,0:T(8,128)(2,1)S(1)} collective-permute-done((bf16[128,2560]{1,0:T(8,128)(2,1)}, bf16[128,2560]{1,0:T(8,128)(2,1)S(1)}, u32[]{:S(2)}, u32[]{:S(2)}) %collective-permute-start.10) | collective-permute-done | bytes 655392 | tf_op jit(solution)/shard_map/ppermute | solution.py:56
  64.4 2.9 %collective-permute-start.9 = (bf16[128,4096]{1,0:T(8,128)(2,1)S(1)}, bf16[128,4096]{1,0:T(8,128)(2,1)S(1)}, u32[]{:S(2)}, u32[]{:S(2)}) collective-permute-start(bf16[128,4096]{1,0:T(8,128)(2,1)S(1)} %bitcast.14), channel_id=1, source_target_pairs={{0,2},{6,4},{1,3},{7,5},{8,10},{14,12},{9,11},{15,13},{16,18},{22,... | collective-permute-start | bytes 3145736 | tf_op jit(solution)/shard_map/ppermute | solution.py:48
  67.3 0.7 collective-permute-start.11
  68.0 0.1 fusion.43
  68.1 6.3 %collective-permute-done.13 = bf16[192,2048]{1,0:T(8,128)(2,1)S(1)} collective-permute-done((bf16[192,2048]{1,0:T(8,128)(2,1)}, bf16[192,2048]{1,0:T(8,128)(2,1)S(1)}, u32[]{:S(2)}, u32[]{:S(2)}) %collective-permute-start.13) | collective-permute-done | bytes 786464 | tf_op jit(solution)/shard_map/ppermute | solution.py:48
  74.5 0.7 collective-permute-start.15
  75.2 2.8 %collective-permute-done.12 = bf16[128,2560]{1,0:T(8,128)(2,1)S(1)} collective-permute-done((bf16[128,2560]{1,0:T(8,128)(2,1)}, bf16[128,2560]{1,0:T(8,128)(2,1)S(1)}, u32[]{:S(2)}, u32[]{:S(2)}) %collective-permute-start.12) | collective-permute-done | bytes 655392 | tf_op jit(solution)/shard_map/ppermute | solution.py:56
  78.1 2.5 %convolution_convert_fusion.5 = bf16[256,2048]{1,0:T(8,128)(2,1)S(1)} fusion(bf16[768,256]{1,0:T(8,128)(2,1)S(1)} %pad_maximum_fusion.8, bf16[192,2048]{1,0:T(8,128)(2,1)S(1)} %collective-permute-done.8, bf16[192,2048]{1,0:T(8,128)(2,1)S(1)} %get-tuple-element.30, bf16[192,2048]{1,0:T(8,128)(2,1)} %collective-permute-done.6, ...), kind=kOutput, calls=%fused_computation.18 | convolution fusion | flops 818413568 | bytes 4587520 | tf_op jit(solution)/shard_map/dot_general | solution.py:72
  80.7 0.7 maximum_select_fusion
  81.4 14.3 %collective-permute-done.9 = bf16[128,4096]{1,0:T(8,128)(2,1)S(1)} collective-permute-done((bf16[128,4096]{1,0:T(8,128)(2,1)S(1)}, bf16[128,4096]{1,0:T(8,128)(2,1)S(1)}, u32[]{:S(2)}, u32[]{:S(2)}) %collective-permute-start.9) | collective-permute-done | bytes 1048608 | tf_op jit(solution)/shard_map/ppermute | solution.py:48
  95.7 2.4 %fusion.19 = f32[768,256]{1,0:T(8,128)S(1)} fusion(bf16[128,4096]{1,0:T(8,128)(2,1)S(1)} %bitcast.15, bf16[128,4096]{1,0:T(8,128)(2,1)S(1)} %collective-permute-done.9, bf16[192,2048]{1,0:T(8,128)(2,1)S(1)} %collective-permute-done.8, bf16[192,2048]{1,0:T(8,128)(2,1)S(1)} %get-tuple-element.30, bf16[192,2048]{1,0:T(8,128)(2,1)} %collective-permute-done.6, ...), kind=kOutput, calls=%fused_computation.31 | convolution fusion | flops 819986432 | bytes 6029312 | tf_op jit(solution)/shard_map/dot_general | solution.py:68
  98.1 0.9 fusion.25
  99.0 1.6 collective-permute-start.14
  100.6 1.3 collective-permute-start.17
  101.9 5.0 %collective-permute-done.14 = bf16[576,256]{1,0:T(8,128)(2,1)S(1)} collective-permute-done((bf16[576,256]{1,0:T(8,128)(2,1)S(1)}, bf16[576,256]{1,0:T(8,128)(2,1)S(1)}, u32[]{:S(2)}, u32[]{:S(2)}) %collective-permute-start.14) | collective-permute-done | bytes 294944 | tf_op jit(solution)/shard_map/ppermute | solution.py:60
  107.1 0.5 fusion.26
  107.6 1.6 collective-permute-start.16
  109.1 1.2 fusion.9
  110.4 1.3 collective-permute-start.26
  111.7 0.6 collective-permute-done.16
  112.3 4.0 %collective-permute-done.17 = bf16[128,2048]{1,0:T(8,128)(2,1)S(1)} collective-permute-done((bf16[128,2048]{1,0:T(8,128)(2,1)S(1)}, bf16[128,2048]{1,0:T(8,128)(2,1)S(1)}, u32[]{:S(2)}, u32[]{:S(2)}) %collective-permute-start.17) | collective-permute-done | bytes 524320 | tf_op jit(solution)/shard_map/ppermute | solution.py:56
  116.3 0.7 collective-permute-start.18
  117.1 0.3 multiply_reduce_fusion
  117.4 0.2 multiply_convert_fusion
  117.7 0.6 copy-done.13
  118.3 0.3 copy-done.15
  118.6 0.5 convolution_convert_fusion.3
  119.1 0.5 convolution_convert_fusion.1
  119.7 1.3 collective-permute-start.19
  121.0 0.7 collective-permute-start.21
  121.7 0.5 convolution_convert_fusion.2
  122.2 0.7 collective-permute-start.24
  122.9 9.9 %collective-permute-done.19 = bf16[192,512]{1,0:T(8,128)(2,1)S(1)} collective-permute-done((bf16[192,512]{1,0:T(8,128)(2,1)S(1)}, bf16[192,512]{1,0:T(8,128)(2,1)S(1)}, u32[]{:S(2)}, u32[]{:S(2)}) %collective-permute-start.19) | collective-permute-done | bytes 196640 | tf_op jit(solution)/shard_map/ppermute | solution.py:56
  132.8 0.7 convolution_convert_fusion
  133.5 1.9 %collective-permute-start.20 = (bf16[192,2560]{1,0:T(8,128)(2,1)S(1)}, bf16[192,2560]{1,0:T(8,128)(2,1)S(1)}, u32[]{:S(2)}, u32[]{:S(2)}) collective-permute-start(bf16[192,2560]{1,0:T(8,128)(2,1)S(1)} %convolution_convert_fusion), channel_id=1, source_target_pairs={{8,0},{16,8},{24,16},{9,1},{17,9},{25,17},{10,2},{18,10},{26,18},{... | collective-permute-start | bytes 2949128 | tf_op jit(solution)/shard_map/ppermute | solution.py:13
  135.5 1.3 collective-permute-start.23
  136.8 0.7 collective-permute-start.22
  137.6 0.1 add_convert_fusion.1
  137.7 1.3 collective-permute-start.25
  139.0 1.1 maximum_bitcast_fusion
  140.1 6.9 %collective-permute-done.20 = bf16[192,2560]{1,0:T(8,128)(2,1)S(1)} collective-permute-done((bf16[192,2560]{1,0:T(8,128)(2,1)S(1)}, bf16[192,2560]{1,0:T(8,128)(2,1)S(1)}, u32[]{:S(2)}, u32[]{:S(2)}) %collective-permute-start.20) | collective-permute-done | bytes 983072 | tf_op jit(solution)/shard_map/ppermute | solution.py:13
  147.0 8.1 %collective-permute-done.25 = bf16[128,1280]{1,0:T(8,128)(2,1)S(1)} collective-permute-done((bf16[128,1280]{1,0:T(8,128)(2,1)S(1)}, bf16[128,1280]{1,0:T(8,128)(2,1)S(1)}, u32[]{:S(2)}, u32[]{:S(2)}) %collective-permute-start.25) | collective-permute-done | bytes 327712 | tf_op jit(solution)/shard_map/ppermute | solution.py:56
  155.1 1.5 fusion.23
  156.6 0.9 copy.8
  (60 shorter events, 0.8 us)
Async XLA Ops:
  0.6 40.2 %copy-start.2 = (bf16[1,128,2560]{2,1,0:T(8,128)(2,1)S(1)}, bf16[1,128,2560]{2,1,0:T(8,128)(2,1)}, u32[]{:S(2)}) copy-start(bf16[1,128,2560]{2,1,0:T(8,128)(2,1)} %param.5) | copy-start | bytes 1966084
  0.6 40.2 %copy-start.12 = (bf16[1,192,2560]{2,1,0:T(8,128)(2,1)S(1)}, bf16[1,192,2560]{2,1,0:T(8,128)(2,1)}, u32[]{:S(2)}) copy-start(bf16[1,192,2560]{2,1,0:T(8,128)(2,1)} %param.4) | copy-start | bytes 2949124
  0.7 19.1 %collective-permute-start.2 = (bf16[128,2560]{1,0:T(8,128)(2,1)}, bf16[128,2560]{1,0:T(8,128)(2,1)S(1)}, u32[]{:S(2)}, u32[]{:S(2)}) collective-permute-start(bf16[128,2560]{1,0:T(8,128)(2,1)} %bitcast.19), channel_id=1, source_target_pairs={{0,2},{6,4},{1,3},{7,5},{8,10},{14,12},{9,11},{15,13},{16,18},{22,... | collective-permute-start | bytes 1966088 | tf_op jit(solution)/shard_map/ppermute | solution.py:48
  4.3 36.5 %collective-permute-start = (bf16[192,2560]{1,0:T(8,128)(2,1)}, bf16[192,2560]{1,0:T(8,128)(2,1)S(1)}, u32[]{:S(2)}, u32[]{:S(2)}) collective-permute-start(bf16[192,2560]{1,0:T(8,128)(2,1)} %bitcast.24), channel_id=1, source_target_pairs={{0,2},{6,4},{1,3},{7,5},{8,10},{14,12},{9,11},{15,13},{16,18},{22,... | collective-permute-start | bytes 2949128 | tf_op jit(solution)/shard_map/ppermute | solution.py:48
  5.7 18.3 %collective-permute-start.1 = (bf16[128,2560]{1,0:T(8,128)(2,1)}, bf16[128,2560]{1,0:T(8,128)(2,1)S(1)}, u32[]{:S(2)}, u32[]{:S(2)}) collective-permute-start(bf16[128,2560]{1,0:T(8,128)(2,1)} %bitcast.20), channel_id=1, source_target_pairs={{2,0},{4,6},{3,1},{5,7},{10,8},{12,14},{11,9},{13,15},{18,16},{20,... | collective-permute-start | bytes 1966088 | tf_op jit(solution)/shard_map/ppermute | solution.py:56
  7.0 33.8 %collective-permute-start.3 = (bf16[128,2560]{1,0:T(8,128)(2,1)}, bf16[128,2560]{1,0:T(8,128)(2,1)S(1)}, u32[]{:S(2)}, u32[]{:S(2)}) collective-permute-start(bf16[128,2560]{1,0:T(8,128)(2,1)} %bitcast.21), channel_id=1, source_target_pairs={{2,4},{4,2},{3,5},{5,3},{10,12},{12,10},{11,13},{13,11},{18,20},{2... | collective-permute-start | bytes 1966088 | tf_op jit(solution)/shard_map/ppermute | solution.py:52
  19.7 22.3 %copy-start.4 = (bf16[128,2560]{1,0:T(8,128)(2,1)}, bf16[128,2560]{1,0:T(8,128)(2,1)S(1)}, u32[]{:S(2)}) copy-start(bf16[128,2560]{1,0:T(8,128)(2,1)S(1)} %collective-permute-done.2) | copy-start | bytes 1966084
  19.7 21.1 %collective-permute-start.4 = (bf16[128,2560]{1,0:T(8,128)(2,1)S(1)}, bf16[128,2560]{1,0:T(8,128)(2,1)S(1)}, u32[]{:S(2)}, u32[]{:S(2)}) collective-permute-start(bf16[128,2560]{1,0:T(8,128)(2,1)S(1)} %collective-permute-done.2), channel_id=1, source_target_pairs={{2,4},{4,2},{3,5},{5,3},{10,12},{12,10},{11,13},{13,11},{18,20},{2... | collective-permute-start | bytes 1966088 | tf_op jit(solution)/shard_map/ppermute | solution.py:52
  20.4 46.9 %collective-permute-start.7 = (bf16[192,4096]{1,0:T(8,128)(2,1)}, bf16[192,4096]{1,0:T(8,128)(2,1)S(1)}, u32[]{:S(2)}, u32[]{:S(2)}) collective-permute-start(bf16[192,4096]{1,0:T(8,128)(2,1)} %bitcast.12), channel_id=1, source_target_pairs={{2,4},{4,2},{3,5},{5,3},{10,12},{12,10},{11,13},{13,11},{18,20},{2... | collective-permute-start | bytes 4718600 | tf_op jit(solution)/shard_map/ppermute | solution.py:52
  24.0 16.8 %copy-start.6 = (bf16[128,2560]{1,0:T(8,128)(2,1)}, bf16[128,2560]{1,0:T(8,128)(2,1)S(1)}, u32[]{:S(2)}) copy-start(bf16[128,2560]{1,0:T(8,128)(2,1)S(1)} %collective-permute-done.1) | copy-start | bytes 1966084
  24.0 33.6 %collective-permute-start.6 = (bf16[192,2048]{1,0:T(8,128)(2,1)}, bf16[192,2048]{1,0:T(8,128)(2,1)}, u32[]{:S(2)}, u32[]{:S(2)}) collective-permute-start(bf16[192,2048]{1,0:T(8,128)(2,1)} %get-tuple-element.32), channel_id=1, source_target_pairs={{0,2},{6,4},{1,3},{7,5},{8,10},{14,12},{9,11},{15,13},{16,18},{22,... | collective-permute-start | bytes 2359304 | tf_op jit(solution)/shard_map/ppermute | solution.py:48
  40.8 1.3 copy-start.14
  40.8 1.3 copy-start.8
  40.8 1.3 copy-start.10
  42.2 22.3 %copy-start = (bf16[1,128,4096]{2,1,0:T(8,128)(2,1)S(1)}, bf16[1,128,4096]{2,1,0:T(8,128)(2,1)}, u32[]{:S(2)}) copy-start(bf16[1,128,4096]{2,1,0:T(8,128)(2,1)} %param.6) | copy-start | bytes 3145732
  42.2 16.2 %collective-permute-start.5 = (bf16[384,512]{1,0:T(8,128)(2,1)S(1)}, bf16[384,512]{1,0:T(8,128)(2,1)S(1)}, u32[]{:S(2)}, u32[]{:S(2)}) collective-permute-start(bf16[384,512]{1,0:T(8,128)(2,1)S(1)} %convolution_convert_fusion.6), channel_id=1, source_target_pairs={{0,1},{1,0},{2,3},{3,2},{4,5},{5,4},{6,7},{7,6},{8,9},{9,8},{10,11... | collective-permute-start | bytes 1179656 | tf_op jit(solution)/shard_map/ppermute | solution.py:60
  43.7 30.8 %collective-permute-start.13 = (bf16[192,2048]{1,0:T(8,128)(2,1)}, bf16[192,2048]{1,0:T(8,128)(2,1)S(1)}, u32[]{:S(2)}, u32[]{:S(2)}) collective-permute-start(bf16[192,2048]{1,0:T(8,128)(2,1)} %get-tuple-element.21), channel_id=1, source_target_pairs={{0,2},{6,4},{1,3},{7,5},{8,10},{14,12},{9,11},{15,13},{16,18},{22,... | collective-permute-start | bytes 2359304 | tf_op jit(solution)/shard_map/ppermute | solution.py:48
  48.3 16.2 %collective-permute-start.10 = (bf16[128,2560]{1,0:T(8,128)(2,1)}, bf16[128,2560]{1,0:T(8,128)(2,1)S(1)}, u32[]{:S(2)}, u32[]{:S(2)}) collective-permute-start(bf16[128,2560]{1,0:T(8,128)(2,1)} %copy-done.8), channel_id=1, source_target_pairs={{2,0},{4,6},{3,1},{5,7},{10,8},{12,14},{11,9},{13,15},{18,16},{20,... | collective-permute-start | bytes 1966088 | tf_op jit(solution)/shard_map/ppermute | solution.py:56
  57.6 20.4 %collective-permute-start.8 = (bf16[192,2048]{1,0:T(8,128)(2,1)}, bf16[192,2048]{1,0:T(8,128)(2,1)S(1)}, u32[]{:S(2)}, u32[]{:S(2)}) collective-permute-start(bf16[192,2048]{1,0:T(8,128)(2,1)} %collective-permute-done.6), channel_id=1, source_target_pairs={{2,4},{4,2},{3,5},{5,3},{10,12},{12,10},{11,13},{13,11},{18,20},{2... | collective-permute-start | bytes 2359304 | tf_op jit(solution)/shard_map/ppermute | solution.py:52
  58.3 19.7 %collective-permute-start.12 = (bf16[128,2560]{1,0:T(8,128)(2,1)}, bf16[128,2560]{1,0:T(8,128)(2,1)S(1)}, u32[]{:S(2)}, u32[]{:S(2)}) collective-permute-start(bf16[128,2560]{1,0:T(8,128)(2,1)} %copy-done.10), channel_id=1, source_target_pairs={{2,0},{4,6},{3,1},{5,7},{10,8},{12,14},{11,9},{13,15},{18,16},{20,... | collective-permute-start | bytes 1966088 | tf_op jit(solution)/shard_map/ppermute | solution.py:56
  64.4 31.3 %collective-permute-start.9 = (bf16[128,4096]{1,0:T(8,128)(2,1)S(1)}, bf16[128,4096]{1,0:T(8,128)(2,1)S(1)}, u32[]{:S(2)}, u32[]{:S(2)}) collective-permute-start(bf16[128,4096]{1,0:T(8,128)(2,1)S(1)} %bitcast.14), channel_id=1, source_target_pairs={{0,2},{6,4},{1,3},{7,5},{8,10},{14,12},{9,11},{15,13},{16,18},{22,... | collective-permute-start | bytes 3145736 | tf_op jit(solution)/shard_map/ppermute | solution.py:48
  67.3 7.8 %collective-permute-start.11 = (bf16[384,256]{1,0:T(8,128)(2,1)S(1)}, bf16[384,256]{1,0:T(8,128)(2,1)S(1)}, u32[]{:S(2)}, u32[]{:S(2)}) collective-permute-start(bf16[384,256]{1,0:T(8,128)(2,1)S(1)} %get-tuple-element.18), channel_id=1, source_target_pairs={{2,4},{4,2},{3,5},{5,3},{10,12},{12,10},{11,13},{13,11},{18,20},{2... | collective-permute-start | bytes 589832 | tf_op jit(solution)/shard_map/ppermute | solution.py:52
  74.5 32.6 %collective-permute-start.15 = (bf16[192,2048]{1,0:T(8,128)(2,1)S(1)}, bf16[192,2048]{1,0:T(8,128)(2,1)S(1)}, u32[]{:S(2)}, u32[]{:S(2)}) collective-permute-start(bf16[192,2048]{1,0:T(8,128)(2,1)S(1)} %collective-permute-done.13), channel_id=1, source_target_pairs={{2,4},{4,2},{3,5},{5,3},{10,12},{12,10},{11,13},{13,11},{18,20},{2... | collective-permute-start | bytes 2359304 | tf_op jit(solution)/shard_map/ppermute | solution.py:52
  78.0 2.6 %copy-start.3 = (bf16[1,128,2560]{2,1,0:T(8,128)(2,1)S(1)}, bf16[1,128,2560]{2,1,0:T(8,128)(2,1)}, u32[]{:S(2)}) copy-start(bf16[1,128,2560]{2,1,0:T(8,128)(2,1)} %param.5) | copy-start | bytes 1966084
  78.0 2.6 %copy-start.5 = (bf16[128,2560]{1,0:T(8,128)(2,1)S(1)}, bf16[128,2560]{1,0:T(8,128)(2,1)}, u32[]{:S(2)}) copy-start(bf16[128,2560]{1,0:T(8,128)(2,1)} %copy-done.4) | copy-start | bytes 1966084
  78.0 2.6 %copy-start.7 = (bf16[128,2560]{1,0:T(8,128)(2,1)S(1)}, bf16[128,2560]{1,0:T(8,128)(2,1)}, u32[]{:S(2)}) copy-start(bf16[128,2560]{1,0:T(8,128)(2,1)} %copy-done.6) | copy-start | bytes 1966084
  78.0 2.6 %copy-start.9 = (bf16[128,2560]{1,0:T(8,128)(2,1)S(1)}, bf16[128,2560]{1,0:T(8,128)(2,1)}, u32[]{:S(2)}) copy-start(bf16[128,2560]{1,0:T(8,128)(2,1)} %copy-done.8) | copy-start | bytes 1966084
  78.1 2.6 %copy-start.11 = (bf16[128,2560]{1,0:T(8,128)(2,1)S(1)}, bf16[128,2560]{1,0:T(8,128)(2,1)}, u32[]{:S(2)}) copy-start(bf16[128,2560]{1,0:T(8,128)(2,1)} %copy-done.10) | copy-start | bytes 1966084
  81.4 16.7 %copy-start.1 = (bf16[192,2048]{1,0:T(8,128)(2,1)S(1)}, bf16[192,2048]{1,0:T(8,128)(2,1)}, u32[]{:S(2)}) copy-start(bf16[192,2048]{1,0:T(8,128)(2,1)} %get-tuple-element.21) | copy-start | bytes 2359300
  99.0 7.9 %collective-permute-start.14 = (bf16[576,256]{1,0:T(8,128)(2,1)S(1)}, bf16[576,256]{1,0:T(8,128)(2,1)S(1)}, u32[]{:S(2)}, u32[]{:S(2)}) collective-permute-start(bf16[576,256]{1,0:T(8,128)(2,1)S(1)} %fusion.25), channel_id=1, source_target_pairs={{0,1},{1,0},{2,3},{3,2},{4,5},{5,4},{6,7},{7,6},{8,9},{9,8},{10,11... | collective-permute-start | bytes 884744 | tf_op jit(solution)/shard_map/ppermute | solution.py:60
  100.6 15.7 %collective-permute-start.17 = (bf16[128,2048]{1,0:T(8,128)(2,1)S(1)}, bf16[128,2048]{1,0:T(8,128)(2,1)S(1)}, u32[]{:S(2)}, u32[]{:S(2)}) collective-permute-start(bf16[128,2048]{1,0:T(8,128)(2,1)S(1)} %slice.122), channel_id=1, source_target_pairs={{2,0},{4,6},{3,1},{5,7},{10,8},{12,14},{11,9},{13,15},{18,16},{20,... | collective-permute-start | bytes 1572872 | tf_op jit(solution)/shard_map/ppermute | solution.py:56
  107.6 4.7 %collective-permute-start.16 = (bf16[192,256]{1,0:T(8,128)(2,1)S(1)}, bf16[192,256]{1,0:T(8,128)(2,1)S(1)}, u32[]{:S(2)}, u32[]{:S(2)}) collective-permute-start(bf16[192,256]{1,0:T(8,128)(2,1)S(1)} %fusion.26), channel_id=1, source_target_pairs={{0,1},{1,0},{2,3},{3,2},{4,5},{5,4},{6,7},{7,6},{8,9},{9,8},{10,11... | collective-permute-start | bytes 294920 | tf_op jit(solution)/shard_map/ppermute | solution.py:60
  110.4 28.6 %collective-permute-start.26 = (bf16[128,2048]{1,0:T(8,128)(2,1)S(1)}, bf16[128,2048]{1,0:T(8,128)(2,1)S(1)}, u32[]{:S(2)}, u32[]{:S(2)}) collective-permute-start(bf16[128,2048]{1,0:T(8,128)(2,1)S(1)} %slice.135), channel_id=1, source_target_pairs={{2,0},{4,6},{3,1},{5,7},{10,8},{12,14},{11,9},{13,15},{18,16},{20,... | collective-permute-start | bytes 1572872 | tf_op jit(solution)/shard_map/ppermute | solution.py:56
  116.3 0.8 collective-permute-start.18
  117.1 1.2 copy-start.13
  117.1 1.5 copy-start.15
  119.7 13.2 %collective-permute-start.19 = (bf16[192,512]{1,0:T(8,128)(2,1)S(1)}, bf16[192,512]{1,0:T(8,128)(2,1)S(1)}, u32[]{:S(2)}, u32[]{:S(2)}) collective-permute-start(bf16[192,512]{1,0:T(8,128)(2,1)S(1)} %slice.124), channel_id=1, source_target_pairs={{2,0},{4,6},{3,1},{5,7},{10,8},{12,14},{11,9},{13,15},{18,16},{20,... | collective-permute-start | bytes 589832 | tf_op jit(solution)/shard_map/ppermute | solution.py:56
  121.0 14.4 %collective-permute-start.21 = (bf16[128,1280]{1,0:T(8,128)(2,1)S(1)}, bf16[128,1280]{1,0:T(8,128)(2,1)S(1)}, u32[]{:S(2)}, u32[]{:S(2)}) collective-permute-start(bf16[128,1280]{1,0:T(8,128)(2,1)S(1)} %get-tuple-element.34), channel_id=1, source_target_pairs={{2,4},{4,2},{3,5},{5,3},{10,12},{12,10},{11,13},{13,11},{18,20},{2... | collective-permute-start | bytes 983048 | tf_op jit(solution)/shard_map/ppermute | solution.py:52
  122.2 15.3 %collective-permute-start.24 = (bf16[128,1280]{1,0:T(8,128)(2,1)S(1)}, bf16[128,1280]{1,0:T(8,128)(2,1)S(1)}, u32[]{:S(2)}, u32[]{:S(2)}) collective-permute-start(bf16[128,1280]{1,0:T(8,128)(2,1)S(1)} %get-tuple-element.33), channel_id=1, source_target_pairs={{2,4},{4,2},{3,5},{5,3},{10,12},{12,10},{11,13},{13,11},{18,20},{2... | collective-permute-start | bytes 983048 | tf_op jit(solution)/shard_map/ppermute | solution.py:52
  133.5 13.5 %collective-permute-start.20 = (bf16[192,2560]{1,0:T(8,128)(2,1)S(1)}, bf16[192,2560]{1,0:T(8,128)(2,1)S(1)}, u32[]{:S(2)}, u32[]{:S(2)}) collective-permute-start(bf16[192,2560]{1,0:T(8,128)(2,1)S(1)} %convolution_convert_fusion), channel_id=1, source_target_pairs={{8,0},{16,8},{24,16},{9,1},{17,9},{25,17},{10,2},{18,10},{26,18},{... | collective-permute-start | bytes 2949128 | tf_op jit(solution)/shard_map/ppermute | solution.py:13
  135.5 19.6 %collective-permute-start.23 = (bf16[128,1280]{1,0:T(8,128)(2,1)S(1)}, bf16[128,1280]{1,0:T(8,128)(2,1)S(1)}, u32[]{:S(2)}, u32[]{:S(2)}) collective-permute-start(bf16[128,1280]{1,0:T(8,128)(2,1)S(1)} %add_convert_fusion.2), channel_id=1, source_target_pairs={{2,0},{4,6},{3,1},{5,7},{10,8},{12,14},{11,9},{13,15},{18,16},{20,... | collective-permute-start | bytes 983048 | tf_op jit(solution)/shard_map/ppermute | solution.py:56
  136.8 10.2 %collective-permute-start.22 = (bf16[128,2560]{1,0:T(8,128)(2,1)S(1)}, bf16[128,2560]{1,0:T(8,128)(2,1)S(1)}, u32[]{:S(2)}, u32[]{:S(2)}) collective-permute-start(bf16[128,2560]{1,0:T(8,128)(2,1)S(1)} %convolution_convert_fusion.3), channel_id=1, source_target_pairs={{2,4},{4,2},{3,5},{5,3},{10,12},{12,10},{11,13},{13,11},{18,20},{2... | collective-permute-start | bytes 1966088 | tf_op jit(solution)/shard_map/ppermute | solution.py:52
  137.7 17.5 %collective-permute-start.25 = (bf16[128,1280]{1,0:T(8,128)(2,1)S(1)}, bf16[128,1280]{1,0:T(8,128)(2,1)S(1)}, u32[]{:S(2)}, u32[]{:S(2)}) collective-permute-start(bf16[128,1280]{1,0:T(8,128)(2,1)S(1)} %add_convert_fusion.1), channel_id=1, source_target_pairs={{2,0},{4,6},{3,1},{5,7},{10,8},{12,14},{11,9},{13,15},{18,16},{20,... | collective-permute-start | bytes 983048 | tf_op jit(solution)/shard_map/ppermute | solution.py:56

commit v10 on v9

--- a/solution.py
+++ b/solution.py
@@ -137,8 +137,6 @@
     normed_grad = jnp.concatenate([early_sum[: 2 * rows], from_across.astype(F32)], axis=1)
     inner = jnp.mean(normed_grad * normed, axis=-1, keepdims=True)
     latent_bf = (inv_rms * (normed_grad - normed * inner)).astype(BF16)
-    latent_there = outward(latent_bf[rows:])
-    latent_used = jnp.where(middle, latent_bf[:rows], latent_there)
 
     sums = [
         tokens_dot(latent_bf[:, j * lat : (j + 1) * lat], tokens_mine).astype(BF16)
@@ -161,11 +159,13 @@
         axis=1,
     )
 
+    latent_there = outward(latent_bf[rows:])
+    latent_used = jnp.where(middle, latent_bf[:rows], after(latent_there, end_first))
     input_grad = jnp.dot(latent_used, down_used, preferred_element_type=F32).astype(BF16)
-    passed = shifted(input_grad, "section", -1)
+    passed = shifted(input_grad[None], "section", -1)
     down_own_grad = (sums[0] + after(from_own, passed).astype(F32)).astype(BF16)
     down_grad = jnp.where(middle, down_own_grad, down_end_grad)
-    return (passed[None], down_grad[None], up_grad[None])
+    return (passed, down_grad[None], up_grad[None])
 
 
 def solution(mesh):

time: 160 us -> 165 us (1.031)
  the two profiles are of different devices: /device:TPU:4 before, /device:TPU:14 now
where the time goes in v10:
time: 165 us; the launch traced here: 164 us
  waiting for transfers between devices  84.5 us (51%)
  starting transfers between devices  58.3 us (35%)
  matrix products  12.5 us (8%)
  local copies, waits for them, and re-layouts  4.03 us (2%)
  other arithmetic  3.12 us (2%)
    ppermute x10, waiting for transfers between devices, across(): return lax.ppermute(value, 'row', [(1, 2), (2, 1)])  49.2 us
    ppermute x10, starting transfers between devices, across(): return lax.ppermute(value, 'row', [(1, 2), (2, 1)])  30.8 us
    ppermute x5, waiting for transfers between devices, inward(): return lax.ppermute(value, 'row', [(0, 1), (3, 2)])  29 us
    ppermute x8, starting transfers between devices, outward(): return lax.ppermute(value, 'row', [(1, 0), (2, 3)])  17.2 us
    dot_general x6, matrix products, tokens_dot(): lax.dot_general(left, right, (((0,), (0,)), ((), ())), preferred_element_...  6.8 us
    ppermute x5, starting transfers between devices, inward(): return lax.ppermute(value, 'row', [(0, 1), (3, 2)])  6.57 us
    ppermute x3, waiting for transfers between devices, other_col(): return lax.ppermute(value, 'col', [(0, 1), (1, 0)])  6.31 us
    dot_general x4, matrix products, rows_dot(): lax.dot_general(left, right, (((1,), (1,)), ((), ())), preferred_element_...  5.05 us
  transfers between devices with their start and end apart: 27, of which 12 were waited for; matrix products, arithmetic and copies ran while one was open for 11% of the time, Pallas kernels for 0%

profile of v10, /device:TPU:14, one launch (start us, length us, event | category | flops | bytes accessed | tf_op | source)
XLA Modules:
  0.0 163.8 jit_solution(5683150321419707940)
XLA Ops:
  0.7 1.4 collective-permute-start.2
  2.1 1.3 collective-permute-start
  3.4 4.7 %collective-permute-start.1 = (bf16[128,2560]{1,0:T(8,128)(2,1)}, bf16[128,2560]{1,0:T(8,128)(2,1)S(1)}, u32[]{:S(2)}, u32[]{:S(2)}) collective-permute-start(bf16[128,2560]{1,0:T(8,128)(2,1)} %bitcast.20), channel_id=1, source_target_pairs={{2,0},{4,6},{3,1},{5,7},{10,8},{12,14},{11,9},{13,15},{18,16},{20,... | collective-permute-start | bytes 1966088 | tf_op jit(solution)/shard_map/ppermute | solution.py:56
  8.1 3.5 %collective-permute-start.3 = (bf16[128,2560]{1,0:T(8,128)(2,1)}, bf16[128,2560]{1,0:T(8,128)(2,1)S(1)}, u32[]{:S(2)}, u32[]{:S(2)}) collective-permute-start(bf16[128,2560]{1,0:T(8,128)(2,1)} %bitcast.21), channel_id=1, source_target_pairs={{2,4},{4,2},{3,5},{5,3},{10,12},{12,10},{11,13},{13,11},{18,20},{2... | collective-permute-start | bytes 1966088 | tf_op jit(solution)/shard_map/ppermute | solution.py:52
  11.6 8.9 %collective-permute-done.2 = bf16[128,2560]{1,0:T(8,128)(2,1)S(1)} collective-permute-done((bf16[128,2560]{1,0:T(8,128)(2,1)}, bf16[128,2560]{1,0:T(8,128)(2,1)S(1)}, u32[]{:S(2)}, u32[]{:S(2)}) %collective-permute-start.2) | collective-permute-done | bytes 655392 | tf_op jit(solution)/shard_map/ppermute | solution.py:48
  20.5 3.5 %collective-permute-start.4 = (bf16[128,2560]{1,0:T(8,128)(2,1)S(1)}, bf16[128,2560]{1,0:T(8,128)(2,1)S(1)}, u32[]{:S(2)}, u32[]{:S(2)}) collective-permute-start(bf16[128,2560]{1,0:T(8,128)(2,1)S(1)} %collective-permute-done.2), channel_id=1, source_target_pairs={{2,4},{4,2},{3,5},{5,3},{10,12},{12,10},{11,13},{13,11},{18,20},{2... | collective-permute-start | bytes 1966088 | tf_op jit(solution)/shard_map/ppermute | solution.py:52
  24.0 2.4 %collective-permute-start.7 = (bf16[192,4096]{1,0:T(8,128)(2,1)}, bf16[192,4096]{1,0:T(8,128)(2,1)S(1)}, u32[]{:S(2)}, u32[]{:S(2)}) collective-permute-start(bf16[192,4096]{1,0:T(8,128)(2,1)} %bitcast.13), channel_id=1, source_target_pairs={{2,4},{4,2},{3,5},{5,3},{10,12},{12,10},{11,13},{13,11},{18,20},{2... | collective-permute-start | bytes 4718600 | tf_op jit(solution)/shard_map/ppermute | solution.py:52
  26.4 2.7 %fusion.45 = (bf16[192,2048]{1,0:T(8,128)(2,1)}, bf16[192,2048]{1,0:T(8,128)(2,1)}) fusion(bf16[192,4096]{1,0:T(8,128)(2,1)} %bitcast.14), kind=kLoop, calls=%fused_computation.73 | loop fusion | bytes 3145728 | tf_op jit(solution)/shard_map/slice | solution.py:119
  29.1 1.3 collective-permute-start.6
  30.4 11.2 %collective-permute-done = bf16[192,2560]{1,0:T(8,128)(2,1)S(1)} collective-permute-done((bf16[192,2560]{1,0:T(8,128)(2,1)}, bf16[192,2560]{1,0:T(8,128)(2,1)S(1)}, u32[]{:S(2)}, u32[]{:S(2)}) %collective-permute-start) | collective-permute-done | bytes 983072 | tf_op jit(solution)/shard_map/ppermute | solution.py:48
  41.6 0.3 collective-permute-done.4
  41.9 1.2 convolution_convert_fusion.6
  43.2 0.6 collective-permute-start.5
  43.8 1.3 collective-permute-start.13
  45.1 4.6 %collective-permute-start.10 = (bf16[128,2560]{1,0:T(8,128)(2,1)}, bf16[128,2560]{1,0:T(8,128)(2,1)S(1)}, u32[]{:S(2)}, u32[]{:S(2)}) collective-permute-start(bf16[128,2560]{1,0:T(8,128)(2,1)} %copy-done.8), channel_id=1, source_target_pairs={{2,0},{4,6},{3,1},{5,7},{10,8},{12,14},{11,9},{13,15},{18,16},{20,... | collective-permute-start | bytes 1966088 | tf_op jit(solution)/shard_map/ppermute | solution.py:56
  49.7 8.8 %collective-permute-done.6 = bf16[192,2048]{1,0:T(8,128)(2,1)} collective-permute-done((bf16[192,2048]{1,0:T(8,128)(2,1)}, bf16[192,2048]{1,0:T(8,128)(2,1)}, u32[]{:S(2)}, u32[]{:S(2)}) %collective-permute-start.6) | collective-permute-done | bytes 786464 | tf_op jit(solution)/shard_map/ppermute | solution.py:48
  58.5 3.5 %collective-permute-start.8 = (bf16[192,2048]{1,0:T(8,128)(2,1)}, bf16[192,2048]{1,0:T(8,128)(2,1)S(1)}, u32[]{:S(2)}, u32[]{:S(2)}) collective-permute-start(bf16[192,2048]{1,0:T(8,128)(2,1)} %collective-permute-done.6), channel_id=1, source_target_pairs={{2,4},{4,2},{3,5},{5,3},{10,12},{12,10},{11,13},{13,11},{18,20},{2... | collective-permute-start | bytes 2359304 | tf_op jit(solution)/shard_map/ppermute | solution.py:52
  62.0 1.3 collective-permute-start.12
  63.4 0.2 multiply_reduce_fusion.1
  63.6 0.1 fusion.25
  63.8 1.3 collective-permute-start.9
  65.1 10.5 %collective-permute-done.7 = bf16[192,4096]{1,0:T(8,128)(2,1)S(1)} collective-permute-done((bf16[192,4096]{1,0:T(8,128)(2,1)}, bf16[192,4096]{1,0:T(8,128)(2,1)S(1)}, u32[]{:S(2)}, u32[]{:S(2)}) %collective-permute-start.7) | collective-permute-done | bytes 1572896 | tf_op jit(solution)/shard_map/ppermute | solution.py:52
  75.6 3.5 %collective-permute-start.11 = (bf16[384,256]{1,0:T(8,128)(2,1)S(1)}, bf16[384,256]{1,0:T(8,128)(2,1)S(1)}, u32[]{:S(2)}, u32[]{:S(2)}) collective-permute-start(bf16[384,256]{1,0:T(8,128)(2,1)S(1)} %get-tuple-element.19), channel_id=1, source_target_pairs={{2,4},{4,2},{3,5},{5,3},{10,12},{12,10},{11,13},{13,11},{18,20},{2... | collective-permute-start | bytes 589832 | tf_op jit(solution)/shard_map/ppermute | solution.py:52
  79.1 0.1 fusion.44
  79.2 2.4 %collective-permute-start.15 = (bf16[192,2048]{1,0:T(8,128)(2,1)S(1)}, bf16[192,2048]{1,0:T(8,128)(2,1)S(1)}, u32[]{:S(2)}, u32[]{:S(2)}) collective-permute-start(bf16[192,2048]{1,0:T(8,128)(2,1)S(1)} %collective-permute-done.13), channel_id=1, source_target_pairs={{2,4},{4,2},{3,5},{5,3},{10,12},{12,10},{11,13},{13,11},{18,20},{2... | collective-permute-start | bytes 2359304 | tf_op jit(solution)/shard_map/ppermute | solution.py:52
  81.6 15.1 %collective-permute-done.11 = bf16[384,256]{1,0:T(8,128)(2,1)S(1)} collective-permute-done((bf16[384,256]{1,0:T(8,128)(2,1)S(1)}, bf16[384,256]{1,0:T(8,128)(2,1)S(1)}, u32[]{:S(2)}, u32[]{:S(2)}) %collective-permute-start.11) | collective-permute-done | bytes 196640 | tf_op jit(solution)/shard_map/ppermute | solution.py:52
  96.8 2.5 %convolution_convert_fusion.5 = bf16[256,2048]{1,0:T(8,128)(2,1)S(1)} fusion(bf16[768,256]{1,0:T(8,128)(2,1)S(1)} %pad_maximum_fusion.8, bf16[192,2048]{1,0:T(8,128)(2,1)S(1)} %collective-permute-done.8, bf16[192,2048]{1,0:T(8,128)(2,1)S(1)} %get-tuple-element.32, bf16[192,2048]{1,0:T(8,128)(2,1)} %collective-permute-done.6, ...), kind=kOutput, calls=%fused_computation.19 | convolution fusion | flops 818413568 | bytes 4587520 | tf_op jit(solution)/shard_map/dot_general | solution.py:72
  99.4 0.7 maximum_select_fusion
  100.1 2.5 %fusion.20 = f32[768,256]{1,0:T(8,128)S(1)} fusion(bf16[128,4096]{1,0:T(8,128)(2,1)S(1)} %bitcast.16, bf16[128,4096]{1,0:T(8,128)(2,1)S(1)} %collective-permute-done.9, bf16[192,2048]{1,0:T(8,128)(2,1)S(1)} %collective-permute-done.8, bf16[192,2048]{1,0:T(8,128)(2,1)S(1)} %get-tuple-element.32, bf16[192,2048]{1,0:T(8,128)(2,1)} %collective-permute-done.6, ...), kind=kOutput, calls=%fused_computation.32 | convolution fusion | flops 819986432 | bytes 6029312 | tf_op jit(solution)/shard_map/dot_general | solution.py:68
  102.6 0.9 fusion.26
  103.5 0.6 collective-permute-start.14
  104.1 1.3 collective-permute-start.17
  105.5 4.8 %collective-permute-done.14 = bf16[576,256]{1,0:T(8,128)(2,1)S(1)} collective-permute-done((bf16[576,256]{1,0:T(8,128)(2,1)S(1)}, bf16[576,256]{1,0:T(8,128)(2,1)S(1)}, u32[]{:S(2)}, u32[]{:S(2)}) %collective-permute-start.14) | collective-permute-done | bytes 294944 | tf_op jit(solution)/shard_map/ppermute | solution.py:60
  110.3 0.1 convert_add_fusion.1
  110.4 1.4 collective-permute-done.15
  111.8 0.5 fusion.27
  112.3 0.6 collective-permute-start.16
  112.9 1.2 fusion.10
  114.1 1.3 collective-permute-start.26
  115.5 1.5 collective-permute-done.16
  117.1 3.6 %collective-permute-start.18 = (bf16[384,256]{1,0:T(8,128)(2,1)S(1)}, bf16[384,256]{1,0:T(8,128)(2,1)S(1)}, u32[]{:S(2)}, u32[]{:S(2)}) collective-permute-start(bf16[384,256]{1,0:T(8,128)(2,1)S(1)} %pad_maximum_fusion.9), channel_id=1, source_target_pairs={{2,4},{4,2},{3,5},{5,3},{10,12},{12,10},{11,13},{13,11},{18,20},{2... | collective-permute-start | bytes 589832 | tf_op jit(solution)/shard_map/ppermute | solution.py:52
  120.7 0.1 slice_select_fusion.1
  120.7 4.0 %collective-permute-done.18 = bf16[384,256]{1,0:T(8,128)(2,1)S(1)} collective-permute-done((bf16[384,256]{1,0:T(8,128)(2,1)S(1)}, bf16[384,256]{1,0:T(8,128)(2,1)S(1)}, u32[]{:S(2)}, u32[]{:S(2)}) %collective-permute-start.18) | collective-permute-done | bytes 196640 | tf_op jit(solution)/shard_map/ppermute | solution.py:52
  124.8 0.3 multiply_reduce_fusion
  125.1 0.2 multiply_convert_fusion
  125.3 0.5 convolution_convert_fusion.3
  125.9 3.5 %collective-permute-start.20 = (bf16[128,1280]{1,0:T(8,128)(2,1)S(1)}, bf16[128,1280]{1,0:T(8,128)(2,1)S(1)}, u32[]{:S(2)}, u32[]{:S(2)}) collective-permute-start(bf16[128,1280]{1,0:T(8,128)(2,1)S(1)} %get-tuple-element.36), channel_id=1, source_target_pairs={{2,4},{4,2},{3,5},{5,3},{10,12},{12,10},{11,13},{13,11},{18,20},{2... | collective-permute-start | bytes 983048 | tf_op jit(solution)/shard_map/ppermute | solution.py:52
  129.4 0.5 convolution_convert_fusion.4
  130.0 1.3 collective-permute-start.19
  131.3 2.4 %collective-permute-start.24 = (bf16[128,1280]{1,0:T(8,128)(2,1)S(1)}, bf16[128,1280]{1,0:T(8,128)(2,1)S(1)}, u32[]{:S(2)}, u32[]{:S(2)}) collective-permute-start(bf16[128,1280]{1,0:T(8,128)(2,1)S(1)} %get-tuple-element.35), channel_id=1, source_target_pairs={{2,4},{4,2},{3,5},{5,3},{10,12},{12,10},{11,13},{13,11},{18,20},{2... | collective-permute-start | bytes 983048 | tf_op jit(solution)/shard_map/ppermute | solution.py:52
  133.7 0.5 convolution_convert_fusion.1
  134.2 4.0 %collective-permute-done.20 = bf16[128,1280]{1,0:T(8,128)(2,1)S(1)} collective-permute-done((bf16[128,1280]{1,0:T(8,128)(2,1)S(1)}, bf16[128,1280]{1,0:T(8,128)(2,1)S(1)}, u32[]{:S(2)}, u32[]{:S(2)}) %collective-permute-start.20) | collective-permute-done | bytes 327712 | tf_op jit(solution)/shard_map/ppermute | solution.py:52
  138.2 0.1 add_convert_fusion.2
  138.3 1.3 collective-permute-start.23
  139.7 0.7 fusion
  140.4 1.9 %collective-permute-start.21 = (bf16[1,192,2560]{2,1,0:T(8,128)(2,1)S(1)}, bf16[1,192,2560]{2,1,0:T(8,128)(2,1)S(1)}, u32[]{:S(2)}, u32[]{:S(2)}) collective-permute-start(bf16[1,192,2560]{2,1,0:T(8,128)(2,1)S(1)} %fusion), channel_id=1, source_target_pairs={{8,0},{16,8},{24,16},{9,1},{17,9},{25,17},{10,2},{18,10},{26,18},{... | collective-permute-start | bytes 2949128 | tf_op jit(solution)/shard_map/ppermute | solution.py:13
  142.3 2.7 %collective-permute-start.22 = (bf16[128,2560]{1,0:T(8,128)(2,1)S(1)}, bf16[128,2560]{1,0:T(8,128)(2,1)S(1)}, u32[]{:S(2)}, u32[]{:S(2)}) collective-permute-start(bf16[128,2560]{1,0:T(8,128)(2,1)S(1)} %convolution_convert_fusion.1), channel_id=1, source_target_pairs={{2,4},{4,2},{3,5},{5,3},{10,12},{12,10},{11,13},{13,11},{18,20},{2... | collective-permute-start | bytes 1966088 | tf_op jit(solution)/shard_map/ppermute | solution.py:52
  145.0 0.1 add_convert_fusion.1
  145.1 1.3 collective-permute-start.25
  146.4 0.1 slice_select_fusion
  146.5 1.1 maximum_bitcast_fusion
  147.6 13.8 %collective-permute-done.22 = bf16[128,2560]{1,0:T(8,128)(2,1)S(1)} collective-permute-done((bf16[128,2560]{1,0:T(8,128)(2,1)S(1)}, bf16[128,2560]{1,0:T(8,128)(2,1)S(1)}, u32[]{:S(2)}, u32[]{:S(2)}) %collective-permute-start.22) | collective-permute-done | bytes 655392 | tf_op jit(solution)/shard_map/ppermute | solution.py:52
  161.4 1.5 fusion.24
  162.9 0.9 copy.8
  (60 shorter events, 0.4 us)
Async XLA Ops:
  0.6 41.3 %copy-start.2 = (bf16[1,128,2560]{2,1,0:T(8,128)(2,1)S(1)}, bf16[1,128,2560]{2,1,0:T(8,128)(2,1)}, u32[]{:S(2)}) copy-start(bf16[1,128,2560]{2,1,0:T(8,128)(2,1)} %param.5) | copy-start | bytes 1966084
  0.6 41.3 %copy-start.12 = (bf16[1,192,2560]{2,1,0:T(8,128)(2,1)S(1)}, bf16[1,192,2560]{2,1,0:T(8,128)(2,1)}, u32[]{:S(2)}) copy-start(bf16[1,192,2560]{2,1,0:T(8,128)(2,1)} %param.4) | copy-start | bytes 2949124
  0.7 19.9 %collective-permute-start.2 = (bf16[128,2560]{1,0:T(8,128)(2,1)}, bf16[128,2560]{1,0:T(8,128)(2,1)S(1)}, u32[]{:S(2)}, u32[]{:S(2)}) collective-permute-start(bf16[128,2560]{1,0:T(8,128)(2,1)} %bitcast.19), channel_id=1, source_target_pairs={{0,2},{6,4},{1,3},{7,5},{8,10},{14,12},{9,11},{15,13},{16,18},{22,... | collective-permute-start | bytes 1966088 | tf_op jit(solution)/shard_map/ppermute | solution.py:48
  2.1 39.5 %collective-permute-start = (bf16[192,2560]{1,0:T(8,128)(2,1)}, bf16[192,2560]{1,0:T(8,128)(2,1)S(1)}, u32[]{:S(2)}, u32[]{:S(2)}) collective-permute-start(bf16[192,2560]{1,0:T(8,128)(2,1)} %bitcast.24), channel_id=1, source_target_pairs={{0,2},{6,4},{1,3},{7,5},{8,10},{14,12},{9,11},{15,13},{16,18},{22,... | collective-permute-start | bytes 2949128 | tf_op jit(solution)/shard_map/ppermute | solution.py:48
  3.4 25.7 %collective-permute-start.1 = (bf16[128,2560]{1,0:T(8,128)(2,1)}, bf16[128,2560]{1,0:T(8,128)(2,1)S(1)}, u32[]{:S(2)}, u32[]{:S(2)}) collective-permute-start(bf16[128,2560]{1,0:T(8,128)(2,1)} %bitcast.20), channel_id=1, source_target_pairs={{2,0},{4,6},{3,1},{5,7},{10,8},{12,14},{11,9},{13,15},{18,16},{20,... | collective-permute-start | bytes 1966088 | tf_op jit(solution)/shard_map/ppermute | solution.py:56
  8.1 33.5 %collective-permute-start.3 = (bf16[128,2560]{1,0:T(8,128)(2,1)}, bf16[128,2560]{1,0:T(8,128)(2,1)S(1)}, u32[]{:S(2)}, u32[]{:S(2)}) collective-permute-start(bf16[128,2560]{1,0:T(8,128)(2,1)} %bitcast.21), channel_id=1, source_target_pairs={{2,4},{4,2},{3,5},{5,3},{10,12},{12,10},{11,13},{13,11},{18,20},{2... | collective-permute-start | bytes 1966088 | tf_op jit(solution)/shard_map/ppermute | solution.py:52
  20.5 22.6 %copy-start.4 = (bf16[128,2560]{1,0:T(8,128)(2,1)}, bf16[128,2560]{1,0:T(8,128)(2,1)S(1)}, u32[]{:S(2)}) copy-start(bf16[128,2560]{1,0:T(8,128)(2,1)S(1)} %collective-permute-done.2) | copy-start | bytes 1966084
  20.5 21.4 %collective-permute-start.4 = (bf16[128,2560]{1,0:T(8,128)(2,1)S(1)}, bf16[128,2560]{1,0:T(8,128)(2,1)S(1)}, u32[]{:S(2)}, u32[]{:S(2)}) collective-permute-start(bf16[128,2560]{1,0:T(8,128)(2,1)S(1)} %collective-permute-done.2), channel_id=1, source_target_pairs={{2,4},{4,2},{3,5},{5,3},{10,12},{12,10},{11,13},{13,11},{18,20},{2... | collective-permute-start | bytes 1966088 | tf_op jit(solution)/shard_map/ppermute | solution.py:52
  24.0 51.6 %collective-permute-start.7 = (bf16[192,4096]{1,0:T(8,128)(2,1)}, bf16[192,4096]{1,0:T(8,128)(2,1)S(1)}, u32[]{:S(2)}, u32[]{:S(2)}) collective-permute-start(bf16[192,4096]{1,0:T(8,128)(2,1)} %bitcast.13), channel_id=1, source_target_pairs={{2,4},{4,2},{3,5},{5,3},{10,12},{12,10},{11,13},{13,11},{18,20},{2... | collective-permute-start | bytes 4718600 | tf_op jit(solution)/shard_map/ppermute | solution.py:52
  29.1 12.5 %copy-start.6 = (bf16[128,2560]{1,0:T(8,128)(2,1)}, bf16[128,2560]{1,0:T(8,128)(2,1)S(1)}, u32[]{:S(2)}) copy-start(bf16[128,2560]{1,0:T(8,128)(2,1)S(1)} %collective-permute-done.1) | copy-start | bytes 1966084
  29.1 29.5 %collective-permute-start.6 = (bf16[192,2048]{1,0:T(8,128)(2,1)}, bf16[192,2048]{1,0:T(8,128)(2,1)}, u32[]{:S(2)}, u32[]{:S(2)}) collective-permute-start(bf16[192,2048]{1,0:T(8,128)(2,1)} %get-tuple-element.34), channel_id=1, source_target_pairs={{0,2},{6,4},{1,3},{7,5},{8,10},{14,12},{9,11},{15,13},{16,18},{22,... | collective-permute-start | bytes 2359304 | tf_op jit(solution)/shard_map/ppermute | solution.py:48
  41.6 1.6 copy-start.14
  41.6 1.6 copy-start.8
  41.9 1.2 copy-start.10
  43.2 20.6 %copy-start = (bf16[1,128,4096]{2,1,0:T(8,128)(2,1)S(1)}, bf16[1,128,4096]{2,1,0:T(8,128)(2,1)}, u32[]{:S(2)}) copy-start(bf16[1,128,4096]{2,1,0:T(8,128)(2,1)} %param.6) | copy-start | bytes 3145732
  43.2 18.8 %collective-permute-start.5 = (bf16[384,512]{1,0:T(8,128)(2,1)S(1)}, bf16[384,512]{1,0:T(8,128)(2,1)S(1)}, u32[]{:S(2)}, u32[]{:S(2)}) collective-permute-start(bf16[384,512]{1,0:T(8,128)(2,1)S(1)} %convolution_convert_fusion.6), channel_id=1, source_target_pairs={{0,1},{1,0},{2,3},{3,2},{4,5},{5,4},{6,7},{7,6},{8,9},{9,8},{10,11... | collective-permute-start | bytes 1179656 | tf_op jit(solution)/shard_map/ppermute | solution.py:60
  43.8 35.4 %collective-permute-start.13 = (bf16[192,2048]{1,0:T(8,128)(2,1)}, bf16[192,2048]{1,0:T(8,128)(2,1)S(1)}, u32[]{:S(2)}, u32[]{:S(2)}) collective-permute-start(bf16[192,2048]{1,0:T(8,128)(2,1)} %get-tuple-element.22), channel_id=1, source_target_pairs={{0,2},{6,4},{1,3},{7,5},{8,10},{14,12},{9,11},{15,13},{16,18},{22,... | collective-permute-start | bytes 2359304 | tf_op jit(solution)/shard_map/ppermute | solution.py:48
  45.1 18.7 %collective-permute-start.10 = (bf16[128,2560]{1,0:T(8,128)(2,1)}, bf16[128,2560]{1,0:T(8,128)(2,1)S(1)}, u32[]{:S(2)}, u32[]{:S(2)}) collective-permute-start(bf16[128,2560]{1,0:T(8,128)(2,1)} %copy-done.8), channel_id=1, source_target_pairs={{2,0},{4,6},{3,1},{5,7},{10,8},{12,14},{11,9},{13,15},{18,16},{20,... | collective-permute-start | bytes 1966088 | tf_op jit(solution)/shard_map/ppermute | solution.py:56
  58.5 38.2 %collective-permute-start.8 = (bf16[192,2048]{1,0:T(8,128)(2,1)}, bf16[192,2048]{1,0:T(8,128)(2,1)S(1)}, u32[]{:S(2)}, u32[]{:S(2)}) collective-permute-start(bf16[192,2048]{1,0:T(8,128)(2,1)} %collective-permute-done.6), channel_id=1, source_target_pairs={{2,4},{4,2},{3,5},{5,3},{10,12},{12,10},{11,13},{13,11},{18,20},{2... | collective-permute-start | bytes 2359304 | tf_op jit(solution)/shard_map/ppermute | solution.py:52
  62.0 34.7 %collective-permute-start.12 = (bf16[128,2560]{1,0:T(8,128)(2,1)}, bf16[128,2560]{1,0:T(8,128)(2,1)S(1)}, u32[]{:S(2)}, u32[]{:S(2)}) collective-permute-start(bf16[128,2560]{1,0:T(8,128)(2,1)} %copy-done.10), channel_id=1, source_target_pairs={{2,0},{4,6},{3,1},{5,7},{10,8},{12,14},{11,9},{13,15},{18,16},{20,... | collective-permute-start | bytes 1966088 | tf_op jit(solution)/shard_map/ppermute | solution.py:56
  63.8 36.3 %collective-permute-start.9 = (bf16[128,4096]{1,0:T(8,128)(2,1)S(1)}, bf16[128,4096]{1,0:T(8,128)(2,1)S(1)}, u32[]{:S(2)}, u32[]{:S(2)}) collective-permute-start(bf16[128,4096]{1,0:T(8,128)(2,1)S(1)} %bitcast.15), channel_id=1, source_target_pairs={{0,2},{6,4},{1,3},{7,5},{8,10},{14,12},{9,11},{15,13},{16,18},{22,... | collective-permute-start | bytes 3145736 | tf_op jit(solution)/shard_map/ppermute | solution.py:48
  75.6 21.1 %collective-permute-start.11 = (bf16[384,256]{1,0:T(8,128)(2,1)S(1)}, bf16[384,256]{1,0:T(8,128)(2,1)S(1)}, u32[]{:S(2)}, u32[]{:S(2)}) collective-permute-start(bf16[384,256]{1,0:T(8,128)(2,1)S(1)} %get-tuple-element.19), channel_id=1, source_target_pairs={{2,4},{4,2},{3,5},{5,3},{10,12},{12,10},{11,13},{13,11},{18,20},{2... | collective-permute-start | bytes 589832 | tf_op jit(solution)/shard_map/ppermute | solution.py:52
  79.2 32.6 %collective-permute-start.15 = (bf16[192,2048]{1,0:T(8,128)(2,1)S(1)}, bf16[192,2048]{1,0:T(8,128)(2,1)S(1)}, u32[]{:S(2)}, u32[]{:S(2)}) collective-permute-start(bf16[192,2048]{1,0:T(8,128)(2,1)S(1)} %collective-permute-done.13), channel_id=1, source_target_pairs={{2,4},{4,2},{3,5},{5,3},{10,12},{12,10},{11,13},{13,11},{18,20},{2... | collective-permute-start | bytes 2359304 | tf_op jit(solution)/shard_map/ppermute | solution.py:52
  96.7 2.6 %copy-start.3 = (bf16[1,128,2560]{2,1,0:T(8,128)(2,1)S(1)}, bf16[1,128,2560]{2,1,0:T(8,128)(2,1)}, u32[]{:S(2)}) copy-start(bf16[1,128,2560]{2,1,0:T(8,128)(2,1)} %param.5) | copy-start | bytes 1966084
  96.7 2.6 %copy-start.5 = (bf16[128,2560]{1,0:T(8,128)(2,1)S(1)}, bf16[128,2560]{1,0:T(8,128)(2,1)}, u32[]{:S(2)}) copy-start(bf16[128,2560]{1,0:T(8,128)(2,1)} %copy-done.4) | copy-start | bytes 1966084
  96.8 2.6 %copy-start.7 = (bf16[128,2560]{1,0:T(8,128)(2,1)S(1)}, bf16[128,2560]{1,0:T(8,128)(2,1)}, u32[]{:S(2)}) copy-start(bf16[128,2560]{1,0:T(8,128)(2,1)} %copy-done.6) | copy-start | bytes 1966084
  96.8 2.6 %copy-start.9 = (bf16[128,2560]{1,0:T(8,128)(2,1)S(1)}, bf16[128,2560]{1,0:T(8,128)(2,1)}, u32[]{:S(2)}) copy-start(bf16[128,2560]{1,0:T(8,128)(2,1)} %copy-done.8) | copy-start | bytes 1966084
  96.8 2.6 %copy-start.11 = (bf16[128,2560]{1,0:T(8,128)(2,1)S(1)}, bf16[128,2560]{1,0:T(8,128)(2,1)}, u32[]{:S(2)}) copy-start(bf16[128,2560]{1,0:T(8,128)(2,1)} %copy-done.10) | copy-start | bytes 1966084
  100.1 2.5 %copy-start.1 = (bf16[192,2048]{1,0:T(8,128)(2,1)S(1)}, bf16[192,2048]{1,0:T(8,128)(2,1)}, u32[]{:S(2)}) copy-start(bf16[192,2048]{1,0:T(8,128)(2,1)} %get-tuple-element.22) | copy-start | bytes 2359300
  103.5 6.8 %collective-permute-start.14 = (bf16[576,256]{1,0:T(8,128)(2,1)S(1)}, bf16[576,256]{1,0:T(8,128)(2,1)S(1)}, u32[]{:S(2)}, u32[]{:S(2)}) collective-permute-start(bf16[576,256]{1,0:T(8,128)(2,1)S(1)} %fusion.26), channel_id=1, source_target_pairs={{0,1},{1,0},{2,3},{3,2},{4,5},{5,4},{6,7},{7,6},{8,9},{9,8},{10,11... | collective-permute-start | bytes 884744 | tf_op jit(solution)/shard_map/ppermute | solution.py:60
  104.1 12.9 %collective-permute-start.17 = (bf16[128,2048]{1,0:T(8,128)(2,1)S(1)}, bf16[128,2048]{1,0:T(8,128)(2,1)S(1)}, u32[]{:S(2)}, u32[]{:S(2)}) collective-permute-start(bf16[128,2048]{1,0:T(8,128)(2,1)S(1)} %slice.122), channel_id=1, source_target_pairs={{2,0},{4,6},{3,1},{5,7},{10,8},{12,14},{11,9},{13,15},{18,16},{20,... | collective-permute-start | bytes 1572872 | tf_op jit(solution)/shard_map/ppermute | solution.py:56
  112.3 4.7 %collective-permute-start.16 = (bf16[192,256]{1,0:T(8,128)(2,1)S(1)}, bf16[192,256]{1,0:T(8,128)(2,1)S(1)}, u32[]{:S(2)}, u32[]{:S(2)}) collective-permute-start(bf16[192,256]{1,0:T(8,128)(2,1)S(1)} %fusion.27), channel_id=1, source_target_pairs={{0,1},{1,0},{2,3},{3,2},{4,5},{5,4},{6,7},{7,6},{8,9},{9,8},{10,11... | collective-permute-start | bytes 294920 | tf_op jit(solution)/shard_map/ppermute | solution.py:60
  114.1 32.3 %collective-permute-start.26 = (bf16[128,2048]{1,0:T(8,128)(2,1)S(1)}, bf16[128,2048]{1,0:T(8,128)(2,1)S(1)}, u32[]{:S(2)}, u32[]{:S(2)}) collective-permute-start(bf16[128,2048]{1,0:T(8,128)(2,1)S(1)} %slice.135), channel_id=1, source_target_pairs={{2,0},{4,6},{3,1},{5,7},{10,8},{12,14},{11,9},{13,15},{18,16},{20,... | collective-permute-start | bytes 1572872 | tf_op jit(solution)/shard_map/ppermute | solution.py:56
  117.0 8.3 %copy-start.13 = (bf16[1,192,2560]{2,1,0:T(8,128)(2,1)S(1)}, bf16[1,192,2560]{2,1,0:T(8,128)(2,1)}, u32[]{:S(2)}) copy-start(bf16[1,192,2560]{2,1,0:T(8,128)(2,1)} %param.4) | copy-start | bytes 2949124
  117.0 8.3 %copy-start.15 = (bf16[192,2560]{1,0:T(8,128)(2,1)S(1)}, bf16[192,2560]{1,0:T(8,128)(2,1)}, u32[]{:S(2)}) copy-start(bf16[192,2560]{1,0:T(8,128)(2,1)} %copy-done.14) | copy-start | bytes 2949124
  117.1 7.7 %collective-permute-start.18 = (bf16[384,256]{1,0:T(8,128)(2,1)S(1)}, bf16[384,256]{1,0:T(8,128)(2,1)S(1)}, u32[]{:S(2)}, u32[]{:S(2)}) collective-permute-start(bf16[384,256]{1,0:T(8,128)(2,1)S(1)} %pad_maximum_fusion.9), channel_id=1, source_target_pairs={{2,4},{4,2},{3,5},{5,3},{10,12},{12,10},{11,13},{13,11},{18,20},{2... | collective-permute-start | bytes 589832 | tf_op jit(solution)/shard_map/ppermute | solution.py:52
  125.9 12.3 %collective-permute-start.20 = (bf16[128,1280]{1,0:T(8,128)(2,1)S(1)}, bf16[128,1280]{1,0:T(8,128)(2,1)S(1)}, u32[]{:S(2)}, u32[]{:S(2)}) collective-permute-start(bf16[128,1280]{1,0:T(8,128)(2,1)S(1)} %get-tuple-element.36), channel_id=1, source_target_pairs={{2,4},{4,2},{3,5},{5,3},{10,12},{12,10},{11,13},{13,11},{18,20},{2... | collective-permute-start | bytes 983048 | tf_op jit(solution)/shard_map/ppermute | solution.py:52
  130.0 9.7 %collective-permute-start.19 = (bf16[192,512]{1,0:T(8,128)(2,1)S(1)}, bf16[192,512]{1,0:T(8,128)(2,1)S(1)}, u32[]{:S(2)}, u32[]{:S(2)}) collective-permute-start(bf16[192,512]{1,0:T(8,128)(2,1)S(1)} %slice.124), channel_id=1, source_target_pairs={{2,0},{4,6},{3,1},{5,7},{10,8},{12,14},{11,9},{13,15},{18,16},{20,... | collective-permute-start | bytes 589832 | tf_op jit(solution)/shard_map/ppermute | solution.py:56
  131.3 13.7 %collective-permute-start.24 = (bf16[128,1280]{1,0:T(8,128)(2,1)S(1)}, bf16[128,1280]{1,0:T(8,128)(2,1)S(1)}, u32[]{:S(2)}, u32[]{:S(2)}) collective-permute-start(bf16[128,1280]{1,0:T(8,128)(2,1)S(1)} %get-tuple-element.35), channel_id=1, source_target_pairs={{2,4},{4,2},{3,5},{5,3},{10,12},{12,10},{11,13},{13,11},{18,20},{2... | collective-permute-start | bytes 983048 | tf_op jit(solution)/shard_map/ppermute | solution.py:52
  138.3 23.1 %collective-permute-start.23 = (bf16[128,1280]{1,0:T(8,128)(2,1)S(1)}, bf16[128,1280]{1,0:T(8,128)(2,1)S(1)}, u32[]{:S(2)}, u32[]{:S(2)}) collective-permute-start(bf16[128,1280]{1,0:T(8,128)(2,1)S(1)} %add_convert_fusion.2), channel_id=1, source_target_pairs={{2,0},{4,6},{3,1},{5,7},{10,8},{12,14},{11,9},{13,15},{18,16},{20,... | collective-permute-start | bytes 983048 | tf_op jit(solution)/shard_map/ppermute | solution.py:56
  140.4 21.0 %collective-permute-start.21 = (bf16[1,192,2560]{2,1,0:T(8,128)(2,1)S(1)}, bf16[1,192,2560]{2,1,0:T(8,128)(2,1)S(1)}, u32[]{:S(2)}, u32[]{:S(2)}) collective-permute-start(bf16[1,192,2560]{2,1,0:T(8,128)(2,1)S(1)} %fusion), channel_id=1, source_target_pairs={{8,0},{16,8},{24,16},{9,1},{17,9},{25,17},{10,2},{18,10},{26,18},{... | collective-permute-start | bytes 2949128 | tf_op jit(solution)/shard_map/ppermute | solution.py:13
  142.3 19.1 %collective-permute-start.22 = (bf16[128,2560]{1,0:T(8,128)(2,1)S(1)}, bf16[128,2560]{1,0:T(8,128)(2,1)S(1)}, u32[]{:S(2)}, u32[]{:S(2)}) collective-permute-start(bf16[128,2560]{1,0:T(8,128)(2,1)S(1)} %convolution_convert_fusion.1), channel_id=1, source_target_pairs={{2,4},{4,2},{3,5},{5,3},{10,12},{12,10},{11,13},{13,11},{18,20},{2... | collective-permute-start | bytes 1966088 | tf_op jit(solution)/shard_map/ppermute | solution.py:52
  145.1 16.3 %collective-permute-start.25 = (bf16[128,1280]{1,0:T(8,128)(2,1)S(1)}, bf16[128,1280]{1,0:T(8,128)(2,1)S(1)}, u32[]{:S(2)}, u32[]{:S(2)}) collective-permute-start(bf16[128,1280]{1,0:T(8,128)(2,1)S(1)} %add_convert_fusion.1), channel_id=1, source_target_pairs={{2,0},{4,6},{3,1},{5,7},{10,8},{12,14},{11,9},{13,15},{18,16},{20,... | collective-permute-start | bytes 983048 | tf_op jit(solution)/shard_map/ppermute | solution.py:56

commit v11 on v9

--- a/solution.py
+++ b/solution.py
@@ -137,17 +137,16 @@
     normed_grad = jnp.concatenate([early_sum[: 2 * rows], from_across.astype(F32)], axis=1)
     inner = jnp.mean(normed_grad * normed, axis=-1, keepdims=True)
     latent_bf = (inv_rms * (normed_grad - normed * inner)).astype(BF16)
-    latent_there = outward(latent_bf[rows:])
-    latent_used = jnp.where(middle, latent_bf[:rows], latent_there)
 
     sums = [
         tokens_dot(latent_bf[:, j * lat : (j + 1) * lat], tokens_mine).astype(BF16)
-        for j in range(4)
+        for j in range(3)
     ]
     width = tokens.shape[1] // 2
     halves = (slice(0, width), slice(width, 2 * width))
-    sent_end, sent_own = sums[3], sums[2]
-    from_end = [across(sent_end[:, half]) for half in halves]
+    sent_own = sums[2]
+    sent_halves = [tokens_dot(latent_bf[:, 3 * lat :], tokens_mine[:, half]).astype(BF16) for half in halves]
+    from_end = [across(half) for half in sent_halves]
     end_first = (sums[1][:, halves[0]] + from_end[0].astype(F32)).astype(BF16)
     from_own = across(after(sent_own, end_first))
     end_second = sums[1][:, halves[1]] + after(from_end[1], end_first).astype(F32)
@@ -161,8 +160,12 @@
         axis=1,
     )
 
+    latent_there = outward(after(latent_bf[rows:], *sent_halves))
+    latent_used = jnp.where(middle, latent_bf[:rows], latent_there)
     input_grad = jnp.dot(latent_used, down_used, preferred_element_type=F32).astype(BF16)
     passed = shifted(input_grad, "section", -1)
+    final = lax.axis_index("section") == lax.axis_size("section") - 1
+    passed = jnp.where(final, jnp.zeros_like(passed), passed)
     down_own_grad = (sums[0] + after(from_own, passed).astype(F32)).astype(BF16)
     down_grad = jnp.where(middle, down_own_grad, down_end_grad)
     return (passed[None], down_grad[None], up_grad[None])

time: 160 us -> 169 us (1.056)
  matrix products: 12.5 us -> 18.9 us
  other arithmetic: 3.12 us -> 5.19 us
    dot_general x4, matrix products: 4.98 us -> 9.07 us  [rows_dot(): lax.dot_general(left, right, (((1,), (1,)), ((), ())), preferred_element_...]
    ppermute x8, waiting for transfers between devices: 29.2 us -> 33.3 us  [outward(): return lax.ppermute(value, 'row', [(1, 0), (2, 3)])]
    ppermute x5, waiting for transfers between devices: 48.1 us -> 45.4 us  [inward(): return lax.ppermute(value, 'row', [(0, 1), (3, 2)])]
    dot_general x6 -> x7, matrix products: 6.81 us -> 9.09 us  [tokens_dot(): lax.dot_general(left, right, (((0,), (0,)), ((), ())), preferred_element_...]
  transfers between devices with their start and end apart: 27 -> 27, of which waited for: 14 -> 13; matrix products, arithmetic and copies ran while one was open for 11% -> 16% of each run, Pallas kernels for 0% -> 0%
where the time goes in v11:
time: 169 us; the launch traced here: 166 us
  waiting for transfers between devices  89.7 us (53%)
  starting transfers between devices  46 us (27%)
  matrix products  18.9 us (11%)
  other arithmetic  5.19 us (3%)
  local copies, waits for them, and re-layouts  4.85 us (3%)
    ppermute x5, waiting for transfers between devices, inward(): return lax.ppermute(value, 'row', [(0, 1), (3, 2)])  45.4 us
    ppermute x8, waiting for transfers between devices, outward(): return lax.ppermute(value, 'row', [(1, 0), (2, 3)])  33.3 us
    ppermute x5, starting transfers between devices, inward(): return lax.ppermute(value, 'row', [(0, 1), (3, 2)])  21.2 us
    ppermute x8, starting transfers between devices, outward(): return lax.ppermute(value, 'row', [(1, 0), (2, 3)])  10.5 us
    dot_general x7, matrix products, tokens_dot(): lax.dot_general(left, right, (((0,), (0,)), ((), ())), preferred_element_...  9.09 us
    dot_general x4, matrix products, rows_dot(): lax.dot_general(left, right, (((1,), (1,)), ((), ())), preferred_element_...  9.07 us
    ppermute x10, starting transfers between devices, across(): return lax.ppermute(value, 'row', [(1, 2), (2, 1)])  7.82 us
    ppermute x1, waiting for transfers between devices, shifted(): lax.ppermute(value, axis, [(source, source + steps) for source in range(l...  6.93 us
  transfers between devices with their start and end apart: 27, of which 13 were waited for; matrix products, arithmetic and copies ran while one was open for 16% of the time, Pallas kernels for 0%

profile of v11, /device:TPU:4, one launch (start us, length us, event | category | flops | bytes accessed | tf_op | source)
XLA Modules:
  0.0 166.0 jit_solution(7645241757891247980)
XLA Ops:
  0.7 3.7 %collective-permute-start.2 = (bf16[128,2560]{1,0:T(8,128)(2,1)}, bf16[128,2560]{1,0:T(8,128)(2,1)S(1)}, u32[]{:S(2)}, u32[]{:S(2)}) collective-permute-start(bf16[128,2560]{1,0:T(8,128)(2,1)} %bitcast.15), channel_id=1, source_target_pairs={{0,2},{6,4},{1,3},{7,5},{8,10},{14,12},{9,11},{15,13},{16,18},{22,... | collective-permute-start | bytes 1966088 | tf_op jit(solution)/shard_map/ppermute | solution.py:48
  4.3 1.4 collective-permute-start
  5.7 1.3 collective-permute-start.1
  7.0 0.7 collective-permute-start.3
  7.7 12.0 %collective-permute-done.2 = bf16[128,2560]{1,0:T(8,128)(2,1)S(1)} collective-permute-done((bf16[128,2560]{1,0:T(8,128)(2,1)}, bf16[128,2560]{1,0:T(8,128)(2,1)S(1)}, u32[]{:S(2)}, u32[]{:S(2)}) %collective-permute-start.2) | collective-permute-done | bytes 655392 | tf_op jit(solution)/shard_map/ppermute | solution.py:48
  19.7 0.7 collective-permute-start.4
  20.4 0.8 collective-permute-start.7
  21.2 2.4 %fusion.51 = (bf16[192,2048]{1,0:T(8,128)(2,1)S(1)}, bf16[192,2048]{1,0:T(8,128)(2,1)}) fusion(bf16[192,4096]{1,0:T(8,128)(2,1)} %bitcast.14), kind=kLoop, calls=%fused_computation.83 | loop fusion | bytes 3145728 | tf_op jit(solution)/shard_map/slice | solution.py:119
  23.6 0.4 collective-permute-done.1
  24.0 9.2 %collective-permute-start.6 = (bf16[192,2048]{1,0:T(8,128)(2,1)}, bf16[192,2048]{1,0:T(8,128)(2,1)}, u32[]{:S(2)}, u32[]{:S(2)}) collective-permute-start(bf16[192,2048]{1,0:T(8,128)(2,1)} %get-tuple-element.34), channel_id=1, source_target_pairs={{0,2},{6,4},{1,3},{7,5},{8,10},{14,12},{9,11},{15,13},{16,18},{22,... | collective-permute-start | bytes 2359304 | tf_op jit(solution)/shard_map/ppermute | solution.py:48
  33.2 7.6 %collective-permute-done = bf16[192,2560]{1,0:T(8,128)(2,1)S(1)} collective-permute-done((bf16[192,2560]{1,0:T(8,128)(2,1)}, bf16[192,2560]{1,0:T(8,128)(2,1)S(1)}, u32[]{:S(2)}, u32[]{:S(2)}) %collective-permute-start) | collective-permute-done | bytes 983072 | tf_op jit(solution)/shard_map/ppermute | solution.py:48
  40.8 1.2 convolution_convert_fusion.7
  42.2 1.5 collective-permute-start.5
  43.7 5.4 %collective-permute-start.13 = (bf16[192,2048]{1,0:T(8,128)(2,1)S(1)}, bf16[192,2048]{1,0:T(8,128)(2,1)}, u32[]{:S(2)}, u32[]{:S(2)}) collective-permute-start(bf16[192,2048]{1,0:T(8,128)(2,1)S(1)} %get-tuple-element.22), channel_id=1, source_target_pairs={{0,2},{6,4},{1,3},{7,5},{8,10},{14,12},{9,11},{15,13},{16,18},{22,... | collective-permute-start | bytes 2359304 | tf_op jit(solution)/shard_map/ppermute | solution.py:48
  49.1 1.3 collective-permute-start.10
  50.4 7.3 %collective-permute-done.6 = bf16[192,2048]{1,0:T(8,128)(2,1)} collective-permute-done((bf16[192,2048]{1,0:T(8,128)(2,1)}, bf16[192,2048]{1,0:T(8,128)(2,1)}, u32[]{:S(2)}, u32[]{:S(2)}) %collective-permute-start.6) | collective-permute-done | bytes 786464 | tf_op jit(solution)/shard_map/ppermute | solution.py:48
  57.6 0.7 collective-permute-start.8
  58.3 1.3 collective-permute-start.12
  59.6 0.2 multiply_reduce_fusion.1
  59.9 0.1 fusion.28
  60.1 6.0 %collective-permute-done.10 = bf16[128,2560]{1,0:T(8,128)(2,1)S(1)} collective-permute-done((bf16[128,2560]{1,0:T(8,128)(2,1)}, bf16[128,2560]{1,0:T(8,128)(2,1)S(1)}, u32[]{:S(2)}, u32[]{:S(2)}) %collective-permute-start.10) | collective-permute-done | bytes 655392 | tf_op jit(solution)/shard_map/ppermute | solution.py:56
  66.1 1.6 collective-permute-start.9
  67.7 0.7 collective-permute-start.11
  68.5 5.9 %collective-permute-done.13 = bf16[192,2048]{1,0:T(8,128)(2,1)} collective-permute-done((bf16[192,2048]{1,0:T(8,128)(2,1)S(1)}, bf16[192,2048]{1,0:T(8,128)(2,1)}, u32[]{:S(2)}, u32[]{:S(2)}) %collective-permute-start.13) | collective-permute-done | bytes 786464 | tf_op jit(solution)/shard_map/ppermute | solution.py:48
  74.4 1.6 collective-permute-start.15
  76.0 2.9 %collective-permute-done.12 = bf16[128,2560]{1,0:T(8,128)(2,1)S(1)} collective-permute-done((bf16[128,2560]{1,0:T(8,128)(2,1)}, bf16[128,2560]{1,0:T(8,128)(2,1)S(1)}, u32[]{:S(2)}, u32[]{:S(2)}) %collective-permute-start.12) | collective-permute-done | bytes 655392 | tf_op jit(solution)/shard_map/ppermute | solution.py:56
  78.9 3.5 %convolution_convert_fusion.4 = bf16[256,2048]{1,0:T(8,128)(2,1)} fusion(bf16[768,256]{1,0:T(8,128)(2,1)S(1)} %pad_maximum_fusion.8, bf16[192,2048]{1,0:T(8,128)(2,1)S(1)} %collective-permute-done.8, bf16[192,2048]{1,0:T(8,128)(2,1)S(1)} %get-tuple-element.32, bf16[192,2048]{1,0:T(8,128)(2,1)} %collective-permute-done.6, ...), kind=kOutput, calls=%fused_computation.17 | convolution fusion | flops 818413568 | bytes 4587520 | tf_op jit(solution)/shard_map/dot_general | solution.py:72
  82.4 0.7 maximum_select_fusion
  83.2 12.6 %collective-permute-done.9 = bf16[128,4096]{1,0:T(8,128)(2,1)S(1)} collective-permute-done((bf16[128,4096]{1,0:T(8,128)(2,1)}, bf16[128,4096]{1,0:T(8,128)(2,1)S(1)}, u32[]{:S(2)}, u32[]{:S(2)}) %collective-permute-start.9) | collective-permute-done | bytes 1048608 | tf_op jit(solution)/shard_map/ppermute | solution.py:48
  95.8 2.9 %fusion.19 = f32[768,256]{1,0:T(8,128)S(1)} fusion(bf16[128,4096]{1,0:T(8,128)(2,1)} %bitcast.3, bf16[128,4096]{1,0:T(8,128)(2,1)S(1)} %collective-permute-done.9, bf16[192,2048]{1,0:T(8,128)(2,1)S(1)} %collective-permute-done.8, bf16[192,2048]{1,0:T(8,128)(2,1)S(1)} %get-tuple-element.32, bf16[192,2048]{1,0:T(8,128)(2,1)} %collective-permute-done.6, ...), kind=kOutput, calls=%fused_computation.36 | convolution fusion | flops 819986432 | bytes 6029312 | tf_op jit(solution)/shard_map/dot_general | solution.py:68
  98.8 3.1 %fusion.29 = bf16[576,256]{1,0:T(8,128)(2,1)} fusion(f32[768,256]{1,0:T(8,128)S(1)} %fusion.19, bf16[128,4096]{1,0:T(8,128)(2,1)S(1)} %collective-permute-done.9, bf16[128,4096]{1,0:T(8,128)(2,1)} %bitcast.3, bf16[192,2048]{1,0:T(8,128)(2,1)S(1)} %get-tuple-element.31, bf16[192,2048]{1,0:T(8,128)(2,1)} %collective-permute-done.13, ...), kind=kOutput, calls=%fused_computation.54 | convolution fusion | flops 613449728 | bytes 5341184 | tf_op jit(solution)/shard_map/dot_general | solution.py:68
  101.9 1.5 collective-permute-start.14
  103.4 1.2 slice.123
  104.6 1.4 collective-permute-start.17
  106.0 4.1 %collective-permute-done.14 = bf16[576,256]{1,0:T(8,128)(2,1)} collective-permute-done((bf16[576,256]{1,0:T(8,128)(2,1)}, bf16[576,256]{1,0:T(8,128)(2,1)}, u32[]{:S(2)}, u32[]{:S(2)}) %collective-permute-start.14) | collective-permute-done | bytes 294944 | tf_op jit(solution)/shard_map/ppermute | solution.py:60
  110.1 1.1 convert_add_fusion.1
  111.3 1.8 %fusion.30 = bf16[192,256]{1,0:T(8,128)(2,1)S(1)} fusion(f32[768,256]{1,0:T(8,128)} %copy-done.22, bf16[192,2048]{1,0:T(8,128)(2,1)} %collective-permute-done.15, bf16[128,4096]{1,0:T(8,128)(2,1)S(1)} %copy-done.1, bf16[128,4096]{1,0:T(8,128)(2,1)} %bitcast.3), kind=kOutput, calls=%fused_computation.61 | convolution fusion | flops 203522048 | bytes 3178496 | tf_op jit(solution)/shard_map/dot_general | solution.py:68
  113.1 1.6 collective-permute-start.16
  114.7 2.4 %fusion.9 = bf16[256,2048]{1,0:T(8,128)(2,1)S(1)} fusion(bf16[192,2048]{1,0:T(8,128)(2,1)} %collective-permute-done.15, bf16[192,2048]{1,0:T(8,128)(2,1)S(1)} %copy-done.7, bf16[192,2048]{1,0:T(8,128)(2,1)} %collective-permute-done.13, bf16[192,2048]{1,0:T(8,128)(2,1)S(1)} %copy-done.5, bf16[384,256]{1,0:T(8,128)(2,1)S(1)} %copy-done.21, ...), kind=kOutput, calls=%fused_computation.16 | convolution fusion | flops 819200000 | bytes 4587520 | tf_op jit(solution)/shard_map/dot_general | solution.py:72
  117.1 1.3 collective-permute-start.26
  118.5 4.1 %collective-permute-done.17 = bf16[128,2048]{1,0:T(8,128)(2,1)S(1)} collective-permute-done((bf16[128,2048]{1,0:T(8,128)(2,1)S(1)}, bf16[128,2048]{1,0:T(8,128)(2,1)S(1)}, u32[]{:S(2)}, u32[]{:S(2)}) %collective-permute-start.17) | collective-permute-done | bytes 524320 | tf_op jit(solution)/shard_map/ppermute | solution.py:56
  122.6 0.7 collective-permute-start.18
  123.4 0.3 multiply_reduce_fusion
  123.7 0.2 multiply_convert_fusion
  124.0 0.6 copy-done.24
  124.6 0.3 copy-done.26
  124.9 0.4 convolution_convert_fusion.6
  125.2 0.4 convolution_convert_fusion.5
  125.6 0.5 convolution_convert_fusion.2
  126.1 0.7 collective-permute-start.21
  126.8 1.3 collective-permute-start.19
  128.1 0.5 convolution_convert_fusion.1
  128.7 0.7 collective-permute-start.24
  129.3 13.4 %collective-permute-done.19 = bf16[192,512]{1,0:T(8,128)(2,1)S(1)} collective-permute-done((bf16[192,512]{1,0:T(8,128)(2,1)S(1)}, bf16[192,512]{1,0:T(8,128)(2,1)S(1)}, u32[]{:S(2)}, u32[]{:S(2)}) %collective-permute-start.19) | collective-permute-done | bytes 196640 | tf_op jit(solution)/shard_map/ppermute | solution.py:56
  142.7 0.7 convolution_convert_fusion
  143.4 1.9 %collective-permute-start.20 = (bf16[192,2560]{1,0:T(8,128)(2,1)S(1)}, bf16[192,2560]{1,0:T(8,128)(2,1)S(1)}, u32[]{:S(2)}, u32[]{:S(2)}) collective-permute-start(bf16[192,2560]{1,0:T(8,128)(2,1)S(1)} %convolution_convert_fusion), channel_id=1, source_target_pairs={{8,0},{16,8},{24,16},{9,1},{17,9},{25,17},{10,2},{18,10},{26,18},{... | collective-permute-start | bytes 2949128 | tf_op jit(solution)/shard_map/ppermute | solution.py:13
  145.4 1.3 collective-permute-start.23
  146.7 0.7 collective-permute-start.22
  147.6 1.3 collective-permute-start.25
  148.9 1.1 maximum_bitcast_fusion
  150.0 6.9 %collective-permute-done.20 = bf16[192,2560]{1,0:T(8,128)(2,1)S(1)} collective-permute-done((bf16[192,2560]{1,0:T(8,128)(2,1)S(1)}, bf16[192,2560]{1,0:T(8,128)(2,1)S(1)}, u32[]{:S(2)}, u32[]{:S(2)}) %collective-permute-start.20) | collective-permute-done | bytes 983072 | tf_op jit(solution)/shard_map/ppermute | solution.py:13
  156.9 1.0 fusion.56
  157.9 6.6 %collective-permute-done.25 = bf16[128,1280]{1,0:T(8,128)(2,1)S(1)} collective-permute-done((bf16[128,1280]{1,0:T(8,128)(2,1)S(1)}, bf16[128,1280]{1,0:T(8,128)(2,1)S(1)}, u32[]{:S(2)}, u32[]{:S(2)}) %collective-permute-start.25) | collective-permute-done | bytes 327712 | tf_op jit(solution)/shard_map/ppermute | solution.py:56
  164.5 1.4 fusion.27
  (82 shorter events, 0.9 us)
Async XLA Ops:
  0.6 40.2 %copy-start.10 = (bf16[1,128,2560]{2,1,0:T(8,128)(2,1)S(1)}, bf16[1,128,2560]{2,1,0:T(8,128)(2,1)}, u32[]{:S(2)}) copy-start(bf16[1,128,2560]{2,1,0:T(8,128)(2,1)} %param.5) | copy-start | bytes 1966084
  0.6 40.2 %copy-start.23 = (bf16[1,192,2560]{2,1,0:T(8,128)(2,1)S(1)}, bf16[1,192,2560]{2,1,0:T(8,128)(2,1)}, u32[]{:S(2)}) copy-start(bf16[1,192,2560]{2,1,0:T(8,128)(2,1)} %param.4) | copy-start | bytes 2949124
  0.7 19.1 %collective-permute-start.2 = (bf16[128,2560]{1,0:T(8,128)(2,1)}, bf16[128,2560]{1,0:T(8,128)(2,1)S(1)}, u32[]{:S(2)}, u32[]{:S(2)}) collective-permute-start(bf16[128,2560]{1,0:T(8,128)(2,1)} %bitcast.15), channel_id=1, source_target_pairs={{0,2},{6,4},{1,3},{7,5},{8,10},{14,12},{9,11},{15,13},{16,18},{22,... | collective-permute-start | bytes 1966088 | tf_op jit(solution)/shard_map/ppermute | solution.py:48
  4.3 36.5 %collective-permute-start = (bf16[192,2560]{1,0:T(8,128)(2,1)}, bf16[192,2560]{1,0:T(8,128)(2,1)S(1)}, u32[]{:S(2)}, u32[]{:S(2)}) collective-permute-start(bf16[192,2560]{1,0:T(8,128)(2,1)} %bitcast.20), channel_id=1, source_target_pairs={{0,2},{6,4},{1,3},{7,5},{8,10},{14,12},{9,11},{15,13},{16,18},{22,... | collective-permute-start | bytes 2949128 | tf_op jit(solution)/shard_map/ppermute | solution.py:48
  5.7 18.3 %collective-permute-start.1 = (bf16[128,2560]{1,0:T(8,128)(2,1)}, bf16[128,2560]{1,0:T(8,128)(2,1)S(1)}, u32[]{:S(2)}, u32[]{:S(2)}) collective-permute-start(bf16[128,2560]{1,0:T(8,128)(2,1)} %bitcast.16), channel_id=1, source_target_pairs={{2,0},{4,6},{3,1},{5,7},{10,8},{12,14},{11,9},{13,15},{18,16},{20,... | collective-permute-start | bytes 1966088 | tf_op jit(solution)/shard_map/ppermute | solution.py:56
  7.0 33.8 %collective-permute-start.3 = (bf16[128,2560]{1,0:T(8,128)(2,1)}, bf16[128,2560]{1,0:T(8,128)(2,1)S(1)}, u32[]{:S(2)}, u32[]{:S(2)}) collective-permute-start(bf16[128,2560]{1,0:T(8,128)(2,1)} %bitcast.17), channel_id=1, source_target_pairs={{2,4},{4,2},{3,5},{5,3},{10,12},{12,10},{11,13},{13,11},{18,20},{2... | collective-permute-start | bytes 1966088 | tf_op jit(solution)/shard_map/ppermute | solution.py:52
  19.7 22.3 %copy-start.12 = (bf16[128,2560]{1,0:T(8,128)(2,1)}, bf16[128,2560]{1,0:T(8,128)(2,1)S(1)}, u32[]{:S(2)}) copy-start(bf16[128,2560]{1,0:T(8,128)(2,1)S(1)} %collective-permute-done.2) | copy-start | bytes 1966084
  19.7 21.1 %collective-permute-start.4 = (bf16[128,2560]{1,0:T(8,128)(2,1)S(1)}, bf16[128,2560]{1,0:T(8,128)(2,1)S(1)}, u32[]{:S(2)}, u32[]{:S(2)}) collective-permute-start(bf16[128,2560]{1,0:T(8,128)(2,1)S(1)} %collective-permute-done.2), channel_id=1, source_target_pairs={{2,4},{4,2},{3,5},{5,3},{10,12},{12,10},{11,13},{13,11},{18,20},{2... | collective-permute-start | bytes 1966088 | tf_op jit(solution)/shard_map/ppermute | solution.py:52
  20.4 47.3 %collective-permute-start.7 = (bf16[192,4096]{1,0:T(8,128)(2,1)}, bf16[192,4096]{1,0:T(8,128)(2,1)S(1)}, u32[]{:S(2)}, u32[]{:S(2)}) collective-permute-start(bf16[192,4096]{1,0:T(8,128)(2,1)} %bitcast.13), channel_id=1, source_target_pairs={{2,4},{4,2},{3,5},{5,3},{10,12},{12,10},{11,13},{13,11},{18,20},{2... | collective-permute-start | bytes 4718600 | tf_op jit(solution)/shard_map/ppermute | solution.py:52
  23.6 20.1 %copy-start.3 = (bf16[192,2048]{1,0:T(8,128)(2,1)}, bf16[192,2048]{1,0:T(8,128)(2,1)S(1)}, u32[]{:S(2)}) copy-start(bf16[192,2048]{1,0:T(8,128)(2,1)S(1)} %get-tuple-element.22) | copy-start | bytes 2359300
  24.0 16.8 %copy-start.14 = (bf16[128,2560]{1,0:T(8,128)(2,1)}, bf16[128,2560]{1,0:T(8,128)(2,1)S(1)}, u32[]{:S(2)}) copy-start(bf16[128,2560]{1,0:T(8,128)(2,1)S(1)} %collective-permute-done.1) | copy-start | bytes 1966084
  24.0 33.6 %collective-permute-start.6 = (bf16[192,2048]{1,0:T(8,128)(2,1)}, bf16[192,2048]{1,0:T(8,128)(2,1)}, u32[]{:S(2)}, u32[]{:S(2)}) collective-permute-start(bf16[192,2048]{1,0:T(8,128)(2,1)} %get-tuple-element.34), channel_id=1, source_target_pairs={{0,2},{6,4},{1,3},{7,5},{8,10},{14,12},{9,11},{15,13},{16,18},{22,... | collective-permute-start | bytes 2359304 | tf_op jit(solution)/shard_map/ppermute | solution.py:48
  40.8 1.3 copy-start.25
  40.8 1.3 copy-start.16
  40.8 1.3 copy-start.18
  42.2 16.2 %collective-permute-start.5 = (bf16[384,512]{1,0:T(8,128)(2,1)S(1)}, bf16[384,512]{1,0:T(8,128)(2,1)S(1)}, u32[]{:S(2)}, u32[]{:S(2)}) collective-permute-start(bf16[384,512]{1,0:T(8,128)(2,1)S(1)} %convolution_convert_fusion.7), channel_id=1, source_target_pairs={{0,1},{1,0},{2,3},{3,2},{4,5},{5,4},{6,7},{7,6},{8,9},{9,8},{10,11... | collective-permute-start | bytes 1179656 | tf_op jit(solution)/shard_map/ppermute | solution.py:60
  43.7 30.7 %collective-permute-start.13 = (bf16[192,2048]{1,0:T(8,128)(2,1)S(1)}, bf16[192,2048]{1,0:T(8,128)(2,1)}, u32[]{:S(2)}, u32[]{:S(2)}) collective-permute-start(bf16[192,2048]{1,0:T(8,128)(2,1)S(1)} %get-tuple-element.22), channel_id=1, source_target_pairs={{0,2},{6,4},{1,3},{7,5},{8,10},{14,12},{9,11},{15,13},{16,18},{22,... | collective-permute-start | bytes 2359304 | tf_op jit(solution)/shard_map/ppermute | solution.py:48
  49.1 17.0 %collective-permute-start.10 = (bf16[128,2560]{1,0:T(8,128)(2,1)}, bf16[128,2560]{1,0:T(8,128)(2,1)S(1)}, u32[]{:S(2)}, u32[]{:S(2)}) collective-permute-start(bf16[128,2560]{1,0:T(8,128)(2,1)} %copy-done.16), channel_id=1, source_target_pairs={{2,0},{4,6},{3,1},{5,7},{10,8},{12,14},{11,9},{13,15},{18,16},{20,... | collective-permute-start | bytes 1966088 | tf_op jit(solution)/shard_map/ppermute | solution.py:56
  57.6 21.2 %collective-permute-start.8 = (bf16[192,2048]{1,0:T(8,128)(2,1)}, bf16[192,2048]{1,0:T(8,128)(2,1)S(1)}, u32[]{:S(2)}, u32[]{:S(2)}) collective-permute-start(bf16[192,2048]{1,0:T(8,128)(2,1)} %collective-permute-done.6), channel_id=1, source_target_pairs={{2,4},{4,2},{3,5},{5,3},{10,12},{12,10},{11,13},{13,11},{18,20},{2... | collective-permute-start | bytes 2359304 | tf_op jit(solution)/shard_map/ppermute | solution.py:52
  58.3 20.5 %collective-permute-start.12 = (bf16[128,2560]{1,0:T(8,128)(2,1)}, bf16[128,2560]{1,0:T(8,128)(2,1)S(1)}, u32[]{:S(2)}, u32[]{:S(2)}) collective-permute-start(bf16[128,2560]{1,0:T(8,128)(2,1)} %copy-done.18), channel_id=1, source_target_pairs={{2,0},{4,6},{3,1},{5,7},{10,8},{12,14},{11,9},{13,15},{18,16},{20,... | collective-permute-start | bytes 1966088 | tf_op jit(solution)/shard_map/ppermute | solution.py:56
  60.0 15.9 %copy-start.8 = (bf16[384,256]{1,0:T(8,128)(2,1)}, bf16[384,256]{1,0:T(8,128)(2,1)S(1)}, u32[]{:S(2)}) copy-start(bf16[384,256]{1,0:T(8,128)(2,1)S(1)} %get-tuple-element.35) | copy-start | bytes 589828
  66.1 29.7 %collective-permute-start.9 = (bf16[128,4096]{1,0:T(8,128)(2,1)}, bf16[128,4096]{1,0:T(8,128)(2,1)S(1)}, u32[]{:S(2)}, u32[]{:S(2)}) collective-permute-start(bf16[128,4096]{1,0:T(8,128)(2,1)} %bitcast.3), channel_id=1, source_target_pairs={{0,2},{6,4},{1,3},{7,5},{8,10},{14,12},{9,11},{15,13},{16,18},{22,... | collective-permute-start | bytes 3145736 | tf_op jit(solution)/shard_map/ppermute | solution.py:48
  67.7 8.3 %collective-permute-start.11 = (bf16[384,256]{1,0:T(8,128)(2,1)S(1)}, bf16[384,256]{1,0:T(8,128)(2,1)S(1)}, u32[]{:S(2)}, u32[]{:S(2)}) collective-permute-start(bf16[384,256]{1,0:T(8,128)(2,1)S(1)} %get-tuple-element.19), channel_id=1, source_target_pairs={{2,4},{4,2},{3,5},{5,3},{10,12},{12,10},{11,13},{13,11},{18,20},{2... | collective-permute-start | bytes 589832 | tf_op jit(solution)/shard_map/ppermute | solution.py:52
  68.5 30.3 %copy-start.6 = (bf16[192,2048]{1,0:T(8,128)(2,1)}, bf16[192,2048]{1,0:T(8,128)(2,1)S(1)}, u32[]{:S(2)}) copy-start(bf16[192,2048]{1,0:T(8,128)(2,1)S(1)} %get-tuple-element.31) | copy-start | bytes 2359300
  74.4 36.9 %collective-permute-start.15 = (bf16[192,2048]{1,0:T(8,128)(2,1)}, bf16[192,2048]{1,0:T(8,128)(2,1)}, u32[]{:S(2)}, u32[]{:S(2)}) collective-permute-start(bf16[192,2048]{1,0:T(8,128)(2,1)} %collective-permute-done.13), channel_id=1, source_target_pairs={{2,4},{4,2},{3,5},{5,3},{10,12},{12,10},{11,13},{13,11},{18,20},{2... | collective-permute-start | bytes 2359304 | tf_op jit(solution)/shard_map/ppermute | solution.py:52
  75.9 2.9 %copy-start.20 = (bf16[384,256]{1,0:T(8,128)(2,1)}, bf16[384,256]{1,0:T(8,128)(2,1)S(1)}, u32[]{:S(2)}) copy-start(bf16[384,256]{1,0:T(8,128)(2,1)S(1)} %collective-permute-done.11) | copy-start | bytes 589828
  78.9 3.6 %copy-start.11 = (bf16[1,128,2560]{2,1,0:T(8,128)(2,1)S(1)}, bf16[1,128,2560]{2,1,0:T(8,128)(2,1)}, u32[]{:S(2)}) copy-start(bf16[1,128,2560]{2,1,0:T(8,128)(2,1)} %param.5) | copy-start | bytes 1966084
  78.9 3.6 %copy-start.13 = (bf16[128,2560]{1,0:T(8,128)(2,1)S(1)}, bf16[128,2560]{1,0:T(8,128)(2,1)}, u32[]{:S(2)}) copy-start(bf16[128,2560]{1,0:T(8,128)(2,1)} %copy-done.12) | copy-start | bytes 1966084
  78.9 3.6 %copy-start.15 = (bf16[128,2560]{1,0:T(8,128)(2,1)S(1)}, bf16[128,2560]{1,0:T(8,128)(2,1)}, u32[]{:S(2)}) copy-start(bf16[128,2560]{1,0:T(8,128)(2,1)} %copy-done.14) | copy-start | bytes 1966084
  78.9 3.6 %copy-start.17 = (bf16[128,2560]{1,0:T(8,128)(2,1)S(1)}, bf16[128,2560]{1,0:T(8,128)(2,1)}, u32[]{:S(2)}) copy-start(bf16[128,2560]{1,0:T(8,128)(2,1)} %copy-done.16) | copy-start | bytes 1966084
  78.9 3.6 %copy-start.19 = (bf16[128,2560]{1,0:T(8,128)(2,1)S(1)}, bf16[128,2560]{1,0:T(8,128)(2,1)}, u32[]{:S(2)}) copy-start(bf16[128,2560]{1,0:T(8,128)(2,1)} %copy-done.18) | copy-start | bytes 1966084
  83.2 15.6 %copy-start.4 = (bf16[192,2048]{1,0:T(8,128)(2,1)S(1)}, bf16[192,2048]{1,0:T(8,128)(2,1)}, u32[]{:S(2)}) copy-start(bf16[192,2048]{1,0:T(8,128)(2,1)} %copy-done.3) | copy-start | bytes 2359300
  95.8 2.9 %copy-start = (bf16[128,4096]{1,0:T(8,128)(2,1)}, bf16[128,4096]{1,0:T(8,128)(2,1)S(1)}, u32[]{:S(2)}) copy-start(bf16[128,4096]{1,0:T(8,128)(2,1)S(1)} %collective-permute-done.9) | copy-start | bytes 3145732
  98.7 3.1 %copy-start.22 = (f32[768,256]{1,0:T(8,128)}, f32[768,256]{1,0:T(8,128)S(1)}, u32[]{:S(2)}) copy-start(f32[768,256]{1,0:T(8,128)S(1)} %fusion.19) | copy-start | bytes 2359300
  101.9 8.2 %collective-permute-start.14 = (bf16[576,256]{1,0:T(8,128)(2,1)}, bf16[576,256]{1,0:T(8,128)(2,1)}, u32[]{:S(2)}, u32[]{:S(2)}) collective-permute-start(bf16[576,256]{1,0:T(8,128)(2,1)} %fusion.29), channel_id=1, source_target_pairs={{0,1},{1,0},{2,3},{3,2},{4,5},{5,4},{6,7},{7,6},{8,9},{9,8},{10,11... | collective-permute-start | bytes 884744 | tf_op jit(solution)/shard_map/ppermute | solution.py:60
  103.4 7.9 %copy-start.1 = (bf16[128,4096]{1,0:T(8,128)(2,1)S(1)}, bf16[128,4096]{1,0:T(8,128)(2,1)}, u32[]{:S(2)}) copy-start(bf16[128,4096]{1,0:T(8,128)(2,1)} %copy-done) | copy-start | bytes 3145732
  104.5 10.1 %copy-start.5 = (bf16[192,2048]{1,0:T(8,128)(2,1)S(1)}, bf16[192,2048]{1,0:T(8,128)(2,1)}, u32[]{:S(2)}) copy-start(bf16[192,2048]{1,0:T(8,128)(2,1)} %copy-done.3) | copy-start | bytes 2359300
  104.6 10.1 %copy-start.7 = (bf16[192,2048]{1,0:T(8,128)(2,1)S(1)}, bf16[192,2048]{1,0:T(8,128)(2,1)}, u32[]{:S(2)}) copy-start(bf16[192,2048]{1,0:T(8,128)(2,1)} %copy-done.6) | copy-start | bytes 2359300
  104.6 10.1 %copy-start.9 = (bf16[384,256]{1,0:T(8,128)(2,1)S(1)}, bf16[384,256]{1,0:T(8,128)(2,1)}, u32[]{:S(2)}) copy-start(bf16[384,256]{1,0:T(8,128)(2,1)} %copy-done.8) | copy-start | bytes 589828
  104.6 10.1 %copy-start.21 = (bf16[384,256]{1,0:T(8,128)(2,1)S(1)}, bf16[384,256]{1,0:T(8,128)(2,1)}, u32[]{:S(2)}) copy-start(bf16[384,256]{1,0:T(8,128)(2,1)} %copy-done.20) | copy-start | bytes 589828
  104.6 18.0 %collective-permute-start.17 = (bf16[128,2048]{1,0:T(8,128)(2,1)S(1)}, bf16[128,2048]{1,0:T(8,128)(2,1)S(1)}, u32[]{:S(2)}, u32[]{:S(2)}) collective-permute-start(bf16[128,2048]{1,0:T(8,128)(2,1)S(1)} %slice.123), channel_id=1, source_target_pairs={{2,0},{4,6},{3,1},{5,7},{10,8},{12,14},{11,9},{13,15},{18,16},{20,... | collective-permute-start | bytes 1572872 | tf_op jit(solution)/shard_map/ppermute | solution.py:56
  113.1 10.2 %copy-start.2 = (bf16[256,2048]{1,0:T(8,128)(2,1)S(1)}, bf16[256,2048]{1,0:T(8,128)(2,1)}, u32[]{:S(2)}) copy-start(bf16[256,2048]{1,0:T(8,128)(2,1)} %convolution_convert_fusion.4) | copy-start | bytes 3145732
  113.1 5.3 %collective-permute-start.16 = (bf16[192,256]{1,0:T(8,128)(2,1)S(1)}, bf16[192,256]{1,0:T(8,128)(2,1)S(1)}, u32[]{:S(2)}, u32[]{:S(2)}) collective-permute-start(bf16[192,256]{1,0:T(8,128)(2,1)S(1)} %fusion.30), channel_id=1, source_target_pairs={{0,1},{1,0},{2,3},{3,2},{4,5},{5,4},{6,7},{7,6},{8,9},{9,8},{10,11... | collective-permute-start | bytes 294920 | tf_op jit(solution)/shard_map/ppermute | solution.py:60
  117.1 31.7 %collective-permute-start.26 = (bf16[128,2048]{1,0:T(8,128)(2,1)S(1)}, bf16[128,2048]{1,0:T(8,128)(2,1)S(1)}, u32[]{:S(2)}, u32[]{:S(2)}) collective-permute-start(bf16[128,2048]{1,0:T(8,128)(2,1)S(1)} %slice.138), channel_id=1, source_target_pairs={{2,0},{4,6},{3,1},{5,7},{10,8},{12,14},{11,9},{13,15},{18,16},{20,... | collective-permute-start | bytes 1572872 | tf_op jit(solution)/shard_map/ppermute | solution.py:56
  122.6 0.8 collective-permute-start.18
  123.4 1.2 copy-start.24
  123.4 1.5 copy-start.26
  126.1 19.2 %collective-permute-start.21 = (bf16[128,1280]{1,0:T(8,128)(2,1)S(1)}, bf16[128,1280]{1,0:T(8,128)(2,1)S(1)}, u32[]{:S(2)}, u32[]{:S(2)}) collective-permute-start(bf16[128,1280]{1,0:T(8,128)(2,1)S(1)} %convolution_convert_fusion.6), channel_id=1, source_target_pairs={{2,4},{4,2},{3,5},{5,3},{10,12},{12,10},{11,13},{13,11},{18,20},{2... | collective-permute-start | bytes 983048 | tf_op jit(solution)/shard_map/ppermute | solution.py:52
  126.8 15.9 %collective-permute-start.19 = (bf16[192,512]{1,0:T(8,128)(2,1)S(1)}, bf16[192,512]{1,0:T(8,128)(2,1)S(1)}, u32[]{:S(2)}, u32[]{:S(2)}) collective-permute-start(bf16[192,512]{1,0:T(8,128)(2,1)S(1)} %slice.125), channel_id=1, source_target_pairs={{2,0},{4,6},{3,1},{5,7},{10,8},{12,14},{11,9},{13,15},{18,16},{20,... | collective-permute-start | bytes 589832 | tf_op jit(solution)/shard_map/ppermute | solution.py:56
  128.7 18.8 %collective-permute-start.24 = (bf16[128,1280]{1,0:T(8,128)(2,1)S(1)}, bf16[128,1280]{1,0:T(8,128)(2,1)S(1)}, u32[]{:S(2)}, u32[]{:S(2)}) collective-permute-start(bf16[128,1280]{1,0:T(8,128)(2,1)S(1)} %convolution_convert_fusion.5), channel_id=1, source_target_pairs={{2,4},{4,2},{3,5},{5,3},{10,12},{12,10},{11,13},{13,11},{18,20},{2... | collective-permute-start | bytes 983048 | tf_op jit(solution)/shard_map/ppermute | solution.py:52
  143.4 13.5 %collective-permute-start.20 = (bf16[192,2560]{1,0:T(8,128)(2,1)S(1)}, bf16[192,2560]{1,0:T(8,128)(2,1)S(1)}, u32[]{:S(2)}, u32[]{:S(2)}) collective-permute-start(bf16[192,2560]{1,0:T(8,128)(2,1)S(1)} %convolution_convert_fusion), channel_id=1, source_target_pairs={{8,0},{16,8},{24,16},{9,1},{17,9},{25,17},{10,2},{18,10},{26,18},{... | collective-permute-start | bytes 2949128 | tf_op jit(solution)/shard_map/ppermute | solution.py:13
  145.4 19.1 %collective-permute-start.23 = (bf16[128,1280]{1,0:T(8,128)(2,1)S(1)}, bf16[128,1280]{1,0:T(8,128)(2,1)S(1)}, u32[]{:S(2)}, u32[]{:S(2)}) collective-permute-start(bf16[128,1280]{1,0:T(8,128)(2,1)S(1)} %add_convert_fusion.2), channel_id=1, source_target_pairs={{2,0},{4,6},{3,1},{5,7},{10,8},{12,14},{11,9},{13,15},{18,16},{20,... | collective-permute-start | bytes 983048 | tf_op jit(solution)/shard_map/ppermute | solution.py:56
  146.7 11.2 %collective-permute-start.22 = (bf16[128,2560]{1,0:T(8,128)(2,1)S(1)}, bf16[128,2560]{1,0:T(8,128)(2,1)S(1)}, u32[]{:S(2)}, u32[]{:S(2)}) collective-permute-start(bf16[128,2560]{1,0:T(8,128)(2,1)S(1)} %convolution_convert_fusion.2), channel_id=1, source_target_pairs={{2,4},{4,2},{3,5},{5,3},{10,12},{12,10},{11,13},{13,11},{18,20},{2... | collective-permute-start | bytes 1966088 | tf_op jit(solution)/shard_map/ppermute | solution.py:52
  147.6 17.0 %collective-permute-start.25 = (bf16[128,1280]{1,0:T(8,128)(2,1)S(1)}, bf16[128,1280]{1,0:T(8,128)(2,1)S(1)}, u32[]{:S(2)}, u32[]{:S(2)}) collective-permute-start(bf16[128,1280]{1,0:T(8,128)(2,1)S(1)} %add_convert_fusion.1), channel_id=1, source_target_pairs={{2,0},{4,6},{3,1},{5,7},{10,8},{12,14},{11,9},{13,15},{18,16},{20,... | collective-permute-start | bytes 983048 | tf_op jit(solution)/shard_map/ppermute | solution.py:56

commit v12 on v11

--- a/solution.py
+++ b/solution.py
@@ -164,8 +164,6 @@
     latent_used = jnp.where(middle, latent_bf[:rows], latent_there)
     input_grad = jnp.dot(latent_used, down_used, preferred_element_type=F32).astype(BF16)
     passed = shifted(input_grad, "section", -1)
-    final = lax.axis_index("section") == lax.axis_size("section") - 1
-    passed = jnp.where(final, jnp.zeros_like(passed), passed)
     down_own_grad = (sums[0] + after(from_own, passed).astype(F32)).astype(BF16)
     down_grad = jnp.where(middle, down_own_grad, down_end_grad)
     return (passed[None], down_grad[None], up_grad[None])

time: 169 us -> 164 us (0.970)
  matrix products: 18.9 us -> 12.6 us
  waiting for transfers between devices: 89.7 us -> 93 us
  other arithmetic: 5.19 us -> 3.1 us
    dot_general x4, matrix products: 9.07 us -> 4.98 us  [rows_dot(): lax.dot_general(left, right, (((1,), (1,)), ((), ())), preferred_element_...]
    ppermute x5, waiting for transfers between devices: 45.4 us -> 48.1 us  [inward(): return lax.ppermute(value, 'row', [(0, 1), (3, 2)])]
    dot_general x7, matrix products: 9.09 us -> 6.97 us  [tokens_dot(): lax.dot_general(left, right, (((0,), (0,)), ((), ())), preferred_element_...]
  transfers between devices with their start and end apart: 27 -> 27, of which waited for: 13 -> 14; matrix products, arithmetic and copies ran while one was open for 16% -> 11% of each run, Pallas kernels for 0% -> 0%
where the time goes in v12:
time: 164 us; the launch traced here: 161 us
  waiting for transfers between devices  93 us (57%)
  starting transfers between devices  45.8 us (28%)
  matrix products  12.6 us (8%)
  local copies, waits for them, and re-layouts  4.91 us (3%)
  other arithmetic  3.1 us (2%)
    ppermute x5, waiting for transfers between devices, inward(): return lax.ppermute(value, 'row', [(0, 1), (3, 2)])  48.1 us
    ppermute x8, waiting for transfers between devices, outward(): return lax.ppermute(value, 'row', [(1, 0), (2, 3)])  32.3 us
    ppermute x5, starting transfers between devices, inward(): return lax.ppermute(value, 'row', [(0, 1), (3, 2)])  22 us
    ppermute x8, starting transfers between devices, outward(): return lax.ppermute(value, 'row', [(1, 0), (2, 3)])  10.3 us
    dot_general x7, matrix products, tokens_dot(): lax.dot_general(left, right, (((0,), (0,)), ((), ())), preferred_element_...  6.97 us
    ppermute x10, starting transfers between devices, across(): return lax.ppermute(value, 'row', [(1, 2), (2, 1)])  6.95 us
    ppermute x1, waiting for transfers between devices, shifted(): lax.ppermute(value, axis, [(source, source + steps) for source in range(l...  6.94 us
    ppermute x3, waiting for transfers between devices, other_col(): return lax.ppermute(value, 'col', [(0, 1), (1, 0)])  5.62 us
  transfers between devices with their start and end apart: 27, of which 14 were waited for; matrix products, arithmetic and copies ran while one was open for 11% of the time, Pallas kernels for 0%

profile of v12, /device:TPU:4, one launch (start us, length us, event | category | flops | bytes accessed | tf_op | source)
XLA Modules:
  0.0 160.7 jit_solution(11350497148637649350)
XLA Ops:
  0.7 3.7 %collective-permute-start.2 = (bf16[128,2560]{1,0:T(8,128)(2,1)}, bf16[128,2560]{1,0:T(8,128)(2,1)S(1)}, u32[]{:S(2)}, u32[]{:S(2)}) collective-permute-start(bf16[128,2560]{1,0:T(8,128)(2,1)} %bitcast.19), channel_id=1, source_target_pairs={{0,2},{6,4},{1,3},{7,5},{8,10},{14,12},{9,11},{15,13},{16,18},{22,... | collective-permute-start | bytes 1966088 | tf_op jit(solution)/shard_map/ppermute | solution.py:48
  4.3 1.4 collective-permute-start
  5.7 1.3 collective-permute-start.1
  7.0 0.7 collective-permute-start.3
  7.7 12.0 %collective-permute-done.2 = bf16[128,2560]{1,0:T(8,128)(2,1)S(1)} collective-permute-done((bf16[128,2560]{1,0:T(8,128)(2,1)}, bf16[128,2560]{1,0:T(8,128)(2,1)S(1)}, u32[]{:S(2)}, u32[]{:S(2)}) %collective-permute-start.2) | collective-permute-done | bytes 655392 | tf_op jit(solution)/shard_map/ppermute | solution.py:48
  19.7 0.7 collective-permute-start.4
  20.4 0.8 collective-permute-start.7
  21.2 2.7 %fusion.51 = (bf16[192,2048]{1,0:T(8,128)(2,1)}, bf16[192,2048]{1,0:T(8,128)(2,1)}) fusion(bf16[192,4096]{1,0:T(8,128)(2,1)} %bitcast.13), kind=kLoop, calls=%fused_computation.82 | loop fusion | bytes 3145728 | tf_op jit(solution)/shard_map/slice | solution.py:119
  23.9 0.1 collective-permute-done.1
  24.0 9.5 %collective-permute-start.6 = (bf16[192,2048]{1,0:T(8,128)(2,1)}, bf16[192,2048]{1,0:T(8,128)(2,1)}, u32[]{:S(2)}, u32[]{:S(2)}) collective-permute-start(bf16[192,2048]{1,0:T(8,128)(2,1)} %get-tuple-element.34), channel_id=1, source_target_pairs={{0,2},{6,4},{1,3},{7,5},{8,10},{14,12},{9,11},{15,13},{16,18},{22,... | collective-permute-start | bytes 2359304 | tf_op jit(solution)/shard_map/ppermute | solution.py:48
  33.4 7.3 %collective-permute-done = bf16[192,2560]{1,0:T(8,128)(2,1)S(1)} collective-permute-done((bf16[192,2560]{1,0:T(8,128)(2,1)}, bf16[192,2560]{1,0:T(8,128)(2,1)S(1)}, u32[]{:S(2)}, u32[]{:S(2)}) %collective-permute-start) | collective-permute-done | bytes 983072 | tf_op jit(solution)/shard_map/ppermute | solution.py:48
  40.8 1.2 convolution_convert_fusion.7
  42.2 1.5 collective-permute-start.5
  43.7 4.6 %collective-permute-start.13 = (bf16[192,2048]{1,0:T(8,128)(2,1)}, bf16[192,2048]{1,0:T(8,128)(2,1)S(1)}, u32[]{:S(2)}, u32[]{:S(2)}) collective-permute-start(bf16[192,2048]{1,0:T(8,128)(2,1)} %get-tuple-element.22), channel_id=1, source_target_pairs={{0,2},{6,4},{1,3},{7,5},{8,10},{14,12},{9,11},{15,13},{16,18},{22,... | collective-permute-start | bytes 2359304 | tf_op jit(solution)/shard_map/ppermute | solution.py:48
  48.3 1.3 collective-permute-start.10
  49.6 8.1 %collective-permute-done.6 = bf16[192,2048]{1,0:T(8,128)(2,1)} collective-permute-done((bf16[192,2048]{1,0:T(8,128)(2,1)}, bf16[192,2048]{1,0:T(8,128)(2,1)}, u32[]{:S(2)}, u32[]{:S(2)}) %collective-permute-start.6) | collective-permute-done | bytes 786464 | tf_op jit(solution)/shard_map/ppermute | solution.py:48
  57.6 0.7 collective-permute-start.8
  58.3 1.3 collective-permute-start.12
  59.6 0.2 multiply_reduce_fusion.1
  59.9 0.1 fusion.28
  60.0 4.4 %collective-permute-done.10 = bf16[128,2560]{1,0:T(8,128)(2,1)S(1)} collective-permute-done((bf16[128,2560]{1,0:T(8,128)(2,1)}, bf16[128,2560]{1,0:T(8,128)(2,1)S(1)}, u32[]{:S(2)}, u32[]{:S(2)}) %collective-permute-start.10) | collective-permute-done | bytes 655392 | tf_op jit(solution)/shard_map/ppermute | solution.py:56
  64.4 2.9 %collective-permute-start.9 = (bf16[128,4096]{1,0:T(8,128)(2,1)S(1)}, bf16[128,4096]{1,0:T(8,128)(2,1)S(1)}, u32[]{:S(2)}, u32[]{:S(2)}) collective-permute-start(bf16[128,4096]{1,0:T(8,128)(2,1)S(1)} %bitcast.14), channel_id=1, source_target_pairs={{0,2},{6,4},{1,3},{7,5},{8,10},{14,12},{9,11},{15,13},{16,18},{22,... | collective-permute-start | bytes 3145736 | tf_op jit(solution)/shard_map/ppermute | solution.py:48
  67.3 0.7 collective-permute-start.11
  68.0 0.1 fusion.50
  68.1 6.3 %collective-permute-done.13 = bf16[192,2048]{1,0:T(8,128)(2,1)S(1)} collective-permute-done((bf16[192,2048]{1,0:T(8,128)(2,1)}, bf16[192,2048]{1,0:T(8,128)(2,1)S(1)}, u32[]{:S(2)}, u32[]{:S(2)}) %collective-permute-start.13) | collective-permute-done | bytes 786464 | tf_op jit(solution)/shard_map/ppermute | solution.py:48
  74.5 0.7 collective-permute-start.15
  75.2 2.8 %collective-permute-done.12 = bf16[128,2560]{1,0:T(8,128)(2,1)S(1)} collective-permute-done((bf16[128,2560]{1,0:T(8,128)(2,1)}, bf16[128,2560]{1,0:T(8,128)(2,1)S(1)}, u32[]{:S(2)}, u32[]{:S(2)}) %collective-permute-start.12) | collective-permute-done | bytes 655392 | tf_op jit(solution)/shard_map/ppermute | solution.py:56
  78.1 2.5 %convolution_convert_fusion.4 = bf16[256,2048]{1,0:T(8,128)(2,1)S(1)} fusion(bf16[768,256]{1,0:T(8,128)(2,1)S(1)} %pad_maximum_fusion.8, bf16[192,2048]{1,0:T(8,128)(2,1)S(1)} %collective-permute-done.8, bf16[192,2048]{1,0:T(8,128)(2,1)S(1)} %get-tuple-element.32, bf16[192,2048]{1,0:T(8,128)(2,1)} %collective-permute-done.6, ...), kind=kOutput, calls=%fused_computation.17 | convolution fusion | flops 818413568 | bytes 4587520 | tf_op jit(solution)/shard_map/dot_general | solution.py:72
  80.7 0.7 maximum_select_fusion
  81.4 14.3 %collective-permute-done.9 = bf16[128,4096]{1,0:T(8,128)(2,1)S(1)} collective-permute-done((bf16[128,4096]{1,0:T(8,128)(2,1)S(1)}, bf16[128,4096]{1,0:T(8,128)(2,1)S(1)}, u32[]{:S(2)}, u32[]{:S(2)}) %collective-permute-start.9) | collective-permute-done | bytes 1048608 | tf_op jit(solution)/shard_map/ppermute | solution.py:48
  95.7 2.4 %fusion.19 = f32[768,256]{1,0:T(8,128)S(1)} fusion(bf16[128,4096]{1,0:T(8,128)(2,1)S(1)} %bitcast.15, bf16[128,4096]{1,0:T(8,128)(2,1)S(1)} %collective-permute-done.9, bf16[192,2048]{1,0:T(8,128)(2,1)S(1)} %collective-permute-done.8, bf16[192,2048]{1,0:T(8,128)(2,1)S(1)} %get-tuple-element.32, bf16[192,2048]{1,0:T(8,128)(2,1)} %collective-permute-done.6, ...), kind=kOutput, calls=%fused_computation.36 | convolution fusion | flops 819986432 | bytes 6029312 | tf_op jit(solution)/shard_map/dot_general | solution.py:68
  98.1 0.9 fusion.29
  99.0 1.6 collective-permute-start.14
  100.6 1.3 collective-permute-start.17
  101.9 5.0 %collective-permute-done.14 = bf16[576,256]{1,0:T(8,128)(2,1)S(1)} collective-permute-done((bf16[576,256]{1,0:T(8,128)(2,1)S(1)}, bf16[576,256]{1,0:T(8,128)(2,1)S(1)}, u32[]{:S(2)}, u32[]{:S(2)}) %collective-permute-start.14) | collective-permute-done | bytes 294944 | tf_op jit(solution)/shard_map/ppermute | solution.py:60
  107.1 0.5 fusion.30
  107.6 1.6 collective-permute-start.16
  109.1 1.2 fusion.9
  110.4 1.3 collective-permute-start.26
  111.7 0.6 collective-permute-done.16
  112.3 4.0 %collective-permute-done.17 = bf16[128,2048]{1,0:T(8,128)(2,1)S(1)} collective-permute-done((bf16[128,2048]{1,0:T(8,128)(2,1)S(1)}, bf16[128,2048]{1,0:T(8,128)(2,1)S(1)}, u32[]{:S(2)}, u32[]{:S(2)}) %collective-permute-start.17) | collective-permute-done | bytes 524320 | tf_op jit(solution)/shard_map/ppermute | solution.py:56
  116.3 0.7 collective-permute-start.18
  117.1 0.3 multiply_reduce_fusion
  117.4 0.2 multiply_convert_fusion
  117.7 0.6 copy-done.13
  118.3 0.3 copy-done.15
  118.6 0.4 convolution_convert_fusion.6
  118.9 0.4 convolution_convert_fusion.5
  119.3 0.5 convolution_convert_fusion.2
  119.8 0.7 collective-permute-start.21
  120.5 1.3 collective-permute-start.19
  121.8 0.5 convolution_convert_fusion.1
  122.4 0.7 collective-permute-start.24
  123.1 13.4 %collective-permute-done.19 = bf16[192,512]{1,0:T(8,128)(2,1)S(1)} collective-permute-done((bf16[192,512]{1,0:T(8,128)(2,1)S(1)}, bf16[192,512]{1,0:T(8,128)(2,1)S(1)}, u32[]{:S(2)}, u32[]{:S(2)}) %collective-permute-start.19) | collective-permute-done | bytes 196640 | tf_op jit(solution)/shard_map/ppermute | solution.py:56
  136.5 0.7 convolution_convert_fusion
  137.2 1.9 %collective-permute-start.20 = (bf16[192,2560]{1,0:T(8,128)(2,1)S(1)}, bf16[192,2560]{1,0:T(8,128)(2,1)S(1)}, u32[]{:S(2)}, u32[]{:S(2)}) collective-permute-start(bf16[192,2560]{1,0:T(8,128)(2,1)S(1)} %convolution_convert_fusion), channel_id=1, source_target_pairs={{8,0},{16,8},{24,16},{9,1},{17,9},{25,17},{10,2},{18,10},{26,18},{... | collective-permute-start | bytes 2949128 | tf_op jit(solution)/shard_map/ppermute | solution.py:13
  139.2 1.3 collective-permute-start.23
  140.5 0.7 collective-permute-start.22
  141.3 1.3 collective-permute-start.25
  142.7 1.1 maximum_bitcast_fusion
  143.8 6.9 %collective-permute-done.20 = bf16[192,2560]{1,0:T(8,128)(2,1)S(1)} collective-permute-done((bf16[192,2560]{1,0:T(8,128)(2,1)S(1)}, bf16[192,2560]{1,0:T(8,128)(2,1)S(1)}, u32[]{:S(2)}, u32[]{:S(2)}) %collective-permute-start.20) | collective-permute-done | bytes 983072 | tf_op jit(solution)/shard_map/ppermute | solution.py:13
  150.7 7.6 %collective-permute-done.25 = bf16[128,1280]{1,0:T(8,128)(2,1)S(1)} collective-permute-done((bf16[128,1280]{1,0:T(8,128)(2,1)S(1)}, bf16[128,1280]{1,0:T(8,128)(2,1)S(1)}, u32[]{:S(2)}, u32[]{:S(2)}) %collective-permute-start.25) | collective-permute-done | bytes 327712 | tf_op jit(solution)/shard_map/ppermute | solution.py:56
  158.3 1.5 fusion.27
  159.8 0.9 copy.8
  (60 shorter events, 0.8 us)
Async XLA Ops:
  0.6 40.2 %copy-start.2 = (bf16[1,128,2560]{2,1,0:T(8,128)(2,1)S(1)}, bf16[1,128,2560]{2,1,0:T(8,128)(2,1)}, u32[]{:S(2)}) copy-start(bf16[1,128,2560]{2,1,0:T(8,128)(2,1)} %param.5) | copy-start | bytes 1966084
  0.6 40.2 %copy-start.12 = (bf16[1,192,2560]{2,1,0:T(8,128)(2,1)S(1)}, bf16[1,192,2560]{2,1,0:T(8,128)(2,1)}, u32[]{:S(2)}) copy-start(bf16[1,192,2560]{2,1,0:T(8,128)(2,1)} %param.4) | copy-start | bytes 2949124
  0.7 19.1 %collective-permute-start.2 = (bf16[128,2560]{1,0:T(8,128)(2,1)}, bf16[128,2560]{1,0:T(8,128)(2,1)S(1)}, u32[]{:S(2)}, u32[]{:S(2)}) collective-permute-start(bf16[128,2560]{1,0:T(8,128)(2,1)} %bitcast.19), channel_id=1, source_target_pairs={{0,2},{6,4},{1,3},{7,5},{8,10},{14,12},{9,11},{15,13},{16,18},{22,... | collective-permute-start | bytes 1966088 | tf_op jit(solution)/shard_map/ppermute | solution.py:48
  4.3 36.5 %collective-permute-start = (bf16[192,2560]{1,0:T(8,128)(2,1)}, bf16[192,2560]{1,0:T(8,128)(2,1)S(1)}, u32[]{:S(2)}, u32[]{:S(2)}) collective-permute-start(bf16[192,2560]{1,0:T(8,128)(2,1)} %bitcast.24), channel_id=1, source_target_pairs={{0,2},{6,4},{1,3},{7,5},{8,10},{14,12},{9,11},{15,13},{16,18},{22,... | collective-permute-start | bytes 2949128 | tf_op jit(solution)/shard_map/ppermute | solution.py:48
  5.7 18.3 %collective-permute-start.1 = (bf16[128,2560]{1,0:T(8,128)(2,1)}, bf16[128,2560]{1,0:T(8,128)(2,1)S(1)}, u32[]{:S(2)}, u32[]{:S(2)}) collective-permute-start(bf16[128,2560]{1,0:T(8,128)(2,1)} %bitcast.20), channel_id=1, source_target_pairs={{2,0},{4,6},{3,1},{5,7},{10,8},{12,14},{11,9},{13,15},{18,16},{20,... | collective-permute-start | bytes 1966088 | tf_op jit(solution)/shard_map/ppermute | solution.py:56
  7.0 33.8 %collective-permute-start.3 = (bf16[128,2560]{1,0:T(8,128)(2,1)}, bf16[128,2560]{1,0:T(8,128)(2,1)S(1)}, u32[]{:S(2)}, u32[]{:S(2)}) collective-permute-start(bf16[128,2560]{1,0:T(8,128)(2,1)} %bitcast.21), channel_id=1, source_target_pairs={{2,4},{4,2},{3,5},{5,3},{10,12},{12,10},{11,13},{13,11},{18,20},{2... | collective-permute-start | bytes 1966088 | tf_op jit(solution)/shard_map/ppermute | solution.py:52
  19.7 21.1 %copy-start.4 = (bf16[128,2560]{1,0:T(8,128)(2,1)}, bf16[128,2560]{1,0:T(8,128)(2,1)S(1)}, u32[]{:S(2)}) copy-start(bf16[128,2560]{1,0:T(8,128)(2,1)S(1)} %collective-permute-done.2) | copy-start | bytes 1966084
  19.7 21.1 %collective-permute-start.4 = (bf16[128,2560]{1,0:T(8,128)(2,1)S(1)}, bf16[128,2560]{1,0:T(8,128)(2,1)S(1)}, u32[]{:S(2)}, u32[]{:S(2)}) collective-permute-start(bf16[128,2560]{1,0:T(8,128)(2,1)S(1)} %collective-permute-done.2), channel_id=1, source_target_pairs={{2,4},{4,2},{3,5},{5,3},{10,12},{12,10},{11,13},{13,11},{18,20},{2... | collective-permute-start | bytes 1966088 | tf_op jit(solution)/shard_map/ppermute | solution.py:52
  20.4 46.9 %collective-permute-start.7 = (bf16[192,4096]{1,0:T(8,128)(2,1)}, bf16[192,4096]{1,0:T(8,128)(2,1)S(1)}, u32[]{:S(2)}, u32[]{:S(2)}) collective-permute-start(bf16[192,4096]{1,0:T(8,128)(2,1)} %bitcast.12), channel_id=1, source_target_pairs={{2,4},{4,2},{3,5},{5,3},{10,12},{12,10},{11,13},{13,11},{18,20},{2... | collective-permute-start | bytes 4718600 | tf_op jit(solution)/shard_map/ppermute | solution.py:52
  24.0 16.8 %copy-start.6 = (bf16[128,2560]{1,0:T(8,128)(2,1)}, bf16[128,2560]{1,0:T(8,128)(2,1)S(1)}, u32[]{:S(2)}) copy-start(bf16[128,2560]{1,0:T(8,128)(2,1)S(1)} %collective-permute-done.1) | copy-start | bytes 1966084
  24.0 33.6 %collective-permute-start.6 = (bf16[192,2048]{1,0:T(8,128)(2,1)}, bf16[192,2048]{1,0:T(8,128)(2,1)}, u32[]{:S(2)}, u32[]{:S(2)}) collective-permute-start(bf16[192,2048]{1,0:T(8,128)(2,1)} %get-tuple-element.34), channel_id=1, source_target_pairs={{0,2},{6,4},{1,3},{7,5},{8,10},{14,12},{9,11},{15,13},{16,18},{22,... | collective-permute-start | bytes 2359304 | tf_op jit(solution)/shard_map/ppermute | solution.py:48
  40.8 1.3 copy-start.14
  40.8 1.3 copy-start.8
  40.8 1.3 copy-start.10
  42.2 22.3 %copy-start = (bf16[1,128,4096]{2,1,0:T(8,128)(2,1)S(1)}, bf16[1,128,4096]{2,1,0:T(8,128)(2,1)}, u32[]{:S(2)}) copy-start(bf16[1,128,4096]{2,1,0:T(8,128)(2,1)} %param.6) | copy-start | bytes 3145732
  42.2 16.2 %collective-permute-start.5 = (bf16[384,512]{1,0:T(8,128)(2,1)S(1)}, bf16[384,512]{1,0:T(8,128)(2,1)S(1)}, u32[]{:S(2)}, u32[]{:S(2)}) collective-permute-start(bf16[384,512]{1,0:T(8,128)(2,1)S(1)} %convolution_convert_fusion.7), channel_id=1, source_target_pairs={{0,1},{1,0},{2,3},{3,2},{4,5},{5,4},{6,7},{7,6},{8,9},{9,8},{10,11... | collective-permute-start | bytes 1179656 | tf_op jit(solution)/shard_map/ppermute | solution.py:60
  43.7 30.8 %collective-permute-start.13 = (bf16[192,2048]{1,0:T(8,128)(2,1)}, bf16[192,2048]{1,0:T(8,128)(2,1)S(1)}, u32[]{:S(2)}, u32[]{:S(2)}) collective-permute-start(bf16[192,2048]{1,0:T(8,128)(2,1)} %get-tuple-element.22), channel_id=1, source_target_pairs={{0,2},{6,4},{1,3},{7,5},{8,10},{14,12},{9,11},{15,13},{16,18},{22,... | collective-permute-start | bytes 2359304 | tf_op jit(solution)/shard_map/ppermute | solution.py:48
  48.3 16.2 %collective-permute-start.10 = (bf16[128,2560]{1,0:T(8,128)(2,1)}, bf16[128,2560]{1,0:T(8,128)(2,1)S(1)}, u32[]{:S(2)}, u32[]{:S(2)}) collective-permute-start(bf16[128,2560]{1,0:T(8,128)(2,1)} %copy-done.8), channel_id=1, source_target_pairs={{2,0},{4,6},{3,1},{5,7},{10,8},{12,14},{11,9},{13,15},{18,16},{20,... | collective-permute-start | bytes 1966088 | tf_op jit(solution)/shard_map/ppermute | solution.py:56
  57.6 20.4 %collective-permute-start.8 = (bf16[192,2048]{1,0:T(8,128)(2,1)}, bf16[192,2048]{1,0:T(8,128)(2,1)S(1)}, u32[]{:S(2)}, u32[]{:S(2)}) collective-permute-start(bf16[192,2048]{1,0:T(8,128)(2,1)} %collective-permute-done.6), channel_id=1, source_target_pairs={{2,4},{4,2},{3,5},{5,3},{10,12},{12,10},{11,13},{13,11},{18,20},{2... | collective-permute-start | bytes 2359304 | tf_op jit(solution)/shard_map/ppermute | solution.py:52
  58.3 19.7 %collective-permute-start.12 = (bf16[128,2560]{1,0:T(8,128)(2,1)}, bf16[128,2560]{1,0:T(8,128)(2,1)S(1)}, u32[]{:S(2)}, u32[]{:S(2)}) collective-permute-start(bf16[128,2560]{1,0:T(8,128)(2,1)} %copy-done.10), channel_id=1, source_target_pairs={{2,0},{4,6},{3,1},{5,7},{10,8},{12,14},{11,9},{13,15},{18,16},{20,... | collective-permute-start | bytes 1966088 | tf_op jit(solution)/shard_map/ppermute | solution.py:56
  64.4 31.3 %collective-permute-start.9 = (bf16[128,4096]{1,0:T(8,128)(2,1)S(1)}, bf16[128,4096]{1,0:T(8,128)(2,1)S(1)}, u32[]{:S(2)}, u32[]{:S(2)}) collective-permute-start(bf16[128,4096]{1,0:T(8,128)(2,1)S(1)} %bitcast.14), channel_id=1, source_target_pairs={{0,2},{6,4},{1,3},{7,5},{8,10},{14,12},{9,11},{15,13},{16,18},{22,... | collective-permute-start | bytes 3145736 | tf_op jit(solution)/shard_map/ppermute | solution.py:48
  67.3 7.8 %collective-permute-start.11 = (bf16[384,256]{1,0:T(8,128)(2,1)S(1)}, bf16[384,256]{1,0:T(8,128)(2,1)S(1)}, u32[]{:S(2)}, u32[]{:S(2)}) collective-permute-start(bf16[384,256]{1,0:T(8,128)(2,1)S(1)} %get-tuple-element.19), channel_id=1, source_target_pairs={{2,4},{4,2},{3,5},{5,3},{10,12},{12,10},{11,13},{13,11},{18,20},{2... | collective-permute-start | bytes 589832 | tf_op jit(solution)/shard_map/ppermute | solution.py:52
  74.5 32.6 %collective-permute-start.15 = (bf16[192,2048]{1,0:T(8,128)(2,1)S(1)}, bf16[192,2048]{1,0:T(8,128)(2,1)S(1)}, u32[]{:S(2)}, u32[]{:S(2)}) collective-permute-start(bf16[192,2048]{1,0:T(8,128)(2,1)S(1)} %collective-permute-done.13), channel_id=1, source_target_pairs={{2,4},{4,2},{3,5},{5,3},{10,12},{12,10},{11,13},{13,11},{18,20},{2... | collective-permute-start | bytes 2359304 | tf_op jit(solution)/shard_map/ppermute | solution.py:52
  78.0 2.6 %copy-start.3 = (bf16[1,128,2560]{2,1,0:T(8,128)(2,1)S(1)}, bf16[1,128,2560]{2,1,0:T(8,128)(2,1)}, u32[]{:S(2)}) copy-start(bf16[1,128,2560]{2,1,0:T(8,128)(2,1)} %param.5) | copy-start | bytes 1966084
  78.0 2.6 %copy-start.5 = (bf16[128,2560]{1,0:T(8,128)(2,1)S(1)}, bf16[128,2560]{1,0:T(8,128)(2,1)}, u32[]{:S(2)}) copy-start(bf16[128,2560]{1,0:T(8,128)(2,1)} %copy-done.4) | copy-start | bytes 1966084
  78.0 2.6 %copy-start.7 = (bf16[128,2560]{1,0:T(8,128)(2,1)S(1)}, bf16[128,2560]{1,0:T(8,128)(2,1)}, u32[]{:S(2)}) copy-start(bf16[128,2560]{1,0:T(8,128)(2,1)} %copy-done.6) | copy-start | bytes 1966084
  78.0 2.6 %copy-start.9 = (bf16[128,2560]{1,0:T(8,128)(2,1)S(1)}, bf16[128,2560]{1,0:T(8,128)(2,1)}, u32[]{:S(2)}) copy-start(bf16[128,2560]{1,0:T(8,128)(2,1)} %copy-done.8) | copy-start | bytes 1966084
  78.1 2.6 %copy-start.11 = (bf16[128,2560]{1,0:T(8,128)(2,1)S(1)}, bf16[128,2560]{1,0:T(8,128)(2,1)}, u32[]{:S(2)}) copy-start(bf16[128,2560]{1,0:T(8,128)(2,1)} %copy-done.10) | copy-start | bytes 1966084
  81.4 16.7 %copy-start.1 = (bf16[192,2048]{1,0:T(8,128)(2,1)S(1)}, bf16[192,2048]{1,0:T(8,128)(2,1)}, u32[]{:S(2)}) copy-start(bf16[192,2048]{1,0:T(8,128)(2,1)} %get-tuple-element.22) | copy-start | bytes 2359300
  99.0 7.9 %collective-permute-start.14 = (bf16[576,256]{1,0:T(8,128)(2,1)S(1)}, bf16[576,256]{1,0:T(8,128)(2,1)S(1)}, u32[]{:S(2)}, u32[]{:S(2)}) collective-permute-start(bf16[576,256]{1,0:T(8,128)(2,1)S(1)} %fusion.29), channel_id=1, source_target_pairs={{0,1},{1,0},{2,3},{3,2},{4,5},{5,4},{6,7},{7,6},{8,9},{9,8},{10,11... | collective-permute-start | bytes 884744 | tf_op jit(solution)/shard_map/ppermute | solution.py:60
  100.6 15.7 %collective-permute-start.17 = (bf16[128,2048]{1,0:T(8,128)(2,1)S(1)}, bf16[128,2048]{1,0:T(8,128)(2,1)S(1)}, u32[]{:S(2)}, u32[]{:S(2)}) collective-permute-start(bf16[128,2048]{1,0:T(8,128)(2,1)S(1)} %slice.123), channel_id=1, source_target_pairs={{2,0},{4,6},{3,1},{5,7},{10,8},{12,14},{11,9},{13,15},{18,16},{20,... | collective-permute-start | bytes 1572872 | tf_op jit(solution)/shard_map/ppermute | solution.py:56
  107.6 4.7 %collective-permute-start.16 = (bf16[192,256]{1,0:T(8,128)(2,1)S(1)}, bf16[192,256]{1,0:T(8,128)(2,1)S(1)}, u32[]{:S(2)}, u32[]{:S(2)}) collective-permute-start(bf16[192,256]{1,0:T(8,128)(2,1)S(1)} %fusion.30), channel_id=1, source_target_pairs={{0,1},{1,0},{2,3},{3,2},{4,5},{5,4},{6,7},{7,6},{8,9},{9,8},{10,11... | collective-permute-start | bytes 294920 | tf_op jit(solution)/shard_map/ppermute | solution.py:60
  110.4 32.2 %collective-permute-start.26 = (bf16[128,2048]{1,0:T(8,128)(2,1)S(1)}, bf16[128,2048]{1,0:T(8,128)(2,1)S(1)}, u32[]{:S(2)}, u32[]{:S(2)}) collective-permute-start(bf16[128,2048]{1,0:T(8,128)(2,1)S(1)} %slice.138), channel_id=1, source_target_pairs={{2,0},{4,6},{3,1},{5,7},{10,8},{12,14},{11,9},{13,15},{18,16},{20,... | collective-permute-start | bytes 1572872 | tf_op jit(solution)/shard_map/ppermute | solution.py:56
  116.3 0.8 collective-permute-start.18
  117.1 1.2 copy-start.13
  117.1 1.5 copy-start.15
  119.8 19.3 %collective-permute-start.21 = (bf16[128,1280]{1,0:T(8,128)(2,1)S(1)}, bf16[128,1280]{1,0:T(8,128)(2,1)S(1)}, u32[]{:S(2)}, u32[]{:S(2)}) collective-permute-start(bf16[128,1280]{1,0:T(8,128)(2,1)S(1)} %convolution_convert_fusion.6), channel_id=1, source_target_pairs={{2,4},{4,2},{3,5},{5,3},{10,12},{12,10},{11,13},{13,11},{18,20},{2... | collective-permute-start | bytes 983048 | tf_op jit(solution)/shard_map/ppermute | solution.py:52
  120.5 16.0 %collective-permute-start.19 = (bf16[192,512]{1,0:T(8,128)(2,1)S(1)}, bf16[192,512]{1,0:T(8,128)(2,1)S(1)}, u32[]{:S(2)}, u32[]{:S(2)}) collective-permute-start(bf16[192,512]{1,0:T(8,128)(2,1)S(1)} %slice.125), channel_id=1, source_target_pairs={{2,0},{4,6},{3,1},{5,7},{10,8},{12,14},{11,9},{13,15},{18,16},{20,... | collective-permute-start | bytes 589832 | tf_op jit(solution)/shard_map/ppermute | solution.py:56
  122.4 18.9 %collective-permute-start.24 = (bf16[128,1280]{1,0:T(8,128)(2,1)S(1)}, bf16[128,1280]{1,0:T(8,128)(2,1)S(1)}, u32[]{:S(2)}, u32[]{:S(2)}) collective-permute-start(bf16[128,1280]{1,0:T(8,128)(2,1)S(1)} %convolution_convert_fusion.5), channel_id=1, source_target_pairs={{2,4},{4,2},{3,5},{5,3},{10,12},{12,10},{11,13},{13,11},{18,20},{2... | collective-permute-start | bytes 983048 | tf_op jit(solution)/shard_map/ppermute | solution.py:52
  137.2 13.5 %collective-permute-start.20 = (bf16[192,2560]{1,0:T(8,128)(2,1)S(1)}, bf16[192,2560]{1,0:T(8,128)(2,1)S(1)}, u32[]{:S(2)}, u32[]{:S(2)}) collective-permute-start(bf16[192,2560]{1,0:T(8,128)(2,1)S(1)} %convolution_convert_fusion), channel_id=1, source_target_pairs={{8,0},{16,8},{24,16},{9,1},{17,9},{25,17},{10,2},{18,10},{26,18},{... | collective-permute-start | bytes 2949128 | tf_op jit(solution)/shard_map/ppermute | solution.py:13
  139.2 19.1 %collective-permute-start.23 = (bf16[128,1280]{1,0:T(8,128)(2,1)S(1)}, bf16[128,1280]{1,0:T(8,128)(2,1)S(1)}, u32[]{:S(2)}, u32[]{:S(2)}) collective-permute-start(bf16[128,1280]{1,0:T(8,128)(2,1)S(1)} %add_convert_fusion.2), channel_id=1, source_target_pairs={{2,0},{4,6},{3,1},{5,7},{10,8},{12,14},{11,9},{13,15},{18,16},{20,... | collective-permute-start | bytes 983048 | tf_op jit(solution)/shard_map/ppermute | solution.py:56
  140.5 10.2 %collective-permute-start.22 = (bf16[128,2560]{1,0:T(8,128)(2,1)S(1)}, bf16[128,2560]{1,0:T(8,128)(2,1)S(1)}, u32[]{:S(2)}, u32[]{:S(2)}) collective-permute-start(bf16[128,2560]{1,0:T(8,128)(2,1)S(1)} %convolution_convert_fusion.2), channel_id=1, source_target_pairs={{2,4},{4,2},{3,5},{5,3},{10,12},{12,10},{11,13},{13,11},{18,20},{2... | collective-permute-start | bytes 1966088 | tf_op jit(solution)/shard_map/ppermute | solution.py:52
  141.3 17.0 %collective-permute-start.25 = (bf16[128,1280]{1,0:T(8,128)(2,1)S(1)}, bf16[128,1280]{1,0:T(8,128)(2,1)S(1)}, u32[]{:S(2)}, u32[]{:S(2)}) collective-permute-start(bf16[128,1280]{1,0:T(8,128)(2,1)S(1)} %add_convert_fusion.1), channel_id=1, source_target_pairs={{2,0},{4,6},{3,1},{5,7},{10,8},{12,14},{11,9},{13,15},{18,16},{20,... | collective-permute-start | bytes 983048 | tf_op jit(solution)/shard_map/ppermute | solution.py:56

commit v13 on v9

--- a/solution.py
+++ b/solution.py
@@ -149,7 +149,7 @@
     sent_end, sent_own = sums[3], sums[2]
     from_end = [across(sent_end[:, half]) for half in halves]
     end_first = (sums[1][:, halves[0]] + from_end[0].astype(F32)).astype(BF16)
-    from_own = across(after(sent_own, end_first))
+    from_own = across(after(sent_own, latent_there))
     end_second = sums[1][:, halves[1]] + after(from_end[1], end_first).astype(F32)
     end_second = end_second.astype(BF16)
     down_end_grad = jnp.concatenate([outward(end_first), outward(end_second)], axis=1)

time: 160 us -> 162 us (1.012)
  waiting for transfers between devices: 89.9 us -> 93.1 us
    ppermute x8, waiting for transfers between devices: 29.2 us -> 32.5 us  [outward(): return lax.ppermute(value, 'row', [(1, 0), (2, 3)])]
where the time goes in v13:
time: 162 us; the launch traced here: 161 us
  waiting for transfers between devices  93.1 us (57%)
  starting transfers between devices  45.8 us (28%)
  matrix products  12.5 us (8%)
  local copies, waits for them, and re-layouts  4.96 us (3%)
  other arithmetic  3.12 us (2%)
    ppermute x5, waiting for transfers between devices, inward(): return lax.ppermute(value, 'row', [(0, 1), (3, 2)])  48.1 us
    ppermute x8, waiting for transfers between devices, outward(): return lax.ppermute(value, 'row', [(1, 0), (2, 3)])  32.5 us
    ppermute x5, starting transfers between devices, inward(): return lax.ppermute(value, 'row', [(0, 1), (3, 2)])  22 us
    ppermute x8, starting transfers between devices, outward(): return lax.ppermute(value, 'row', [(1, 0), (2, 3)])  10.3 us
    ppermute x10, starting transfers between devices, across(): return lax.ppermute(value, 'row', [(1, 2), (2, 1)])  6.95 us
    ppermute x1, waiting for transfers between devices, shifted(): lax.ppermute(value, axis, [(source, source + steps) for source in range(l...  6.93 us
    dot_general x6, matrix products, tokens_dot(): lax.dot_general(left, right, (((0,), (0,)), ((), ())), preferred_element_...  6.81 us
    ppermute x3, waiting for transfers between devices, other_col(): return lax.ppermute(value, 'col', [(0, 1), (1, 0)])  5.62 us
  transfers between devices with their start and end apart: 27, of which 14 were waited for; matrix products, arithmetic and copies ran while one was open for 11% of the time, Pallas kernels for 0%

profile of v13, /device:TPU:4, one launch (start us, length us, event | category | flops | bytes accessed | tf_op | source)
XLA Modules:
  0.0 160.7 jit_solution(3911368648419204492)
XLA Ops:
  0.7 3.7 %collective-permute-start.2 = (bf16[128,2560]{1,0:T(8,128)(2,1)}, bf16[128,2560]{1,0:T(8,128)(2,1)S(1)}, u32[]{:S(2)}, u32[]{:S(2)}) collective-permute-start(bf16[128,2560]{1,0:T(8,128)(2,1)} %bitcast.19), channel_id=1, source_target_pairs={{0,2},{6,4},{1,3},{7,5},{8,10},{14,12},{9,11},{15,13},{16,18},{22,... | collective-permute-start | bytes 1966088 | tf_op jit(solution)/shard_map/ppermute | solution.py:48
  4.3 1.4 collective-permute-start
  5.7 1.3 collective-permute-start.1
  7.0 0.7 collective-permute-start.3
  7.7 12.0 %collective-permute-done.2 = bf16[128,2560]{1,0:T(8,128)(2,1)S(1)} collective-permute-done((bf16[128,2560]{1,0:T(8,128)(2,1)}, bf16[128,2560]{1,0:T(8,128)(2,1)S(1)}, u32[]{:S(2)}, u32[]{:S(2)}) %collective-permute-start.2) | collective-permute-done | bytes 655392 | tf_op jit(solution)/shard_map/ppermute | solution.py:48
  19.7 0.7 collective-permute-start.4
  20.4 0.8 collective-permute-start.7
  21.2 2.7 %fusion.44 = (bf16[192,2048]{1,0:T(8,128)(2,1)}, bf16[192,2048]{1,0:T(8,128)(2,1)}) fusion(bf16[192,4096]{1,0:T(8,128)(2,1)} %bitcast.13), kind=kLoop, calls=%fused_computation.72 | loop fusion | bytes 3145728 | tf_op jit(solution)/shard_map/slice | solution.py:119
  23.9 0.1 collective-permute-done.1
  24.0 9.5 %collective-permute-start.6 = (bf16[192,2048]{1,0:T(8,128)(2,1)}, bf16[192,2048]{1,0:T(8,128)(2,1)}, u32[]{:S(2)}, u32[]{:S(2)}) collective-permute-start(bf16[192,2048]{1,0:T(8,128)(2,1)} %get-tuple-element.32), channel_id=1, source_target_pairs={{0,2},{6,4},{1,3},{7,5},{8,10},{14,12},{9,11},{15,13},{16,18},{22,... | collective-permute-start | bytes 2359304 | tf_op jit(solution)/shard_map/ppermute | solution.py:48
  33.4 7.3 %collective-permute-done = bf16[192,2560]{1,0:T(8,128)(2,1)S(1)} collective-permute-done((bf16[192,2560]{1,0:T(8,128)(2,1)}, bf16[192,2560]{1,0:T(8,128)(2,1)S(1)}, u32[]{:S(2)}, u32[]{:S(2)}) %collective-permute-start) | collective-permute-done | bytes 983072 | tf_op jit(solution)/shard_map/ppermute | solution.py:48
  40.8 1.2 convolution_convert_fusion.6
  42.2 1.5 collective-permute-start.5
  43.7 4.6 %collective-permute-start.13 = (bf16[192,2048]{1,0:T(8,128)(2,1)}, bf16[192,2048]{1,0:T(8,128)(2,1)S(1)}, u32[]{:S(2)}, u32[]{:S(2)}) collective-permute-start(bf16[192,2048]{1,0:T(8,128)(2,1)} %get-tuple-element.21), channel_id=1, source_target_pairs={{0,2},{6,4},{1,3},{7,5},{8,10},{14,12},{9,11},{15,13},{16,18},{22,... | collective-permute-start | bytes 2359304 | tf_op jit(solution)/shard_map/ppermute | solution.py:48
  48.3 1.3 collective-permute-start.10
  49.6 8.1 %collective-permute-done.6 = bf16[192,2048]{1,0:T(8,128)(2,1)} collective-permute-done((bf16[192,2048]{1,0:T(8,128)(2,1)}, bf16[192,2048]{1,0:T(8,128)(2,1)}, u32[]{:S(2)}, u32[]{:S(2)}) %collective-permute-start.6) | collective-permute-done | bytes 786464 | tf_op jit(solution)/shard_map/ppermute | solution.py:48
  57.6 0.7 collective-permute-start.8
  58.3 1.3 collective-permute-start.12
  59.6 0.2 multiply_reduce_fusion.1
  59.9 0.1 fusion.24
  60.0 4.4 %collective-permute-done.10 = bf16[128,2560]{1,0:T(8,128)(2,1)S(1)} collective-permute-done((bf16[128,2560]{1,0:T(8,128)(2,1)}, bf16[128,2560]{1,0:T(8,128)(2,1)S(1)}, u32[]{:S(2)}, u32[]{:S(2)}) %collective-permute-start.10) | collective-permute-done | bytes 655392 | tf_op jit(solution)/shard_map/ppermute | solution.py:56
  64.4 2.9 %collective-permute-start.9 = (bf16[128,4096]{1,0:T(8,128)(2,1)S(1)}, bf16[128,4096]{1,0:T(8,128)(2,1)S(1)}, u32[]{:S(2)}, u32[]{:S(2)}) collective-permute-start(bf16[128,4096]{1,0:T(8,128)(2,1)S(1)} %bitcast.14), channel_id=1, source_target_pairs={{0,2},{6,4},{1,3},{7,5},{8,10},{14,12},{9,11},{15,13},{16,18},{22,... | collective-permute-start | bytes 3145736 | tf_op jit(solution)/shard_map/ppermute | solution.py:48
  67.3 0.7 collective-permute-start.11
  68.0 0.1 fusion.43
  68.1 6.3 %collective-permute-done.13 = bf16[192,2048]{1,0:T(8,128)(2,1)S(1)} collective-permute-done((bf16[192,2048]{1,0:T(8,128)(2,1)}, bf16[192,2048]{1,0:T(8,128)(2,1)S(1)}, u32[]{:S(2)}, u32[]{:S(2)}) %collective-permute-start.13) | collective-permute-done | bytes 786464 | tf_op jit(solution)/shard_map/ppermute | solution.py:48
  74.5 0.7 collective-permute-start.15
  75.2 2.8 %collective-permute-done.12 = bf16[128,2560]{1,0:T(8,128)(2,1)S(1)} collective-permute-done((bf16[128,2560]{1,0:T(8,128)(2,1)}, bf16[128,2560]{1,0:T(8,128)(2,1)S(1)}, u32[]{:S(2)}, u32[]{:S(2)}) %collective-permute-start.12) | collective-permute-done | bytes 655392 | tf_op jit(solution)/shard_map/ppermute | solution.py:56
  78.1 2.5 %convolution_convert_fusion.5 = bf16[256,2048]{1,0:T(8,128)(2,1)S(1)} fusion(bf16[768,256]{1,0:T(8,128)(2,1)S(1)} %pad_maximum_fusion.8, bf16[192,2048]{1,0:T(8,128)(2,1)S(1)} %collective-permute-done.8, bf16[192,2048]{1,0:T(8,128)(2,1)S(1)} %get-tuple-element.30, bf16[192,2048]{1,0:T(8,128)(2,1)} %collective-permute-done.6, ...), kind=kOutput, calls=%fused_computation.18 | convolution fusion | flops 818413568 | bytes 4587520 | tf_op jit(solution)/shard_map/dot_general | solution.py:72
  80.7 0.7 maximum_select_fusion
  81.4 14.3 %collective-permute-done.9 = bf16[128,4096]{1,0:T(8,128)(2,1)S(1)} collective-permute-done((bf16[128,4096]{1,0:T(8,128)(2,1)S(1)}, bf16[128,4096]{1,0:T(8,128)(2,1)S(1)}, u32[]{:S(2)}, u32[]{:S(2)}) %collective-permute-start.9) | collective-permute-done | bytes 1048608 | tf_op jit(solution)/shard_map/ppermute | solution.py:48
  95.7 2.4 %fusion.19 = f32[768,256]{1,0:T(8,128)S(1)} fusion(bf16[128,4096]{1,0:T(8,128)(2,1)S(1)} %bitcast.15, bf16[128,4096]{1,0:T(8,128)(2,1)S(1)} %collective-permute-done.9, bf16[192,2048]{1,0:T(8,128)(2,1)S(1)} %collective-permute-done.8, bf16[192,2048]{1,0:T(8,128)(2,1)S(1)} %get-tuple-element.30, bf16[192,2048]{1,0:T(8,128)(2,1)} %collective-permute-done.6, ...), kind=kOutput, calls=%fused_computation.31 | convolution fusion | flops 819986432 | bytes 6029312 | tf_op jit(solution)/shard_map/dot_general | solution.py:68
  98.1 0.9 fusion.25
  99.0 1.6 collective-permute-start.14
  100.6 1.3 collective-permute-start.17
  101.9 5.0 %collective-permute-done.14 = bf16[576,256]{1,0:T(8,128)(2,1)S(1)} collective-permute-done((bf16[576,256]{1,0:T(8,128)(2,1)S(1)}, bf16[576,256]{1,0:T(8,128)(2,1)S(1)}, u32[]{:S(2)}, u32[]{:S(2)}) %collective-permute-start.14) | collective-permute-done | bytes 294944 | tf_op jit(solution)/shard_map/ppermute | solution.py:60
  107.1 0.5 fusion.26
  107.6 1.6 collective-permute-start.16
  109.1 1.2 fusion.9
  110.4 1.3 collective-permute-start.26
  111.7 0.6 collective-permute-done.16
  112.3 4.0 %collective-permute-done.17 = bf16[128,2048]{1,0:T(8,128)(2,1)S(1)} collective-permute-done((bf16[128,2048]{1,0:T(8,128)(2,1)S(1)}, bf16[128,2048]{1,0:T(8,128)(2,1)S(1)}, u32[]{:S(2)}, u32[]{:S(2)}) %collective-permute-start.17) | collective-permute-done | bytes 524320 | tf_op jit(solution)/shard_map/ppermute | solution.py:56
  116.3 0.7 collective-permute-start.18
  117.1 0.3 multiply_reduce_fusion
  117.4 0.2 multiply_convert_fusion
  117.7 0.6 copy-done.13
  118.3 0.3 copy-done.15
  118.6 0.5 convolution_convert_fusion.3
  119.1 0.5 convolution_convert_fusion.1
  119.7 1.3 collective-permute-start.19
  121.0 0.7 collective-permute-start.22
  121.7 0.5 convolution_convert_fusion.2
  122.2 0.7 collective-permute-start.24
  122.9 9.9 %collective-permute-done.19 = bf16[192,512]{1,0:T(8,128)(2,1)S(1)} collective-permute-done((bf16[192,512]{1,0:T(8,128)(2,1)S(1)}, bf16[192,512]{1,0:T(8,128)(2,1)S(1)}, u32[]{:S(2)}, u32[]{:S(2)}) %collective-permute-start.19) | collective-permute-done | bytes 196640 | tf_op jit(solution)/shard_map/ppermute | solution.py:56
  132.8 0.7 convolution_convert_fusion
  133.5 1.9 %collective-permute-start.20 = (bf16[192,2560]{1,0:T(8,128)(2,1)S(1)}, bf16[192,2560]{1,0:T(8,128)(2,1)S(1)}, u32[]{:S(2)}, u32[]{:S(2)}) collective-permute-start(bf16[192,2560]{1,0:T(8,128)(2,1)S(1)} %convolution_convert_fusion), channel_id=1, source_target_pairs={{8,0},{16,8},{24,16},{9,1},{17,9},{25,17},{10,2},{18,10},{26,18},{... | collective-permute-start | bytes 2949128 | tf_op jit(solution)/shard_map/ppermute | solution.py:13
  135.4 0.7 collective-permute-start.21
  136.2 1.3 collective-permute-start.23
  137.6 0.1 add_convert_fusion.1
  137.7 1.3 collective-permute-start.25
  139.0 1.1 maximum_bitcast_fusion
  140.1 6.9 %collective-permute-done.20 = bf16[192,2560]{1,0:T(8,128)(2,1)S(1)} collective-permute-done((bf16[192,2560]{1,0:T(8,128)(2,1)S(1)}, bf16[192,2560]{1,0:T(8,128)(2,1)S(1)}, u32[]{:S(2)}, u32[]{:S(2)}) %collective-permute-start.20) | collective-permute-done | bytes 983072 | tf_op jit(solution)/shard_map/ppermute | solution.py:13
  147.0 11.3 %collective-permute-done.25 = bf16[128,1280]{1,0:T(8,128)(2,1)S(1)} collective-permute-done((bf16[128,1280]{1,0:T(8,128)(2,1)S(1)}, bf16[128,1280]{1,0:T(8,128)(2,1)S(1)}, u32[]{:S(2)}, u32[]{:S(2)}) %collective-permute-start.25) | collective-permute-done | bytes 327712 | tf_op jit(solution)/shard_map/ppermute | solution.py:56
  158.3 1.5 fusion.23
  159.8 0.9 copy.8
  (60 shorter events, 0.8 us)
Async XLA Ops:
  0.6 40.2 %copy-start.2 = (bf16[1,128,2560]{2,1,0:T(8,128)(2,1)S(1)}, bf16[1,128,2560]{2,1,0:T(8,128)(2,1)}, u32[]{:S(2)}) copy-start(bf16[1,128,2560]{2,1,0:T(8,128)(2,1)} %param.5) | copy-start | bytes 1966084
  0.6 40.2 %copy-start.12 = (bf16[1,192,2560]{2,1,0:T(8,128)(2,1)S(1)}, bf16[1,192,2560]{2,1,0:T(8,128)(2,1)}, u32[]{:S(2)}) copy-start(bf16[1,192,2560]{2,1,0:T(8,128)(2,1)} %param.4) | copy-start | bytes 2949124
  0.7 19.1 %collective-permute-start.2 = (bf16[128,2560]{1,0:T(8,128)(2,1)}, bf16[128,2560]{1,0:T(8,128)(2,1)S(1)}, u32[]{:S(2)}, u32[]{:S(2)}) collective-permute-start(bf16[128,2560]{1,0:T(8,128)(2,1)} %bitcast.19), channel_id=1, source_target_pairs={{0,2},{6,4},{1,3},{7,5},{8,10},{14,12},{9,11},{15,13},{16,18},{22,... | collective-permute-start | bytes 1966088 | tf_op jit(solution)/shard_map/ppermute | solution.py:48
  4.3 36.5 %collective-permute-start = (bf16[192,2560]{1,0:T(8,128)(2,1)}, bf16[192,2560]{1,0:T(8,128)(2,1)S(1)}, u32[]{:S(2)}, u32[]{:S(2)}) collective-permute-start(bf16[192,2560]{1,0:T(8,128)(2,1)} %bitcast.24), channel_id=1, source_target_pairs={{0,2},{6,4},{1,3},{7,5},{8,10},{14,12},{9,11},{15,13},{16,18},{22,... | collective-permute-start | bytes 2949128 | tf_op jit(solution)/shard_map/ppermute | solution.py:48
  5.7 18.3 %collective-permute-start.1 = (bf16[128,2560]{1,0:T(8,128)(2,1)}, bf16[128,2560]{1,0:T(8,128)(2,1)S(1)}, u32[]{:S(2)}, u32[]{:S(2)}) collective-permute-start(bf16[128,2560]{1,0:T(8,128)(2,1)} %bitcast.20), channel_id=1, source_target_pairs={{2,0},{4,6},{3,1},{5,7},{10,8},{12,14},{11,9},{13,15},{18,16},{20,... | collective-permute-start | bytes 1966088 | tf_op jit(solution)/shard_map/ppermute | solution.py:56
  7.0 33.8 %collective-permute-start.3 = (bf16[128,2560]{1,0:T(8,128)(2,1)}, bf16[128,2560]{1,0:T(8,128)(2,1)S(1)}, u32[]{:S(2)}, u32[]{:S(2)}) collective-permute-start(bf16[128,2560]{1,0:T(8,128)(2,1)} %bitcast.21), channel_id=1, source_target_pairs={{2,4},{4,2},{3,5},{5,3},{10,12},{12,10},{11,13},{13,11},{18,20},{2... | collective-permute-start | bytes 1966088 | tf_op jit(solution)/shard_map/ppermute | solution.py:52
  19.7 22.3 %copy-start.4 = (bf16[128,2560]{1,0:T(8,128)(2,1)}, bf16[128,2560]{1,0:T(8,128)(2,1)S(1)}, u32[]{:S(2)}) copy-start(bf16[128,2560]{1,0:T(8,128)(2,1)S(1)} %collective-permute-done.2) | copy-start | bytes 1966084
  19.7 21.1 %collective-permute-start.4 = (bf16[128,2560]{1,0:T(8,128)(2,1)S(1)}, bf16[128,2560]{1,0:T(8,128)(2,1)S(1)}, u32[]{:S(2)}, u32[]{:S(2)}) collective-permute-start(bf16[128,2560]{1,0:T(8,128)(2,1)S(1)} %collective-permute-done.2), channel_id=1, source_target_pairs={{2,4},{4,2},{3,5},{5,3},{10,12},{12,10},{11,13},{13,11},{18,20},{2... | collective-permute-start | bytes 1966088 | tf_op jit(solution)/shard_map/ppermute | solution.py:52
  20.4 46.9 %collective-permute-start.7 = (bf16[192,4096]{1,0:T(8,128)(2,1)}, bf16[192,4096]{1,0:T(8,128)(2,1)S(1)}, u32[]{:S(2)}, u32[]{:S(2)}) collective-permute-start(bf16[192,4096]{1,0:T(8,128)(2,1)} %bitcast.12), channel_id=1, source_target_pairs={{2,4},{4,2},{3,5},{5,3},{10,12},{12,10},{11,13},{13,11},{18,20},{2... | collective-permute-start | bytes 4718600 | tf_op jit(solution)/shard_map/ppermute | solution.py:52
  24.0 16.8 %copy-start.6 = (bf16[128,2560]{1,0:T(8,128)(2,1)}, bf16[128,2560]{1,0:T(8,128)(2,1)S(1)}, u32[]{:S(2)}) copy-start(bf16[128,2560]{1,0:T(8,128)(2,1)S(1)} %collective-permute-done.1) | copy-start | bytes 1966084
  24.0 33.6 %collective-permute-start.6 = (bf16[192,2048]{1,0:T(8,128)(2,1)}, bf16[192,2048]{1,0:T(8,128)(2,1)}, u32[]{:S(2)}, u32[]{:S(2)}) collective-permute-start(bf16[192,2048]{1,0:T(8,128)(2,1)} %get-tuple-element.32), channel_id=1, source_target_pairs={{0,2},{6,4},{1,3},{7,5},{8,10},{14,12},{9,11},{15,13},{16,18},{22,... | collective-permute-start | bytes 2359304 | tf_op jit(solution)/shard_map/ppermute | solution.py:48
  40.8 1.3 copy-start.14
  40.8 1.3 copy-start.8
  40.8 1.3 copy-start.10
  42.2 22.3 %copy-start = (bf16[1,128,4096]{2,1,0:T(8,128)(2,1)S(1)}, bf16[1,128,4096]{2,1,0:T(8,128)(2,1)}, u32[]{:S(2)}) copy-start(bf16[1,128,4096]{2,1,0:T(8,128)(2,1)} %param.6) | copy-start | bytes 3145732
  42.2 16.2 %collective-permute-start.5 = (bf16[384,512]{1,0:T(8,128)(2,1)S(1)}, bf16[384,512]{1,0:T(8,128)(2,1)S(1)}, u32[]{:S(2)}, u32[]{:S(2)}) collective-permute-start(bf16[384,512]{1,0:T(8,128)(2,1)S(1)} %convolution_convert_fusion.6), channel_id=1, source_target_pairs={{0,1},{1,0},{2,3},{3,2},{4,5},{5,4},{6,7},{7,6},{8,9},{9,8},{10,11... | collective-permute-start | bytes 1179656 | tf_op jit(solution)/shard_map/ppermute | solution.py:60
  43.7 30.8 %collective-permute-start.13 = (bf16[192,2048]{1,0:T(8,128)(2,1)}, bf16[192,2048]{1,0:T(8,128)(2,1)S(1)}, u32[]{:S(2)}, u32[]{:S(2)}) collective-permute-start(bf16[192,2048]{1,0:T(8,128)(2,1)} %get-tuple-element.21), channel_id=1, source_target_pairs={{0,2},{6,4},{1,3},{7,5},{8,10},{14,12},{9,11},{15,13},{16,18},{22,... | collective-permute-start | bytes 2359304 | tf_op jit(solution)/shard_map/ppermute | solution.py:48
  48.3 16.2 %collective-permute-start.10 = (bf16[128,2560]{1,0:T(8,128)(2,1)}, bf16[128,2560]{1,0:T(8,128)(2,1)S(1)}, u32[]{:S(2)}, u32[]{:S(2)}) collective-permute-start(bf16[128,2560]{1,0:T(8,128)(2,1)} %copy-done.8), channel_id=1, source_target_pairs={{2,0},{4,6},{3,1},{5,7},{10,8},{12,14},{11,9},{13,15},{18,16},{20,... | collective-permute-start | bytes 1966088 | tf_op jit(solution)/shard_map/ppermute | solution.py:56
  57.6 20.4 %collective-permute-start.8 = (bf16[192,2048]{1,0:T(8,128)(2,1)}, bf16[192,2048]{1,0:T(8,128)(2,1)S(1)}, u32[]{:S(2)}, u32[]{:S(2)}) collective-permute-start(bf16[192,2048]{1,0:T(8,128)(2,1)} %collective-permute-done.6), channel_id=1, source_target_pairs={{2,4},{4,2},{3,5},{5,3},{10,12},{12,10},{11,13},{13,11},{18,20},{2... | collective-permute-start | bytes 2359304 | tf_op jit(solution)/shard_map/ppermute | solution.py:52
  58.3 19.7 %collective-permute-start.12 = (bf16[128,2560]{1,0:T(8,128)(2,1)}, bf16[128,2560]{1,0:T(8,128)(2,1)S(1)}, u32[]{:S(2)}, u32[]{:S(2)}) collective-permute-start(bf16[128,2560]{1,0:T(8,128)(2,1)} %copy-done.10), channel_id=1, source_target_pairs={{2,0},{4,6},{3,1},{5,7},{10,8},{12,14},{11,9},{13,15},{18,16},{20,... | collective-permute-start | bytes 1966088 | tf_op jit(solution)/shard_map/ppermute | solution.py:56
  64.4 31.3 %collective-permute-start.9 = (bf16[128,4096]{1,0:T(8,128)(2,1)S(1)}, bf16[128,4096]{1,0:T(8,128)(2,1)S(1)}, u32[]{:S(2)}, u32[]{:S(2)}) collective-permute-start(bf16[128,4096]{1,0:T(8,128)(2,1)S(1)} %bitcast.14), channel_id=1, source_target_pairs={{0,2},{6,4},{1,3},{7,5},{8,10},{14,12},{9,11},{15,13},{16,18},{22,... | collective-permute-start | bytes 3145736 | tf_op jit(solution)/shard_map/ppermute | solution.py:48
  67.3 7.8 %collective-permute-start.11 = (bf16[384,256]{1,0:T(8,128)(2,1)S(1)}, bf16[384,256]{1,0:T(8,128)(2,1)S(1)}, u32[]{:S(2)}, u32[]{:S(2)}) collective-permute-start(bf16[384,256]{1,0:T(8,128)(2,1)S(1)} %get-tuple-element.18), channel_id=1, source_target_pairs={{2,4},{4,2},{3,5},{5,3},{10,12},{12,10},{11,13},{13,11},{18,20},{2... | collective-permute-start | bytes 589832 | tf_op jit(solution)/shard_map/ppermute | solution.py:52
  74.5 32.6 %collective-permute-start.15 = (bf16[192,2048]{1,0:T(8,128)(2,1)S(1)}, bf16[192,2048]{1,0:T(8,128)(2,1)S(1)}, u32[]{:S(2)}, u32[]{:S(2)}) collective-permute-start(bf16[192,2048]{1,0:T(8,128)(2,1)S(1)} %collective-permute-done.13), channel_id=1, source_target_pairs={{2,4},{4,2},{3,5},{5,3},{10,12},{12,10},{11,13},{13,11},{18,20},{2... | collective-permute-start | bytes 2359304 | tf_op jit(solution)/shard_map/ppermute | solution.py:52
  78.0 2.6 %copy-start.3 = (bf16[1,128,2560]{2,1,0:T(8,128)(2,1)S(1)}, bf16[1,128,2560]{2,1,0:T(8,128)(2,1)}, u32[]{:S(2)}) copy-start(bf16[1,128,2560]{2,1,0:T(8,128)(2,1)} %param.5) | copy-start | bytes 1966084
  78.0 2.6 %copy-start.5 = (bf16[128,2560]{1,0:T(8,128)(2,1)S(1)}, bf16[128,2560]{1,0:T(8,128)(2,1)}, u32[]{:S(2)}) copy-start(bf16[128,2560]{1,0:T(8,128)(2,1)} %copy-done.4) | copy-start | bytes 1966084
  78.0 2.6 %copy-start.7 = (bf16[128,2560]{1,0:T(8,128)(2,1)S(1)}, bf16[128,2560]{1,0:T(8,128)(2,1)}, u32[]{:S(2)}) copy-start(bf16[128,2560]{1,0:T(8,128)(2,1)} %copy-done.6) | copy-start | bytes 1966084
  78.0 2.6 %copy-start.9 = (bf16[128,2560]{1,0:T(8,128)(2,1)S(1)}, bf16[128,2560]{1,0:T(8,128)(2,1)}, u32[]{:S(2)}) copy-start(bf16[128,2560]{1,0:T(8,128)(2,1)} %copy-done.8) | copy-start | bytes 1966084
  78.1 2.6 %copy-start.11 = (bf16[128,2560]{1,0:T(8,128)(2,1)S(1)}, bf16[128,2560]{1,0:T(8,128)(2,1)}, u32[]{:S(2)}) copy-start(bf16[128,2560]{1,0:T(8,128)(2,1)} %copy-done.10) | copy-start | bytes 1966084
  81.4 16.7 %copy-start.1 = (bf16[192,2048]{1,0:T(8,128)(2,1)S(1)}, bf16[192,2048]{1,0:T(8,128)(2,1)}, u32[]{:S(2)}) copy-start(bf16[192,2048]{1,0:T(8,128)(2,1)} %get-tuple-element.21) | copy-start | bytes 2359300
  99.0 7.9 %collective-permute-start.14 = (bf16[576,256]{1,0:T(8,128)(2,1)S(1)}, bf16[576,256]{1,0:T(8,128)(2,1)S(1)}, u32[]{:S(2)}, u32[]{:S(2)}) collective-permute-start(bf16[576,256]{1,0:T(8,128)(2,1)S(1)} %fusion.25), channel_id=1, source_target_pairs={{0,1},{1,0},{2,3},{3,2},{4,5},{5,4},{6,7},{7,6},{8,9},{9,8},{10,11... | collective-permute-start | bytes 884744 | tf_op jit(solution)/shard_map/ppermute | solution.py:60
  100.6 15.7 %collective-permute-start.17 = (bf16[128,2048]{1,0:T(8,128)(2,1)S(1)}, bf16[128,2048]{1,0:T(8,128)(2,1)S(1)}, u32[]{:S(2)}, u32[]{:S(2)}) collective-permute-start(bf16[128,2048]{1,0:T(8,128)(2,1)S(1)} %slice.122), channel_id=1, source_target_pairs={{2,0},{4,6},{3,1},{5,7},{10,8},{12,14},{11,9},{13,15},{18,16},{20,... | collective-permute-start | bytes 1572872 | tf_op jit(solution)/shard_map/ppermute | solution.py:56
  107.6 4.7 %collective-permute-start.16 = (bf16[192,256]{1,0:T(8,128)(2,1)S(1)}, bf16[192,256]{1,0:T(8,128)(2,1)S(1)}, u32[]{:S(2)}, u32[]{:S(2)}) collective-permute-start(bf16[192,256]{1,0:T(8,128)(2,1)S(1)} %fusion.26), channel_id=1, source_target_pairs={{0,1},{1,0},{2,3},{3,2},{4,5},{5,4},{6,7},{7,6},{8,9},{9,8},{10,11... | collective-permute-start | bytes 294920 | tf_op jit(solution)/shard_map/ppermute | solution.py:60
  110.4 28.6 %collective-permute-start.26 = (bf16[128,2048]{1,0:T(8,128)(2,1)S(1)}, bf16[128,2048]{1,0:T(8,128)(2,1)S(1)}, u32[]{:S(2)}, u32[]{:S(2)}) collective-permute-start(bf16[128,2048]{1,0:T(8,128)(2,1)S(1)} %slice.135), channel_id=1, source_target_pairs={{2,0},{4,6},{3,1},{5,7},{10,8},{12,14},{11,9},{13,15},{18,16},{20,... | collective-permute-start | bytes 1572872 | tf_op jit(solution)/shard_map/ppermute | solution.py:56
  116.3 0.8 collective-permute-start.18
  117.1 1.2 copy-start.13
  117.1 1.5 copy-start.15
  119.7 13.2 %collective-permute-start.19 = (bf16[192,512]{1,0:T(8,128)(2,1)S(1)}, bf16[192,512]{1,0:T(8,128)(2,1)S(1)}, u32[]{:S(2)}, u32[]{:S(2)}) collective-permute-start(bf16[192,512]{1,0:T(8,128)(2,1)S(1)} %slice.124), channel_id=1, source_target_pairs={{2,0},{4,6},{3,1},{5,7},{10,8},{12,14},{11,9},{13,15},{18,16},{20,... | collective-permute-start | bytes 589832 | tf_op jit(solution)/shard_map/ppermute | solution.py:56
  121.0 15.1 %collective-permute-start.22 = (bf16[128,1280]{1,0:T(8,128)(2,1)S(1)}, bf16[128,1280]{1,0:T(8,128)(2,1)S(1)}, u32[]{:S(2)}, u32[]{:S(2)}) collective-permute-start(bf16[128,1280]{1,0:T(8,128)(2,1)S(1)} %get-tuple-element.33), channel_id=1, source_target_pairs={{2,4},{4,2},{3,5},{5,3},{10,12},{12,10},{11,13},{13,11},{18,20},{2... | collective-permute-start | bytes 983048 | tf_op jit(solution)/shard_map/ppermute | solution.py:52
  122.2 15.3 %collective-permute-start.24 = (bf16[128,1280]{1,0:T(8,128)(2,1)S(1)}, bf16[128,1280]{1,0:T(8,128)(2,1)S(1)}, u32[]{:S(2)}, u32[]{:S(2)}) collective-permute-start(bf16[128,1280]{1,0:T(8,128)(2,1)S(1)} %get-tuple-element.34), channel_id=1, source_target_pairs={{2,4},{4,2},{3,5},{5,3},{10,12},{12,10},{11,13},{13,11},{18,20},{2... | collective-permute-start | bytes 983048 | tf_op jit(solution)/shard_map/ppermute | solution.py:52
  133.5 13.5 %collective-permute-start.20 = (bf16[192,2560]{1,0:T(8,128)(2,1)S(1)}, bf16[192,2560]{1,0:T(8,128)(2,1)S(1)}, u32[]{:S(2)}, u32[]{:S(2)}) collective-permute-start(bf16[192,2560]{1,0:T(8,128)(2,1)S(1)} %convolution_convert_fusion), channel_id=1, source_target_pairs={{8,0},{16,8},{24,16},{9,1},{17,9},{25,17},{10,2},{18,10},{26,18},{... | collective-permute-start | bytes 2949128 | tf_op jit(solution)/shard_map/ppermute | solution.py:13
  135.4 11.6 %collective-permute-start.21 = (bf16[128,2560]{1,0:T(8,128)(2,1)S(1)}, bf16[128,2560]{1,0:T(8,128)(2,1)S(1)}, u32[]{:S(2)}, u32[]{:S(2)}) collective-permute-start(bf16[128,2560]{1,0:T(8,128)(2,1)S(1)} %convolution_convert_fusion.3), channel_id=1, source_target_pairs={{2,4},{4,2},{3,5},{5,3},{10,12},{12,10},{11,13},{13,11},{18,20},{2... | collective-permute-start | bytes 1966088 | tf_op jit(solution)/shard_map/ppermute | solution.py:52
  136.2 22.1 %collective-permute-start.23 = (bf16[128,1280]{1,0:T(8,128)(2,1)S(1)}, bf16[128,1280]{1,0:T(8,128)(2,1)S(1)}, u32[]{:S(2)}, u32[]{:S(2)}) collective-permute-start(bf16[128,1280]{1,0:T(8,128)(2,1)S(1)} %add_convert_fusion.2), channel_id=1, source_target_pairs={{2,0},{4,6},{3,1},{5,7},{10,8},{12,14},{11,9},{13,15},{18,16},{20,... | collective-permute-start | bytes 983048 | tf_op jit(solution)/shard_map/ppermute | solution.py:56
  137.7 20.7 %collective-permute-start.25 = (bf16[128,1280]{1,0:T(8,128)(2,1)S(1)}, bf16[128,1280]{1,0:T(8,128)(2,1)S(1)}, u32[]{:S(2)}, u32[]{:S(2)}) collective-permute-start(bf16[128,1280]{1,0:T(8,128)(2,1)S(1)} %add_convert_fusion.1), channel_id=1, source_target_pairs={{2,0},{4,6},{3,1},{5,7},{10,8},{12,14},{11,9},{13,15},{18,16},{20,... | collective-permute-start | bytes 983048 | tf_op jit(solution)/shard_map/ppermute | solution.py:56

commit v14 on v9

--- a/solution.py
+++ b/solution.py
@@ -144,8 +144,9 @@
         tokens_dot(latent_bf[:, j * lat : (j + 1) * lat], tokens_mine).astype(BF16)
         for j in range(4)
     ]
-    width = tokens.shape[1] // 2
-    halves = (slice(0, width), slice(width, 2 * width))
+    width = tokens.shape[1]
+    first = width * 2 // 5 // 128 * 128
+    halves = (slice(0, first), slice(first, width))
     sent_end, sent_own = sums[3], sums[2]
     from_end = [across(sent_end[:, half]) for half in halves]
     end_first = (sums[1][:, halves[0]] + from_end[0].astype(F32)).astype(BF16)

time: 160 us -> 160 us (level)
  transfers between devices with their start and end apart: 27 -> 27, of which waited for: 14 -> 15; matrix products, arithmetic and copies ran while one was open for 11% -> 11% of each run, Pallas kernels for 0% -> 0%
where the time goes in v14:
time: 160 us; the launch traced here: 158 us
  waiting for transfers between devices  89.9 us (56%)
  starting transfers between devices  45.8 us (29%)
  matrix products  12.5 us (8%)
  local copies, waits for them, and re-layouts  4.96 us (3%)
  other arithmetic  3.1 us (2%)
    ppermute x5, waiting for transfers between devices, inward(): return lax.ppermute(value, 'row', [(0, 1), (3, 2)])  48.1 us
    ppermute x8, waiting for transfers between devices, outward(): return lax.ppermute(value, 'row', [(1, 0), (2, 3)])  29.2 us
    ppermute x5, starting transfers between devices, inward(): return lax.ppermute(value, 'row', [(0, 1), (3, 2)])  22 us
    ppermute x8, starting transfers between devices, outward(): return lax.ppermute(value, 'row', [(1, 0), (2, 3)])  10.3 us
    ppermute x10, starting transfers between devices, across(): return lax.ppermute(value, 'row', [(1, 2), (2, 1)])  6.95 us
    ppermute x1, waiting for transfers between devices, shifted(): lax.ppermute(value, axis, [(source, source + steps) for source in range(l...  6.94 us
    dot_general x6, matrix products, tokens_dot(): lax.dot_general(left, right, (((0,), (0,)), ((), ())), preferred_element_...  6.79 us
    ppermute x3, waiting for transfers between devices, other_col(): return lax.ppermute(value, 'col', [(0, 1), (1, 0)])  5.62 us
  transfers between devices with their start and end apart: 27, of which 15 were waited for; matrix products, arithmetic and copies ran while one was open for 11% of the time, Pallas kernels for 0%

profile of v14, /device:TPU:4, one launch (start us, length us, event | category | flops | bytes accessed | tf_op | source)
XLA Modules:
  0.0 157.5 jit_solution(9083596078187991865)
XLA Ops:
  0.7 3.7 %collective-permute-start.2 = (bf16[128,2560]{1,0:T(8,128)(2,1)}, bf16[128,2560]{1,0:T(8,128)(2,1)S(1)}, u32[]{:S(2)}, u32[]{:S(2)}) collective-permute-start(bf16[128,2560]{1,0:T(8,128)(2,1)} %bitcast.19), channel_id=1, source_target_pairs={{0,2},{6,4},{1,3},{7,5},{8,10},{14,12},{9,11},{15,13},{16,18},{22,... | collective-permute-start | bytes 1966088 | tf_op jit(solution)/shard_map/ppermute | solution.py:48
  4.3 1.4 collective-permute-start
  5.7 1.3 collective-permute-start.1
  7.0 0.7 collective-permute-start.3
  7.7 12.0 %collective-permute-done.2 = bf16[128,2560]{1,0:T(8,128)(2,1)S(1)} collective-permute-done((bf16[128,2560]{1,0:T(8,128)(2,1)}, bf16[128,2560]{1,0:T(8,128)(2,1)S(1)}, u32[]{:S(2)}, u32[]{:S(2)}) %collective-permute-start.2) | collective-permute-done | bytes 655392 | tf_op jit(solution)/shard_map/ppermute | solution.py:48
  19.7 0.7 collective-permute-start.4
  20.4 0.8 collective-permute-start.7
  21.2 2.7 %fusion.44 = (bf16[192,2048]{1,0:T(8,128)(2,1)}, bf16[192,2048]{1,0:T(8,128)(2,1)}) fusion(bf16[192,4096]{1,0:T(8,128)(2,1)} %bitcast.13), kind=kLoop, calls=%fused_computation.72 | loop fusion | bytes 3145728 | tf_op jit(solution)/shard_map/slice | solution.py:119
  23.9 0.1 collective-permute-done.1
  24.0 9.5 %collective-permute-start.6 = (bf16[192,2048]{1,0:T(8,128)(2,1)}, bf16[192,2048]{1,0:T(8,128)(2,1)}, u32[]{:S(2)}, u32[]{:S(2)}) collective-permute-start(bf16[192,2048]{1,0:T(8,128)(2,1)} %get-tuple-element.32), channel_id=1, source_target_pairs={{0,2},{6,4},{1,3},{7,5},{8,10},{14,12},{9,11},{15,13},{16,18},{22,... | collective-permute-start | bytes 2359304 | tf_op jit(solution)/shard_map/ppermute | solution.py:48
  33.4 7.3 %collective-permute-done = bf16[192,2560]{1,0:T(8,128)(2,1)S(1)} collective-permute-done((bf16[192,2560]{1,0:T(8,128)(2,1)}, bf16[192,2560]{1,0:T(8,128)(2,1)S(1)}, u32[]{:S(2)}, u32[]{:S(2)}) %collective-permute-start) | collective-permute-done | bytes 983072 | tf_op jit(solution)/shard_map/ppermute | solution.py:48
  40.8 1.2 convolution_convert_fusion.6
  42.2 1.5 collective-permute-start.5
  43.7 4.6 %collective-permute-start.13 = (bf16[192,2048]{1,0:T(8,128)(2,1)}, bf16[192,2048]{1,0:T(8,128)(2,1)S(1)}, u32[]{:S(2)}, u32[]{:S(2)}) collective-permute-start(bf16[192,2048]{1,0:T(8,128)(2,1)} %get-tuple-element.21), channel_id=1, source_target_pairs={{0,2},{6,4},{1,3},{7,5},{8,10},{14,12},{9,11},{15,13},{16,18},{22,... | collective-permute-start | bytes 2359304 | tf_op jit(solution)/shard_map/ppermute | solution.py:48
  48.3 1.3 collective-permute-start.10
  49.6 8.1 %collective-permute-done.6 = bf16[192,2048]{1,0:T(8,128)(2,1)} collective-permute-done((bf16[192,2048]{1,0:T(8,128)(2,1)}, bf16[192,2048]{1,0:T(8,128)(2,1)}, u32[]{:S(2)}, u32[]{:S(2)}) %collective-permute-start.6) | collective-permute-done | bytes 786464 | tf_op jit(solution)/shard_map/ppermute | solution.py:48
  57.6 0.7 collective-permute-start.8
  58.3 1.3 collective-permute-start.12
  59.6 0.2 multiply_reduce_fusion.1
  59.9 0.1 fusion.24
  60.0 4.4 %collective-permute-done.10 = bf16[128,2560]{1,0:T(8,128)(2,1)S(1)} collective-permute-done((bf16[128,2560]{1,0:T(8,128)(2,1)}, bf16[128,2560]{1,0:T(8,128)(2,1)S(1)}, u32[]{:S(2)}, u32[]{:S(2)}) %collective-permute-start.10) | collective-permute-done | bytes 655392 | tf_op jit(solution)/shard_map/ppermute | solution.py:56
  64.4 2.9 %collective-permute-start.9 = (bf16[128,4096]{1,0:T(8,128)(2,1)S(1)}, bf16[128,4096]{1,0:T(8,128)(2,1)S(1)}, u32[]{:S(2)}, u32[]{:S(2)}) collective-permute-start(bf16[128,4096]{1,0:T(8,128)(2,1)S(1)} %bitcast.14), channel_id=1, source_target_pairs={{0,2},{6,4},{1,3},{7,5},{8,10},{14,12},{9,11},{15,13},{16,18},{22,... | collective-permute-start | bytes 3145736 | tf_op jit(solution)/shard_map/ppermute | solution.py:48
  67.3 0.7 collective-permute-start.11
  68.0 0.1 fusion.43
  68.1 6.3 %collective-permute-done.13 = bf16[192,2048]{1,0:T(8,128)(2,1)S(1)} collective-permute-done((bf16[192,2048]{1,0:T(8,128)(2,1)}, bf16[192,2048]{1,0:T(8,128)(2,1)S(1)}, u32[]{:S(2)}, u32[]{:S(2)}) %collective-permute-start.13) | collective-permute-done | bytes 786464 | tf_op jit(solution)/shard_map/ppermute | solution.py:48
  74.5 0.7 collective-permute-start.15
  75.2 2.8 %collective-permute-done.12 = bf16[128,2560]{1,0:T(8,128)(2,1)S(1)} collective-permute-done((bf16[128,2560]{1,0:T(8,128)(2,1)}, bf16[128,2560]{1,0:T(8,128)(2,1)S(1)}, u32[]{:S(2)}, u32[]{:S(2)}) %collective-permute-start.12) | collective-permute-done | bytes 655392 | tf_op jit(solution)/shard_map/ppermute | solution.py:56
  78.1 2.5 %convolution_convert_fusion.5 = bf16[256,2048]{1,0:T(8,128)(2,1)S(1)} fusion(bf16[768,256]{1,0:T(8,128)(2,1)S(1)} %pad_maximum_fusion.8, bf16[192,2048]{1,0:T(8,128)(2,1)S(1)} %collective-permute-done.8, bf16[192,2048]{1,0:T(8,128)(2,1)S(1)} %get-tuple-element.30, bf16[192,2048]{1,0:T(8,128)(2,1)} %collective-permute-done.6, ...), kind=kOutput, calls=%fused_computation.18 | convolution fusion | flops 818413568 | bytes 4587520 | tf_op jit(solution)/shard_map/dot_general | solution.py:72
  80.7 0.7 maximum_select_fusion
  81.4 14.3 %collective-permute-done.9 = bf16[128,4096]{1,0:T(8,128)(2,1)S(1)} collective-permute-done((bf16[128,4096]{1,0:T(8,128)(2,1)S(1)}, bf16[128,4096]{1,0:T(8,128)(2,1)S(1)}, u32[]{:S(2)}, u32[]{:S(2)}) %collective-permute-start.9) | collective-permute-done | bytes 1048608 | tf_op jit(solution)/shard_map/ppermute | solution.py:48
  95.7 2.4 %fusion.19 = f32[768,256]{1,0:T(8,128)S(1)} fusion(bf16[128,4096]{1,0:T(8,128)(2,1)S(1)} %bitcast.15, bf16[128,4096]{1,0:T(8,128)(2,1)S(1)} %collective-permute-done.9, bf16[192,2048]{1,0:T(8,128)(2,1)S(1)} %collective-permute-done.8, bf16[192,2048]{1,0:T(8,128)(2,1)S(1)} %get-tuple-element.30, bf16[192,2048]{1,0:T(8,128)(2,1)} %collective-permute-done.6, ...), kind=kOutput, calls=%fused_computation.31 | convolution fusion | flops 819986432 | bytes 6029312 | tf_op jit(solution)/shard_map/dot_general | solution.py:68
  98.1 0.9 fusion.25
  99.0 1.6 collective-permute-start.14
  100.6 1.3 collective-permute-start.17
  101.9 5.0 %collective-permute-done.14 = bf16[576,256]{1,0:T(8,128)(2,1)S(1)} collective-permute-done((bf16[576,256]{1,0:T(8,128)(2,1)S(1)}, bf16[576,256]{1,0:T(8,128)(2,1)S(1)}, u32[]{:S(2)}, u32[]{:S(2)}) %collective-permute-start.14) | collective-permute-done | bytes 294944 | tf_op jit(solution)/shard_map/ppermute | solution.py:60
  107.1 0.5 fusion.26
  107.6 1.6 collective-permute-start.16
  109.1 1.2 fusion.9
  110.4 1.3 collective-permute-start.26
  111.7 0.6 collective-permute-done.16
  112.3 4.0 %collective-permute-done.17 = bf16[128,2048]{1,0:T(8,128)(2,1)S(1)} collective-permute-done((bf16[128,2048]{1,0:T(8,128)(2,1)S(1)}, bf16[128,2048]{1,0:T(8,128)(2,1)S(1)}, u32[]{:S(2)}, u32[]{:S(2)}) %collective-permute-start.17) | collective-permute-done | bytes 524320 | tf_op jit(solution)/shard_map/ppermute | solution.py:56
  116.3 0.7 collective-permute-start.18
  117.1 0.3 multiply_reduce_fusion
  117.4 0.2 multiply_convert_fusion
  117.7 0.6 copy-done.13
  118.3 0.3 copy-done.15
  118.6 0.5 convolution_convert_fusion.3
  119.1 0.5 convolution_convert_fusion.1
  119.7 1.3 collective-permute-start.19
  121.0 0.7 collective-permute-start.21
  121.7 0.7 collective-permute-start.24
  122.4 0.5 convolution_convert_fusion.2
  122.9 9.9 %collective-permute-done.19 = bf16[192,512]{1,0:T(8,128)(2,1)S(1)} collective-permute-done((bf16[192,512]{1,0:T(8,128)(2,1)S(1)}, bf16[192,512]{1,0:T(8,128)(2,1)S(1)}, u32[]{:S(2)}, u32[]{:S(2)}) %collective-permute-start.19) | collective-permute-done | bytes 196640 | tf_op jit(solution)/shard_map/ppermute | solution.py:56
  132.9 0.7 convolution_convert_fusion
  133.6 1.9 %collective-permute-start.20 = (bf16[192,2560]{1,0:T(8,128)(2,1)S(1)}, bf16[192,2560]{1,0:T(8,128)(2,1)S(1)}, u32[]{:S(2)}, u32[]{:S(2)}) collective-permute-start(bf16[192,2560]{1,0:T(8,128)(2,1)S(1)} %convolution_convert_fusion), channel_id=1, source_target_pairs={{8,0},{16,8},{24,16},{9,1},{17,9},{25,17},{10,2},{18,10},{26,18},{... | collective-permute-start | bytes 2949128 | tf_op jit(solution)/shard_map/ppermute | solution.py:13
  135.6 1.3 collective-permute-start.23
  136.9 0.7 collective-permute-start.22
  137.7 1.3 collective-permute-start.25
  139.1 1.1 maximum_bitcast_fusion
  140.1 6.9 %collective-permute-done.20 = bf16[192,2560]{1,0:T(8,128)(2,1)S(1)} collective-permute-done((bf16[192,2560]{1,0:T(8,128)(2,1)S(1)}, bf16[192,2560]{1,0:T(8,128)(2,1)S(1)}, u32[]{:S(2)}, u32[]{:S(2)}) %collective-permute-start.20) | collective-permute-done | bytes 983072 | tf_op jit(solution)/shard_map/ppermute | solution.py:13
  147.1 0.5 collective-permute-done.23
  147.6 7.5 %collective-permute-done.25 = bf16[128,1536]{1,0:T(8,128)(2,1)S(1)} collective-permute-done((bf16[128,1536]{1,0:T(8,128)(2,1)S(1)}, bf16[128,1536]{1,0:T(8,128)(2,1)S(1)}, u32[]{:S(2)}, u32[]{:S(2)}) %collective-permute-start.25) | collective-permute-done | bytes 393248 | tf_op jit(solution)/shard_map/ppermute | solution.py:56
  155.1 1.4 fusion.23
  156.6 0.9 copy.8
  (61 shorter events, 0.8 us)
Async XLA Ops:
  0.6 40.2 %copy-start.2 = (bf16[1,128,2560]{2,1,0:T(8,128)(2,1)S(1)}, bf16[1,128,2560]{2,1,0:T(8,128)(2,1)}, u32[]{:S(2)}) copy-start(bf16[1,128,2560]{2,1,0:T(8,128)(2,1)} %param.5) | copy-start | bytes 1966084
  0.6 40.2 %copy-start.12 = (bf16[1,192,2560]{2,1,0:T(8,128)(2,1)S(1)}, bf16[1,192,2560]{2,1,0:T(8,128)(2,1)}, u32[]{:S(2)}) copy-start(bf16[1,192,2560]{2,1,0:T(8,128)(2,1)} %param.4) | copy-start | bytes 2949124
  0.7 19.1 %collective-permute-start.2 = (bf16[128,2560]{1,0:T(8,128)(2,1)}, bf16[128,2560]{1,0:T(8,128)(2,1)S(1)}, u32[]{:S(2)}, u32[]{:S(2)}) collective-permute-start(bf16[128,2560]{1,0:T(8,128)(2,1)} %bitcast.19), channel_id=1, source_target_pairs={{0,2},{6,4},{1,3},{7,5},{8,10},{14,12},{9,11},{15,13},{16,18},{22,... | collective-permute-start | bytes 1966088 | tf_op jit(solution)/shard_map/ppermute | solution.py:48
  4.3 36.5 %collective-permute-start = (bf16[192,2560]{1,0:T(8,128)(2,1)}, bf16[192,2560]{1,0:T(8,128)(2,1)S(1)}, u32[]{:S(2)}, u32[]{:S(2)}) collective-permute-start(bf16[192,2560]{1,0:T(8,128)(2,1)} %bitcast.24), channel_id=1, source_target_pairs={{0,2},{6,4},{1,3},{7,5},{8,10},{14,12},{9,11},{15,13},{16,18},{22,... | collective-permute-start | bytes 2949128 | tf_op jit(solution)/shard_map/ppermute | solution.py:48
  5.7 18.3 %collective-permute-start.1 = (bf16[128,2560]{1,0:T(8,128)(2,1)}, bf16[128,2560]{1,0:T(8,128)(2,1)S(1)}, u32[]{:S(2)}, u32[]{:S(2)}) collective-permute-start(bf16[128,2560]{1,0:T(8,128)(2,1)} %bitcast.20), channel_id=1, source_target_pairs={{2,0},{4,6},{3,1},{5,7},{10,8},{12,14},{11,9},{13,15},{18,16},{20,... | collective-permute-start | bytes 1966088 | tf_op jit(solution)/shard_map/ppermute | solution.py:56
  7.0 33.8 %collective-permute-start.3 = (bf16[128,2560]{1,0:T(8,128)(2,1)}, bf16[128,2560]{1,0:T(8,128)(2,1)S(1)}, u32[]{:S(2)}, u32[]{:S(2)}) collective-permute-start(bf16[128,2560]{1,0:T(8,128)(2,1)} %bitcast.21), channel_id=1, source_target_pairs={{2,4},{4,2},{3,5},{5,3},{10,12},{12,10},{11,13},{13,11},{18,20},{2... | collective-permute-start | bytes 1966088 | tf_op jit(solution)/shard_map/ppermute | solution.py:52
  19.7 22.3 %copy-start.4 = (bf16[128,2560]{1,0:T(8,128)(2,1)}, bf16[128,2560]{1,0:T(8,128)(2,1)S(1)}, u32[]{:S(2)}) copy-start(bf16[128,2560]{1,0:T(8,128)(2,1)S(1)} %collective-permute-done.2) | copy-start | bytes 1966084
  19.7 21.1 %collective-permute-start.4 = (bf16[128,2560]{1,0:T(8,128)(2,1)S(1)}, bf16[128,2560]{1,0:T(8,128)(2,1)S(1)}, u32[]{:S(2)}, u32[]{:S(2)}) collective-permute-start(bf16[128,2560]{1,0:T(8,128)(2,1)S(1)} %collective-permute-done.2), channel_id=1, source_target_pairs={{2,4},{4,2},{3,5},{5,3},{10,12},{12,10},{11,13},{13,11},{18,20},{2... | collective-permute-start | bytes 1966088 | tf_op jit(solution)/shard_map/ppermute | solution.py:52
  20.4 46.9 %collective-permute-start.7 = (bf16[192,4096]{1,0:T(8,128)(2,1)}, bf16[192,4096]{1,0:T(8,128)(2,1)S(1)}, u32[]{:S(2)}, u32[]{:S(2)}) collective-permute-start(bf16[192,4096]{1,0:T(8,128)(2,1)} %bitcast.12), channel_id=1, source_target_pairs={{2,4},{4,2},{3,5},{5,3},{10,12},{12,10},{11,13},{13,11},{18,20},{2... | collective-permute-start | bytes 4718600 | tf_op jit(solution)/shard_map/ppermute | solution.py:52
  24.0 16.8 %copy-start.6 = (bf16[128,2560]{1,0:T(8,128)(2,1)}, bf16[128,2560]{1,0:T(8,128)(2,1)S(1)}, u32[]{:S(2)}) copy-start(bf16[128,2560]{1,0:T(8,128)(2,1)S(1)} %collective-permute-done.1) | copy-start | bytes 1966084
  24.0 33.6 %collective-permute-start.6 = (bf16[192,2048]{1,0:T(8,128)(2,1)}, bf16[192,2048]{1,0:T(8,128)(2,1)}, u32[]{:S(2)}, u32[]{:S(2)}) collective-permute-start(bf16[192,2048]{1,0:T(8,128)(2,1)} %get-tuple-element.32), channel_id=1, source_target_pairs={{0,2},{6,4},{1,3},{7,5},{8,10},{14,12},{9,11},{15,13},{16,18},{22,... | collective-permute-start | bytes 2359304 | tf_op jit(solution)/shard_map/ppermute | solution.py:48
  40.8 1.3 copy-start.14
  40.8 1.3 copy-start.8
  40.8 1.3 copy-start.10
  42.2 22.3 %copy-start = (bf16[1,128,4096]{2,1,0:T(8,128)(2,1)S(1)}, bf16[1,128,4096]{2,1,0:T(8,128)(2,1)}, u32[]{:S(2)}) copy-start(bf16[1,128,4096]{2,1,0:T(8,128)(2,1)} %param.6) | copy-start | bytes 3145732
  42.2 16.2 %collective-permute-start.5 = (bf16[384,512]{1,0:T(8,128)(2,1)S(1)}, bf16[384,512]{1,0:T(8,128)(2,1)S(1)}, u32[]{:S(2)}, u32[]{:S(2)}) collective-permute-start(bf16[384,512]{1,0:T(8,128)(2,1)S(1)} %convolution_convert_fusion.6), channel_id=1, source_target_pairs={{0,1},{1,0},{2,3},{3,2},{4,5},{5,4},{6,7},{7,6},{8,9},{9,8},{10,11... | collective-permute-start | bytes 1179656 | tf_op jit(solution)/shard_map/ppermute | solution.py:60
  43.7 30.8 %collective-permute-start.13 = (bf16[192,2048]{1,0:T(8,128)(2,1)}, bf16[192,2048]{1,0:T(8,128)(2,1)S(1)}, u32[]{:S(2)}, u32[]{:S(2)}) collective-permute-start(bf16[192,2048]{1,0:T(8,128)(2,1)} %get-tuple-element.21), channel_id=1, source_target_pairs={{0,2},{6,4},{1,3},{7,5},{8,10},{14,12},{9,11},{15,13},{16,18},{22,... | collective-permute-start | bytes 2359304 | tf_op jit(solution)/shard_map/ppermute | solution.py:48
  48.3 16.2 %collective-permute-start.10 = (bf16[128,2560]{1,0:T(8,128)(2,1)}, bf16[128,2560]{1,0:T(8,128)(2,1)S(1)}, u32[]{:S(2)}, u32[]{:S(2)}) collective-permute-start(bf16[128,2560]{1,0:T(8,128)(2,1)} %copy-done.8), channel_id=1, source_target_pairs={{2,0},{4,6},{3,1},{5,7},{10,8},{12,14},{11,9},{13,15},{18,16},{20,... | collective-permute-start | bytes 1966088 | tf_op jit(solution)/shard_map/ppermute | solution.py:56
  57.6 20.4 %collective-permute-start.8 = (bf16[192,2048]{1,0:T(8,128)(2,1)}, bf16[192,2048]{1,0:T(8,128)(2,1)S(1)}, u32[]{:S(2)}, u32[]{:S(2)}) collective-permute-start(bf16[192,2048]{1,0:T(8,128)(2,1)} %collective-permute-done.6), channel_id=1, source_target_pairs={{2,4},{4,2},{3,5},{5,3},{10,12},{12,10},{11,13},{13,11},{18,20},{2... | collective-permute-start | bytes 2359304 | tf_op jit(solution)/shard_map/ppermute | solution.py:52
  58.3 19.7 %collective-permute-start.12 = (bf16[128,2560]{1,0:T(8,128)(2,1)}, bf16[128,2560]{1,0:T(8,128)(2,1)S(1)}, u32[]{:S(2)}, u32[]{:S(2)}) collective-permute-start(bf16[128,2560]{1,0:T(8,128)(2,1)} %copy-done.10), channel_id=1, source_target_pairs={{2,0},{4,6},{3,1},{5,7},{10,8},{12,14},{11,9},{13,15},{18,16},{20,... | collective-permute-start | bytes 1966088 | tf_op jit(solution)/shard_map/ppermute | solution.py:56
  64.4 31.3 %collective-permute-start.9 = (bf16[128,4096]{1,0:T(8,128)(2,1)S(1)}, bf16[128,4096]{1,0:T(8,128)(2,1)S(1)}, u32[]{:S(2)}, u32[]{:S(2)}) collective-permute-start(bf16[128,4096]{1,0:T(8,128)(2,1)S(1)} %bitcast.14), channel_id=1, source_target_pairs={{0,2},{6,4},{1,3},{7,5},{8,10},{14,12},{9,11},{15,13},{16,18},{22,... | collective-permute-start | bytes 3145736 | tf_op jit(solution)/shard_map/ppermute | solution.py:48
  67.3 7.8 %collective-permute-start.11 = (bf16[384,256]{1,0:T(8,128)(2,1)S(1)}, bf16[384,256]{1,0:T(8,128)(2,1)S(1)}, u32[]{:S(2)}, u32[]{:S(2)}) collective-permute-start(bf16[384,256]{1,0:T(8,128)(2,1)S(1)} %get-tuple-element.18), channel_id=1, source_target_pairs={{2,4},{4,2},{3,5},{5,3},{10,12},{12,10},{11,13},{13,11},{18,20},{2... | collective-permute-start | bytes 589832 | tf_op jit(solution)/shard_map/ppermute | solution.py:52
  74.5 32.6 %collective-permute-start.15 = (bf16[192,2048]{1,0:T(8,128)(2,1)S(1)}, bf16[192,2048]{1,0:T(8,128)(2,1)S(1)}, u32[]{:S(2)}, u32[]{:S(2)}) collective-permute-start(bf16[192,2048]{1,0:T(8,128)(2,1)S(1)} %collective-permute-done.13), channel_id=1, source_target_pairs={{2,4},{4,2},{3,5},{5,3},{10,12},{12,10},{11,13},{13,11},{18,20},{2... | collective-permute-start | bytes 2359304 | tf_op jit(solution)/shard_map/ppermute | solution.py:52
  78.0 2.6 %copy-start.3 = (bf16[1,128,2560]{2,1,0:T(8,128)(2,1)S(1)}, bf16[1,128,2560]{2,1,0:T(8,128)(2,1)}, u32[]{:S(2)}) copy-start(bf16[1,128,2560]{2,1,0:T(8,128)(2,1)} %param.5) | copy-start | bytes 1966084
  78.0 2.6 %copy-start.5 = (bf16[128,2560]{1,0:T(8,128)(2,1)S(1)}, bf16[128,2560]{1,0:T(8,128)(2,1)}, u32[]{:S(2)}) copy-start(bf16[128,2560]{1,0:T(8,128)(2,1)} %copy-done.4) | copy-start | bytes 1966084
  78.0 2.6 %copy-start.7 = (bf16[128,2560]{1,0:T(8,128)(2,1)S(1)}, bf16[128,2560]{1,0:T(8,128)(2,1)}, u32[]{:S(2)}) copy-start(bf16[128,2560]{1,0:T(8,128)(2,1)} %copy-done.6) | copy-start | bytes 1966084
  78.0 2.6 %copy-start.9 = (bf16[128,2560]{1,0:T(8,128)(2,1)S(1)}, bf16[128,2560]{1,0:T(8,128)(2,1)}, u32[]{:S(2)}) copy-start(bf16[128,2560]{1,0:T(8,128)(2,1)} %copy-done.8) | copy-start | bytes 1966084
  78.1 2.6 %copy-start.11 = (bf16[128,2560]{1,0:T(8,128)(2,1)S(1)}, bf16[128,2560]{1,0:T(8,128)(2,1)}, u32[]{:S(2)}) copy-start(bf16[128,2560]{1,0:T(8,128)(2,1)} %copy-done.10) | copy-start | bytes 1966084
  81.4 16.7 %copy-start.1 = (bf16[192,2048]{1,0:T(8,128)(2,1)S(1)}, bf16[192,2048]{1,0:T(8,128)(2,1)}, u32[]{:S(2)}) copy-start(bf16[192,2048]{1,0:T(8,128)(2,1)} %get-tuple-element.21) | copy-start | bytes 2359300
  99.0 7.9 %collective-permute-start.14 = (bf16[576,256]{1,0:T(8,128)(2,1)S(1)}, bf16[576,256]{1,0:T(8,128)(2,1)S(1)}, u32[]{:S(2)}, u32[]{:S(2)}) collective-permute-start(bf16[576,256]{1,0:T(8,128)(2,1)S(1)} %fusion.25), channel_id=1, source_target_pairs={{0,1},{1,0},{2,3},{3,2},{4,5},{5,4},{6,7},{7,6},{8,9},{9,8},{10,11... | collective-permute-start | bytes 884744 | tf_op jit(solution)/shard_map/ppermute | solution.py:60
  100.6 15.7 %collective-permute-start.17 = (bf16[128,2048]{1,0:T(8,128)(2,1)S(1)}, bf16[128,2048]{1,0:T(8,128)(2,1)S(1)}, u32[]{:S(2)}, u32[]{:S(2)}) collective-permute-start(bf16[128,2048]{1,0:T(8,128)(2,1)S(1)} %slice.122), channel_id=1, source_target_pairs={{2,0},{4,6},{3,1},{5,7},{10,8},{12,14},{11,9},{13,15},{18,16},{20,... | collective-permute-start | bytes 1572872 | tf_op jit(solution)/shard_map/ppermute | solution.py:56
  107.6 4.7 %collective-permute-start.16 = (bf16[192,256]{1,0:T(8,128)(2,1)S(1)}, bf16[192,256]{1,0:T(8,128)(2,1)S(1)}, u32[]{:S(2)}, u32[]{:S(2)}) collective-permute-start(bf16[192,256]{1,0:T(8,128)(2,1)S(1)} %fusion.26), channel_id=1, source_target_pairs={{0,1},{1,0},{2,3},{3,2},{4,5},{5,4},{6,7},{7,6},{8,9},{9,8},{10,11... | collective-permute-start | bytes 294920 | tf_op jit(solution)/shard_map/ppermute | solution.py:60
  110.4 28.6 %collective-permute-start.26 = (bf16[128,2048]{1,0:T(8,128)(2,1)S(1)}, bf16[128,2048]{1,0:T(8,128)(2,1)S(1)}, u32[]{:S(2)}, u32[]{:S(2)}) collective-permute-start(bf16[128,2048]{1,0:T(8,128)(2,1)S(1)} %slice.135), channel_id=1, source_target_pairs={{2,0},{4,6},{3,1},{5,7},{10,8},{12,14},{11,9},{13,15},{18,16},{20,... | collective-permute-start | bytes 1572872 | tf_op jit(solution)/shard_map/ppermute | solution.py:56
  116.3 0.8 collective-permute-start.18
  117.1 1.2 copy-start.13
  117.1 1.5 copy-start.15
  119.7 13.2 %collective-permute-start.19 = (bf16[192,512]{1,0:T(8,128)(2,1)S(1)}, bf16[192,512]{1,0:T(8,128)(2,1)S(1)}, u32[]{:S(2)}, u32[]{:S(2)}) collective-permute-start(bf16[192,512]{1,0:T(8,128)(2,1)S(1)} %slice.124), channel_id=1, source_target_pairs={{2,0},{4,6},{3,1},{5,7},{10,8},{12,14},{11,9},{13,15},{18,16},{20,... | collective-permute-start | bytes 589832 | tf_op jit(solution)/shard_map/ppermute | solution.py:56
  121.0 14.5 %collective-permute-start.21 = (bf16[128,1024]{1,0:T(8,128)(2,1)S(1)}, bf16[128,1024]{1,0:T(8,128)(2,1)S(1)}, u32[]{:S(2)}, u32[]{:S(2)}) collective-permute-start(bf16[128,1024]{1,0:T(8,128)(2,1)S(1)} %slice.130), channel_id=1, source_target_pairs={{2,4},{4,2},{3,5},{5,3},{10,12},{12,10},{11,13},{13,11},{18,20},{2... | collective-permute-start | bytes 786440 | tf_op jit(solution)/shard_map/ppermute | solution.py:52
  121.7 15.9 %collective-permute-start.24 = (bf16[128,1536]{1,0:T(8,128)(2,1)S(1)}, bf16[128,1536]{1,0:T(8,128)(2,1)S(1)}, u32[]{:S(2)}, u32[]{:S(2)}) collective-permute-start(bf16[128,1536]{1,0:T(8,128)(2,1)S(1)} %slice.132), channel_id=1, source_target_pairs={{2,4},{4,2},{3,5},{5,3},{10,12},{12,10},{11,13},{13,11},{18,20},{2... | collective-permute-start | bytes 1179656 | tf_op jit(solution)/shard_map/ppermute | solution.py:52
  133.6 13.5 %collective-permute-start.20 = (bf16[192,2560]{1,0:T(8,128)(2,1)S(1)}, bf16[192,2560]{1,0:T(8,128)(2,1)S(1)}, u32[]{:S(2)}, u32[]{:S(2)}) collective-permute-start(bf16[192,2560]{1,0:T(8,128)(2,1)S(1)} %convolution_convert_fusion), channel_id=1, source_target_pairs={{8,0},{16,8},{24,16},{9,1},{17,9},{25,17},{10,2},{18,10},{26,18},{... | collective-permute-start | bytes 2949128 | tf_op jit(solution)/shard_map/ppermute | solution.py:13
  135.6 12.0 %collective-permute-start.23 = (bf16[128,1024]{1,0:T(8,128)(2,1)S(1)}, bf16[128,1024]{1,0:T(8,128)(2,1)S(1)}, u32[]{:S(2)}, u32[]{:S(2)}) collective-permute-start(bf16[128,1024]{1,0:T(8,128)(2,1)S(1)} %add_convert_fusion.2), channel_id=1, source_target_pairs={{2,0},{4,6},{3,1},{5,7},{10,8},{12,14},{11,9},{13,15},{18,16},{20,... | collective-permute-start | bytes 786440 | tf_op jit(solution)/shard_map/ppermute | solution.py:56
  136.9 10.2 %collective-permute-start.22 = (bf16[128,2560]{1,0:T(8,128)(2,1)S(1)}, bf16[128,2560]{1,0:T(8,128)(2,1)S(1)}, u32[]{:S(2)}, u32[]{:S(2)}) collective-permute-start(bf16[128,2560]{1,0:T(8,128)(2,1)S(1)} %convolution_convert_fusion.3), channel_id=1, source_target_pairs={{2,4},{4,2},{3,5},{5,3},{10,12},{12,10},{11,13},{13,11},{18,20},{2... | collective-permute-start | bytes 1966088 | tf_op jit(solution)/shard_map/ppermute | solution.py:52
  137.7 17.4 %collective-permute-start.25 = (bf16[128,1536]{1,0:T(8,128)(2,1)S(1)}, bf16[128,1536]{1,0:T(8,128)(2,1)S(1)}, u32[]{:S(2)}, u32[]{:S(2)}) collective-permute-start(bf16[128,1536]{1,0:T(8,128)(2,1)S(1)} %add_convert_fusion.1), channel_id=1, source_target_pairs={{2,0},{4,6},{3,1},{5,7},{10,8},{12,14},{11,9},{13,15},{18,16},{20,... | collective-permute-start | bytes 1179656 | tf_op jit(solution)/shard_map/ppermute | solution.py:56

commit v15 on v14

--- a/solution.py
+++ b/solution.py
@@ -145,7 +145,7 @@
         for j in range(4)
     ]
     width = tokens.shape[1]
-    first = width * 2 // 5 // 128 * 128
+    first = width * 3 // 10 // 128 * 128
     halves = (slice(0, first), slice(first, width))
     sent_end, sent_own = sums[3], sums[2]
     from_end = [across(sent_end[:, half]) for half in halves]

time: 160 us -> 161 us (level)
  transfers between devices with their start and end apart: 27 -> 27, of which waited for: 15 -> 14; matrix products, arithmetic and copies ran while one was open for 11% -> 11% of each run, Pallas kernels for 0% -> 0%
where the time goes in v15:
time: 161 us; the launch traced here: 158 us
  waiting for transfers between devices  90.3 us (56%)
  starting transfers between devices  45.8 us (28%)
  matrix products  12.5 us (8%)
  local copies, waits for them, and re-layouts  4.96 us (3%)
  other arithmetic  3.12 us (2%)
    ppermute x5, waiting for transfers between devices, inward(): return lax.ppermute(value, 'row', [(0, 1), (3, 2)])  48.1 us
    ppermute x8, waiting for transfers between devices, outward(): return lax.ppermute(value, 'row', [(1, 0), (2, 3)])  29.7 us
    ppermute x5, starting transfers between devices, inward(): return lax.ppermute(value, 'row', [(0, 1), (3, 2)])  22 us
    ppermute x8, starting transfers between devices, outward(): return lax.ppermute(value, 'row', [(1, 0), (2, 3)])  10.3 us
    ppermute x10, starting transfers between devices, across(): return lax.ppermute(value, 'row', [(1, 2), (2, 1)])  6.95 us
    ppermute x1, waiting for transfers between devices, shifted(): lax.ppermute(value, axis, [(source, source + steps) for source in range(l...  6.93 us
    dot_general x6, matrix products, tokens_dot(): lax.dot_general(left, right, (((0,), (0,)), ((), ())), preferred_element_...  6.79 us
    ppermute x3, waiting for transfers between devices, other_col(): return lax.ppermute(value, 'col', [(0, 1), (1, 0)])  5.62 us
  transfers between devices with their start and end apart: 27, of which 14 were waited for; matrix products, arithmetic and copies ran while one was open for 11% of the time, Pallas kernels for 0%

profile of v15, /device:TPU:4, one launch (start us, length us, event | category | flops | bytes accessed | tf_op | source)
XLA Modules:
  0.0 157.9 jit_solution(3884417588154370187)
XLA Ops:
  0.7 3.7 %collective-permute-start.2 = (bf16[128,2560]{1,0:T(8,128)(2,1)}, bf16[128,2560]{1,0:T(8,128)(2,1)S(1)}, u32[]{:S(2)}, u32[]{:S(2)}) collective-permute-start(bf16[128,2560]{1,0:T(8,128)(2,1)} %bitcast.19), channel_id=1, source_target_pairs={{0,2},{6,4},{1,3},{7,5},{8,10},{14,12},{9,11},{15,13},{16,18},{22,... | collective-permute-start | bytes 1966088 | tf_op jit(solution)/shard_map/ppermute | solution.py:48
  4.3 1.4 collective-permute-start
  5.7 1.3 collective-permute-start.1
  7.0 0.7 collective-permute-start.3
  7.7 12.0 %collective-permute-done.2 = bf16[128,2560]{1,0:T(8,128)(2,1)S(1)} collective-permute-done((bf16[128,2560]{1,0:T(8,128)(2,1)}, bf16[128,2560]{1,0:T(8,128)(2,1)S(1)}, u32[]{:S(2)}, u32[]{:S(2)}) %collective-permute-start.2) | collective-permute-done | bytes 655392 | tf_op jit(solution)/shard_map/ppermute | solution.py:48
  19.7 0.7 collective-permute-start.4
  20.4 0.8 collective-permute-start.7
  21.2 2.7 %fusion.44 = (bf16[192,2048]{1,0:T(8,128)(2,1)}, bf16[192,2048]{1,0:T(8,128)(2,1)}) fusion(bf16[192,4096]{1,0:T(8,128)(2,1)} %bitcast.13), kind=kLoop, calls=%fused_computation.72 | loop fusion | bytes 3145728 | tf_op jit(solution)/shard_map/slice | solution.py:119
  23.9 0.1 collective-permute-done.1
  24.0 9.5 %collective-permute-start.6 = (bf16[192,2048]{1,0:T(8,128)(2,1)}, bf16[192,2048]{1,0:T(8,128)(2,1)}, u32[]{:S(2)}, u32[]{:S(2)}) collective-permute-start(bf16[192,2048]{1,0:T(8,128)(2,1)} %get-tuple-element.32), channel_id=1, source_target_pairs={{0,2},{6,4},{1,3},{7,5},{8,10},{14,12},{9,11},{15,13},{16,18},{22,... | collective-permute-start | bytes 2359304 | tf_op jit(solution)/shard_map/ppermute | solution.py:48
  33.4 7.3 %collective-permute-done = bf16[192,2560]{1,0:T(8,128)(2,1)S(1)} collective-permute-done((bf16[192,2560]{1,0:T(8,128)(2,1)}, bf16[192,2560]{1,0:T(8,128)(2,1)S(1)}, u32[]{:S(2)}, u32[]{:S(2)}) %collective-permute-start) | collective-permute-done | bytes 983072 | tf_op jit(solution)/shard_map/ppermute | solution.py:48
  40.8 1.2 convolution_convert_fusion.6
  42.2 1.5 collective-permute-start.5
  43.7 4.6 %collective-permute-start.13 = (bf16[192,2048]{1,0:T(8,128)(2,1)}, bf16[192,2048]{1,0:T(8,128)(2,1)S(1)}, u32[]{:S(2)}, u32[]{:S(2)}) collective-permute-start(bf16[192,2048]{1,0:T(8,128)(2,1)} %get-tuple-element.21), channel_id=1, source_target_pairs={{0,2},{6,4},{1,3},{7,5},{8,10},{14,12},{9,11},{15,13},{16,18},{22,... | collective-permute-start | bytes 2359304 | tf_op jit(solution)/shard_map/ppermute | solution.py:48
  48.3 1.3 collective-permute-start.10
  49.6 8.1 %collective-permute-done.6 = bf16[192,2048]{1,0:T(8,128)(2,1)} collective-permute-done((bf16[192,2048]{1,0:T(8,128)(2,1)}, bf16[192,2048]{1,0:T(8,128)(2,1)}, u32[]{:S(2)}, u32[]{:S(2)}) %collective-permute-start.6) | collective-permute-done | bytes 786464 | tf_op jit(solution)/shard_map/ppermute | solution.py:48
  57.6 0.7 collective-permute-start.8
  58.3 1.3 collective-permute-start.12
  59.6 0.2 multiply_reduce_fusion.1
  59.9 0.1 fusion.24
  60.0 4.4 %collective-permute-done.10 = bf16[128,2560]{1,0:T(8,128)(2,1)S(1)} collective-permute-done((bf16[128,2560]{1,0:T(8,128)(2,1)}, bf16[128,2560]{1,0:T(8,128)(2,1)S(1)}, u32[]{:S(2)}, u32[]{:S(2)}) %collective-permute-start.10) | collective-permute-done | bytes 655392 | tf_op jit(solution)/shard_map/ppermute | solution.py:56
  64.4 2.9 %collective-permute-start.9 = (bf16[128,4096]{1,0:T(8,128)(2,1)S(1)}, bf16[128,4096]{1,0:T(8,128)(2,1)S(1)}, u32[]{:S(2)}, u32[]{:S(2)}) collective-permute-start(bf16[128,4096]{1,0:T(8,128)(2,1)S(1)} %bitcast.14), channel_id=1, source_target_pairs={{0,2},{6,4},{1,3},{7,5},{8,10},{14,12},{9,11},{15,13},{16,18},{22,... | collective-permute-start | bytes 3145736 | tf_op jit(solution)/shard_map/ppermute | solution.py:48
  67.3 0.7 collective-permute-start.11
  68.0 0.1 fusion.43
  68.1 6.3 %collective-permute-done.13 = bf16[192,2048]{1,0:T(8,128)(2,1)S(1)} collective-permute-done((bf16[192,2048]{1,0:T(8,128)(2,1)}, bf16[192,2048]{1,0:T(8,128)(2,1)S(1)}, u32[]{:S(2)}, u32[]{:S(2)}) %collective-permute-start.13) | collective-permute-done | bytes 786464 | tf_op jit(solution)/shard_map/ppermute | solution.py:48
  74.5 0.7 collective-permute-start.15
  75.2 2.8 %collective-permute-done.12 = bf16[128,2560]{1,0:T(8,128)(2,1)S(1)} collective-permute-done((bf16[128,2560]{1,0:T(8,128)(2,1)}, bf16[128,2560]{1,0:T(8,128)(2,1)S(1)}, u32[]{:S(2)}, u32[]{:S(2)}) %collective-permute-start.12) | collective-permute-done | bytes 655392 | tf_op jit(solution)/shard_map/ppermute | solution.py:56
  78.1 2.5 %convolution_convert_fusion.5 = bf16[256,2048]{1,0:T(8,128)(2,1)S(1)} fusion(bf16[768,256]{1,0:T(8,128)(2,1)S(1)} %pad_maximum_fusion.8, bf16[192,2048]{1,0:T(8,128)(2,1)S(1)} %collective-permute-done.8, bf16[192,2048]{1,0:T(8,128)(2,1)S(1)} %get-tuple-element.30, bf16[192,2048]{1,0:T(8,128)(2,1)} %collective-permute-done.6, ...), kind=kOutput, calls=%fused_computation.18 | convolution fusion | flops 818413568 | bytes 4587520 | tf_op jit(solution)/shard_map/dot_general | solution.py:72
  80.7 0.7 maximum_select_fusion
  81.4 14.3 %collective-permute-done.9 = bf16[128,4096]{1,0:T(8,128)(2,1)S(1)} collective-permute-done((bf16[128,4096]{1,0:T(8,128)(2,1)S(1)}, bf16[128,4096]{1,0:T(8,128)(2,1)S(1)}, u32[]{:S(2)}, u32[]{:S(2)}) %collective-permute-start.9) | collective-permute-done | bytes 1048608 | tf_op jit(solution)/shard_map/ppermute | solution.py:48
  95.7 2.4 %fusion.19 = f32[768,256]{1,0:T(8,128)S(1)} fusion(bf16[128,4096]{1,0:T(8,128)(2,1)S(1)} %bitcast.15, bf16[128,4096]{1,0:T(8,128)(2,1)S(1)} %collective-permute-done.9, bf16[192,2048]{1,0:T(8,128)(2,1)S(1)} %collective-permute-done.8, bf16[192,2048]{1,0:T(8,128)(2,1)S(1)} %get-tuple-element.30, bf16[192,2048]{1,0:T(8,128)(2,1)} %collective-permute-done.6, ...), kind=kOutput, calls=%fused_computation.31 | convolution fusion | flops 819986432 | bytes 6029312 | tf_op jit(solution)/shard_map/dot_general | solution.py:68
  98.1 0.9 fusion.25
  99.0 1.6 collective-permute-start.14
  100.6 1.3 collective-permute-start.17
  101.9 5.0 %collective-permute-done.14 = bf16[576,256]{1,0:T(8,128)(2,1)S(1)} collective-permute-done((bf16[576,256]{1,0:T(8,128)(2,1)S(1)}, bf16[576,256]{1,0:T(8,128)(2,1)S(1)}, u32[]{:S(2)}, u32[]{:S(2)}) %collective-permute-start.14) | collective-permute-done | bytes 294944 | tf_op jit(solution)/shard_map/ppermute | solution.py:60
  107.1 0.5 fusion.26
  107.6 1.6 collective-permute-start.16
  109.1 1.2 fusion.9
  110.4 1.3 collective-permute-start.26
  111.7 0.6 collective-permute-done.16
  112.3 4.0 %collective-permute-done.17 = bf16[128,2048]{1,0:T(8,128)(2,1)S(1)} collective-permute-done((bf16[128,2048]{1,0:T(8,128)(2,1)S(1)}, bf16[128,2048]{1,0:T(8,128)(2,1)S(1)}, u32[]{:S(2)}, u32[]{:S(2)}) %collective-permute-start.17) | collective-permute-done | bytes 524320 | tf_op jit(solution)/shard_map/ppermute | solution.py:56
  116.3 0.7 collective-permute-start.18
  117.1 0.3 multiply_reduce_fusion
  117.4 0.2 multiply_convert_fusion
  117.7 0.6 copy-done.13
  118.3 0.3 copy-done.15
  118.6 0.5 convolution_convert_fusion.3
  119.1 0.5 convolution_convert_fusion.1
  119.7 1.3 collective-permute-start.19
  121.0 0.7 collective-permute-start.21
  121.7 0.7 collective-permute-start.24
  122.4 0.5 convolution_convert_fusion.2
  122.9 9.9 %collective-permute-done.19 = bf16[192,512]{1,0:T(8,128)(2,1)S(1)} collective-permute-done((bf16[192,512]{1,0:T(8,128)(2,1)S(1)}, bf16[192,512]{1,0:T(8,128)(2,1)S(1)}, u32[]{:S(2)}, u32[]{:S(2)}) %collective-permute-start.19) | collective-permute-done | bytes 196640 | tf_op jit(solution)/shard_map/ppermute | solution.py:56
  132.9 0.7 convolution_convert_fusion
  133.6 1.9 %collective-permute-start.20 = (bf16[192,2560]{1,0:T(8,128)(2,1)S(1)}, bf16[192,2560]{1,0:T(8,128)(2,1)S(1)}, u32[]{:S(2)}, u32[]{:S(2)}) collective-permute-start(bf16[192,2560]{1,0:T(8,128)(2,1)S(1)} %convolution_convert_fusion), channel_id=1, source_target_pairs={{8,0},{16,8},{24,16},{9,1},{17,9},{25,17},{10,2},{18,10},{26,18},{... | collective-permute-start | bytes 2949128 | tf_op jit(solution)/shard_map/ppermute | solution.py:13
  135.6 1.3 collective-permute-start.23
  136.9 0.7 collective-permute-start.22
  137.6 0.1 add_convert_fusion.1
  137.7 1.3 collective-permute-start.25
  139.1 1.1 maximum_bitcast_fusion
  140.2 6.9 %collective-permute-done.20 = bf16[192,2560]{1,0:T(8,128)(2,1)S(1)} collective-permute-done((bf16[192,2560]{1,0:T(8,128)(2,1)S(1)}, bf16[192,2560]{1,0:T(8,128)(2,1)S(1)}, u32[]{:S(2)}, u32[]{:S(2)}) %collective-permute-start.20) | collective-permute-done | bytes 983072 | tf_op jit(solution)/shard_map/ppermute | solution.py:13
  147.1 8.5 %collective-permute-done.25 = bf16[128,1792]{1,0:T(8,128)(2,1)S(1)} collective-permute-done((bf16[128,1792]{1,0:T(8,128)(2,1)S(1)}, bf16[128,1792]{1,0:T(8,128)(2,1)S(1)}, u32[]{:S(2)}, u32[]{:S(2)}) %collective-permute-start.25) | collective-permute-done | bytes 458784 | tf_op jit(solution)/shard_map/ppermute | solution.py:56
  155.5 1.4 fusion.23
  157.0 0.9 copy.8
  (61 shorter events, 0.7 us)
Async XLA Ops:
  0.6 40.2 %copy-start.2 = (bf16[1,128,2560]{2,1,0:T(8,128)(2,1)S(1)}, bf16[1,128,2560]{2,1,0:T(8,128)(2,1)}, u32[]{:S(2)}) copy-start(bf16[1,128,2560]{2,1,0:T(8,128)(2,1)} %param.5) | copy-start | bytes 1966084
  0.6 40.2 %copy-start.12 = (bf16[1,192,2560]{2,1,0:T(8,128)(2,1)S(1)}, bf16[1,192,2560]{2,1,0:T(8,128)(2,1)}, u32[]{:S(2)}) copy-start(bf16[1,192,2560]{2,1,0:T(8,128)(2,1)} %param.4) | copy-start | bytes 2949124
  0.7 19.1 %collective-permute-start.2 = (bf16[128,2560]{1,0:T(8,128)(2,1)}, bf16[128,2560]{1,0:T(8,128)(2,1)S(1)}, u32[]{:S(2)}, u32[]{:S(2)}) collective-permute-start(bf16[128,2560]{1,0:T(8,128)(2,1)} %bitcast.19), channel_id=1, source_target_pairs={{0,2},{6,4},{1,3},{7,5},{8,10},{14,12},{9,11},{15,13},{16,18},{22,... | collective-permute-start | bytes 1966088 | tf_op jit(solution)/shard_map/ppermute | solution.py:48
  4.3 36.5 %collective-permute-start = (bf16[192,2560]{1,0:T(8,128)(2,1)}, bf16[192,2560]{1,0:T(8,128)(2,1)S(1)}, u32[]{:S(2)}, u32[]{:S(2)}) collective-permute-start(bf16[192,2560]{1,0:T(8,128)(2,1)} %bitcast.24), channel_id=1, source_target_pairs={{0,2},{6,4},{1,3},{7,5},{8,10},{14,12},{9,11},{15,13},{16,18},{22,... | collective-permute-start | bytes 2949128 | tf_op jit(solution)/shard_map/ppermute | solution.py:48
  5.7 18.3 %collective-permute-start.1 = (bf16[128,2560]{1,0:T(8,128)(2,1)}, bf16[128,2560]{1,0:T(8,128)(2,1)S(1)}, u32[]{:S(2)}, u32[]{:S(2)}) collective-permute-start(bf16[128,2560]{1,0:T(8,128)(2,1)} %bitcast.20), channel_id=1, source_target_pairs={{2,0},{4,6},{3,1},{5,7},{10,8},{12,14},{11,9},{13,15},{18,16},{20,... | collective-permute-start | bytes 1966088 | tf_op jit(solution)/shard_map/ppermute | solution.py:56
  7.0 33.8 %collective-permute-start.3 = (bf16[128,2560]{1,0:T(8,128)(2,1)}, bf16[128,2560]{1,0:T(8,128)(2,1)S(1)}, u32[]{:S(2)}, u32[]{:S(2)}) collective-permute-start(bf16[128,2560]{1,0:T(8,128)(2,1)} %bitcast.21), channel_id=1, source_target_pairs={{2,4},{4,2},{3,5},{5,3},{10,12},{12,10},{11,13},{13,11},{18,20},{2... | collective-permute-start | bytes 1966088 | tf_op jit(solution)/shard_map/ppermute | solution.py:52
  19.7 22.3 %copy-start.4 = (bf16[128,2560]{1,0:T(8,128)(2,1)}, bf16[128,2560]{1,0:T(8,128)(2,1)S(1)}, u32[]{:S(2)}) copy-start(bf16[128,2560]{1,0:T(8,128)(2,1)S(1)} %collective-permute-done.2) | copy-start | bytes 1966084
  19.7 21.1 %collective-permute-start.4 = (bf16[128,2560]{1,0:T(8,128)(2,1)S(1)}, bf16[128,2560]{1,0:T(8,128)(2,1)S(1)}, u32[]{:S(2)}, u32[]{:S(2)}) collective-permute-start(bf16[128,2560]{1,0:T(8,128)(2,1)S(1)} %collective-permute-done.2), channel_id=1, source_target_pairs={{2,4},{4,2},{3,5},{5,3},{10,12},{12,10},{11,13},{13,11},{18,20},{2... | collective-permute-start | bytes 1966088 | tf_op jit(solution)/shard_map/ppermute | solution.py:52
  20.4 46.9 %collective-permute-start.7 = (bf16[192,4096]{1,0:T(8,128)(2,1)}, bf16[192,4096]{1,0:T(8,128)(2,1)S(1)}, u32[]{:S(2)}, u32[]{:S(2)}) collective-permute-start(bf16[192,4096]{1,0:T(8,128)(2,1)} %bitcast.12), channel_id=1, source_target_pairs={{2,4},{4,2},{3,5},{5,3},{10,12},{12,10},{11,13},{13,11},{18,20},{2... | collective-permute-start | bytes 4718600 | tf_op jit(solution)/shard_map/ppermute | solution.py:52
  24.0 16.8 %copy-start.6 = (bf16[128,2560]{1,0:T(8,128)(2,1)}, bf16[128,2560]{1,0:T(8,128)(2,1)S(1)}, u32[]{:S(2)}) copy-start(bf16[128,2560]{1,0:T(8,128)(2,1)S(1)} %collective-permute-done.1) | copy-start | bytes 1966084
  24.0 33.6 %collective-permute-start.6 = (bf16[192,2048]{1,0:T(8,128)(2,1)}, bf16[192,2048]{1,0:T(8,128)(2,1)}, u32[]{:S(2)}, u32[]{:S(2)}) collective-permute-start(bf16[192,2048]{1,0:T(8,128)(2,1)} %get-tuple-element.32), channel_id=1, source_target_pairs={{0,2},{6,4},{1,3},{7,5},{8,10},{14,12},{9,11},{15,13},{16,18},{22,... | collective-permute-start | bytes 2359304 | tf_op jit(solution)/shard_map/ppermute | solution.py:48
  40.8 1.3 copy-start.14
  40.8 1.3 copy-start.8
  40.8 1.3 copy-start.10
  42.2 22.3 %copy-start = (bf16[1,128,4096]{2,1,0:T(8,128)(2,1)S(1)}, bf16[1,128,4096]{2,1,0:T(8,128)(2,1)}, u32[]{:S(2)}) copy-start(bf16[1,128,4096]{2,1,0:T(8,128)(2,1)} %param.6) | copy-start | bytes 3145732
  42.2 16.2 %collective-permute-start.5 = (bf16[384,512]{1,0:T(8,128)(2,1)S(1)}, bf16[384,512]{1,0:T(8,128)(2,1)S(1)}, u32[]{:S(2)}, u32[]{:S(2)}) collective-permute-start(bf16[384,512]{1,0:T(8,128)(2,1)S(1)} %convolution_convert_fusion.6), channel_id=1, source_target_pairs={{0,1},{1,0},{2,3},{3,2},{4,5},{5,4},{6,7},{7,6},{8,9},{9,8},{10,11... | collective-permute-start | bytes 1179656 | tf_op jit(solution)/shard_map/ppermute | solution.py:60
  43.7 30.8 %collective-permute-start.13 = (bf16[192,2048]{1,0:T(8,128)(2,1)}, bf16[192,2048]{1,0:T(8,128)(2,1)S(1)}, u32[]{:S(2)}, u32[]{:S(2)}) collective-permute-start(bf16[192,2048]{1,0:T(8,128)(2,1)} %get-tuple-element.21), channel_id=1, source_target_pairs={{0,2},{6,4},{1,3},{7,5},{8,10},{14,12},{9,11},{15,13},{16,18},{22,... | collective-permute-start | bytes 2359304 | tf_op jit(solution)/shard_map/ppermute | solution.py:48
  48.3 16.2 %collective-permute-start.10 = (bf16[128,2560]{1,0:T(8,128)(2,1)}, bf16[128,2560]{1,0:T(8,128)(2,1)S(1)}, u32[]{:S(2)}, u32[]{:S(2)}) collective-permute-start(bf16[128,2560]{1,0:T(8,128)(2,1)} %copy-done.8), channel_id=1, source_target_pairs={{2,0},{4,6},{3,1},{5,7},{10,8},{12,14},{11,9},{13,15},{18,16},{20,... | collective-permute-start | bytes 1966088 | tf_op jit(solution)/shard_map/ppermute | solution.py:56
  57.6 20.4 %collective-permute-start.8 = (bf16[192,2048]{1,0:T(8,128)(2,1)}, bf16[192,2048]{1,0:T(8,128)(2,1)S(1)}, u32[]{:S(2)}, u32[]{:S(2)}) collective-permute-start(bf16[192,2048]{1,0:T(8,128)(2,1)} %collective-permute-done.6), channel_id=1, source_target_pairs={{2,4},{4,2},{3,5},{5,3},{10,12},{12,10},{11,13},{13,11},{18,20},{2... | collective-permute-start | bytes 2359304 | tf_op jit(solution)/shard_map/ppermute | solution.py:52
  58.3 19.7 %collective-permute-start.12 = (bf16[128,2560]{1,0:T(8,128)(2,1)}, bf16[128,2560]{1,0:T(8,128)(2,1)S(1)}, u32[]{:S(2)}, u32[]{:S(2)}) collective-permute-start(bf16[128,2560]{1,0:T(8,128)(2,1)} %copy-done.10), channel_id=1, source_target_pairs={{2,0},{4,6},{3,1},{5,7},{10,8},{12,14},{11,9},{13,15},{18,16},{20,... | collective-permute-start | bytes 1966088 | tf_op jit(solution)/shard_map/ppermute | solution.py:56
  64.4 31.3 %collective-permute-start.9 = (bf16[128,4096]{1,0:T(8,128)(2,1)S(1)}, bf16[128,4096]{1,0:T(8,128)(2,1)S(1)}, u32[]{:S(2)}, u32[]{:S(2)}) collective-permute-start(bf16[128,4096]{1,0:T(8,128)(2,1)S(1)} %bitcast.14), channel_id=1, source_target_pairs={{0,2},{6,4},{1,3},{7,5},{8,10},{14,12},{9,11},{15,13},{16,18},{22,... | collective-permute-start | bytes 3145736 | tf_op jit(solution)/shard_map/ppermute | solution.py:48
  67.3 7.8 %collective-permute-start.11 = (bf16[384,256]{1,0:T(8,128)(2,1)S(1)}, bf16[384,256]{1,0:T(8,128)(2,1)S(1)}, u32[]{:S(2)}, u32[]{:S(2)}) collective-permute-start(bf16[384,256]{1,0:T(8,128)(2,1)S(1)} %get-tuple-element.18), channel_id=1, source_target_pairs={{2,4},{4,2},{3,5},{5,3},{10,12},{12,10},{11,13},{13,11},{18,20},{2... | collective-permute-start | bytes 589832 | tf_op jit(solution)/shard_map/ppermute | solution.py:52
  74.5 32.6 %collective-permute-start.15 = (bf16[192,2048]{1,0:T(8,128)(2,1)S(1)}, bf16[192,2048]{1,0:T(8,128)(2,1)S(1)}, u32[]{:S(2)}, u32[]{:S(2)}) collective-permute-start(bf16[192,2048]{1,0:T(8,128)(2,1)S(1)} %collective-permute-done.13), channel_id=1, source_target_pairs={{2,4},{4,2},{3,5},{5,3},{10,12},{12,10},{11,13},{13,11},{18,20},{2... | collective-permute-start | bytes 2359304 | tf_op jit(solution)/shard_map/ppermute | solution.py:52
  78.0 2.6 %copy-start.3 = (bf16[1,128,2560]{2,1,0:T(8,128)(2,1)S(1)}, bf16[1,128,2560]{2,1,0:T(8,128)(2,1)}, u32[]{:S(2)}) copy-start(bf16[1,128,2560]{2,1,0:T(8,128)(2,1)} %param.5) | copy-start | bytes 1966084
  78.0 2.6 %copy-start.5 = (bf16[128,2560]{1,0:T(8,128)(2,1)S(1)}, bf16[128,2560]{1,0:T(8,128)(2,1)}, u32[]{:S(2)}) copy-start(bf16[128,2560]{1,0:T(8,128)(2,1)} %copy-done.4) | copy-start | bytes 1966084
  78.0 2.6 %copy-start.7 = (bf16[128,2560]{1,0:T(8,128)(2,1)S(1)}, bf16[128,2560]{1,0:T(8,128)(2,1)}, u32[]{:S(2)}) copy-start(bf16[128,2560]{1,0:T(8,128)(2,1)} %copy-done.6) | copy-start | bytes 1966084
  78.0 2.6 %copy-start.9 = (bf16[128,2560]{1,0:T(8,128)(2,1)S(1)}, bf16[128,2560]{1,0:T(8,128)(2,1)}, u32[]{:S(2)}) copy-start(bf16[128,2560]{1,0:T(8,128)(2,1)} %copy-done.8) | copy-start | bytes 1966084
  78.1 2.6 %copy-start.11 = (bf16[128,2560]{1,0:T(8,128)(2,1)S(1)}, bf16[128,2560]{1,0:T(8,128)(2,1)}, u32[]{:S(2)}) copy-start(bf16[128,2560]{1,0:T(8,128)(2,1)} %copy-done.10) | copy-start | bytes 1966084
  81.4 16.7 %copy-start.1 = (bf16[192,2048]{1,0:T(8,128)(2,1)S(1)}, bf16[192,2048]{1,0:T(8,128)(2,1)}, u32[]{:S(2)}) copy-start(bf16[192,2048]{1,0:T(8,128)(2,1)} %get-tuple-element.21) | copy-start | bytes 2359300
  99.0 7.9 %collective-permute-start.14 = (bf16[576,256]{1,0:T(8,128)(2,1)S(1)}, bf16[576,256]{1,0:T(8,128)(2,1)S(1)}, u32[]{:S(2)}, u32[]{:S(2)}) collective-permute-start(bf16[576,256]{1,0:T(8,128)(2,1)S(1)} %fusion.25), channel_id=1, source_target_pairs={{0,1},{1,0},{2,3},{3,2},{4,5},{5,4},{6,7},{7,6},{8,9},{9,8},{10,11... | collective-permute-start | bytes 884744 | tf_op jit(solution)/shard_map/ppermute | solution.py:60
  100.6 15.7 %collective-permute-start.17 = (bf16[128,2048]{1,0:T(8,128)(2,1)S(1)}, bf16[128,2048]{1,0:T(8,128)(2,1)S(1)}, u32[]{:S(2)}, u32[]{:S(2)}) collective-permute-start(bf16[128,2048]{1,0:T(8,128)(2,1)S(1)} %slice.122), channel_id=1, source_target_pairs={{2,0},{4,6},{3,1},{5,7},{10,8},{12,14},{11,9},{13,15},{18,16},{20,... | collective-permute-start | bytes 1572872 | tf_op jit(solution)/shard_map/ppermute | solution.py:56
  107.6 4.7 %collective-permute-start.16 = (bf16[192,256]{1,0:T(8,128)(2,1)S(1)}, bf16[192,256]{1,0:T(8,128)(2,1)S(1)}, u32[]{:S(2)}, u32[]{:S(2)}) collective-permute-start(bf16[192,256]{1,0:T(8,128)(2,1)S(1)} %fusion.26), channel_id=1, source_target_pairs={{0,1},{1,0},{2,3},{3,2},{4,5},{5,4},{6,7},{7,6},{8,9},{9,8},{10,11... | collective-permute-start | bytes 294920 | tf_op jit(solution)/shard_map/ppermute | solution.py:60
  110.4 28.6 %collective-permute-start.26 = (bf16[128,2048]{1,0:T(8,128)(2,1)S(1)}, bf16[128,2048]{1,0:T(8,128)(2,1)S(1)}, u32[]{:S(2)}, u32[]{:S(2)}) collective-permute-start(bf16[128,2048]{1,0:T(8,128)(2,1)S(1)} %slice.135), channel_id=1, source_target_pairs={{2,0},{4,6},{3,1},{5,7},{10,8},{12,14},{11,9},{13,15},{18,16},{20,... | collective-permute-start | bytes 1572872 | tf_op jit(solution)/shard_map/ppermute | solution.py:56
  116.3 0.8 collective-permute-start.18
  117.1 1.2 copy-start.13
  117.1 1.5 copy-start.15
  119.7 13.2 %collective-permute-start.19 = (bf16[192,512]{1,0:T(8,128)(2,1)S(1)}, bf16[192,512]{1,0:T(8,128)(2,1)S(1)}, u32[]{:S(2)}, u32[]{:S(2)}) collective-permute-start(bf16[192,512]{1,0:T(8,128)(2,1)S(1)} %slice.124), channel_id=1, source_target_pairs={{2,0},{4,6},{3,1},{5,7},{10,8},{12,14},{11,9},{13,15},{18,16},{20,... | collective-permute-start | bytes 589832 | tf_op jit(solution)/shard_map/ppermute | solution.py:56
  121.0 14.5 %collective-permute-start.21 = (bf16[128,768]{1,0:T(8,128)(2,1)S(1)}, bf16[128,768]{1,0:T(8,128)(2,1)S(1)}, u32[]{:S(2)}, u32[]{:S(2)}) collective-permute-start(bf16[128,768]{1,0:T(8,128)(2,1)S(1)} %slice.130), channel_id=1, source_target_pairs={{2,4},{4,2},{3,5},{5,3},{10,12},{12,10},{11,13},{13,11},{18,20},{2... | collective-permute-start | bytes 589832 | tf_op jit(solution)/shard_map/ppermute | solution.py:52
  121.7 15.9 %collective-permute-start.24 = (bf16[128,1792]{1,0:T(8,128)(2,1)S(1)}, bf16[128,1792]{1,0:T(8,128)(2,1)S(1)}, u32[]{:S(2)}, u32[]{:S(2)}) collective-permute-start(bf16[128,1792]{1,0:T(8,128)(2,1)S(1)} %slice.132), channel_id=1, source_target_pairs={{2,4},{4,2},{3,5},{5,3},{10,12},{12,10},{11,13},{13,11},{18,20},{2... | collective-permute-start | bytes 1376264 | tf_op jit(solution)/shard_map/ppermute | solution.py:52
  133.6 13.5 %collective-permute-start.20 = (bf16[192,2560]{1,0:T(8,128)(2,1)S(1)}, bf16[192,2560]{1,0:T(8,128)(2,1)S(1)}, u32[]{:S(2)}, u32[]{:S(2)}) collective-permute-start(bf16[192,2560]{1,0:T(8,128)(2,1)S(1)} %convolution_convert_fusion), channel_id=1, source_target_pairs={{8,0},{16,8},{24,16},{9,1},{17,9},{25,17},{10,2},{18,10},{26,18},{... | collective-permute-start | bytes 2949128 | tf_op jit(solution)/shard_map/ppermute | solution.py:13
  135.6 11.5 %collective-permute-start.23 = (bf16[128,768]{1,0:T(8,128)(2,1)S(1)}, bf16[128,768]{1,0:T(8,128)(2,1)S(1)}, u32[]{:S(2)}, u32[]{:S(2)}) collective-permute-start(bf16[128,768]{1,0:T(8,128)(2,1)S(1)} %add_convert_fusion.2), channel_id=1, source_target_pairs={{2,0},{4,6},{3,1},{5,7},{10,8},{12,14},{11,9},{13,15},{18,16},{20,... | collective-permute-start | bytes 589832 | tf_op jit(solution)/shard_map/ppermute | solution.py:56
  136.9 10.2 %collective-permute-start.22 = (bf16[128,2560]{1,0:T(8,128)(2,1)S(1)}, bf16[128,2560]{1,0:T(8,128)(2,1)S(1)}, u32[]{:S(2)}, u32[]{:S(2)}) collective-permute-start(bf16[128,2560]{1,0:T(8,128)(2,1)S(1)} %convolution_convert_fusion.3), channel_id=1, source_target_pairs={{2,4},{4,2},{3,5},{5,3},{10,12},{12,10},{11,13},{13,11},{18,20},{2... | collective-permute-start | bytes 1966088 | tf_op jit(solution)/shard_map/ppermute | solution.py:52
  137.7 17.8 %collective-permute-start.25 = (bf16[128,1792]{1,0:T(8,128)(2,1)S(1)}, bf16[128,1792]{1,0:T(8,128)(2,1)S(1)}, u32[]{:S(2)}, u32[]{:S(2)}) collective-permute-start(bf16[128,1792]{1,0:T(8,128)(2,1)S(1)} %add_convert_fusion.1), channel_id=1, source_target_pairs={{2,0},{4,6},{3,1},{5,7},{10,8},{12,14},{11,9},{13,15},{18,16},{20,... | collective-permute-start | bytes 1376264 | tf_op jit(solution)/shard_map/ppermute | solution.py:56

commit v16 on v14

--- a/solution.py
+++ b/solution.py
@@ -85,7 +85,7 @@
     place = lax.axis_index("row")
     middle = (place == 1) | (place == 2)
 
-    cut = feat // 2
+    cut = feat * 5 // 8 // 128 * 128
     cuts = (slice(0, cut), slice(cut, feat))
     down_end = inward(down)
     tokens_end = inward(tokens)

time: 160 us -> 164 us (1.025)
  waiting for transfers between devices: 89.9 us -> 80.9 us
  matrix products: 12.5 us -> 17 us
  starting transfers between devices: 45.8 us -> 49.8 us
  local copies, waits for them, and re-layouts: 4.96 us -> 6.98 us
  other arithmetic: 3.1 us -> 5.05 us
    ppermute x5, waiting for transfers between devices: 48.1 us -> 39.6 us  [inward(): return lax.ppermute(value, 'row', [(0, 1), (3, 2)])]
    ppermute x3, waiting for transfers between devices: 5.62 us -> 1.66 us  [other_col(): return lax.ppermute(value, 'col', [(0, 1), (1, 0)])]
    dot_general x4, matrix products: 4.98 us -> 8.4 us  [rows_dot(): lax.dot_general(left, right, (((1,), (1,)), ((), ())), preferred_element_...]
    ppermute x8, waiting for transfers between devices: 29.2 us -> 32.6 us  [outward(): return lax.ppermute(value, 'row', [(1, 0), (2, 3)])]
    ppermute x5, starting transfers between devices: 22 us -> 24.5 us  [inward(): return lax.ppermute(value, 'row', [(0, 1), (3, 2)])]
    ppermute x10, starting transfers between devices: 6.95 us -> 9.33 us  [across(): return lax.ppermute(value, 'row', [(1, 2), (2, 1)])]
  transfers between devices with their start and end apart: 27 -> 27, of which waited for: 15 -> 12; matrix products, arithmetic and copies ran while one was open for 11% -> 15% of each run, Pallas kernels for 0% -> 0%
where the time goes in v16:
time: 164 us; the launch traced here: 161 us
  waiting for transfers between devices  80.9 us (49%)
  starting transfers between devices  49.8 us (30%)
  matrix products  17 us (10%)
  local copies, waits for them, and re-layouts  6.98 us (4%)
  other arithmetic  5.05 us (3%)
    ppermute x5, waiting for transfers between devices, inward(): return lax.ppermute(value, 'row', [(0, 1), (3, 2)])  39.6 us
    ppermute x8, waiting for transfers between devices, outward(): return lax.ppermute(value, 'row', [(1, 0), (2, 3)])  32.6 us
    ppermute x5, starting transfers between devices, inward(): return lax.ppermute(value, 'row', [(0, 1), (3, 2)])  24.5 us
    ppermute x8, starting transfers between devices, outward(): return lax.ppermute(value, 'row', [(1, 0), (2, 3)])  10.3 us
    ppermute x10, starting transfers between devices, across(): return lax.ppermute(value, 'row', [(1, 2), (2, 1)])  9.33 us
    dot_general x4, matrix products, rows_dot(): lax.dot_general(left, right, (((1,), (1,)), ((), ())), preferred_element_...  8.4 us
    dot_general x6, matrix products, tokens_dot(): lax.dot_general(left, right, (((0,), (0,)), ((), ())), preferred_element_...  7.9 us
    ppermute x1, waiting for transfers between devices, shifted(): lax.ppermute(value, axis, [(source, source + steps) for source in range(l...  6.94 us
  transfers between devices with their start and end apart: 27, of which 12 were waited for; matrix products, arithmetic and copies ran while one was open for 15% of the time, Pallas kernels for 0%

profile of v16, /device:TPU:4, one launch (start us, length us, event | category | flops | bytes accessed | tf_op | source)
XLA Modules:
  0.0 160.9 jit_solution(3764425685404568800)
XLA Ops:
  0.6 3.5 %collective-permute-start.2 = (bf16[128,2560]{1,0:T(8,128)(2,1)}, bf16[128,2560]{1,0:T(8,128)(2,1)S(1)}, u32[]{:S(2)}, u32[]{:S(2)}) collective-permute-start(bf16[128,2560]{1,0:T(8,128)(2,1)} %bitcast.20), channel_id=1, source_target_pairs={{0,2},{6,4},{1,3},{7,5},{8,10},{14,12},{9,11},{15,13},{16,18},{22,... | collective-permute-start | bytes 1966088 | tf_op jit(solution)/shard_map/ppermute | solution.py:48
  4.2 1.4 collective-permute-start
  5.5 1.3 collective-permute-start.1
  6.8 0.7 collective-permute-start.3
  7.5 12.0 %collective-permute-done.2 = bf16[128,2560]{1,0:T(8,128)(2,1)S(1)} collective-permute-done((bf16[128,2560]{1,0:T(8,128)(2,1)}, bf16[128,2560]{1,0:T(8,128)(2,1)S(1)}, u32[]{:S(2)}, u32[]{:S(2)}) %collective-permute-start.2) | collective-permute-done | bytes 655392 | tf_op jit(solution)/shard_map/ppermute | solution.py:48
  19.6 1.5 collective-permute-start.4
  21.1 1.3 slice.110
  22.3 7.2 %collective-permute-start.6 = (bf16[192,2560]{1,0:T(8,128)(2,1)S(1)}, bf16[192,2560]{1,0:T(8,128)(2,1)}, u32[]{:S(2)}, u32[]{:S(2)}) collective-permute-start(bf16[192,2560]{1,0:T(8,128)(2,1)S(1)} %slice.110), channel_id=1, source_target_pairs={{0,2},{6,4},{1,3},{7,5},{8,10},{14,12},{9,11},{15,13},{16,18},{22,... | collective-permute-start | bytes 2949128 | tf_op jit(solution)/shard_map/ppermute | solution.py:48
  29.6 0.8 collective-permute-start.7
  30.3 10.3 %collective-permute-done = bf16[192,2560]{1,0:T(8,128)(2,1)S(1)} collective-permute-done((bf16[192,2560]{1,0:T(8,128)(2,1)}, bf16[192,2560]{1,0:T(8,128)(2,1)S(1)}, u32[]{:S(2)}, u32[]{:S(2)}) %collective-permute-start) | collective-permute-done | bytes 983072 | tf_op jit(solution)/shard_map/ppermute | solution.py:48
  40.6 3.4 %convolution_convert_fusion.7 = bf16[384,512]{1,0:T(8,128)(2,1)S(1)} fusion(bf16[128,2560]{1,0:T(8,128)(2,1)} %collective-permute-done.4, bf16[128,2560]{1,0:T(8,128)(2,1)S(1)} %collective-permute-done.3, bf16[128,2560]{1,0:T(8,128)(2,1)S(1)} %collective-permute-done.2, bf16[128,2560]{1,0:T(8,128)(2,1)} %bitcast.23, ...), kind=kOutput, calls=%fused_computation.30 | convolution fusion | flops 1021247488 | bytes 4980736 | tf_op jit(solution)/shard_map/dot_general | solution.py:68
  44.1 1.6 collective-permute-start.5
  45.6 1.9 %slice.117 = bf16[192,1536]{1,0:T(8,128)(2,1)} slice(bf16[192,4096]{1,0:T(8,128)(2,1)} %bitcast.14), slice={[0:192], [2560:4096]} | slice | bytes 1179648 | tf_op jit(solution)/shard_map/slice | solution.py:119
  47.5 5.1 %collective-permute-start.13 = (bf16[192,1536]{1,0:T(8,128)(2,1)}, bf16[192,1536]{1,0:T(8,128)(2,1)}, u32[]{:S(2)}, u32[]{:S(2)}) collective-permute-start(bf16[192,1536]{1,0:T(8,128)(2,1)} %slice.117), channel_id=1, source_target_pairs={{0,2},{6,4},{1,3},{7,5},{8,10},{14,12},{9,11},{15,13},{16,18},{22,... | collective-permute-start | bytes 1769480 | tf_op jit(solution)/shard_map/ppermute | solution.py:48
  52.6 1.3 collective-permute-start.10
  53.9 7.7 %collective-permute-done.6 = bf16[192,2560]{1,0:T(8,128)(2,1)} collective-permute-done((bf16[192,2560]{1,0:T(8,128)(2,1)S(1)}, bf16[192,2560]{1,0:T(8,128)(2,1)}, u32[]{:S(2)}, u32[]{:S(2)}) %collective-permute-start.6) | collective-permute-done | bytes 983072 | tf_op jit(solution)/shard_map/ppermute | solution.py:48
  61.6 1.6 collective-permute-start.8
  63.2 1.3 collective-permute-start.12
  64.5 0.2 multiply_reduce_fusion.1
  64.7 0.1 fusion.20
  64.8 0.8 fusion.38
  65.6 3.8 %collective-permute-done.10 = bf16[128,2560]{1,0:T(8,128)(2,1)S(1)} collective-permute-done((bf16[128,2560]{1,0:T(8,128)(2,1)S(1)}, bf16[128,2560]{1,0:T(8,128)(2,1)S(1)}, u32[]{:S(2)}, u32[]{:S(2)}) %collective-permute-start.10) | collective-permute-done | bytes 655392 | tf_op jit(solution)/shard_map/ppermute | solution.py:56
  69.4 0.8 copy-done.11
  70.3 1.3 collective-permute-start.11
  71.6 7.4 %collective-permute-start.9 = (bf16[128,4096]{1,0:T(8,128)(2,1)S(1)}, bf16[128,4096]{1,0:T(8,128)(2,1)S(1)}, u32[]{:S(2)}, u32[]{:S(2)}) collective-permute-start(bf16[128,4096]{1,0:T(8,128)(2,1)S(1)} %bitcast.15), channel_id=1, source_target_pairs={{0,2},{6,4},{1,3},{7,5},{8,10},{14,12},{9,11},{15,13},{16,18},{22,... | collective-permute-start | bytes 3145736 | tf_op jit(solution)/shard_map/ppermute | solution.py:48
  79.1 0.7 collective-permute-start.15
  79.9 1.0 pad_maximum_fusion.8
  80.9 1.8 %collective-permute-done.12 = bf16[128,2560]{1,0:T(8,128)(2,1)} collective-permute-done((bf16[128,2560]{1,0:T(8,128)(2,1)}, bf16[128,2560]{1,0:T(8,128)(2,1)}, u32[]{:S(2)}, u32[]{:S(2)}) %collective-permute-start.12) | collective-permute-done | bytes 655392 | tf_op jit(solution)/shard_map/ppermute | solution.py:56
  82.7 2.7 %convolution_convert_fusion = bf16[256,2560]{1,0:T(8,128)(2,1)S(1)} fusion(bf16[768,256]{1,0:T(8,128)(2,1)S(1)} %pad_maximum_fusion.8, bf16[192,2560]{1,0:T(8,128)(2,1)} %collective-permute-done.8, bf16[192,2560]{1,0:T(8,128)(2,1)S(1)} %slice.111, bf16[192,2560]{1,0:T(8,128)(2,1)} %collective-permute-done.6, bf16[192,2560]{1,0:T(8,128)(2,1)S(1)} %copy-done.2), kind=kOutput, calls=%fused_computation.1 | convolution fusion | flops 1023016960 | bytes 5636096 | tf_op jit(solution)/shard_map/dot_general | solution.py:72
  85.4 1.3 collective-permute-start.17
  86.8 1.8 %maximum_select_fusion = bf16[512,2560]{1,0:T(8,128)(2,1)S(1)} fusion(bf16[128,2560]{1,0:T(8,128)(2,1)} %collective-permute-done.12, bf16[128,2560]{1,0:T(8,128)(2,1)S(1)} %copy-done.12, bf16[128,2560]{1,0:T(8,128)(2,1)S(1)} %bitcast.24, bf16[128,2560]{1,0:T(8,128)(2,1)S(1)} %copy-done.8, pred[]{:T(512)S(6)} %or.3, ...), kind=kLoop, calls=%fused_computation.9 | loop fusion | flops 22282240 | bytes 7208961 | tf_op jit(solution)/shard_map/jit(_where)/select_n | solution.py:103
  88.6 9.6 %collective-permute-done.9 = bf16[128,4096]{1,0:T(8,128)(2,1)S(1)} collective-permute-done((bf16[128,4096]{1,0:T(8,128)(2,1)S(1)}, bf16[128,4096]{1,0:T(8,128)(2,1)S(1)}, u32[]{:S(2)}, u32[]{:S(2)}) %collective-permute-start.9) | collective-permute-done | bytes 1048608 | tf_op jit(solution)/shard_map/ppermute | solution.py:48
  98.2 2.7 %fusion.15 = f32[768,256]{1,0:T(8,128)S(1)} fusion(bf16[128,4096]{1,0:T(8,128)(2,1)S(1)} %bitcast.16, bf16[128,4096]{1,0:T(8,128)(2,1)S(1)} %collective-permute-done.9, bf16[192,2560]{1,0:T(8,128)(2,1)} %collective-permute-done.8, bf16[192,2560]{1,0:T(8,128)(2,1)S(1)} %slice.111, bf16[192,2560]{1,0:T(8,128)(2,1)} %collective-permute-done.6, ...), kind=kOutput, calls=%fused_computation.28 | convolution fusion | flops 1024983040 | bytes 6815744 | tf_op jit(solution)/shard_map/dot_general | solution.py:68
  100.9 1.9 %fusion.21 = bf16[576,256]{1,0:T(8,128)(2,1)S(1)} fusion(f32[768,256]{1,0:T(8,128)S(1)} %fusion.15, bf16[192,1536]{1,0:T(8,128)(2,1)S(1)} %slice.118, bf16[192,1536]{1,0:T(8,128)(2,1)} %collective-permute-done.13, bf16[192,1536]{1,0:T(8,128)(2,1)} %slice.117, bf16[128,4096]{1,0:T(8,128)(2,1)S(1)} %collective-permute-done.9, bf16[128,4096]{1,0:T(8,128)(2,1)S(1)} %bitcast.17), kind=kOutput, calls=%fused_computation.45 | convolution fusion | flops 460161024 | bytes 4751360 | tf_op jit(solution)/shard_map/dot_general | solution.py:68
  102.8 1.6 collective-permute-start.14
  104.4 0.4 fusion.22
  104.8 0.6 collective-permute-start.16
  105.4 2.1 %convolution_convert_fusion.6 = bf16[256,1536]{1,0:T(8,128)(2,1)S(1)} fusion(bf16[192,1536]{1,0:T(8,128)(2,1)S(1)} %collective-permute-done.15, bf16[192,1536]{1,0:T(8,128)(2,1)S(1)} %slice.118, bf16[192,1536]{1,0:T(8,128)(2,1)} %collective-permute-done.13, bf16[192,1536]{1,0:T(8,128)(2,1)} %slice.117, bf16[384,256]{1,0:T(8,128)(2,1)} %collective-permute-done.11, ...), kind=kOutput, calls=%fused_computation.10 | convolution fusion | flops 614596608 | bytes 3538944 | tf_op jit(solution)/shard_map/dot_general | solution.py:72
  107.6 1.3 collective-permute-start.26
  108.9 0.7 collective-permute-done.14
  109.7 0.9 collective-permute-done.16
  110.7 9.9 %collective-permute-done.17 = bf16[128,2560]{1,0:T(8,128)(2,1)S(1)} collective-permute-done((bf16[128,2560]{1,0:T(8,128)(2,1)S(1)}, bf16[128,2560]{1,0:T(8,128)(2,1)S(1)}, u32[]{:S(2)}, u32[]{:S(2)}) %collective-permute-start.17) | collective-permute-done | bytes 655392 | tf_op jit(solution)/shard_map/ppermute | solution.py:56
  120.7 0.7 collective-permute-start.18
  121.5 0.3 multiply_reduce_fusion
  121.7 0.2 multiply_convert_fusion
  122.0 0.6 copy-done.13
  122.6 0.3 copy-done.15
  122.9 0.5 convolution_convert_fusion.2
  123.5 0.5 convolution_convert_fusion.3
  124.0 1.3 collective-permute-start.19
  125.3 0.7 collective-permute-start.21
  126.0 0.7 collective-permute-start.24
  126.7 0.5 convolution_convert_fusion.4
  127.3 9.0 %collective-permute-done.19 = bf16[192,512]{1,0:T(8,128)(2,1)S(1)} collective-permute-done((bf16[192,512]{1,0:T(8,128)(2,1)S(1)}, bf16[192,512]{1,0:T(8,128)(2,1)S(1)}, u32[]{:S(2)}, u32[]{:S(2)}) %collective-permute-start.19) | collective-permute-done | bytes 196640 | tf_op jit(solution)/shard_map/ppermute | solution.py:56
  136.3 0.7 convolution_convert_fusion.1
  137.0 1.9 %collective-permute-start.20 = (bf16[192,2560]{1,0:T(8,128)(2,1)S(1)}, bf16[192,2560]{1,0:T(8,128)(2,1)S(1)}, u32[]{:S(2)}, u32[]{:S(2)}) collective-permute-start(bf16[192,2560]{1,0:T(8,128)(2,1)S(1)} %convolution_convert_fusion.1), channel_id=1, source_target_pairs={{8,0},{16,8},{24,16},{9,1},{17,9},{25,17},{10,2},{18,10},{26,18},{... | collective-permute-start | bytes 2949128 | tf_op jit(solution)/shard_map/ppermute | solution.py:13
  139.0 1.3 collective-permute-start.23
  140.3 0.7 collective-permute-start.22
  141.1 1.3 collective-permute-start.25
  142.5 1.1 maximum_bitcast_fusion
  143.6 6.9 %collective-permute-done.20 = bf16[192,2560]{1,0:T(8,128)(2,1)S(1)} collective-permute-done((bf16[192,2560]{1,0:T(8,128)(2,1)S(1)}, bf16[192,2560]{1,0:T(8,128)(2,1)S(1)}, u32[]{:S(2)}, u32[]{:S(2)}) %collective-permute-start.20) | collective-permute-done | bytes 983072 | tf_op jit(solution)/shard_map/ppermute | solution.py:13
  150.5 8.0 %collective-permute-done.25 = bf16[128,1536]{1,0:T(8,128)(2,1)S(1)} collective-permute-done((bf16[128,1536]{1,0:T(8,128)(2,1)S(1)}, bf16[128,1536]{1,0:T(8,128)(2,1)S(1)}, u32[]{:S(2)}, u32[]{:S(2)}) %collective-permute-start.25) | collective-permute-done | bytes 393248 | tf_op jit(solution)/shard_map/ppermute | solution.py:56
  158.5 1.4 fusion.19
  160.0 0.9 copy.8
  (63 shorter events, 0.8 us)
Async XLA Ops:
  0.6 18.9 %collective-permute-start.2 = (bf16[128,2560]{1,0:T(8,128)(2,1)}, bf16[128,2560]{1,0:T(8,128)(2,1)S(1)}, u32[]{:S(2)}, u32[]{:S(2)}) collective-permute-start(bf16[128,2560]{1,0:T(8,128)(2,1)} %bitcast.20), channel_id=1, source_target_pairs={{0,2},{6,4},{1,3},{7,5},{8,10},{14,12},{9,11},{15,13},{16,18},{22,... | collective-permute-start | bytes 1966088 | tf_op jit(solution)/shard_map/ppermute | solution.py:48
  4.2 36.5 %collective-permute-start = (bf16[192,2560]{1,0:T(8,128)(2,1)}, bf16[192,2560]{1,0:T(8,128)(2,1)S(1)}, u32[]{:S(2)}, u32[]{:S(2)}) collective-permute-start(bf16[192,2560]{1,0:T(8,128)(2,1)} %bitcast.25), channel_id=1, source_target_pairs={{0,2},{6,4},{1,3},{7,5},{8,10},{14,12},{9,11},{15,13},{16,18},{22,... | collective-permute-start | bytes 2949128 | tf_op jit(solution)/shard_map/ppermute | solution.py:48
  5.5 24.1 %collective-permute-start.1 = (bf16[128,2560]{1,0:T(8,128)(2,1)}, bf16[128,2560]{1,0:T(8,128)(2,1)S(1)}, u32[]{:S(2)}, u32[]{:S(2)}) collective-permute-start(bf16[128,2560]{1,0:T(8,128)(2,1)} %bitcast.21), channel_id=1, source_target_pairs={{2,0},{4,6},{3,1},{5,7},{10,8},{12,14},{11,9},{13,15},{18,16},{20,... | collective-permute-start | bytes 1966088 | tf_op jit(solution)/shard_map/ppermute | solution.py:56
  6.8 33.8 %collective-permute-start.3 = (bf16[128,2560]{1,0:T(8,128)(2,1)}, bf16[128,2560]{1,0:T(8,128)(2,1)S(1)}, u32[]{:S(2)}, u32[]{:S(2)}) collective-permute-start(bf16[128,2560]{1,0:T(8,128)(2,1)} %bitcast.22), channel_id=1, source_target_pairs={{2,4},{4,2},{3,5},{5,3},{10,12},{12,10},{11,13},{13,11},{18,20},{2... | collective-permute-start | bytes 1966088 | tf_op jit(solution)/shard_map/ppermute | solution.py:52
  19.6 24.5 %copy-start.5 = (bf16[128,2560]{1,0:T(8,128)(2,1)}, bf16[128,2560]{1,0:T(8,128)(2,1)S(1)}, u32[]{:S(2)}) copy-start(bf16[128,2560]{1,0:T(8,128)(2,1)S(1)} %collective-permute-done.2) | copy-start | bytes 1966084
  19.6 21.1 %collective-permute-start.4 = (bf16[128,2560]{1,0:T(8,128)(2,1)S(1)}, bf16[128,2560]{1,0:T(8,128)(2,1)}, u32[]{:S(2)}, u32[]{:S(2)}) collective-permute-start(bf16[128,2560]{1,0:T(8,128)(2,1)S(1)} %collective-permute-done.2), channel_id=1, source_target_pairs={{2,4},{4,2},{3,5},{5,3},{10,12},{12,10},{11,13},{13,11},{18,20},{2... | collective-permute-start | bytes 1966088 | tf_op jit(solution)/shard_map/ppermute | solution.py:52
  22.3 21.7 %copy-start.1 = (bf16[192,2560]{1,0:T(8,128)(2,1)}, bf16[192,2560]{1,0:T(8,128)(2,1)S(1)}, u32[]{:S(2)}) copy-start(bf16[192,2560]{1,0:T(8,128)(2,1)S(1)} %slice.110) | copy-start | bytes 2949124
  22.3 39.2 %collective-permute-start.6 = (bf16[192,2560]{1,0:T(8,128)(2,1)S(1)}, bf16[192,2560]{1,0:T(8,128)(2,1)}, u32[]{:S(2)}, u32[]{:S(2)}) collective-permute-start(bf16[192,2560]{1,0:T(8,128)(2,1)S(1)} %slice.110), channel_id=1, source_target_pairs={{0,2},{6,4},{1,3},{7,5},{8,10},{14,12},{9,11},{15,13},{16,18},{22,... | collective-permute-start | bytes 2949128 | tf_op jit(solution)/shard_map/ppermute | solution.py:48
  29.6 11.0 %copy-start.7 = (bf16[128,2560]{1,0:T(8,128)(2,1)}, bf16[128,2560]{1,0:T(8,128)(2,1)S(1)}, u32[]{:S(2)}) copy-start(bf16[128,2560]{1,0:T(8,128)(2,1)S(1)} %collective-permute-done.1) | copy-start | bytes 1966084
  29.6 42.0 %collective-permute-start.7 = (bf16[192,4096]{1,0:T(8,128)(2,1)}, bf16[192,4096]{1,0:T(8,128)(2,1)S(1)}, u32[]{:S(2)}, u32[]{:S(2)}) collective-permute-start(bf16[192,4096]{1,0:T(8,128)(2,1)} %bitcast.13), channel_id=1, source_target_pairs={{2,4},{4,2},{3,5},{5,3},{10,12},{12,10},{11,13},{13,11},{18,20},{2... | collective-permute-start | bytes 4718600 | tf_op jit(solution)/shard_map/ppermute | solution.py:52
  40.6 3.4 %copy-start.14 = (bf16[192,2560]{1,0:T(8,128)(2,1)}, bf16[192,2560]{1,0:T(8,128)(2,1)S(1)}, u32[]{:S(2)}) copy-start(bf16[192,2560]{1,0:T(8,128)(2,1)S(1)} %collective-permute-done) | copy-start | bytes 2949124
  40.6 12.0 %copy-start.9 = (bf16[128,2560]{1,0:T(8,128)(2,1)}, bf16[128,2560]{1,0:T(8,128)(2,1)S(1)}, u32[]{:S(2)}) copy-start(bf16[128,2560]{1,0:T(8,128)(2,1)S(1)} %collective-permute-done.3) | copy-start | bytes 1966084
  44.1 27.6 %copy-start = (bf16[1,128,4096]{2,1,0:T(8,128)(2,1)S(1)}, bf16[1,128,4096]{2,1,0:T(8,128)(2,1)}, u32[]{:S(2)}) copy-start(bf16[1,128,4096]{2,1,0:T(8,128)(2,1)} %param.6) | copy-start | bytes 3145732
  44.1 19.1 %collective-permute-start.5 = (bf16[384,512]{1,0:T(8,128)(2,1)S(1)}, bf16[384,512]{1,0:T(8,128)(2,1)S(1)}, u32[]{:S(2)}, u32[]{:S(2)}) collective-permute-start(bf16[384,512]{1,0:T(8,128)(2,1)S(1)} %convolution_convert_fusion.7), channel_id=1, source_target_pairs={{0,1},{1,0},{2,3},{3,2},{4,5},{5,4},{6,7},{7,6},{8,9},{9,8},{10,11... | collective-permute-start | bytes 1179656 | tf_op jit(solution)/shard_map/ppermute | solution.py:60
  47.5 31.6 %collective-permute-start.13 = (bf16[192,1536]{1,0:T(8,128)(2,1)}, bf16[192,1536]{1,0:T(8,128)(2,1)}, u32[]{:S(2)}, u32[]{:S(2)}) collective-permute-start(bf16[192,1536]{1,0:T(8,128)(2,1)} %slice.117), channel_id=1, source_target_pairs={{0,2},{6,4},{1,3},{7,5},{8,10},{14,12},{9,11},{15,13},{16,18},{22,... | collective-permute-start | bytes 1769480 | tf_op jit(solution)/shard_map/ppermute | solution.py:48
  52.6 16.8 %collective-permute-start.10 = (bf16[128,2560]{1,0:T(8,128)(2,1)S(1)}, bf16[128,2560]{1,0:T(8,128)(2,1)S(1)}, u32[]{:S(2)}, u32[]{:S(2)}) collective-permute-start(bf16[128,2560]{1,0:T(8,128)(2,1)S(1)} %collective-permute-done.3), channel_id=1, source_target_pairs={{2,0},{4,6},{3,1},{5,7},{10,8},{12,14},{11,9},{13,15},{18,16},{20,... | collective-permute-start | bytes 1966088 | tf_op jit(solution)/shard_map/ppermute | solution.py:56
  61.6 21.1 %collective-permute-start.8 = (bf16[192,2560]{1,0:T(8,128)(2,1)}, bf16[192,2560]{1,0:T(8,128)(2,1)}, u32[]{:S(2)}, u32[]{:S(2)}) collective-permute-start(bf16[192,2560]{1,0:T(8,128)(2,1)} %collective-permute-done.6), channel_id=1, source_target_pairs={{2,4},{4,2},{3,5},{5,3},{10,12},{12,10},{11,13},{13,11},{18,20},{2... | collective-permute-start | bytes 2949128 | tf_op jit(solution)/shard_map/ppermute | solution.py:52
  63.2 19.5 %collective-permute-start.12 = (bf16[128,2560]{1,0:T(8,128)(2,1)}, bf16[128,2560]{1,0:T(8,128)(2,1)}, u32[]{:S(2)}, u32[]{:S(2)}) collective-permute-start(bf16[128,2560]{1,0:T(8,128)(2,1)} %collective-permute-done.4), channel_id=1, source_target_pairs={{2,0},{4,6},{3,1},{5,7},{10,8},{12,14},{11,9},{13,15},{18,16},{20,... | collective-permute-start | bytes 1966088 | tf_op jit(solution)/shard_map/ppermute | solution.py:56
  69.4 0.8 copy-start.11
  70.3 9.6 %collective-permute-start.11 = (bf16[384,256]{1,0:T(8,128)(2,1)}, bf16[384,256]{1,0:T(8,128)(2,1)}, u32[]{:S(2)}, u32[]{:S(2)}) collective-permute-start(bf16[384,256]{1,0:T(8,128)(2,1)} %get-tuple-element.18), channel_id=1, source_target_pairs={{2,4},{4,2},{3,5},{5,3},{10,12},{12,10},{11,13},{13,11},{18,20},{2... | collective-permute-start | bytes 589832 | tf_op jit(solution)/shard_map/ppermute | solution.py:52
  71.6 8.2 %copy-start.3 = (bf16[384,256]{1,0:T(8,128)(2,1)S(1)}, bf16[384,256]{1,0:T(8,128)(2,1)}, u32[]{:S(2)}) copy-start(bf16[384,256]{1,0:T(8,128)(2,1)} %get-tuple-element.29) | copy-start | bytes 589828
  71.6 11.1 %copy-start.2 = (bf16[192,2560]{1,0:T(8,128)(2,1)S(1)}, bf16[192,2560]{1,0:T(8,128)(2,1)}, u32[]{:S(2)}) copy-start(bf16[192,2560]{1,0:T(8,128)(2,1)} %copy-done.1) | copy-start | bytes 2949124
  71.6 26.6 %collective-permute-start.9 = (bf16[128,4096]{1,0:T(8,128)(2,1)S(1)}, bf16[128,4096]{1,0:T(8,128)(2,1)S(1)}, u32[]{:S(2)}, u32[]{:S(2)}) collective-permute-start(bf16[128,4096]{1,0:T(8,128)(2,1)S(1)} %bitcast.15), channel_id=1, source_target_pairs={{0,2},{6,4},{1,3},{7,5},{8,10},{14,12},{9,11},{15,13},{16,18},{22,... | collective-permute-start | bytes 3145736 | tf_op jit(solution)/shard_map/ppermute | solution.py:48
  79.1 25.3 %collective-permute-start.15 = (bf16[192,1536]{1,0:T(8,128)(2,1)}, bf16[192,1536]{1,0:T(8,128)(2,1)S(1)}, u32[]{:S(2)}, u32[]{:S(2)}) collective-permute-start(bf16[192,1536]{1,0:T(8,128)(2,1)} %collective-permute-done.13), channel_id=1, source_target_pairs={{2,4},{4,2},{3,5},{5,3},{10,12},{12,10},{11,13},{13,11},{18,20},{2... | collective-permute-start | bytes 1769480 | tf_op jit(solution)/shard_map/ppermute | solution.py:52
  80.8 5.9 %copy-start.4 = (bf16[1,128,2560]{2,1,0:T(8,128)(2,1)S(1)}, bf16[1,128,2560]{2,1,0:T(8,128)(2,1)}, u32[]{:S(2)}) copy-start(bf16[1,128,2560]{2,1,0:T(8,128)(2,1)} %param.5) | copy-start | bytes 1966084
  80.8 5.9 %copy-start.6 = (bf16[128,2560]{1,0:T(8,128)(2,1)S(1)}, bf16[128,2560]{1,0:T(8,128)(2,1)}, u32[]{:S(2)}) copy-start(bf16[128,2560]{1,0:T(8,128)(2,1)} %copy-done.5) | copy-start | bytes 1966084
  80.8 5.9 %copy-start.8 = (bf16[128,2560]{1,0:T(8,128)(2,1)S(1)}, bf16[128,2560]{1,0:T(8,128)(2,1)}, u32[]{:S(2)}) copy-start(bf16[128,2560]{1,0:T(8,128)(2,1)} %copy-done.7) | copy-start | bytes 1966084
  80.9 5.9 %copy-start.10 = (bf16[128,2560]{1,0:T(8,128)(2,1)S(1)}, bf16[128,2560]{1,0:T(8,128)(2,1)}, u32[]{:S(2)}) copy-start(bf16[128,2560]{1,0:T(8,128)(2,1)} %copy-done.9) | copy-start | bytes 1966084
  80.9 5.9 %copy-start.12 = (bf16[128,2560]{1,0:T(8,128)(2,1)S(1)}, bf16[128,2560]{1,0:T(8,128)(2,1)}, u32[]{:S(2)}) copy-start(bf16[128,2560]{1,0:T(8,128)(2,1)} %copy-done.11) | copy-start | bytes 1966084
  85.4 35.2 %collective-permute-start.17 = (bf16[128,2560]{1,0:T(8,128)(2,1)S(1)}, bf16[128,2560]{1,0:T(8,128)(2,1)S(1)}, u32[]{:S(2)}, u32[]{:S(2)}) collective-permute-start(bf16[128,2560]{1,0:T(8,128)(2,1)S(1)} %slice.122), channel_id=1, source_target_pairs={{2,0},{4,6},{3,1},{5,7},{10,8},{12,14},{11,9},{13,15},{18,16},{20,... | collective-permute-start | bytes 1966088 | tf_op jit(solution)/shard_map/ppermute | solution.py:56
  102.8 6.8 %collective-permute-start.14 = (bf16[576,256]{1,0:T(8,128)(2,1)S(1)}, bf16[576,256]{1,0:T(8,128)(2,1)S(1)}, u32[]{:S(2)}, u32[]{:S(2)}) collective-permute-start(bf16[576,256]{1,0:T(8,128)(2,1)S(1)} %fusion.21), channel_id=1, source_target_pairs={{0,1},{1,0},{2,3},{3,2},{4,5},{5,4},{6,7},{7,6},{8,9},{9,8},{10,11... | collective-permute-start | bytes 884744 | tf_op jit(solution)/shard_map/ppermute | solution.py:60
  104.8 5.9 %collective-permute-start.16 = (bf16[192,256]{1,0:T(8,128)(2,1)S(1)}, bf16[192,256]{1,0:T(8,128)(2,1)S(1)}, u32[]{:S(2)}, u32[]{:S(2)}) collective-permute-start(bf16[192,256]{1,0:T(8,128)(2,1)S(1)} %fusion.22), channel_id=1, source_target_pairs={{0,1},{1,0},{2,3},{3,2},{4,5},{5,4},{6,7},{7,6},{8,9},{9,8},{10,11... | collective-permute-start | bytes 294920 | tf_op jit(solution)/shard_map/ppermute | solution.py:60
  107.6 34.8 %collective-permute-start.26 = (bf16[128,1536]{1,0:T(8,128)(2,1)S(1)}, bf16[128,1536]{1,0:T(8,128)(2,1)S(1)}, u32[]{:S(2)}, u32[]{:S(2)}) collective-permute-start(bf16[128,1536]{1,0:T(8,128)(2,1)S(1)} %slice.135), channel_id=1, source_target_pairs={{2,0},{4,6},{3,1},{5,7},{10,8},{12,14},{11,9},{13,15},{18,16},{20,... | collective-permute-start | bytes 1179656 | tf_op jit(solution)/shard_map/ppermute | solution.py:56
  120.7 0.8 collective-permute-start.18
  121.4 1.2 copy-start.13
  121.4 1.5 copy-start.15
  124.0 12.2 %collective-permute-start.19 = (bf16[192,512]{1,0:T(8,128)(2,1)S(1)}, bf16[192,512]{1,0:T(8,128)(2,1)S(1)}, u32[]{:S(2)}, u32[]{:S(2)}) collective-permute-start(bf16[192,512]{1,0:T(8,128)(2,1)S(1)} %slice.124), channel_id=1, source_target_pairs={{2,0},{4,6},{3,1},{5,7},{10,8},{12,14},{11,9},{13,15},{18,16},{20,... | collective-permute-start | bytes 589832 | tf_op jit(solution)/shard_map/ppermute | solution.py:56
  125.3 13.6 %collective-permute-start.21 = (bf16[128,1024]{1,0:T(8,128)(2,1)S(1)}, bf16[128,1024]{1,0:T(8,128)(2,1)S(1)}, u32[]{:S(2)}, u32[]{:S(2)}) collective-permute-start(bf16[128,1024]{1,0:T(8,128)(2,1)S(1)} %slice.130), channel_id=1, source_target_pairs={{2,4},{4,2},{3,5},{5,3},{10,12},{12,10},{11,13},{13,11},{18,20},{2... | collective-permute-start | bytes 786440 | tf_op jit(solution)/shard_map/ppermute | solution.py:52
  126.0 15.0 %collective-permute-start.24 = (bf16[128,1536]{1,0:T(8,128)(2,1)S(1)}, bf16[128,1536]{1,0:T(8,128)(2,1)S(1)}, u32[]{:S(2)}, u32[]{:S(2)}) collective-permute-start(bf16[128,1536]{1,0:T(8,128)(2,1)S(1)} %slice.132), channel_id=1, source_target_pairs={{2,4},{4,2},{3,5},{5,3},{10,12},{12,10},{11,13},{13,11},{18,20},{2... | collective-permute-start | bytes 1179656 | tf_op jit(solution)/shard_map/ppermute | solution.py:52
  137.0 13.5 %collective-permute-start.20 = (bf16[192,2560]{1,0:T(8,128)(2,1)S(1)}, bf16[192,2560]{1,0:T(8,128)(2,1)S(1)}, u32[]{:S(2)}, u32[]{:S(2)}) collective-permute-start(bf16[192,2560]{1,0:T(8,128)(2,1)S(1)} %convolution_convert_fusion.1), channel_id=1, source_target_pairs={{8,0},{16,8},{24,16},{9,1},{17,9},{25,17},{10,2},{18,10},{26,18},{... | collective-permute-start | bytes 2949128 | tf_op jit(solution)/shard_map/ppermute | solution.py:13
  139.0 11.5 %collective-permute-start.23 = (bf16[128,1024]{1,0:T(8,128)(2,1)S(1)}, bf16[128,1024]{1,0:T(8,128)(2,1)S(1)}, u32[]{:S(2)}, u32[]{:S(2)}) collective-permute-start(bf16[128,1024]{1,0:T(8,128)(2,1)S(1)} %add_convert_fusion.2), channel_id=1, source_target_pairs={{2,0},{4,6},{3,1},{5,7},{10,8},{12,14},{11,9},{13,15},{18,16},{20,... | collective-permute-start | bytes 786440 | tf_op jit(solution)/shard_map/ppermute | solution.py:56
  140.3 3.3 %collective-permute-start.22 = (bf16[128,2560]{1,0:T(8,128)(2,1)S(1)}, bf16[128,2560]{1,0:T(8,128)(2,1)S(1)}, u32[]{:S(2)}, u32[]{:S(2)}) collective-permute-start(bf16[128,2560]{1,0:T(8,128)(2,1)S(1)} %convolution_convert_fusion.4), channel_id=1, source_target_pairs={{2,4},{4,2},{3,5},{5,3},{10,12},{12,10},{11,13},{13,11},{18,20},{2... | collective-permute-start | bytes 1966088 | tf_op jit(solution)/shard_map/ppermute | solution.py:52
  141.1 17.4 %collective-permute-start.25 = (bf16[128,1536]{1,0:T(8,128)(2,1)S(1)}, bf16[128,1536]{1,0:T(8,128)(2,1)S(1)}, u32[]{:S(2)}, u32[]{:S(2)}) collective-permute-start(bf16[128,1536]{1,0:T(8,128)(2,1)S(1)} %add_convert_fusion.1), channel_id=1, source_target_pairs={{2,0},{4,6},{3,1},{5,7},{10,8},{12,14},{11,9},{13,15},{18,16},{20,... | collective-permute-start | bytes 1179656 | tf_op jit(solution)/shard_map/ppermute | solution.py:56

commit v17 on v14

--- a/solution.py
+++ b/solution.py
@@ -140,14 +140,16 @@
     latent_there = outward(latent_bf[rows:])
     latent_used = jnp.where(middle, latent_bf[:rows], latent_there)
 
+    sent_end = tokens_dot(latent_bf[:, 3 * lat :], tokens_mine).astype(BF16)
+    latent_late = after(latent_bf, latent_there)
     sums = [
-        tokens_dot(latent_bf[:, j * lat : (j + 1) * lat], tokens_mine).astype(BF16)
-        for j in range(4)
+        tokens_dot(latent_late[:, j * lat : (j + 1) * lat], tokens_mine).astype(BF16)
+        for j in range(3)
     ]
     width = tokens.shape[1]
     first = width * 2 // 5 // 128 * 128
     halves = (slice(0, first), slice(first, width))
-    sent_end, sent_own = sums[3], sums[2]
+    sent_own = sums[2]
     from_end = [across(sent_end[:, half]) for half in halves]
     end_first = (sums[1][:, halves[0]] + from_end[0].astype(F32)).astype(BF16)
     from_own = across(after(sent_own, end_first))

time: 160 us -> 160 us (level)
    ppermute x8, waiting for transfers between devices: 29.2 us -> 31.3 us  [outward(): return lax.ppermute(value, 'row', [(1, 0), (2, 3)])]
where the time goes in v17:
time: 160 us; the launch traced here: 158 us
  waiting for transfers between devices  90.9 us (57%)
  starting transfers between devices  45.8 us (29%)
  matrix products  12.4 us (8%)
  local copies, waits for them, and re-layouts  4.1 us (3%)
  other arithmetic  3.1 us (2%)
    ppermute x5, waiting for transfers between devices, inward(): return lax.ppermute(value, 'row', [(0, 1), (3, 2)])  48.1 us
    ppermute x8, waiting for transfers between devices, outward(): return lax.ppermute(value, 'row', [(1, 0), (2, 3)])  31.3 us
    ppermute x5, starting transfers between devices, inward(): return lax.ppermute(value, 'row', [(0, 1), (3, 2)])  22 us
    ppermute x8, starting transfers between devices, outward(): return lax.ppermute(value, 'row', [(1, 0), (2, 3)])  10.3 us
    ppermute x10, starting transfers between devices, across(): return lax.ppermute(value, 'row', [(1, 2), (2, 1)])  6.95 us
    dot_general x6, matrix products, tokens_dot(): lax.dot_general(left, right, (((0,), (0,)), ((), ())), preferred_element_...  6.77 us
    ppermute x1, waiting for transfers between devices, shifted(): lax.ppermute(value, axis, [(source, source + steps) for source in range(l...  5.86 us
    ppermute x3, waiting for transfers between devices, other_col(): return lax.ppermute(value, 'col', [(0, 1), (1, 0)])  5.62 us
  transfers between devices with their start and end apart: 27, of which 15 were waited for; matrix products, arithmetic and copies ran while one was open for 11% of the time, Pallas kernels for 0%

profile of v17, /device:TPU:4, one launch (start us, length us, event | category | flops | bytes accessed | tf_op | source)
XLA Modules:
  0.0 157.6 jit_solution(3670384156494222169)
XLA Ops:
  0.7 3.7 %collective-permute-start.2 = (bf16[128,2560]{1,0:T(8,128)(2,1)}, bf16[128,2560]{1,0:T(8,128)(2,1)S(1)}, u32[]{:S(2)}, u32[]{:S(2)}) collective-permute-start(bf16[128,2560]{1,0:T(8,128)(2,1)} %bitcast.19), channel_id=1, source_target_pairs={{0,2},{6,4},{1,3},{7,5},{8,10},{14,12},{9,11},{15,13},{16,18},{22,... | collective-permute-start | bytes 1966088 | tf_op jit(solution)/shard_map/ppermute | solution.py:48
  4.3 1.4 collective-permute-start
  5.7 1.3 collective-permute-start.1
  7.0 0.7 collective-permute-start.3
  7.7 12.0 %collective-permute-done.2 = bf16[128,2560]{1,0:T(8,128)(2,1)S(1)} collective-permute-done((bf16[128,2560]{1,0:T(8,128)(2,1)}, bf16[128,2560]{1,0:T(8,128)(2,1)S(1)}, u32[]{:S(2)}, u32[]{:S(2)}) %collective-permute-start.2) | collective-permute-done | bytes 655392 | tf_op jit(solution)/shard_map/ppermute | solution.py:48
  19.7 0.7 collective-permute-start.4
  20.4 0.8 collective-permute-start.7
  21.2 2.7 %fusion.44 = (bf16[192,2048]{1,0:T(8,128)(2,1)}, bf16[192,2048]{1,0:T(8,128)(2,1)}) fusion(bf16[192,4096]{1,0:T(8,128)(2,1)} %bitcast.13), kind=kLoop, calls=%fused_computation.73 | loop fusion | bytes 3145728 | tf_op jit(solution)/shard_map/slice | solution.py:119
  23.9 0.1 collective-permute-done.1
  24.0 9.5 %collective-permute-start.6 = (bf16[192,2048]{1,0:T(8,128)(2,1)}, bf16[192,2048]{1,0:T(8,128)(2,1)}, u32[]{:S(2)}, u32[]{:S(2)}) collective-permute-start(bf16[192,2048]{1,0:T(8,128)(2,1)} %get-tuple-element.34), channel_id=1, source_target_pairs={{0,2},{6,4},{1,3},{7,5},{8,10},{14,12},{9,11},{15,13},{16,18},{22,... | collective-permute-start | bytes 2359304 | tf_op jit(solution)/shard_map/ppermute | solution.py:48
  33.4 7.3 %collective-permute-done = bf16[192,2560]{1,0:T(8,128)(2,1)S(1)} collective-permute-done((bf16[192,2560]{1,0:T(8,128)(2,1)}, bf16[192,2560]{1,0:T(8,128)(2,1)S(1)}, u32[]{:S(2)}, u32[]{:S(2)}) %collective-permute-start) | collective-permute-done | bytes 983072 | tf_op jit(solution)/shard_map/ppermute | solution.py:48
  40.8 1.2 convolution_convert_fusion.6
  42.1 0.1 copy-done.10
  42.2 1.5 collective-permute-start.5
  43.7 4.6 %collective-permute-start.13 = (bf16[192,2048]{1,0:T(8,128)(2,1)}, bf16[192,2048]{1,0:T(8,128)(2,1)S(1)}, u32[]{:S(2)}, u32[]{:S(2)}) collective-permute-start(bf16[192,2048]{1,0:T(8,128)(2,1)} %get-tuple-element.22), channel_id=1, source_target_pairs={{0,2},{6,4},{1,3},{7,5},{8,10},{14,12},{9,11},{15,13},{16,18},{22,... | collective-permute-start | bytes 2359304 | tf_op jit(solution)/shard_map/ppermute | solution.py:48
  48.3 1.3 collective-permute-start.10
  49.6 8.1 %collective-permute-done.6 = bf16[192,2048]{1,0:T(8,128)(2,1)} collective-permute-done((bf16[192,2048]{1,0:T(8,128)(2,1)}, bf16[192,2048]{1,0:T(8,128)(2,1)}, u32[]{:S(2)}, u32[]{:S(2)}) %collective-permute-start.6) | collective-permute-done | bytes 786464 | tf_op jit(solution)/shard_map/ppermute | solution.py:48
  57.6 0.7 collective-permute-start.8
  58.3 1.3 collective-permute-start.12
  59.6 0.2 multiply_reduce_fusion.1
  59.9 0.1 fusion.26
  60.0 4.4 %collective-permute-done.10 = bf16[128,2560]{1,0:T(8,128)(2,1)S(1)} collective-permute-done((bf16[128,2560]{1,0:T(8,128)(2,1)}, bf16[128,2560]{1,0:T(8,128)(2,1)S(1)}, u32[]{:S(2)}, u32[]{:S(2)}) %collective-permute-start.10) | collective-permute-done | bytes 655392 | tf_op jit(solution)/shard_map/ppermute | solution.py:56
  64.4 2.9 %collective-permute-start.9 = (bf16[128,4096]{1,0:T(8,128)(2,1)S(1)}, bf16[128,4096]{1,0:T(8,128)(2,1)S(1)}, u32[]{:S(2)}, u32[]{:S(2)}) collective-permute-start(bf16[128,4096]{1,0:T(8,128)(2,1)S(1)} %bitcast.14), channel_id=1, source_target_pairs={{0,2},{6,4},{1,3},{7,5},{8,10},{14,12},{9,11},{15,13},{16,18},{22,... | collective-permute-start | bytes 3145736 | tf_op jit(solution)/shard_map/ppermute | solution.py:48
  67.3 0.7 collective-permute-start.11
  68.0 0.1 fusion.43
  68.1 6.3 %collective-permute-done.13 = bf16[192,2048]{1,0:T(8,128)(2,1)S(1)} collective-permute-done((bf16[192,2048]{1,0:T(8,128)(2,1)}, bf16[192,2048]{1,0:T(8,128)(2,1)S(1)}, u32[]{:S(2)}, u32[]{:S(2)}) %collective-permute-start.13) | collective-permute-done | bytes 786464 | tf_op jit(solution)/shard_map/ppermute | solution.py:48
  74.5 0.7 collective-permute-start.15
  75.2 2.8 %collective-permute-done.12 = bf16[128,2560]{1,0:T(8,128)(2,1)S(1)} collective-permute-done((bf16[128,2560]{1,0:T(8,128)(2,1)}, bf16[128,2560]{1,0:T(8,128)(2,1)S(1)}, u32[]{:S(2)}, u32[]{:S(2)}) %collective-permute-start.12) | collective-permute-done | bytes 655392 | tf_op jit(solution)/shard_map/ppermute | solution.py:56
  78.1 2.5 %convolution_convert_fusion.5 = bf16[256,2048]{1,0:T(8,128)(2,1)S(1)} fusion(bf16[768,256]{1,0:T(8,128)(2,1)S(1)} %pad_maximum_fusion.8, bf16[192,2048]{1,0:T(8,128)(2,1)S(1)} %collective-permute-done.8, bf16[192,2048]{1,0:T(8,128)(2,1)S(1)} %get-tuple-element.32, bf16[192,2048]{1,0:T(8,128)(2,1)} %collective-permute-done.6, ...), kind=kOutput, calls=%fused_computation.22 | convolution fusion | flops 818413568 | bytes 4587520 | tf_op jit(solution)/shard_map/dot_general | solution.py:72
  80.7 0.7 maximum_select_fusion
  81.4 14.3 %collective-permute-done.9 = bf16[128,4096]{1,0:T(8,128)(2,1)S(1)} collective-permute-done((bf16[128,4096]{1,0:T(8,128)(2,1)S(1)}, bf16[128,4096]{1,0:T(8,128)(2,1)S(1)}, u32[]{:S(2)}, u32[]{:S(2)}) %collective-permute-start.9) | collective-permute-done | bytes 1048608 | tf_op jit(solution)/shard_map/ppermute | solution.py:48
  95.7 2.4 %fusion.23 = f32[768,256]{1,0:T(8,128)S(1)} fusion(bf16[128,4096]{1,0:T(8,128)(2,1)S(1)} %bitcast.15, bf16[128,4096]{1,0:T(8,128)(2,1)S(1)} %collective-permute-done.9, bf16[192,2048]{1,0:T(8,128)(2,1)S(1)} %collective-permute-done.8, bf16[192,2048]{1,0:T(8,128)(2,1)S(1)} %get-tuple-element.32, bf16[192,2048]{1,0:T(8,128)(2,1)} %collective-permute-done.6, ...), kind=kOutput, calls=%fused_computation.34 | convolution fusion | flops 819986432 | bytes 6029312 | tf_op jit(solution)/shard_map/dot_general | solution.py:68
  98.1 0.9 fusion.27
  99.0 1.6 collective-permute-start.14
  100.6 1.3 collective-permute-start.17
  101.9 5.0 %collective-permute-done.14 = bf16[576,256]{1,0:T(8,128)(2,1)S(1)} collective-permute-done((bf16[576,256]{1,0:T(8,128)(2,1)S(1)}, bf16[576,256]{1,0:T(8,128)(2,1)S(1)}, u32[]{:S(2)}, u32[]{:S(2)}) %collective-permute-start.14) | collective-permute-done | bytes 294944 | tf_op jit(solution)/shard_map/ppermute | solution.py:60
  107.1 0.5 fusion.28
  107.6 1.6 collective-permute-start.16
  109.1 1.2 fusion.13
  110.4 1.3 collective-permute-start.26
  111.7 0.6 collective-permute-done.16
  112.3 4.0 %collective-permute-done.17 = bf16[128,2048]{1,0:T(8,128)(2,1)S(1)} collective-permute-done((bf16[128,2048]{1,0:T(8,128)(2,1)S(1)}, bf16[128,2048]{1,0:T(8,128)(2,1)S(1)}, u32[]{:S(2)}, u32[]{:S(2)}) %collective-permute-start.17) | collective-permute-done | bytes 524320 | tf_op jit(solution)/shard_map/ppermute | solution.py:56
  116.3 0.7 collective-permute-start.18
  117.1 0.3 multiply_reduce_fusion
  117.4 0.2 multiply_convert_fusion
  117.7 1.3 collective-permute-start.19
  119.0 0.5 convolution_convert_fusion.1
  119.6 0.7 collective-permute-start.21
  120.3 0.7 collective-permute-start.24
  121.0 11.3 %collective-permute-done.19 = bf16[192,512]{1,0:T(8,128)(2,1)S(1)} collective-permute-done((bf16[192,512]{1,0:T(8,128)(2,1)S(1)}, bf16[192,512]{1,0:T(8,128)(2,1)S(1)}, u32[]{:S(2)}, u32[]{:S(2)}) %collective-permute-start.19) | collective-permute-done | bytes 196640 | tf_op jit(solution)/shard_map/ppermute | solution.py:56
  132.3 0.7 convolution_convert_fusion
  133.0 1.9 %collective-permute-start.20 = (bf16[192,2560]{1,0:T(8,128)(2,1)S(1)}, bf16[192,2560]{1,0:T(8,128)(2,1)S(1)}, u32[]{:S(2)}, u32[]{:S(2)}) collective-permute-start(bf16[192,2560]{1,0:T(8,128)(2,1)S(1)} %convolution_convert_fusion), channel_id=1, source_target_pairs={{8,0},{16,8},{24,16},{9,1},{17,9},{25,17},{10,2},{18,10},{26,18},{... | collective-permute-start | bytes 2949128 | tf_op jit(solution)/shard_map/ppermute | solution.py:13
  134.9 0.5 convolution_convert_fusion.3
  135.5 0.5 convolution_convert_fusion.2
  136.1 1.3 collective-permute-start.23
  137.4 0.7 collective-permute-start.22
  138.1 0.1 add_convert_fusion
  138.2 1.3 collective-permute-start.25
  139.6 1.1 maximum_bitcast_fusion
  140.7 5.9 %collective-permute-done.20 = bf16[192,2560]{1,0:T(8,128)(2,1)S(1)} collective-permute-done((bf16[192,2560]{1,0:T(8,128)(2,1)S(1)}, bf16[192,2560]{1,0:T(8,128)(2,1)S(1)}, u32[]{:S(2)}, u32[]{:S(2)}) %collective-permute-start.20) | collective-permute-done | bytes 983072 | tf_op jit(solution)/shard_map/ppermute | solution.py:13
  146.5 1.1 collective-permute-done.23
  147.7 7.5 %collective-permute-done.25 = bf16[128,1536]{1,0:T(8,128)(2,1)S(1)} collective-permute-done((bf16[128,1536]{1,0:T(8,128)(2,1)S(1)}, bf16[128,1536]{1,0:T(8,128)(2,1)S(1)}, u32[]{:S(2)}, u32[]{:S(2)}) %collective-permute-start.25) | collective-permute-done | bytes 393248 | tf_op jit(solution)/shard_map/ppermute | solution.py:56
  155.2 1.4 fusion.4
  156.6 0.9 copy.8
  (61 shorter events, 0.7 us)
Async XLA Ops:
  0.6 40.2 %copy-start.2 = (bf16[1,128,2560]{2,1,0:T(8,128)(2,1)S(1)}, bf16[1,128,2560]{2,1,0:T(8,128)(2,1)}, u32[]{:S(2)}) copy-start(bf16[1,128,2560]{2,1,0:T(8,128)(2,1)} %param.5) | copy-start | bytes 1966084
  0.6 40.2 %copy-start.12 = (bf16[1,192,2560]{2,1,0:T(8,128)(2,1)S(1)}, bf16[1,192,2560]{2,1,0:T(8,128)(2,1)}, u32[]{:S(2)}) copy-start(bf16[1,192,2560]{2,1,0:T(8,128)(2,1)} %param.4) | copy-start | bytes 2949124
  0.7 19.1 %collective-permute-start.2 = (bf16[128,2560]{1,0:T(8,128)(2,1)}, bf16[128,2560]{1,0:T(8,128)(2,1)S(1)}, u32[]{:S(2)}, u32[]{:S(2)}) collective-permute-start(bf16[128,2560]{1,0:T(8,128)(2,1)} %bitcast.19), channel_id=1, source_target_pairs={{0,2},{6,4},{1,3},{7,5},{8,10},{14,12},{9,11},{15,13},{16,18},{22,... | collective-permute-start | bytes 1966088 | tf_op jit(solution)/shard_map/ppermute | solution.py:48
  4.3 36.5 %collective-permute-start = (bf16[192,2560]{1,0:T(8,128)(2,1)}, bf16[192,2560]{1,0:T(8,128)(2,1)S(1)}, u32[]{:S(2)}, u32[]{:S(2)}) collective-permute-start(bf16[192,2560]{1,0:T(8,128)(2,1)} %bitcast.24), channel_id=1, source_target_pairs={{0,2},{6,4},{1,3},{7,5},{8,10},{14,12},{9,11},{15,13},{16,18},{22,... | collective-permute-start | bytes 2949128 | tf_op jit(solution)/shard_map/ppermute | solution.py:48
  5.7 18.3 %collective-permute-start.1 = (bf16[128,2560]{1,0:T(8,128)(2,1)}, bf16[128,2560]{1,0:T(8,128)(2,1)S(1)}, u32[]{:S(2)}, u32[]{:S(2)}) collective-permute-start(bf16[128,2560]{1,0:T(8,128)(2,1)} %bitcast.20), channel_id=1, source_target_pairs={{2,0},{4,6},{3,1},{5,7},{10,8},{12,14},{11,9},{13,15},{18,16},{20,... | collective-permute-start | bytes 1966088 | tf_op jit(solution)/shard_map/ppermute | solution.py:56
  7.0 33.8 %collective-permute-start.3 = (bf16[128,2560]{1,0:T(8,128)(2,1)}, bf16[128,2560]{1,0:T(8,128)(2,1)S(1)}, u32[]{:S(2)}, u32[]{:S(2)}) collective-permute-start(bf16[128,2560]{1,0:T(8,128)(2,1)} %bitcast.21), channel_id=1, source_target_pairs={{2,4},{4,2},{3,5},{5,3},{10,12},{12,10},{11,13},{13,11},{18,20},{2... | collective-permute-start | bytes 1966088 | tf_op jit(solution)/shard_map/ppermute | solution.py:52
  19.7 22.3 %copy-start.4 = (bf16[128,2560]{1,0:T(8,128)(2,1)}, bf16[128,2560]{1,0:T(8,128)(2,1)S(1)}, u32[]{:S(2)}) copy-start(bf16[128,2560]{1,0:T(8,128)(2,1)S(1)} %collective-permute-done.2) | copy-start | bytes 1966084
  19.7 21.1 %collective-permute-start.4 = (bf16[128,2560]{1,0:T(8,128)(2,1)S(1)}, bf16[128,2560]{1,0:T(8,128)(2,1)S(1)}, u32[]{:S(2)}, u32[]{:S(2)}) collective-permute-start(bf16[128,2560]{1,0:T(8,128)(2,1)S(1)} %collective-permute-done.2), channel_id=1, source_target_pairs={{2,4},{4,2},{3,5},{5,3},{10,12},{12,10},{11,13},{13,11},{18,20},{2... | collective-permute-start | bytes 1966088 | tf_op jit(solution)/shard_map/ppermute | solution.py:52
  20.4 46.9 %collective-permute-start.7 = (bf16[192,4096]{1,0:T(8,128)(2,1)}, bf16[192,4096]{1,0:T(8,128)(2,1)S(1)}, u32[]{:S(2)}, u32[]{:S(2)}) collective-permute-start(bf16[192,4096]{1,0:T(8,128)(2,1)} %bitcast.12), channel_id=1, source_target_pairs={{2,4},{4,2},{3,5},{5,3},{10,12},{12,10},{11,13},{13,11},{18,20},{2... | collective-permute-start | bytes 4718600 | tf_op jit(solution)/shard_map/ppermute | solution.py:52
  24.0 16.8 %copy-start.6 = (bf16[128,2560]{1,0:T(8,128)(2,1)}, bf16[128,2560]{1,0:T(8,128)(2,1)S(1)}, u32[]{:S(2)}) copy-start(bf16[128,2560]{1,0:T(8,128)(2,1)S(1)} %collective-permute-done.1) | copy-start | bytes 1966084
  24.0 33.6 %collective-permute-start.6 = (bf16[192,2048]{1,0:T(8,128)(2,1)}, bf16[192,2048]{1,0:T(8,128)(2,1)}, u32[]{:S(2)}, u32[]{:S(2)}) collective-permute-start(bf16[192,2048]{1,0:T(8,128)(2,1)} %get-tuple-element.34), channel_id=1, source_target_pairs={{0,2},{6,4},{1,3},{7,5},{8,10},{14,12},{9,11},{15,13},{16,18},{22,... | collective-permute-start | bytes 2359304 | tf_op jit(solution)/shard_map/ppermute | solution.py:48
  40.8 1.3 copy-start.14
  40.8 1.3 copy-start.8
  40.8 1.3 copy-start.10
  42.2 22.3 %copy-start = (bf16[1,128,4096]{2,1,0:T(8,128)(2,1)S(1)}, bf16[1,128,4096]{2,1,0:T(8,128)(2,1)}, u32[]{:S(2)}) copy-start(bf16[1,128,4096]{2,1,0:T(8,128)(2,1)} %param.6) | copy-start | bytes 3145732
  42.2 16.2 %collective-permute-start.5 = (bf16[384,512]{1,0:T(8,128)(2,1)S(1)}, bf16[384,512]{1,0:T(8,128)(2,1)S(1)}, u32[]{:S(2)}, u32[]{:S(2)}) collective-permute-start(bf16[384,512]{1,0:T(8,128)(2,1)S(1)} %convolution_convert_fusion.6), channel_id=1, source_target_pairs={{0,1},{1,0},{2,3},{3,2},{4,5},{5,4},{6,7},{7,6},{8,9},{9,8},{10,11... | collective-permute-start | bytes 1179656 | tf_op jit(solution)/shard_map/ppermute | solution.py:60
  43.7 30.8 %collective-permute-start.13 = (bf16[192,2048]{1,0:T(8,128)(2,1)}, bf16[192,2048]{1,0:T(8,128)(2,1)S(1)}, u32[]{:S(2)}, u32[]{:S(2)}) collective-permute-start(bf16[192,2048]{1,0:T(8,128)(2,1)} %get-tuple-element.22), channel_id=1, source_target_pairs={{0,2},{6,4},{1,3},{7,5},{8,10},{14,12},{9,11},{15,13},{16,18},{22,... | collective-permute-start | bytes 2359304 | tf_op jit(solution)/shard_map/ppermute | solution.py:48
  48.3 16.2 %collective-permute-start.10 = (bf16[128,2560]{1,0:T(8,128)(2,1)}, bf16[128,2560]{1,0:T(8,128)(2,1)S(1)}, u32[]{:S(2)}, u32[]{:S(2)}) collective-permute-start(bf16[128,2560]{1,0:T(8,128)(2,1)} %copy-done.8), channel_id=1, source_target_pairs={{2,0},{4,6},{3,1},{5,7},{10,8},{12,14},{11,9},{13,15},{18,16},{20,... | collective-permute-start | bytes 1966088 | tf_op jit(solution)/shard_map/ppermute | solution.py:56
  57.6 20.4 %collective-permute-start.8 = (bf16[192,2048]{1,0:T(8,128)(2,1)}, bf16[192,2048]{1,0:T(8,128)(2,1)S(1)}, u32[]{:S(2)}, u32[]{:S(2)}) collective-permute-start(bf16[192,2048]{1,0:T(8,128)(2,1)} %collective-permute-done.6), channel_id=1, source_target_pairs={{2,4},{4,2},{3,5},{5,3},{10,12},{12,10},{11,13},{13,11},{18,20},{2... | collective-permute-start | bytes 2359304 | tf_op jit(solution)/shard_map/ppermute | solution.py:52
  58.3 19.7 %collective-permute-start.12 = (bf16[128,2560]{1,0:T(8,128)(2,1)}, bf16[128,2560]{1,0:T(8,128)(2,1)S(1)}, u32[]{:S(2)}, u32[]{:S(2)}) collective-permute-start(bf16[128,2560]{1,0:T(8,128)(2,1)} %copy-done.10), channel_id=1, source_target_pairs={{2,0},{4,6},{3,1},{5,7},{10,8},{12,14},{11,9},{13,15},{18,16},{20,... | collective-permute-start | bytes 1966088 | tf_op jit(solution)/shard_map/ppermute | solution.py:56
  64.4 31.3 %collective-permute-start.9 = (bf16[128,4096]{1,0:T(8,128)(2,1)S(1)}, bf16[128,4096]{1,0:T(8,128)(2,1)S(1)}, u32[]{:S(2)}, u32[]{:S(2)}) collective-permute-start(bf16[128,4096]{1,0:T(8,128)(2,1)S(1)} %bitcast.14), channel_id=1, source_target_pairs={{0,2},{6,4},{1,3},{7,5},{8,10},{14,12},{9,11},{15,13},{16,18},{22,... | collective-permute-start | bytes 3145736 | tf_op jit(solution)/shard_map/ppermute | solution.py:48
  67.3 7.8 %collective-permute-start.11 = (bf16[384,256]{1,0:T(8,128)(2,1)S(1)}, bf16[384,256]{1,0:T(8,128)(2,1)S(1)}, u32[]{:S(2)}, u32[]{:S(2)}) collective-permute-start(bf16[384,256]{1,0:T(8,128)(2,1)S(1)} %get-tuple-element.19), channel_id=1, source_target_pairs={{2,4},{4,2},{3,5},{5,3},{10,12},{12,10},{11,13},{13,11},{18,20},{2... | collective-permute-start | bytes 589832 | tf_op jit(solution)/shard_map/ppermute | solution.py:52
  74.5 32.6 %collective-permute-start.15 = (bf16[192,2048]{1,0:T(8,128)(2,1)S(1)}, bf16[192,2048]{1,0:T(8,128)(2,1)S(1)}, u32[]{:S(2)}, u32[]{:S(2)}) collective-permute-start(bf16[192,2048]{1,0:T(8,128)(2,1)S(1)} %collective-permute-done.13), channel_id=1, source_target_pairs={{2,4},{4,2},{3,5},{5,3},{10,12},{12,10},{11,13},{13,11},{18,20},{2... | collective-permute-start | bytes 2359304 | tf_op jit(solution)/shard_map/ppermute | solution.py:52
  78.0 2.6 %copy-start.3 = (bf16[1,128,2560]{2,1,0:T(8,128)(2,1)S(1)}, bf16[1,128,2560]{2,1,0:T(8,128)(2,1)}, u32[]{:S(2)}) copy-start(bf16[1,128,2560]{2,1,0:T(8,128)(2,1)} %param.5) | copy-start | bytes 1966084
  78.0 2.6 %copy-start.5 = (bf16[128,2560]{1,0:T(8,128)(2,1)S(1)}, bf16[128,2560]{1,0:T(8,128)(2,1)}, u32[]{:S(2)}) copy-start(bf16[128,2560]{1,0:T(8,128)(2,1)} %copy-done.4) | copy-start | bytes 1966084
  78.0 2.6 %copy-start.7 = (bf16[128,2560]{1,0:T(8,128)(2,1)S(1)}, bf16[128,2560]{1,0:T(8,128)(2,1)}, u32[]{:S(2)}) copy-start(bf16[128,2560]{1,0:T(8,128)(2,1)} %copy-done.6) | copy-start | bytes 1966084
  78.0 2.6 %copy-start.9 = (bf16[128,2560]{1,0:T(8,128)(2,1)S(1)}, bf16[128,2560]{1,0:T(8,128)(2,1)}, u32[]{:S(2)}) copy-start(bf16[128,2560]{1,0:T(8,128)(2,1)} %copy-done.8) | copy-start | bytes 1966084
  78.1 2.6 %copy-start.11 = (bf16[128,2560]{1,0:T(8,128)(2,1)S(1)}, bf16[128,2560]{1,0:T(8,128)(2,1)}, u32[]{:S(2)}) copy-start(bf16[128,2560]{1,0:T(8,128)(2,1)} %copy-done.10) | copy-start | bytes 1966084
  81.4 16.7 %copy-start.1 = (bf16[192,2048]{1,0:T(8,128)(2,1)S(1)}, bf16[192,2048]{1,0:T(8,128)(2,1)}, u32[]{:S(2)}) copy-start(bf16[192,2048]{1,0:T(8,128)(2,1)} %get-tuple-element.22) | copy-start | bytes 2359300
  99.0 7.9 %collective-permute-start.14 = (bf16[576,256]{1,0:T(8,128)(2,1)S(1)}, bf16[576,256]{1,0:T(8,128)(2,1)S(1)}, u32[]{:S(2)}, u32[]{:S(2)}) collective-permute-start(bf16[576,256]{1,0:T(8,128)(2,1)S(1)} %fusion.27), channel_id=1, source_target_pairs={{0,1},{1,0},{2,3},{3,2},{4,5},{5,4},{6,7},{7,6},{8,9},{9,8},{10,11... | collective-permute-start | bytes 884744 | tf_op jit(solution)/shard_map/ppermute | solution.py:60
  100.6 15.7 %collective-permute-start.17 = (bf16[128,2048]{1,0:T(8,128)(2,1)S(1)}, bf16[128,2048]{1,0:T(8,128)(2,1)S(1)}, u32[]{:S(2)}, u32[]{:S(2)}) collective-permute-start(bf16[128,2048]{1,0:T(8,128)(2,1)S(1)} %slice.122), channel_id=1, source_target_pairs={{2,0},{4,6},{3,1},{5,7},{10,8},{12,14},{11,9},{13,15},{18,16},{20,... | collective-permute-start | bytes 1572872 | tf_op jit(solution)/shard_map/ppermute | solution.py:56
  107.6 4.7 %collective-permute-start.16 = (bf16[192,256]{1,0:T(8,128)(2,1)S(1)}, bf16[192,256]{1,0:T(8,128)(2,1)S(1)}, u32[]{:S(2)}, u32[]{:S(2)}) collective-permute-start(bf16[192,256]{1,0:T(8,128)(2,1)S(1)} %fusion.28), channel_id=1, source_target_pairs={{0,1},{1,0},{2,3},{3,2},{4,5},{5,4},{6,7},{7,6},{8,9},{9,8},{10,11... | collective-permute-start | bytes 294920 | tf_op jit(solution)/shard_map/ppermute | solution.py:60
  110.4 29.1 %collective-permute-start.26 = (bf16[128,2048]{1,0:T(8,128)(2,1)S(1)}, bf16[128,2048]{1,0:T(8,128)(2,1)S(1)}, u32[]{:S(2)}, u32[]{:S(2)}) collective-permute-start(bf16[128,2048]{1,0:T(8,128)(2,1)S(1)} %slice.132), channel_id=1, source_target_pairs={{2,0},{4,6},{3,1},{5,7},{10,8},{12,14},{11,9},{13,15},{18,16},{20,... | collective-permute-start | bytes 1572872 | tf_op jit(solution)/shard_map/ppermute | solution.py:56
  116.3 0.8 collective-permute-start.18
  117.1 1.9 %copy-start.13 = (bf16[1,192,2560]{2,1,0:T(8,128)(2,1)S(1)}, bf16[1,192,2560]{2,1,0:T(8,128)(2,1)}, u32[]{:S(2)}) copy-start(bf16[1,192,2560]{2,1,0:T(8,128)(2,1)} %param.4) | copy-start | bytes 2949124
  117.1 1.9 %copy-start.15 = (bf16[192,2560]{1,0:T(8,128)(2,1)S(1)}, bf16[192,2560]{1,0:T(8,128)(2,1)}, u32[]{:S(2)}) copy-start(bf16[192,2560]{1,0:T(8,128)(2,1)} %copy-done.14) | copy-start | bytes 2949124
  117.7 14.6 %collective-permute-start.19 = (bf16[192,512]{1,0:T(8,128)(2,1)S(1)}, bf16[192,512]{1,0:T(8,128)(2,1)S(1)}, u32[]{:S(2)}, u32[]{:S(2)}) collective-permute-start(bf16[192,512]{1,0:T(8,128)(2,1)S(1)} %slice.124), channel_id=1, source_target_pairs={{2,0},{4,6},{3,1},{5,7},{10,8},{12,14},{11,9},{13,15},{18,16},{20,... | collective-permute-start | bytes 589832 | tf_op jit(solution)/shard_map/ppermute | solution.py:56
  119.6 16.4 %collective-permute-start.21 = (bf16[128,1024]{1,0:T(8,128)(2,1)S(1)}, bf16[128,1024]{1,0:T(8,128)(2,1)S(1)}, u32[]{:S(2)}, u32[]{:S(2)}) collective-permute-start(bf16[128,1024]{1,0:T(8,128)(2,1)S(1)} %slice.127), channel_id=1, source_target_pairs={{2,4},{4,2},{3,5},{5,3},{10,12},{12,10},{11,13},{13,11},{18,20},{2... | collective-permute-start | bytes 786440 | tf_op jit(solution)/shard_map/ppermute | solution.py:52
  120.3 17.8 %collective-permute-start.24 = (bf16[128,1536]{1,0:T(8,128)(2,1)S(1)}, bf16[128,1536]{1,0:T(8,128)(2,1)S(1)}, u32[]{:S(2)}, u32[]{:S(2)}) collective-permute-start(bf16[128,1536]{1,0:T(8,128)(2,1)S(1)} %slice.129), channel_id=1, source_target_pairs={{2,4},{4,2},{3,5},{5,3},{10,12},{12,10},{11,13},{13,11},{18,20},{2... | collective-permute-start | bytes 1179656 | tf_op jit(solution)/shard_map/ppermute | solution.py:52
  133.0 13.5 %collective-permute-start.20 = (bf16[192,2560]{1,0:T(8,128)(2,1)S(1)}, bf16[192,2560]{1,0:T(8,128)(2,1)S(1)}, u32[]{:S(2)}, u32[]{:S(2)}) collective-permute-start(bf16[192,2560]{1,0:T(8,128)(2,1)S(1)} %convolution_convert_fusion), channel_id=1, source_target_pairs={{8,0},{16,8},{24,16},{9,1},{17,9},{25,17},{10,2},{18,10},{26,18},{... | collective-permute-start | bytes 2949128 | tf_op jit(solution)/shard_map/ppermute | solution.py:13
  136.1 11.6 %collective-permute-start.23 = (bf16[128,1024]{1,0:T(8,128)(2,1)S(1)}, bf16[128,1024]{1,0:T(8,128)(2,1)S(1)}, u32[]{:S(2)}, u32[]{:S(2)}) collective-permute-start(bf16[128,1024]{1,0:T(8,128)(2,1)S(1)} %add_convert_fusion.1), channel_id=1, source_target_pairs={{2,0},{4,6},{3,1},{5,7},{10,8},{12,14},{11,9},{13,15},{18,16},{20,... | collective-permute-start | bytes 786440 | tf_op jit(solution)/shard_map/ppermute | solution.py:56
  137.4 9.1 %collective-permute-start.22 = (bf16[128,2560]{1,0:T(8,128)(2,1)S(1)}, bf16[128,2560]{1,0:T(8,128)(2,1)S(1)}, u32[]{:S(2)}, u32[]{:S(2)}) collective-permute-start(bf16[128,2560]{1,0:T(8,128)(2,1)S(1)} %convolution_convert_fusion.3), channel_id=1, source_target_pairs={{2,4},{4,2},{3,5},{5,3},{10,12},{12,10},{11,13},{13,11},{18,20},{2... | collective-permute-start | bytes 1966088 | tf_op jit(solution)/shard_map/ppermute | solution.py:52
  138.2 17.0 %collective-permute-start.25 = (bf16[128,1536]{1,0:T(8,128)(2,1)S(1)}, bf16[128,1536]{1,0:T(8,128)(2,1)S(1)}, u32[]{:S(2)}, u32[]{:S(2)}) collective-permute-start(bf16[128,1536]{1,0:T(8,128)(2,1)S(1)} %add_convert_fusion), channel_id=1, source_target_pairs={{2,0},{4,6},{3,1},{5,7},{10,8},{12,14},{11,9},{13,15},{18,16},{20,... | collective-permute-start | bytes 1179656 | tf_op jit(solution)/shard_map/ppermute | solution.py:56
